TPU v7x, 32 devices: a whole 2x2x4 slice. The times are simulated.
32 devices in a mesh: gx: 16 (over z, x, core), gy: 2 (over y).
Axes of the slice: x: 2, y: 2, z: 4, core: 2. Of those that a mesh axis runs over, the one named last changes fastest.
Arguments:
- iterate: float32 [32, 384, 256], P(None, 'gx', 'gy'), may hold values from -6 to 6
- source: float32 [32, 384, 256], P(None, 'gx', 'gy'), may hold values from -8 to 8
- conduct: float32 [32, 384, 256], P(None, 'gx', 'gy'), may hold values from 0.2 to 5
Outputs:
- updated: float32 [32, 384, 256], P(None, 'gx', 'gy')
All inputs are finite; a program needn't handle non-finite values.
Results may differ from a plain program's by a relative error of at most 0.000041.
Values sent between devices are 32-bit elements; how exact they have to be, the bound alone decides.
No kernel may reach another device: no remote copies, remote signals or barrier semaphores. Data moves between devices by JAX's collectives and lax.ppermute only.
A program may use at most 64 MiB of HBM per device.

v0:
```python
import jax
import jax.numpy as jnp
from jax import lax
from jax.sharding import PartitionSpec as P

SWEEPS = 3
COARSE_SWEEPS = 4
COARSEN = 8


SHIFT = 0.1
LMIN = 0.3
LMAX = 2.0
OMEGA = 0.8


def extended(x, sides, width):
    for axis, dim in sides:
        size, length = (lax.axis_size(axis), x.shape[dim])
        up = [(i, (i + 1) % size) for i in range(size)]
        down = [(j, i) for i, j in up]
        last = lax.slice_in_dim(x, length - width, length, axis=dim)
        first = lax.slice_in_dim(x, 0, width, axis=dim)
        before = lax.ppermute(last, axis, up)
        after = lax.ppermute(first, axis, down)
        x = jnp.concatenate([before, x, after], axis=dim)
    return x


def crop(values, width):
    return values[:, width:-width, width:-width]


def pairs_of(field, cond):
    centre = field[:, 1:-1, 1:-1]
    middle = cond[:, 1:-1, 1:-1]
    listed = [
        (jnp.roll(centre, 1, 0), jnp.roll(middle, 1, 0)),
        (jnp.roll(centre, -1, 0), jnp.roll(middle, -1, 0)),
        (field[:, 2:, 1:-1], cond[:, 2:, 1:-1]),
        (field[:, :-2, 1:-1], cond[:, :-2, 1:-1]),
        (field[:, 1:-1, 2:], cond[:, 1:-1, 2:]),
        (field[:, 1:-1, :-2], cond[:, 1:-1, :-2]),
    ]
    return (centre, middle, listed)


def operate_pad(field, cond, factor):
    centre, middle, listed = pairs_of(field, cond)
    summed = jnp.zeros_like(centre)
    for near_v, near_c in listed:
        summed = summed + 0.5 * (middle + near_c) * (centre - near_v)
    return SHIFT * centre + factor * summed


def diagonal_pad(cond, factor):
    centre, middle, listed = pairs_of(cond, cond)
    summed = jnp.zeros_like(middle)
    for near_v, near_c in listed:
        summed = summed + 0.5 * (middle + near_c)
    return SHIFT + factor * summed


def restrict(values):
    depth, width_x, width_y = values.shape
    blocks = values.reshape(
        depth // COARSEN, COARSEN, width_x // COARSEN, COARSEN, width_y // COARSEN, COARSEN
    )
    return jnp.mean(blocks, axis=(1, 3, 5))


def prolong(values):
    depth, width_x, width_y = values.shape
    spread = jnp.broadcast_to(
        values[:, None, :, None, :, None], (depth, COARSEN, width_x, COARSEN, width_y, COARSEN)
    )
    return spread.reshape(depth * COARSEN, width_x * COARSEN, width_y * COARSEN)


def body(iterate, source, conduct):
    theta = (LMAX + LMIN) / 2.0
    delta = (LMAX - LMIN) / 2.0
    sigma = theta / delta
    rho_now = 1.0 / sigma
    stacked = jnp.stack([iterate, source, conduct])
    padded = extended(stacked, (("gx", 2), ("gy", 3)), SWEEPS + 1)
    iter_pad = padded[0]
    source_pad = padded[1]
    cond_pad = padded[2]
    residual = crop(source_pad, 1) - operate_pad(iter_pad, cond_pad, 1.0)
    diag_fine = diagonal_pad(cond_pad, 1.0)
    correction = jnp.zeros_like(residual)
    remainder = residual
    direction = residual / (theta * diag_fine)
    for sweep_index in range(SWEEPS):
        image = operate_pad(direction, crop(cond_pad, 1 + sweep_index), 1.0)
        correction = crop(correction, 1) + crop(direction, 1)
        remainder = crop(remainder, 1) - image
        rho_next = 1.0 / (2.0 * sigma - rho_now)
        direction = rho_next * rho_now * crop(
            direction, 1
        ) + 2.0 * rho_next / delta * remainder / crop(diag_fine, 1 + sweep_index)
        rho_now = rho_next
    residual_core = crop(residual, SWEEPS)
    correction = correction + direction
    coarse_rhs = restrict(residual_core)
    coarse_cond = restrict(conduct)
    cond_wide = extended(coarse_cond, (("gx", 1), ("gy", 2)), 1)
    diag_coarse = diagonal_pad(cond_wide, 1.0 / 64.0)
    coarse = OMEGA * coarse_rhs / diag_coarse
    for sweep_index in range(COARSE_SWEEPS - 1):
        coarse_wide = extended(coarse, (("gx", 1), ("gy", 2)), 1)
        coarse = (
            coarse
            + OMEGA * (coarse_rhs - operate_pad(coarse_wide, cond_wide, 1.0 / 64.0)) / diag_coarse
        )
    return iterate + correction + prolong(coarse)


def solution(mesh):
    return jax.shard_map(
        body,
        mesh=mesh,
        in_specs=(P(None, "gx", "gy"), P(None, "gx", "gy"), P(None, "gx", "gy")),
        out_specs=P(None, "gx", "gy"),
        check_vma=False,
    )
```

profile of v0, /device:TPU:0, one launch (start us, length us, event | category | flops | bytes accessed | tf_op | source)
XLA Modules:
  0.0 121.5 jit_solution(16886074089129458093)
XLA Ops:
  0.0 1.3 %pad_maximum_fusion.4 = (f32[3,32,4,128]{3,2,1,0:T(4,128)S(1)}, f32[3,32,4,128]{3,2,1,0:T(4,128)S(1)}) fusion(f32[1,32,24,128]{3,2,1,0:T(8,128)} %bitcast.14, f32[1,32,24,128]{3,2,1,0:T(8,128)} %bitcast.17, f32[1,32,24,128]{3,2,1,0:T(8,128)} %bitcast.11), kind=kLoop, calls=%fused_computation.145 | loop fusion | flops 196608 | bytes 1572864 | tf_op jit(solution)/shard_map/slice | solution.py:22
  1.3 5.5 %collective-permute-start.1 = (f32[3,32,4,128]{3,2,1,0:T(4,128)S(1)}, f32[3,32,4,128]{3,2,1,0:T(4,128)S(1)}, u32[]{:S(2)}, u32[]{:S(2)}) collective-permute-start(f32[3,32,4,128]{3,2,1,0:T(4,128)S(1)} %get-tuple-element.23), channel_id=1, source_target_pairs={{2,0},{4,2},{6,4},{8,6},{10,8},{12,10},{14,12},{16,14},{18,16},{20... | collective-permute-start | bytes 589832 | tf_op jit(solution)/shard_map/ppermute | solution.py:25
  6.8 5.0 %reshape.11 = f32[4,8,3,8,16,8]{5,4,3,2,1,0:T(8,128)} reshape(f32[32,24,128]{2,1,0:T(8,128)S(1)} %copy-done.3) | data formatting | bytes 786432 | tf_op jit(solution)/shard_map/reshape | solution.py:66
  11.8 3.4 %reduce_sum.19 = f32[4,3,16]{2,1,0:T(4,128)S(1)} reduce(f32[4,8,3,8,16,8]{5,4,3,2,1,0:T(8,128)} %reshape.11, f32[]{:T(128)} %constant.5.clone.1), dimensions={1,3,5}, to_apply=%region_1.2 | reduce | flops 98112 | bytes 393988 | tf_op jit(solution)/shard_map/reduce_sum | solution.py:69
  15.2 4.5 %collective-permute-start.4 = (f32[4,1,16]{2,1,0:T(1,128)S(1)}, f32[4,1,16]{2,1,0:T(1,128)S(1)}, u32[]{:S(2)}, u32[]{:S(2)}) collective-permute-start(f32[4,1,16]{2,1,0:T(1,128)S(1)} %get-tuple-element.87), channel_id=1, source_target_pairs={{2,0},{4,2},{6,4},{8,6},{10,8},{12,10},{14,12},{16,14},{18,16},{20... | collective-permute-start | bytes 776 | tf_op jit(solution)/shard_map/ppermute | solution.py:25
  19.7 0.6 fusion.196
  21.0 4.4 %collective-permute-done.5 = f32[4,1,16]{2,1,0:T(1,128)S(1)} collective-permute-done((f32[4,1,16]{2,1,0:T(1,128)S(1)}, f32[4,1,16]{2,1,0:T(1,128)S(1)}, u32[]{:S(2)}, u32[]{:S(2)}) %collective-permute-start.5) | collective-permute-done | bytes 288 | tf_op jit(solution)/shard_map/ppermute | solution.py:24
  26.0 1.7 %fusion.165 = (f32[3,32,32,4]{3,2,1,0:T(8,128)S(1)}, f32[3,32,32,4]{3,2,1,0:T(8,128)}) fusion(f32[3,32,32,128]{3,2,1,0:T(8,128)S(1)} %pad_maximum_fusion.1), kind=kLoop, calls=%fused_computation.267 | loop fusion | bytes 196608 | tf_op jit(solution)/shard_map/slice | solution.py:22
  27.7 2.1 %copy.5 = f32[3,32,32,4]{2,1,3,0:T(8,128)S(1)} copy(f32[3,32,32,4]{3,2,1,0:T(8,128)} %get-tuple-element.21) | data formatting | bytes 98304 | tf_op jit(solution)/shard_map/slice | solution.py:23
  29.8 1.6 %collective-permute-start.3 = (f32[3,32,32,4]{2,1,3,0:T(8,128)S(1)}, f32[3,32,32,4]{2,1,3,0:T(8,128)}, u32[]{:S(2)}, u32[]{:S(2)}) collective-permute-start(f32[3,32,32,4]{2,1,3,0:T(8,128)S(1)} %copy.5), channel_id=1, source_target_pairs={{1,0},{0,1},{3,2},{2,3},{5,4},{4,5},{7,6},{6,7},{9,8},{8,9},{11,10... | collective-permute-start | bytes 147464 | tf_op jit(solution)/shard_map/ppermute | solution.py:25
  31.4 1.4 %copy.4 = f32[3,32,32,4]{2,1,3,0:T(8,128)} copy(f32[3,32,32,4]{3,2,1,0:T(8,128)S(1)} %get-tuple-element.20) | data formatting | bytes 98304 | tf_op jit(solution)/shard_map/slice | solution.py:22
  33.4 0.7 fusion.185
  34.0 1.5 %collective-permute-start.6 = (f32[4,5,1]{2,1,0:T(8,128)}, f32[4,5,1]{2,1,0:T(8,128)}, u32[]{:S(2)}, u32[]{:S(2)}) collective-permute-start(f32[4,5,1]{2,1,0:T(8,128)} %get-tuple-element.63), channel_id=1, source_target_pairs={{1,0},{0,1},{3,2},{2,3},{5,4},{4,5},{7,6},{6,7},{9,8},{8,9},{11,10... | collective-permute-start | bytes 248 | tf_op jit(solution)/shard_map/ppermute | solution.py:25
  36.1 1.6 %copy.7 = f32[3,32,32,4]{3,2,1,0:T(8,128)S(1)} copy(f32[3,32,32,4]{2,1,3,0:T(8,128)} %collective-permute-done.3) | data formatting | bytes 98304 | tf_op jit(solution)/shard_map/ppermute | solution.py:25
  37.6 1.2 collective-permute-done.2
  38.8 2.7 %copy.6 = f32[3,32,32,4]{3,2,1,0:T(8,128)} copy(f32[3,32,32,4]{2,1,3,0:T(8,128)} %collective-permute-done.2) | data formatting | bytes 98304 | tf_op jit(solution)/shard_map/ppermute | solution.py:24
  41.6 3.2 %pad_maximum_fusion = f32[3,32,32,136]{3,2,1,0:T(8,128)S(1)} fusion(f32[3,32,32,4]{3,2,1,0:T(8,128)S(1)} %copy.7, f32[3,32,4,128]{3,2,1,0:T(4,128)S(1)} %collective-permute-done.1, f32[1,32,24,128]{3,2,1,0:T(8,128)S(1)} %bitcast.16, f32[1,32,24,128]{3,2,1,0:T(8,128)S(1)} %bitcast.19, f32[1,32,24,128]{3,2,1,0:T(8,128)S(1)} %bitcast.13, ...), kind=kLoop, calls=%fused_computation | loop fusion | flops 2506752 | bytes 3342336 | tf_op jit(solution)/shard_map/concatenate | solution.py:26
  45.1 1.1 fusion.179
  46.2 3.2 %multiply_divide_fusion = (f32[32,30,134]{2,1,0:T(8,128)S(1)}, f32[32,30,134]{2,1,0:T(8,128)S(1)}, f32[32,30,134]{2,1,0:T(8,128)S(1)}) fusion(f32[32,32,136]{2,1,0:T(8,128)S(1)} %get-tuple-element.18, f32[1,30,134]{2,1,0:T(8,128)S(1)} %get-tuple-element.88, f32[31,30,134]{2,1,0:T(8,128)S(1)} %get-tuple-element.90, f32[31,30,134]{2,1,0:T(8,128)S(1)} %get-tuple-element.91, ...), kind=kLoop, calls=%fused_computation.102 | loop fusion | flops 5660160 | bytes 9262080 | tf_op jit(solution)/shard_map/div | solution.py:94
  49.5 1.0 copy-done.4
  50.5 0.9 slice.761
  51.4 5.9 %reshape.10 = f32[4,8,3,8,16,8]{5,4,3,2,1,0:T(8,128)} reshape(f32[32,24,128]{2,1,0:T(8,128)} %slice.761) | data formatting | bytes 786432 | tf_op jit(solution)/shard_map/reshape | solution.py:66
  57.3 3.3 %reduce_sum.18 = f32[4,3,16]{2,1,0:T(4,128)S(1)} reduce(f32[4,8,3,8,16,8]{5,4,3,2,1,0:T(8,128)} %reshape.10, f32[]{:T(128)} %constant.5.clone.1), dimensions={1,3,5}, to_apply=%region_0.1 | reduce | flops 98112 | bytes 393988 | tf_op jit(solution)/shard_map/reduce_sum | solution.py:69
  60.6 0.9 fusion.157
  62.9 0.6 copy-done.5
  63.5 3.4 %fusion.15 = (f32[32,28,132]{2,1,0:T(8,128)S(1)}, f32[32,28,132]{2,1,0:T(8,128)S(1)}) fusion(f32[32,30,134]{2,1,0:T(8,128)S(1)} %get-tuple-element.10, f32[32,30,134]{2,1,0:T(8,128)S(1)} %get-tuple-element.9, f32[32,32,136]{2,1,0:T(8,128)S(1)} %get-tuple-element.18, f32[1,28,132]{2,1,0:T(8,128)S(1)} %get-tuple-element.45, ...), kind=kLoop, calls=%fused_computation.27 | loop fusion | flops 4730880 | bytes 8515584 | tf_op jit(solution)/shard_map/add | solution.py:100
  68.4 1.1 fusion.168
  69.5 0.7 fusion.169
  70.2 4.2 %fusion = (f32[32,26,130]{2,1,0:T(8,128)S(1)}, f32[32,26,130]{2,1,0:T(8,128)}) fusion(f32[32,30,134]{2,1,0:T(8,128)S(1)} %copy-done.1, f32[32,28,132]{2,1,0:T(8,128)S(1)} %get-tuple-element.7, f32[32,32,136]{2,1,0:T(8,128)S(1)} %get-tuple-element.18, f32[1,26,130]{2,1,0:T(8,128)S(1)} %get-tuple-element.37, f32[31,26,130]{2,1,0:T(8,128)S(1)} %get-tuple-element.39, ...), kind=kLoop, calls=%fused_computation.3 | loop fusion | flops 4326400 | bytes 7787520 | tf_op jit(solution)/shard_map/add | solution.py:100
  74.4 1.1 fusion.166
  75.6 0.7 fusion.167
  76.8 1.3 %slice.719 = f32[32,26,130]{2,1,0:T(8,128)} slice(f32[32,28,132]{2,1,0:T(8,128)S(1)} %get-tuple-element.7), slice={[0:32], [1:27], [1:131]} | slice | bytes 865280 | tf_op jit(solution)/shard_map/slice | solution.py:31
  78.1 1.3 %slice.698 = f32[32,26,130]{2,1,0:T(8,128)} slice(f32[32,30,134]{2,1,0:T(8,128)S(1)} %get-tuple-element.9), slice={[0:32], [2:28], [2:132]} | slice | bytes 865280 | tf_op jit(solution)/shard_map/slice | solution.py:31
  79.4 2.6 %collective-permute-done.9 = f32[4,1,16]{2,1,0:T(1,128)S(1)} collective-permute-done((f32[4,1,16]{2,1,0:T(1,128)S(1)}, f32[4,1,16]{2,1,0:T(1,128)S(1)}, u32[]{:S(2)}, u32[]{:S(2)}) %collective-permute-start.9) | collective-permute-done | bytes 288 | tf_op jit(solution)/shard_map/ppermute | solution.py:24
  82.6 1.5 %collective-permute-start.10 = (f32[4,5,1]{2,1,0:T(8,128)S(1)}, f32[4,5,1]{2,1,0:T(8,128)S(1)}, u32[]{:S(2)}, u32[]{:S(2)}) collective-permute-start(f32[4,5,1]{2,1,0:T(8,128)S(1)} %get-tuple-element.60), channel_id=1, source_target_pairs={{1,0},{0,1},{3,2},{2,3},{5,4},{4,5},{7,6},{6,7},{9,8},{8,9},{11,10... | collective-permute-start | bytes 248 | tf_op jit(solution)/shard_map/ppermute | solution.py:25
  84.1 1.7 %collective-permute-done.11 = f32[4,5,1]{2,1,0:T(8,128)S(1)} collective-permute-done((f32[4,5,1]{2,1,0:T(8,128)S(1)}, f32[4,5,1]{2,1,0:T(8,128)S(1)}, u32[]{:S(2)}, u32[]{:S(2)}) %collective-permute-start.11) | collective-permute-done | bytes 112 | tf_op jit(solution)/shard_map/ppermute | solution.py:24
  87.0 0.8 collective-permute-done.12
  87.8 4.5 %collective-permute-done.13 = f32[4,1,16]{2,1,0:T(1,128)S(1)} collective-permute-done((f32[4,1,16]{2,1,0:T(1,128)S(1)}, f32[4,1,16]{2,1,0:T(1,128)S(1)}, u32[]{:S(2)}, u32[]{:S(2)}) %collective-permute-start.13) | collective-permute-done | bytes 288 | tf_op jit(solution)/shard_map/ppermute | solution.py:24
  92.4 1.5 %collective-permute-start.15 = (f32[4,5,1]{2,1,0:T(8,128)S(1)}, f32[4,5,1]{2,1,0:T(8,128)S(1)}, u32[]{:S(2)}, u32[]{:S(2)}) collective-permute-start(f32[4,5,1]{2,1,0:T(8,128)S(1)} %get-tuple-element.59), channel_id=1, source_target_pairs={{0,1},{1,0},{2,3},{3,2},{4,5},{5,4},{6,7},{7,6},{8,9},{9,8},{10,11... | collective-permute-start | bytes 248 | tf_op jit(solution)/shard_map/ppermute | solution.py:24
  94.4 1.7 %collective-permute-done.15 = f32[4,5,1]{2,1,0:T(8,128)S(1)} collective-permute-done((f32[4,5,1]{2,1,0:T(8,128)S(1)}, f32[4,5,1]{2,1,0:T(8,128)S(1)}, u32[]{:S(2)}, u32[]{:S(2)}) %collective-permute-start.15) | collective-permute-done | bytes 112 | tf_op jit(solution)/shard_map/ppermute | solution.py:24
  96.1 1.5 %collective-permute-done.14 = f32[4,5,1]{2,1,0:T(8,128)S(1)} collective-permute-done((f32[4,5,1]{2,1,0:T(8,128)S(1)}, f32[4,5,1]{2,1,0:T(8,128)S(1)}, u32[]{:S(2)}, u32[]{:S(2)}) %collective-permute-start.14) | collective-permute-done | bytes 112 | tf_op jit(solution)/shard_map/ppermute | solution.py:25
  98.4 0.8 collective-permute-done.16
  99.2 4.7 %collective-permute-done.17 = f32[4,1,16]{2,1,0:T(1,128)S(1)} collective-permute-done((f32[4,1,16]{2,1,0:T(1,128)S(1)}, f32[4,1,16]{2,1,0:T(1,128)S(1)}, u32[]{:S(2)}, u32[]{:S(2)}) %collective-permute-start.17) | collective-permute-done | bytes 288 | tf_op jit(solution)/shard_map/ppermute | solution.py:24
  104.4 1.5 %collective-permute-start.18 = (f32[4,5,1]{2,1,0:T(8,128)S(1)}, f32[4,5,1]{2,1,0:T(8,128)S(1)}, u32[]{:S(2)}, u32[]{:S(2)}) collective-permute-start(f32[4,5,1]{2,1,0:T(8,128)S(1)} %get-tuple-element.56), channel_id=1, source_target_pairs={{1,0},{0,1},{3,2},{2,3},{5,4},{4,5},{7,6},{6,7},{9,8},{8,9},{11,10... | collective-permute-start | bytes 248 | tf_op jit(solution)/shard_map/ppermute | solution.py:25
  106.0 1.7 %collective-permute-done.19 = f32[4,5,1]{2,1,0:T(8,128)S(1)} collective-permute-done((f32[4,5,1]{2,1,0:T(8,128)S(1)}, f32[4,5,1]{2,1,0:T(8,128)S(1)}, u32[]{:S(2)}, u32[]{:S(2)}) %collective-permute-start.19) | collective-permute-done | bytes 112 | tf_op jit(solution)/shard_map/ppermute | solution.py:24
  108.3 3.2 %broadcast_in_dim.2 = f32[4,8,3,8,16,8]{5,4,3,2,1,0:T(8,128)} broadcast(f32[4,3,16]{2,1,0:T(4,128)S(1)} %fusion.92), dimensions={0,2,4} | broadcast | bytes 393984 | tf_op jit(solution)/shard_map/broadcast_in_dim | solution.py:74
  111.6 5.3 %reshape.12 = f32[32,24,128]{2,1,0:T(8,128)S(1)} reshape(f32[4,8,3,8,16,8]{5,4,3,2,1,0:T(8,128)} %broadcast_in_dim.2) | data formatting | bytes 786432 | tf_op jit(solution)/shard_map/reshape | solution.py:77
  116.9 4.6 %fusion.62 = f32[32,24,128]{2,1,0:T(8,128)} fusion(f32[32,24,128]{2,1,0:T(8,128)S(1)} %reshape.12, f32[32,24,128]{2,1,0:T(8,128)S(1)} %copy-done.2, f32[32,30,134]{2,1,0:T(8,128)} %copy-done, f32[32,26,130]{2,1,0:T(8,128)S(1)} %get-tuple-element.5, f32[32,32,136]{2,1,0:T(8,128)S(1)} %get-tuple-element.18, f32[32,26,130]{2,1,0:T(8,128)} %get-tuple-element.6, ...), kind=kLoop, calls=%fused_computation.108 | loop fusion | flops 4423680 | bytes 8257536 | tf_op jit(solution)/shard_map/add | solution.py:117
  (87 shorter events, 10.2 us)
Async XLA Ops:
  0.0 6.8 %copy-start.3 = (f32[32,24,128]{2,1,0:T(8,128)S(1)}, f32[32,24,128]{2,1,0:T(8,128)}, u32[]{:S(2)}) copy-start(f32[32,24,128]{2,1,0:T(8,128)} %param.5) | copy-start | bytes 1179652
  1.3 24.1 %collective-permute-start.1 = (f32[3,32,4,128]{3,2,1,0:T(4,128)S(1)}, f32[3,32,4,128]{3,2,1,0:T(4,128)S(1)}, u32[]{:S(2)}, u32[]{:S(2)}) collective-permute-start(f32[3,32,4,128]{3,2,1,0:T(4,128)S(1)} %get-tuple-element.23), channel_id=1, source_target_pairs={{2,0},{4,2},{6,4},{8,6},{10,8},{12,10},{14,12},{16,14},{18,16},{20... | collective-permute-start | bytes 589832 | tf_op jit(solution)/shard_map/ppermute | solution.py:25
  6.8 18.6 %collective-permute-start = (f32[3,32,4,128]{3,2,1,0:T(4,128)S(1)}, f32[3,32,4,128]{3,2,1,0:T(4,128)S(1)}, u32[]{:S(2)}, u32[]{:S(2)}) collective-permute-start(f32[3,32,4,128]{3,2,1,0:T(4,128)S(1)} %get-tuple-element.22), channel_id=1, source_target_pairs={{0,2},{2,4},{4,6},{6,8},{8,10},{10,12},{12,14},{14,16},{16,18},{18... | collective-permute-start | bytes 589832 | tf_op jit(solution)/shard_map/ppermute | solution.py:24
  11.8 13.6 %copy-start.2 = (f32[32,24,128]{2,1,0:T(8,128)S(1)}, f32[32,24,128]{2,1,0:T(8,128)}, u32[]{:S(2)}) copy-start(f32[32,24,128]{2,1,0:T(8,128)} %param.3) | copy-start | bytes 1179652
  11.8 13.7 %copy-start.6 = (f32[32,24,128]{2,1,0:T(8,128)S(1)}, f32[32,24,128]{2,1,0:T(8,128)}, u32[]{:S(2)}) copy-start(f32[32,24,128]{2,1,0:T(8,128)} %param.4) | copy-start | bytes 1179652
  15.2 5.8 %copy-start.8 = (f32[4,3,16]{2,1,0:T(4,128)}, f32[4,3,16]{2,1,0:T(4,128)S(1)}, u32[]{:S(2)}) copy-start(f32[4,3,16]{2,1,0:T(4,128)S(1)} %reduce_sum.19) | copy-start | bytes 2308
  15.2 5.8 %collective-permute-start.4 = (f32[4,1,16]{2,1,0:T(1,128)S(1)}, f32[4,1,16]{2,1,0:T(1,128)S(1)}, u32[]{:S(2)}, u32[]{:S(2)}) collective-permute-start(f32[4,1,16]{2,1,0:T(1,128)S(1)} %get-tuple-element.87), channel_id=1, source_target_pairs={{2,0},{4,2},{6,4},{8,6},{10,8},{12,10},{14,12},{16,14},{18,16},{20... | collective-permute-start | bytes 776 | tf_op jit(solution)/shard_map/ppermute | solution.py:25
  19.7 5.7 %collective-permute-start.5 = (f32[4,1,16]{2,1,0:T(1,128)S(1)}, f32[4,1,16]{2,1,0:T(1,128)S(1)}, u32[]{:S(2)}, u32[]{:S(2)}) collective-permute-start(f32[4,1,16]{2,1,0:T(1,128)S(1)} %get-tuple-element.86), channel_id=1, source_target_pairs={{0,2},{2,4},{4,6},{6,8},{8,10},{10,12},{12,14},{14,16},{16,18},{18... | collective-permute-start | bytes 776 | tf_op jit(solution)/shard_map/ppermute | solution.py:24
  21.0 4.7 %copy-start.9 = (f32[4,1,16]{2,1,0:T(1,128)}, f32[4,1,16]{2,1,0:T(1,128)S(1)}, u32[]{:S(2)}) copy-start(f32[4,1,16]{2,1,0:T(1,128)S(1)} %collective-permute-done.4) | copy-start | bytes 772
  25.4 0.6 copy-start.11
  29.8 6.2 %collective-permute-start.3 = (f32[3,32,32,4]{2,1,3,0:T(8,128)S(1)}, f32[3,32,32,4]{2,1,3,0:T(8,128)}, u32[]{:S(2)}, u32[]{:S(2)}) collective-permute-start(f32[3,32,32,4]{2,1,3,0:T(8,128)S(1)} %copy.5), channel_id=1, source_target_pairs={{1,0},{0,1},{3,2},{2,3},{5,4},{4,5},{7,6},{6,7},{9,8},{8,9},{11,10... | collective-permute-start | bytes 147464 | tf_op jit(solution)/shard_map/ppermute | solution.py:25
  32.8 6.0 %collective-permute-start.2 = (f32[3,32,32,4]{2,1,3,0:T(8,128)}, f32[3,32,32,4]{2,1,3,0:T(8,128)}, u32[]{:S(2)}, u32[]{:S(2)}) collective-permute-start(f32[3,32,32,4]{2,1,3,0:T(8,128)} %copy.4), channel_id=1, source_target_pairs={{0,1},{1,0},{2,3},{3,2},{4,5},{5,4},{6,7},{7,6},{8,9},{9,8},{10,11... | collective-permute-start | bytes 147464 | tf_op jit(solution)/shard_map/ppermute | solution.py:24
  34.0 26.5 %collective-permute-start.6 = (f32[4,5,1]{2,1,0:T(8,128)}, f32[4,5,1]{2,1,0:T(8,128)}, u32[]{:S(2)}, u32[]{:S(2)}) collective-permute-start(f32[4,5,1]{2,1,0:T(8,128)} %get-tuple-element.63), channel_id=1, source_target_pairs={{1,0},{0,1},{3,2},{2,3},{5,4},{4,5},{7,6},{6,7},{9,8},{8,9},{11,10... | collective-permute-start | bytes 248 | tf_op jit(solution)/shard_map/ppermute | solution.py:25
  35.5 25.0 %collective-permute-start.7 = (f32[4,5,1]{2,1,0:T(8,128)}, f32[4,5,1]{2,1,0:T(8,128)}, u32[]{:S(2)}, u32[]{:S(2)}) collective-permute-start(f32[4,5,1]{2,1,0:T(8,128)} %get-tuple-element.62), channel_id=1, source_target_pairs={{0,1},{1,0},{2,3},{3,2},{4,5},{5,4},{6,7},{7,6},{8,9},{9,8},{10,11... | collective-permute-start | bytes 248 | tf_op jit(solution)/shard_map/ppermute | solution.py:24
  49.4 1.0 copy-start.4
  49.4 13.5 %copy-start = (f32[32,30,134]{2,1,0:T(8,128)}, f32[32,30,134]{2,1,0:T(8,128)S(1)}, u32[]{:S(2)}) copy-start(f32[32,30,134]{2,1,0:T(8,128)S(1)} %get-tuple-element.10) | copy-start | bytes 1543684
  62.3 1.2 %copy-start.5 = (f32[32,30,134]{2,1,0:T(8,128)S(1)}, f32[32,30,134]{2,1,0:T(8,128)}, u32[]{:S(2)}) copy-start(f32[32,30,134]{2,1,0:T(8,128)} %copy-done.4) | copy-start | bytes 1543684
  68.4 1.8 %copy-start.1 = (f32[32,30,134]{2,1,0:T(8,128)S(1)}, f32[32,30,134]{2,1,0:T(8,128)}, u32[]{:S(2)}) copy-start(f32[32,30,134]{2,1,0:T(8,128)} %copy-done) | copy-start | bytes 1543684
  76.3 3.1 %collective-permute-start.8 = (f32[4,1,16]{2,1,0:T(1,128)S(1)}, f32[4,1,16]{2,1,0:T(1,128)S(1)}, u32[]{:S(2)}, u32[]{:S(2)}) collective-permute-start(f32[4,1,16]{2,1,0:T(1,128)S(1)} %get-tuple-element.81), channel_id=1, source_target_pairs={{2,0},{4,2},{6,4},{8,6},{10,8},{12,10},{14,12},{16,14},{18,16},{20... | collective-permute-start | bytes 776 | tf_op jit(solution)/shard_map/ppermute | solution.py:25
  76.3 5.7 %collective-permute-start.9 = (f32[4,1,16]{2,1,0:T(1,128)S(1)}, f32[4,1,16]{2,1,0:T(1,128)S(1)}, u32[]{:S(2)}, u32[]{:S(2)}) collective-permute-start(f32[4,1,16]{2,1,0:T(1,128)S(1)} %get-tuple-element.80), channel_id=1, source_target_pairs={{0,2},{2,4},{4,6},{6,8},{8,10},{10,12},{12,14},{14,16},{16,18},{18... | collective-permute-start | bytes 776 | tf_op jit(solution)/shard_map/ppermute | solution.py:24
  78.1 8.2 %copy-start.10 = (f32[4,1,16]{2,1,0:T(1,128)S(1)}, f32[4,1,16]{2,1,0:T(1,128)}, u32[]{:S(2)}) copy-start(f32[4,1,16]{2,1,0:T(1,128)} %copy-done.9) | copy-start | bytes 772
  78.1 8.2 %copy-start.12 = (f32[4,1,16]{2,1,0:T(1,128)S(1)}, f32[4,1,16]{2,1,0:T(1,128)}, u32[]{:S(2)}) copy-start(f32[4,1,16]{2,1,0:T(1,128)} %copy-done.11) | copy-start | bytes 772
  82.1 3.7 %collective-permute-start.11 = (f32[4,5,1]{2,1,0:T(8,128)S(1)}, f32[4,5,1]{2,1,0:T(8,128)S(1)}, u32[]{:S(2)}, u32[]{:S(2)}) collective-permute-start(f32[4,5,1]{2,1,0:T(8,128)S(1)} %get-tuple-element.61), channel_id=1, source_target_pairs={{0,1},{1,0},{2,3},{3,2},{4,5},{5,4},{6,7},{7,6},{8,9},{9,8},{10,11... | collective-permute-start | bytes 248 | tf_op jit(solution)/shard_map/ppermute | solution.py:24
  82.6 3.7 %collective-permute-start.10 = (f32[4,5,1]{2,1,0:T(8,128)S(1)}, f32[4,5,1]{2,1,0:T(8,128)S(1)}, u32[]{:S(2)}, u32[]{:S(2)}) collective-permute-start(f32[4,5,1]{2,1,0:T(8,128)S(1)} %get-tuple-element.60), channel_id=1, source_target_pairs={{1,0},{0,1},{3,2},{2,3},{5,4},{4,5},{7,6},{6,7},{9,8},{8,9},{11,10... | collective-permute-start | bytes 248 | tf_op jit(solution)/shard_map/ppermute | solution.py:25
  86.5 1.4 %collective-permute-start.12 = (f32[4,1,16]{2,1,0:T(1,128)S(1)}, f32[4,1,16]{2,1,0:T(1,128)S(1)}, u32[]{:S(2)}, u32[]{:S(2)}) collective-permute-start(f32[4,1,16]{2,1,0:T(1,128)S(1)} %get-tuple-element.75), channel_id=1, source_target_pairs={{2,0},{4,2},{6,4},{8,6},{10,8},{12,10},{14,12},{16,14},{18,16},{20... | collective-permute-start | bytes 776 | tf_op jit(solution)/shard_map/ppermute | solution.py:25
  86.5 5.8 %collective-permute-start.13 = (f32[4,1,16]{2,1,0:T(1,128)S(1)}, f32[4,1,16]{2,1,0:T(1,128)S(1)}, u32[]{:S(2)}, u32[]{:S(2)}) collective-permute-start(f32[4,1,16]{2,1,0:T(1,128)S(1)} %get-tuple-element.74), channel_id=1, source_target_pairs={{0,2},{2,4},{4,6},{6,8},{8,10},{10,12},{12,14},{14,16},{16,18},{18... | collective-permute-start | bytes 776 | tf_op jit(solution)/shard_map/ppermute | solution.py:24
  92.4 3.7 %collective-permute-start.15 = (f32[4,5,1]{2,1,0:T(8,128)S(1)}, f32[4,5,1]{2,1,0:T(8,128)S(1)}, u32[]{:S(2)}, u32[]{:S(2)}) collective-permute-start(f32[4,5,1]{2,1,0:T(8,128)S(1)} %get-tuple-element.59), channel_id=1, source_target_pairs={{0,1},{1,0},{2,3},{3,2},{4,5},{5,4},{6,7},{7,6},{8,9},{9,8},{10,11... | collective-permute-start | bytes 248 | tf_op jit(solution)/shard_map/ppermute | solution.py:24
  93.9 3.7 %collective-permute-start.14 = (f32[4,5,1]{2,1,0:T(8,128)S(1)}, f32[4,5,1]{2,1,0:T(8,128)S(1)}, u32[]{:S(2)}, u32[]{:S(2)}) collective-permute-start(f32[4,5,1]{2,1,0:T(8,128)S(1)} %get-tuple-element.58), channel_id=1, source_target_pairs={{1,0},{0,1},{3,2},{2,3},{5,4},{4,5},{7,6},{6,7},{9,8},{8,9},{11,10... | collective-permute-start | bytes 248 | tf_op jit(solution)/shard_map/ppermute | solution.py:25
  97.8 1.4 %collective-permute-start.16 = (f32[4,1,16]{2,1,0:T(1,128)S(1)}, f32[4,1,16]{2,1,0:T(1,128)S(1)}, u32[]{:S(2)}, u32[]{:S(2)}) collective-permute-start(f32[4,1,16]{2,1,0:T(1,128)S(1)} %get-tuple-element.69), channel_id=1, source_target_pairs={{2,0},{4,2},{6,4},{8,6},{10,8},{12,10},{14,12},{16,14},{18,16},{20... | collective-permute-start | bytes 776 | tf_op jit(solution)/shard_map/ppermute | solution.py:25
  97.9 6.0 %collective-permute-start.17 = (f32[4,1,16]{2,1,0:T(1,128)S(1)}, f32[4,1,16]{2,1,0:T(1,128)S(1)}, u32[]{:S(2)}, u32[]{:S(2)}) collective-permute-start(f32[4,1,16]{2,1,0:T(1,128)S(1)} %get-tuple-element.68), channel_id=1, source_target_pairs={{0,2},{2,4},{4,6},{6,8},{8,10},{10,12},{12,14},{14,16},{16,18},{18... | collective-permute-start | bytes 776 | tf_op jit(solution)/shard_map/ppermute | solution.py:24
  103.9 3.7 %collective-permute-start.19 = (f32[4,5,1]{2,1,0:T(8,128)S(1)}, f32[4,5,1]{2,1,0:T(8,128)S(1)}, u32[]{:S(2)}, u32[]{:S(2)}) collective-permute-start(f32[4,5,1]{2,1,0:T(8,128)S(1)} %get-tuple-element.57), channel_id=1, source_target_pairs={{0,1},{1,0},{2,3},{3,2},{4,5},{5,4},{6,7},{7,6},{8,9},{9,8},{10,11... | collective-permute-start | bytes 248 | tf_op jit(solution)/shard_map/ppermute | solution.py:24
  104.4 3.7 %collective-permute-start.18 = (f32[4,5,1]{2,1,0:T(8,128)S(1)}, f32[4,5,1]{2,1,0:T(8,128)S(1)}, u32[]{:S(2)}, u32[]{:S(2)}) collective-permute-start(f32[4,5,1]{2,1,0:T(8,128)S(1)} %get-tuple-element.56), channel_id=1, source_target_pairs={{1,0},{0,1},{3,2},{2,3},{5,4},{4,5},{7,6},{6,7},{9,8},{8,9},{11,10... | collective-permute-start | bytes 248 | tf_op jit(solution)/shard_map/ppermute | solution.py:25
  111.5 5.3 %copy-start.7 = (f32[31,24,128]{2,1,0:T(8,128)S(1)}, f32[31,24,128]{2,1,0:T(8,128)}, u32[]{:S(2)}) copy-start(f32[31,24,128]{2,1,0:T(8,128)} %get-tuple-element.28) | copy-start | bytes 1142788
  111.5 5.3 %copy-start.13 = (f32[1,24,128]{2,1,0:T(8,128)S(1)}, f32[1,24,128]{2,1,0:T(8,128)}, u32[]{:S(2)}) copy-start(f32[1,24,128]{2,1,0:T(8,128)} %get-tuple-element.30) | copy-start | bytes 36868
  111.5 5.3 %copy-start.14 = (f32[1,24,128]{2,1,0:T(8,128)S(1)}, f32[1,24,128]{2,1,0:T(8,128)}, u32[]{:S(2)}) copy-start(f32[1,24,128]{2,1,0:T(8,128)} %get-tuple-element.31) | copy-start | bytes 36868
  111.5 5.3 %copy-start.15 = (f32[1,24,128]{2,1,0:T(8,128)S(1)}, f32[1,24,128]{2,1,0:T(8,128)}, u32[]{:S(2)}) copy-start(f32[1,24,128]{2,1,0:T(8,128)} %get-tuple-element.26) | copy-start | bytes 36868
  111.5 5.3 %copy-start.16 = (f32[1,24,128]{2,1,0:T(8,128)S(1)}, f32[1,24,128]{2,1,0:T(8,128)}, u32[]{:S(2)}) copy-start(f32[1,24,128]{2,1,0:T(8,128)} %get-tuple-element.27) | copy-start | bytes 36868
where the time goes:
time: 122 us
  local copies, waits for them, and re-layouts  44.4 us (36%)
  other arithmetic  28.2 us (23%)
  waiting for transfers between devices  26.7 us (22%)
  starting transfers between devices  21.8 us (18%)
    ppermute x10, waiting for transfers between devices, extended(): before = lax.ppermute(last, axis, up)  22.5 us
    ppermute x10, starting transfers between devices, extended(): after = lax.ppermute(first, axis, down)  16.7 us
    reshape x2, local copies, waits for them, and re-layouts, restrict(): values.reshape(depth // COARSEN, COARSEN, width_x // COARSEN, COARSEN, wi...  10.8 us
    add x2, other arithmetic, body(): rho_next * rho_now * crop(direction, 1)  7.67 us
    reduce_sum x2, other arithmetic, restrict(): return jnp.mean(blocks, axis=(1, 3, 5))  6.64 us
    reshape x1, local copies, waits for them, and re-layouts, prolong(): return spread.reshape(depth * COARSEN, width_x * COARSEN, width_y * COARSEN)  5.27 us
    ppermute x10, starting transfers between devices, extended(): before = lax.ppermute(last, axis, up)  5.07 us
    add x1, other arithmetic, body(): return iterate + correction + prolong(coarse)  4.63 us
  transfers between devices with their start and end apart: 20, of which 14 were waited for; matrix products, arithmetic and copies ran while one was open for 30% of the time, Pallas kernels for 0%

commit v1 on v0

v1 whole, which is shorter than its diff:
```python
import functools

import jax
import jax.numpy as jnp
from jax import lax
from jax.experimental import pallas as pl
from jax.experimental.pallas import tpu as pltpu
from jax.sharding import PartitionSpec as P

SWEEPS = 3
COARSE_SWEEPS = 4
COARSEN = 8

SHIFT = 0.1
LMIN = 0.3
LMAX = 2.0
OMEGA = 0.8

THETA = (LMAX + LMIN) / 2.0
DELTA = (LMAX - LMIN) / 2.0
SIGMA = THETA / DELTA

RIM = SWEEPS + 1
SUB = 8
LANES = 128
GROUP = 4 * RIM
INNER = RIM

f32 = jnp.float32
VMEM = pl.BlockSpec(memory_space=pltpu.VMEM)


def steps():
    rho, listed = 1.0 / SIGMA, []
    for _ in range(SWEEPS):
        nxt = 1.0 / (2.0 * SIGMA - rho)
        listed.append((nxt * rho, 2.0 * nxt / DELTA))
        rho = nxt
    return listed


def iota(shape, dim):
    return lax.broadcasted_iota(jnp.int32, shape, dim)


def rolled(x, by, dim):
    size = x.shape[dim]
    return pltpu.roll(x, by % size if isinstance(by, int) else by, dim)


def is_even():
    return lax.axis_index("gx") % 2 == 0


def split_z(nz):
    return nz // (LANES // GROUP)


def compact(rows, place):
    shift = 1
    while shift < COARSEN:
        rows = rows + rolled(rows, -shift, 1)
        shift *= 2
    lane = iota(rows.shape, 1)
    width = LANES // COARSEN
    spread = 2 * width
    source = jnp.clip((lane % spread - INNER) * COARSEN, 0, LANES - 1)
    return jnp.where(lane // spread == place, jnp.take_along_axis(rows, source, axis=1), 0.0)


def block_rows(values):
    sub = iota((SUB, LANES), 0)
    out = jnp.zeros((SUB, LANES), f32)
    for block in range(values.shape[0] // COARSEN):
        tile = values[block * COARSEN : (block + 1) * COARSEN]
        out = jnp.where(sub == block, jnp.sum(tile, axis=0, keepdims=True), out)
    return out


def pack_kernel(u_ref, s_ref, c_ref, p1_ref, p2_ref, e_ref, h1_ref, h2_ref):
    nz, nx, _ = u_ref.shape
    half, zs = nz // 2, split_z(nz)
    even = is_even()
    sub = iota((SUB, LANES), 0)
    lane = iota((nx, LANES), 1)
    low = sub < RIM
    per = half + zs // 2

    def send(index, first_a, first_b, last_a, last_b, small):
        first = jnp.where(low, first_a, rolled(first_b, RIM, 0))
        last = jnp.where(low, rolled(last_b, RIM, 0), last_a)
        one, two = jnp.where(even, last, first), jnp.where(even, first, last)
        p1_ref[index] = one
        p2_ref[index] = two
        if small is not None:
            h1_ref[small] = one
            h2_ref[small] = two

    for a, ref in enumerate((u_ref, c_ref, s_ref)):
        for z in range(half):
            send(
                a * per + z, ref[z, :SUB], ref[z + half, :SUB], ref[z, nx - SUB :], ref[z + half, nx - SUB :], None
            )
        strips = []
        for zi in range(zs):
            strip = jnp.zeros((nx, LANES), f32)
            for g in range(nz // zs):
                strip = jnp.where(lane // GROUP == g, rolled(ref[g * zs + zi], g * GROUP + RIM, 1), strip)
            strip = jnp.where(lane % GROUP < 2 * RIM, strip, rolled(strip, 2 * RIM, 1))
            e_ref[a * zs + zi] = strip
            strips.append(strip)
        for zi in range(zs // 2):
            one, two = strips[zi], strips[zi + zs // 2]
            send(a * per + half + zi, one[:SUB], two[:SUB], one[nx - SUB :], two[nx - SUB :], a * (zs // 2) + zi)
    cond = jnp.zeros((SUB, LANES), f32)
    for Z in range(nz // COARSEN):
        total = c_ref[Z * COARSEN]
        for z in range(1, COARSEN):
            total = total + c_ref[Z * COARSEN + z]
        cond = cond + compact(block_rows(total), Z)
    cond = cond * (1.0 / COARSEN**3)
    p1_ref[3 * per] = cond
    p2_ref[3 * per] = cond
    h1_ref[3 * (zs // 2)] = cond
    h2_ref[3 * (zs // 2)] = cond
    e_ref[3 * zs, :SUB] = cond
    for row in range(SUB, nx, SUB):
        e_ref[3 * zs, row : row + SUB] = cond


def pack(u, s, c):
    nz, nx, ny = u.shape
    zs = split_z(nz)
    per = nz // 2 + zs // 2
    big = jax.ShapeDtypeStruct((3 * per + 1, SUB, LANES), f32)
    small = jax.ShapeDtypeStruct((3 * (zs // 2) + 1, SUB, LANES), f32)
    strip = jax.ShapeDtypeStruct((3 * zs + 1, nx, LANES), f32)
    return pl.pallas_call(
        pack_kernel,
        out_shape=(big, big, strip, small, small),
        in_specs=[VMEM] * 3,
        out_specs=(VMEM,) * 5,
        name="pack",
    )(u, s, c)


def local_kernel(u_ref, s_ref, c_ref, o_ref):
    nz, nx, _ = u_ref.shape
    row, lane = iota((nx, LANES), 0), iota((nx, LANES), 1)

    def up(z):
        after = (z + 1) % nz
        return 0.5 * (c_ref[z] + c_ref[after]) * (u_ref[z] - u_ref[after])

    out = jnp.zeros((SUB, LANES), f32)
    for Z in range(nz // COARSEN):
        plain = along_x = along_y = jnp.zeros((nx, LANES), f32)
        for z in range(Z * COARSEN, (Z + 1) * COARSEN):
            u, c = u_ref[z], c_ref[z]
            plain = plain + (s_ref[z] - SHIFT * u)
            along_x = along_x + (c + rolled(c, -1, 0)) * (u - rolled(u, -1, 0))
            along_y = along_y + (c + rolled(c, -1, 1)) * (u - rolled(u, -1, 1))
        along_x = jnp.where(row == nx - 1, 0.0, 0.5 * along_x)
        along_y = jnp.where(lane == LANES - 1, 0.0, 0.5 * along_y)
        plain = plain - along_x + rolled(along_x, 1, 0) - along_y + rolled(along_y, 1, 1)
        plain = plain - up((Z + 1) * COARSEN - 1) + up((Z * COARSEN - 1) % nz)
        out = out + compact(block_rows(plain), Z)
    o_ref[...] = out


def local(u, s, c):
    return pl.pallas_call(
        local_kernel,
        out_shape=jax.ShapeDtypeStruct((SUB, LANES), f32),
        in_specs=[VMEM] * 3,
        out_specs=VMEM,
        cost_estimate=pl.CostEstimate(flops=20 * u.size, bytes_accessed=12 * u.size, transcendentals=0),
        name="local_part",
    )(u, s, c)


def faces_kernel(part_ref, p1_ref, p2_ref, r1_ref, r2_ref, e_ref, el_ref, er_ref, o_ref, *, nz, nx):
    half, zs = nz // 2, split_z(nz)
    per = half + zs // 2
    even = is_even()
    sub, lane = iota((SUB, LANES), 0), iota((SUB, LANES), 1)
    spread = 2 * (LANES // COARSEN)
    width = LANES // COARSEN
    rows = nx // COARSEN
    total = part_ref[...]

    for group in range(half // COARSEN):
        right = left = jnp.zeros((SUB, LANES), f32)
        for z in range(group * COARSEN, (group + 1) * COARSEN):
            def pick(a):
                one, two = p1_ref[a * per + z], p2_ref[a * per + z]
                near, far = r1_ref[a * per + z], r2_ref[a * per + z]
                last, first = jnp.where(even, one, two), jnp.where(even, two, one)
                after, before = jnp.where(even, near, far), jnp.where(even, far, near)
                return rolled(last, 1, 0), first, after, rolled(before, 1, 0)

            u_last, u_first, u_after, u_before = pick(0)
            c_last, c_first, c_after, c_before = pick(1)
            right = right + (c_last + c_after) * (u_last - u_after)
            left = left + (c_before + c_first) * (u_before - u_first)
        right, left = 0.5 * right, 0.5 * left
        for Z, at in ((group, 0), (group + half // COARSEN, RIM)):
            flux = compact(
                jnp.where(sub == 0, left[at : at + 1], 0.0) - jnp.where(sub == rows - 1, right[at : at + 1], 0.0), Z
            )
            total = total + flux

    wide = iota((nx, LANES), 1) % GROUP

    def strip(a, zi):
        at = a * zs + zi
        return jnp.where(wide < RIM, el_ref[at], jnp.where(wide < 3 * RIM, e_ref[at], er_ref[at]))

    flux = jnp.zeros((nx, LANES), f32)
    for zi in range(zs):
        u, c = strip(0, zi), strip(1, zi)
        flux = flux + (c + rolled(c, -1, 1)) * (u - rolled(u, -1, 1))
    flux = block_rows(0.5 * flux)
    flux = flux + rolled(flux, -GROUP, 1)
    place = lane % spread
    total = total + jnp.where(place == INNER, rolled(flux, INNER - (RIM - 1), 1), 0.0)
    total = total - jnp.where(place == INNER + width - 1, rolled(flux, INNER + width - 1 - (3 * RIM - 1), 1), 0.0)

    own = e_ref[3 * zs, :SUB]
    near, far = r1_ref[3 * per], r2_ref[3 * per]
    right, left = jnp.where(even, near, far), jnp.where(even, far, near)
    y_left, y_right = el_ref[3 * zs, :SUB], er_ref[3 * zs, :SUB]
    up = jnp.where(sub == rows - 1, rolled(right, rows - 1, 0), rolled(own, -1, 0))
    down = jnp.where(sub == 0, rolled(left, -(rows - 1), 0), rolled(own, 1, 0))
    fore = jnp.where(place == INNER + width - 1, rolled(y_right, width - 1, 1), rolled(own, -1, 1))
    back = jnp.where(place == INNER, rolled(y_left, 1 - width, 1), rolled(own, 1, 1))
    around = up + down + fore + back + rolled(own, spread, 1) + rolled(own, -spread, 1)
    diag = SHIFT + (0.5 / COARSEN**2) * (6.0 * own + around)
    weight = OMEGA / diag
    o_ref[0] = weight * (total * (1.0 / COARSEN**3))
    o_ref[1] = weight
    o_ref[2] = own


def faces(part, p1, p2, r1, r2, e, el, er, nz, nx):
    return pl.pallas_call(
        functools.partial(faces_kernel, nz=nz, nx=nx),
        out_shape=jax.ShapeDtypeStruct((3, SUB, LANES), f32),
        in_specs=[VMEM] * 8,
        out_specs=VMEM,
        name="faces",
    )(part, p1, p2, r1, r2, e, el, er)


def fine_kernel(
    u_ref, s_ref, c_ref, r1_ref, r2_ref, e_ref, el_ref, er_ref, d1l_ref, d1r_ref, d2l_ref, d2r_ref,
    o_ref,
    uh, ch, sh, cx, cy, cz, inv, q, va, vb, wu, wc, w0, w1, w2,
):
    nz, nx, _ = u_ref.shape
    half, zs = nz // 2, split_z(nz)
    groups = nz // zs
    per = half + zs // 2
    ext = nx + SUB
    even = is_even()
    low = iota((SUB, LANES), 0) < RIM
    table = steps()

    def halo(near, far):
        after, before = jnp.where(even, near, far), jnp.where(even, far, near)
        return jnp.where(low, after, before), rolled(jnp.where(low, before, after), RIM, 0)

    for a, ref in enumerate((uh, ch, sh)):

        @pl.loop(0, half)
        def _(z, a=a, ref=ref):
            first, second = halo(r1_ref[a * per + z], r2_ref[a * per + z])
            ref[z] = first
            ref[z + half] = second

    wide = iota((nx, LANES), 1) % GROUP
    thin = iota((SUB, LANES), 1) % GROUP
    long = iota((ext, LANES), 1) % GROUP

    def join(left, own, right, place):
        return jnp.where(place < RIM, left, jnp.where(place < 3 * RIM, own, right))

    def strips_of(a):
        rims = [None] * zs
        for zi in range(zs // 2):
            at, small = a * per + half + zi, a * (zs // 2) + zi
            near = join(d1l_ref[small], r1_ref[at], d1r_ref[small], thin)
            far = join(d2l_ref[small], r2_ref[at], d2r_ref[small], thin)
            rims[zi], rims[zi + zs // 2] = halo(near, far)
        listed = []
        for zi in range(zs):
            at = a * zs + zi
            listed.append(jnp.concatenate([join(el_ref[at], e_ref[at], er_ref[at], wide), rims[zi]], axis=0))
        return listed

    def z_up(x):
        return x[1:] + [rolled(x[0], -GROUP, 1)]

    def z_down(x):
        return [rolled(x[-1], GROUP, 1)] + x[:-1]

    def window(left, right):
        return jnp.where(long == RIM - 1, left, rolled(right, -(2 * RIM + 2), 1))

    us, cs, ss = strips_of(0), strips_of(1), strips_of(2)
    for zi in range(zs):
        wu[zi] = window(us[zi], us[zi])
        wc[zi] = window(cs[zi], cs[zi])
    cxs = [0.5 * (c + rolled(c, -1, 0)) for c in cs]
    cys = [0.5 * (c + rolled(c, -1, 1)) for c in cs]
    czs = [0.5 * (c + d) for c, d in zip(cs, z_up(cs))]
    czds = z_down(czs)
    invs, qs, vs = [], [], []
    u_up, u_down = z_up(us), z_down(us)
    for zi in range(zs):
        u = us[zi]
        cxl, cyl = rolled(cxs[zi], 1, 0), rolled(cys[zi], 1, 1)
        diag = SHIFT + (cxs[zi] + cxl) + (cys[zi] + cyl) + (czs[zi] + czds[zi])
        near = cxs[zi] * rolled(u, -1, 0) + cxl * rolled(u, 1, 0) + cys[zi] * rolled(u, -1, 1)
        near = near + cyl * rolled(u, 1, 1) + czs[zi] * u_up[zi] + czds[zi] * u_down[zi]
        invs.append(1.0 / diag)
        qs.append((ss[zi] - diag * u + near) * invs[zi])
        vs.append(qs[zi] * (1.0 / THETA))
    for k, w in enumerate((w0, w1, w2)):
        prod = [cys[zi] * vs[zi] for zi in range(zs)]
        for zi in range(zs):
            w[zi] = window(prod[zi], vs[zi])
        if k == SWEEPS - 1:
            break
        keep, lift = table[k]
        v_up, v_down = z_up(vs), z_down(vs)
        fresh = []
        for zi in range(zs):
            v = vs[zi]
            near = cxs[zi] * rolled(v, -1, 0) + rolled(cxs[zi] * v, 1, 0)
            near = near + cys[zi] * rolled(v, -1, 1) + rolled(prod[zi], 1, 1)
            near = near + czs[zi] * v_up[zi] + czds[zi] * v_down[zi]
            qs[zi] = qs[zi] - v + near * invs[zi]
            fresh.append(keep * v + lift * qs[zi])
        vs = fresh

    lane = iota((ext, LANES), 1)
    first_lane, last_lane = lane == 0, lane == LANES - 1

    def whole(ref, rim, z):
        return jnp.concatenate([ref[z], rim[z]], axis=0)

    def turn(w, zi, g):
        return pltpu.roll(w[zi], (2 * LANES - (RIM - 1) - g * GROUP) % LANES, 1)

    @pl.loop(0, groups)
    def _(g):
        for zi in range(zs):
            z = g * zs + zi
            above, below = (z + 1) % nz, (z + nz - 1) % nz
            u, c, s = whole(u_ref, uh, z), whole(c_ref, ch, z), whole(s_ref, sh, z)
            u_up, u_down = whole(u_ref, uh, above), whole(u_ref, uh, below)
            c_up, c_down = whole(c_ref, ch, above), whole(c_ref, ch, below)
            edge_u, edge_c = turn(wu, zi, g), turn(wc, zi, g)
            gx = 0.5 * (c + rolled(c, -1, 0))
            gxl = rolled(gx, 1, 0)
            gy = 0.5 * (c + jnp.where(last_lane, edge_c, rolled(c, -1, 1)))
            gyl = 0.5 * (c + jnp.where(first_lane, edge_c, rolled(c, 1, 1)))
            gz = 0.5 * (c + c_up)
            gzl = 0.5 * (c + c_down)
            diag = SHIFT + (gx + gxl) + (gy + gyl) + (gz + gzl)
            near = gx * rolled(u, -1, 0) + gxl * rolled(u, 1, 0)
            near = near + gy * jnp.where(last_lane, edge_u, rolled(u, -1, 1))
            near = near + gyl * jnp.where(first_lane, edge_u, rolled(u, 1, 1))
            near = near + gz * u_up + gzl * u_down
            inverse = 1.0 / diag
            scaled = (s - diag * u + near) * inverse
            v = scaled * (1.0 / THETA)
            cx[z] = gx
            cy[z] = gy
            cz[z] = gz
            inv[z] = inverse
            q[z] = scaled
            va[z] = v
            o_ref[z] = (u + v)[:nx]

    for k, w in enumerate((w0, w1, w2)):
        old, new = (va, vb) if k % 2 == 0 else (vb, va)
        keep, lift = table[k]

        @pl.loop(0, groups)
        def _(g, w=w, old=old, new=new, keep=keep, lift=lift, final=k == SWEEPS - 1):
            for zi in range(zs):
                z = g * zs + zi
                above, below = (z + 1) % nz, (z + nz - 1) % nz
                v, gx, gy = old[z], cx[z], cy[z]
                edge = turn(w, zi, g)
                near = gx * rolled(v, -1, 0) + rolled(gx * v, 1, 0)
                near = near + gy * jnp.where(last_lane, edge, rolled(v, -1, 1))
                near = near + jnp.where(first_lane, edge, rolled(gy * v, 1, 1))
                near = near + cz[z] * old[above] + cz[below] * old[below]
                scaled = q[z] - v + near * inv[z]
                fresh = keep * v + lift * scaled
                if not final:
                    q[z] = scaled
                    new[z] = fresh
                o_ref[z] = o_ref[z] + fresh[:nx]


def fine(u, s, c, r1, r2, e, el, er, d1l, d1r, d2l, d2r):
    nz, nx, ny = u.shape
    zs = split_z(nz)
    ext = nx + SUB
    full = pltpu.VMEM((nz, ext, LANES), f32)
    rim = pltpu.VMEM((nz, SUB, LANES), f32)
    strip = pltpu.VMEM((zs, ext, LANES), f32)
    return pl.pallas_call(
        fine_kernel,
        out_shape=jax.ShapeDtypeStruct(u.shape, f32),
        in_specs=[VMEM] * 12,
        out_specs=VMEM,
        scratch_shapes=[rim] * 3 + [full] * 7 + [strip] * 5,
        compiler_params=pltpu.CompilerParams(vmem_limit_bytes=32 * 1024 * 1024),
        cost_estimate=pl.CostEstimate(flops=150 * u.size, bytes_accessed=20 * u.size, transcendentals=0),
        name="fine",
    )(u, s, c, r1, r2, e, el, er, d1l, d1r, d2l, d2r)


def finish_kernel(x_ref, m_ref, r1_ref, r2_ref, yl_ref, yr_ref, d1l_ref, d1r_ref, d2l_ref, d2r_ref, o_ref, scr):
    nz, nx, _ = x_ref.shape
    rows = nx // COARSEN
    width = LANES // COARSEN
    spread = 2 * width
    even = is_even()
    lane = iota((SUB, LANES), 1)
    place = lane % spread

    def join(left, own, right):
        return jnp.where(
            place < INNER,
            rolled(left, -width, 1),
            jnp.where(place < INNER + width, own, rolled(right, width, 1)),
        )

    fields = []
    for a in range(3):
        own = join(yl_ref[a], m_ref[a], yr_ref[a])
        near = join(d1l_ref[a], r1_ref[a], d1r_ref[a])
        far = join(d2l_ref[a], r2_ref[a], d2r_ref[a])
        right, left = jnp.where(even, near, far), jnp.where(even, far, near)
        scr[a] = jnp.ones((2 * SUB, LANES), f32)
        scr[a, 0:rows] = left[:rows]
        scr[a, rows : 2 * rows] = own[:rows]
        scr[a, 2 * rows : 3 * rows] = right[:rows]
        fields.append(scr[a])
    start, weight, cond = fields
    half = 0.5 / COARSEN**2
    gx = half * (cond + rolled(cond, -1, 0))
    gy = half * (cond + rolled(cond, -1, 1))
    gz = half * (cond + rolled(cond, -spread, 1))
    v = start
    for _ in range(COARSE_SWEEPS - 1):
        fx = gx * (v - rolled(v, -1, 0))
        fy = gy * (v - rolled(v, -1, 1))
        fz = gz * (v - rolled(v, -spread, 1))
        image = SHIFT * v + (fx - rolled(fx, 1, 0)) + (fy - rolled(fy, 1, 1)) + (fz - rolled(fz, spread, 1))
        v = v + start - weight * image
    top = v[:SUB]
    for Z in range(nz // COARSEN):
        spread_out = jnp.take_along_axis(top, Z * spread + INNER + lane // COARSEN, axis=1)
        for X in range(rows):
            value = jnp.broadcast_to(spread_out[rows + X : rows + X + 1], (COARSEN, LANES))
            for z in range(Z * COARSEN, (Z + 1) * COARSEN):
                at = slice(X * COARSEN, (X + 1) * COARSEN)
                o_ref[z, at] = x_ref[z, at] + value


def finish(x, *messages):
    return pl.pallas_call(
        finish_kernel,
        out_shape=jax.ShapeDtypeStruct(x.shape, f32),
        in_specs=[VMEM] * (1 + len(messages)),
        out_specs=VMEM,
        scratch_shapes=[pltpu.VMEM((3, 2 * SUB, LANES), f32)],
        name="finish",
    )(x, *messages)


def moves():
    size_x, size_y = lax.axis_size("gx"), lax.axis_size("gy")

    def send(x, go):
        pairs = []
        for i in range(size_x):
            for j in range(size_y):
                k, l = go(i, j)
                pairs.append((i * size_y + j, (k % size_x) * size_y + l % size_y))
        return lax.ppermute(x, ("gx", "gy"), pairs)

    def one(i):
        return i + 1 if i % 2 == 0 else i - 1

    def two(i):
        return i - 1 if i % 2 == 0 else i + 1

    def stay(i):
        return i

    def straight(x, along):
        return send(x, lambda i, j: (along(i), j))

    def across(x, along):
        left = send(x, lambda i, j: (along(i), j + 1))
        if size_y == 2:
            return left, left
        return left, send(x, lambda i, j: (along(i), j - 1))

    return one, two, stay, straight, across


def body(iterate, source, conduct):
    nz, nx, ny = iterate.shape
    one, two, stay, straight, across = moves()
    p1, p2, e, h1, h2 = pack(iterate, source, conduct)
    r2 = straight(p2, two)
    d2l, d2r = across(h2, two)
    el, er = across(e, stay)
    r1 = straight(p1, one)
    d1l, d1r = across(h1, one)
    part = local(iterate, source, conduct)
    m = faces(part, p1, p2, r1, r2, e, el, er, nz, nx)
    x = fine(iterate, source, conduct, r1, r2, e, el, er, d1l, d1r, d2l, d2r)
    m2 = straight(m, two)
    c2l, c2r = across(m, two)
    ml, mr = across(m, stay)
    m1 = straight(m, one)
    c1l, c1r = across(m, one)
    return finish(x, m, m1, m2, ml, mr, c1l, c1r, c2l, c2r)


def solution(mesh):
    spec = P(None, "gx", "gy")
    return jax.shard_map(body, mesh=mesh, in_specs=(spec,) * 3, out_specs=spec, check_vma=False)
```

time: 122 us -> 37.5 us (0.31)
  local copies, waits for them, and re-layouts: 44.4 us -> 6.15 us
  other arithmetic: 28.2 us -> 0 us
  waiting for transfers between devices: 26.7 us -> 0.1 us
  Pallas kernels: 0 us -> 15.8 us
  starting transfers between devices: 21.8 us -> 15 us
    ppermute x20 -> x10, waiting for transfers between devices: 26.7 us -> 0.1 us  [send(): return lax.ppermute(x, ('gx', 'gy'), pairs)]
    slice x36 -> x0, local copies, waits for them, and re-layouts: 18.6 us -> none  [the longest x7 3.83 us: extended(): last = lax.slice_in_dim(x, length - width, length, axis=dim)]
    reshape x3 -> x0, local copies, waits for them, and re-layouts: 16.1 us -> none  [the longest x2 10.8 us: restrict(): values.reshape(depth // COARSEN, COARSEN, width_x // COARSEN, COARSEN, wi...]
    pallas_call x0 -> x5, Pallas kernels: none -> 15.8 us  [the longest x1 5.59 us: fine(): pl.pallas_call(fine_kernel, out_shape=jax.ShapeDtypeStruct(u.shape, f32),...]
    add x6 -> x0, other arithmetic: 12.6 us -> none  [the longest x2 7.67 us: body(): rho_next * rho_now * crop(direction, 1)]
    ppermute x20 -> x10, starting transfers between devices: 21.8 us -> 15 us  [send(): return lax.ppermute(x, ('gx', 'gy'), pairs)]
    reduce_sum x2 -> x0, other arithmetic: 6.64 us -> none  [restrict(): return jnp.mean(blocks, axis=(1, 3, 5))]
    ppermute x2 -> x0, local copies, waits for them, and re-layouts: 4.3 us -> none  [the longest x1 2.73 us: extended(): before = lax.ppermute(last, axis, up)]
  transfers between devices with their start and end apart: 20 -> 10, of which waited for: 14 -> 1; matrix products, arithmetic and copies ran while one was open for 30% -> 0% of each run, Pallas kernels for 0% -> 28%
where the time goes in v1:
time: 37.5 us; the launch traced here: 37.2 us
  Pallas kernels  15.8 us (42%)
  starting transfers between devices  15 us (40%)
  local copies, waits for them, and re-layouts  6.15 us (16%)
    ppermute x10, starting transfers between devices, send(): return lax.ppermute(x, ('gx', 'gy'), pairs)  15 us
    unnamed x32, local copies, waits for them, and re-layouts  6.15 us
    pallas_call x1, Pallas kernels, fine(): pl.pallas_call(fine_kernel, out_shape=jax.ShapeDtypeStruct(u.shape, f32),...  5.59 us
    pallas_call x1, Pallas kernels, pack(): pl.pallas_call(pack_kernel, out_shape=(big, big, strip, small, small), in...  3.03 us
    pallas_call x1, Pallas kernels, local(): pl.pallas_call(local_kernel, out_shape=jax.ShapeDtypeStruct((SUB, LANES),...  2.47 us
    pallas_call x1, Pallas kernels, finish(): pl.pallas_call(finish_kernel, out_shape=jax.ShapeDtypeStruct(x.shape, f32...  2.43 us
    pallas_call x1, Pallas kernels, faces(): pl.pallas_call(functools.partial(faces_kernel, nz=nz, nx=nx), out_shape=j...  2.33 us
  transfers between devices with their start and end apart: 10, of which 1 were waited for; matrix products, arithmetic and copies ran while one was open for 0% of the time, Pallas kernels for 28%

profile of v1, /device:TPU:0, one launch (start us, length us, event | category | flops | bytes accessed | tf_op | source)
XLA Modules:
  0.0 37.2 jit_solution(12188997926678463580)
XLA Ops:
  0.0 3.0 %pack.1 = (f32[55,8,128]{2,1,0:T(8,128)}, f32[55,8,128]{2,1,0:T(8,128)}, f32[13,24,128]{2,1,0:T(8,128)}, f32[7,8,128]{2,1,0:T(8,128)}, f32[7,8,128]{2,1,0:T(8,128)}) custom-call(f32[32,24,128]{2,1,0:T(8,128)} %u_ref.5, f32[32,24,128]{2,1,0:T(8,128)} %s_ref.5, f32[32,24,128]{2,1,0:T(8,128)} %c_ref.5), custom_call_target="tpu_custom_call" | custom-call | tf_op jit(solution)/shard_map/pack/pallas_call | solution.py:138
  3.0 0.5 %collective-permute-start = (f32[55,8,128]{2,1,0:T(8,128)}, f32[55,8,128]{2,1,0:T(8,128)S(1)}, u32[]{:S(2)}, u32[]{:S(2)}) collective-permute-start(f32[55,8,128]{2,1,0:T(8,128)} %get-tuple-element.10.p1_ref), channel_id=1, source_target_pairs={{0,2},{1,3},{2,0},{3,1},{4,6},{5,7},{6,4},{7,5},{8,10},{9,11},{10,... | collective-permute-start | bytes 675848 | tf_op jit(solution)/shard_map/ppermute | solution.py:498
  3.5 5.6 %collective-permute-start.1 = (f32[55,8,128]{2,1,0:T(8,128)}, f32[55,8,128]{2,1,0:T(8,128)S(1)}, u32[]{:S(2)}, u32[]{:S(2)}) collective-permute-start(f32[55,8,128]{2,1,0:T(8,128)} %get-tuple-element.11.p2_ref), channel_id=1, source_target_pairs={{0,30},{1,31},{2,4},{3,5},{4,2},{5,3},{6,8},{7,9},{8,6},{9,7},{10,... | collective-permute-start | bytes 675848 | tf_op jit(solution)/shard_map/ppermute | solution.py:498
  9.1 1.5 %collective-permute-start.2 = (f32[13,24,128]{2,1,0:T(8,128)}, f32[13,24,128]{2,1,0:T(8,128)S(1)}, u32[]{:S(2)}, u32[]{:S(2)}) collective-permute-start(f32[13,24,128]{2,1,0:T(8,128)} %get-tuple-element.12.e_ref), channel_id=1, source_target_pairs={{0,1},{1,0},{2,3},{3,2},{4,5},{5,4},{6,7},{7,6},{8,9},{9,8},{10,11... | collective-permute-start | bytes 479240 | tf_op jit(solution)/shard_map/ppermute | solution.py:498
  10.6 0.0 collective-permute-start.3
  10.6 1.7 %collective-permute-start.4 = (f32[7,8,128]{2,1,0:T(8,128)}, f32[7,8,128]{2,1,0:T(8,128)S(1)}, u32[]{:S(2)}, u32[]{:S(2)}) collective-permute-start(f32[7,8,128]{2,1,0:T(8,128)} %get-tuple-element.14), channel_id=1, source_target_pairs={{0,31},{1,30},{2,5},{3,4},{4,3},{5,2},{6,9},{7,8},{8,7},{9,6},{10,... | collective-permute-start | bytes 86024 | tf_op jit(solution)/shard_map/ppermute | solution.py:498
  12.4 2.5 %local_part.1.part_ref = f32[8,128]{1,0:T(8,128)} custom-call(f32[32,24,128]{2,1,0:T(8,128)} %u_ref.5, f32[32,24,128]{2,1,0:T(8,128)} %s_ref.5, f32[32,24,128]{2,1,0:T(8,128)} %c_ref.5), custom_call_target="tpu_custom_call" | custom-call | flops 1966080 | bytes 1179648 | tf_op jit(solution)/shard_map/local_part/pallas_call | solution.py:172
  14.8 0.0 copy-start
  14.8 0.0 copy-start.1
  14.8 0.1 collective-permute-done.2.el_ref.er_ref
  14.9 0.0 collective-permute-done.r1_ref
  14.9 0.0 collective-permute-done.1.r2_ref
  14.9 0.7 %copy-done.3 = f32[13,24,128]{2,1,0:T(8,128)} copy-done((f32[13,24,128]{2,1,0:T(8,128)}, f32[13,24,128]{2,1,0:T(8,128)S(1)}, u32[]{:S(2)}) %copy-start.3) | copy-done | bytes 159768
  15.6 0.1 copy-done.6
  15.7 0.7 %copy-done.8 = f32[55,8,128]{2,1,0:T(8,128)} copy-done((f32[55,8,128]{2,1,0:T(8,128)}, f32[55,8,128]{2,1,0:T(8,128)S(1)}, u32[]{:S(2)}) %copy-start.8) | copy-done | bytes 225304
  16.4 2.3 %faces.1.m_ref = f32[3,8,128]{2,1,0:T(8,128)} custom-call(f32[8,128]{1,0:T(8,128)} %local_part.1.part_ref, f32[55,8,128]{2,1,0:T(8,128)} %get-tuple-element.10.p1_ref, f32[55,8,128]{2,1,0:T(8,128)} %get-tuple-element.11.p2_ref, f32[55,8,128]{2,1,0:T(8,128)} %copy-done.6, f32[55,8,128]{2,1,0:T(8,128)} %copy-done.8, f32[13,24,128]{2,1,0:T(8,128)} %get-tuple-element.12.e_ref, ...), custom_call_target="tpu_custom_call" | custom-call | tf_op jit(solution)/shard_map/faces/pallas_call | solution.py:246
  18.7 3.6 %collective-permute-start.9 = (f32[3,8,128]{2,1,0:T(8,128)}, f32[3,8,128]{2,1,0:T(8,128)S(1)}, u32[]{:S(2)}, u32[]{:S(2)}) collective-permute-start(f32[3,8,128]{2,1,0:T(8,128)} %faces.1.m_ref), channel_id=1, source_target_pairs={{0,31},{1,30},{2,5},{3,4},{4,3},{5,2},{6,9},{7,8},{8,7},{9,6},{10,... | collective-permute-start | bytes 36872 | tf_op jit(solution)/shard_map/ppermute | solution.py:498
  22.3 0.0 collective-permute-start.8
  22.3 0.5 %collective-permute-start.7 = (f32[3,8,128]{2,1,0:T(8,128)}, f32[3,8,128]{2,1,0:T(8,128)S(1)}, u32[]{:S(2)}, u32[]{:S(2)}) collective-permute-start(f32[3,8,128]{2,1,0:T(8,128)} %faces.1.m_ref), channel_id=1, source_target_pairs={{0,1},{1,0},{2,3},{3,2},{4,5},{5,4},{6,7},{7,6},{8,9},{9,8},{10,11... | collective-permute-start | bytes 36872 | tf_op jit(solution)/shard_map/ppermute | solution.py:498
  22.8 0.0 collective-permute-done.3.d1l_ref.d1r_ref
  22.8 1.6 %collective-permute-start.6 = (f32[3,8,128]{2,1,0:T(8,128)}, f32[3,8,128]{2,1,0:T(8,128)S(1)}, u32[]{:S(2)}, u32[]{:S(2)}) collective-permute-start(f32[3,8,128]{2,1,0:T(8,128)} %faces.1.m_ref), channel_id=1, source_target_pairs={{0,30},{1,31},{2,4},{3,5},{4,2},{5,3},{6,8},{7,9},{8,6},{9,7},{10,... | collective-permute-start | bytes 36872 | tf_op jit(solution)/shard_map/ppermute | solution.py:498
  24.4 0.0 collective-permute-done.4.d2l_ref.d2r_ref
  24.4 0.0 collective-permute-start.5
  24.4 0.0 copy-done
  24.4 0.0 copy-done.1
  24.4 0.0 copy-done.2
  24.4 0.0 copy-done.10
  24.4 0.0 copy-start.4
  24.4 0.9 %copy-done.4 = f32[13,24,128]{2,1,0:T(8,128)S(1)} copy-done((f32[13,24,128]{2,1,0:T(8,128)S(1)}, f32[13,24,128]{2,1,0:T(8,128)}, u32[]{:S(2)}) %copy-start.4) | copy-done | bytes 159768
  25.3 0.9 %copy-done.7 = f32[55,8,128]{2,1,0:T(8,128)S(1)} copy-done((f32[55,8,128]{2,1,0:T(8,128)S(1)}, f32[55,8,128]{2,1,0:T(8,128)}, u32[]{:S(2)}) %copy-start.7) | copy-done | bytes 225304
  26.3 0.9 %copy-done.9 = f32[55,8,128]{2,1,0:T(8,128)S(1)} copy-done((f32[55,8,128]{2,1,0:T(8,128)S(1)}, f32[55,8,128]{2,1,0:T(8,128)}, u32[]{:S(2)}) %copy-start.9) | copy-done | bytes 225304
  27.2 5.6 %fine.1.x_ref = f32[32,24,128]{2,1,0:T(8,128)S(1)} custom-call(f32[32,24,128]{2,1,0:T(8,128)S(1)} %copy-done, f32[32,24,128]{2,1,0:T(8,128)S(1)} %copy-done.1, f32[32,24,128]{2,1,0:T(8,128)S(1)} %copy-done.2, f32[55,8,128]{2,1,0:T(8,128)S(1)} %copy-done.7, f32[55,8,128]{2,1,0:T(8,128)S(1)} %copy-done.9, f32[13,24,128]{2,1,0:T(8,128)S(1)} %copy-done.10, ...), custom_call_target="tpu_custom_call" | custom-call | flops 14745600 | bytes 1966080 | tf_op jit(solution)/shard_map/fine/pallas_call | solution.py:417
  32.8 0.0 copy-start.5
  32.8 0.7 %copy-done.5 = f32[32,24,128]{2,1,0:T(8,128)} copy-done((f32[32,24,128]{2,1,0:T(8,128)}, f32[32,24,128]{2,1,0:T(8,128)S(1)}, u32[]{:S(2)}) %copy-start.5) | copy-done | bytes 393240
  33.5 0.0 collective-permute-done.9.d2l_ref.d2r_ref
  33.5 0.0 collective-permute-done.8.d1l_ref.d1r_ref
  33.6 0.0 copy-start.12
  33.6 0.0 collective-permute-done.7.yl_ref.yr_ref
  33.6 0.0 copy-start.13
  33.6 0.0 collective-permute-done.6.r2_ref
  33.6 0.0 copy-start.14
  33.6 0.0 collective-permute-done.5.r1_ref
  33.6 0.5 %copy-done.11 = f32[3,8,128]{2,1,0:T(8,128)} copy-done((f32[3,8,128]{2,1,0:T(8,128)}, f32[3,8,128]{2,1,0:T(8,128)S(1)}, u32[]{:S(2)}) %copy-start.11) | copy-done | bytes 12312
  34.1 0.0 copy-done.12
  34.2 0.0 copy-done.13
  34.2 0.0 copy-done.14
  34.2 0.6 %copy-done.15 = f32[3,8,128]{2,1,0:T(8,128)} copy-done((f32[3,8,128]{2,1,0:T(8,128)}, f32[3,8,128]{2,1,0:T(8,128)S(1)}, u32[]{:S(2)}) %copy-start.15) | copy-done | bytes 12312
  34.8 2.4 %finish.1 = f32[32,24,128]{2,1,0:T(8,128)} custom-call(f32[32,24,128]{2,1,0:T(8,128)} %copy-done.5, f32[3,8,128]{2,1,0:T(8,128)} %faces.1.m_ref, f32[3,8,128]{2,1,0:T(8,128)} %copy-done.15, f32[3,8,128]{2,1,0:T(8,128)} %copy-done.14, f32[3,8,128]{2,1,0:T(8,128)} %copy-done.13, f32[3,8,128]{2,1,0:T(8,128)} %copy-done.13, f32[3,8,128]{2,1,0:T(8,128)} %copy-done.12, ...), custom_call_target="tpu_custom_call" | custom-call | tf_op jit(solution)/shard_map/finish/pallas_call | solution.py:479
  (9 shorter events, 0.0 us)
Async XLA Ops:
  3.0 11.9 %collective-permute-start = (f32[55,8,128]{2,1,0:T(8,128)}, f32[55,8,128]{2,1,0:T(8,128)S(1)}, u32[]{:S(2)}, u32[]{:S(2)}) collective-permute-start(f32[55,8,128]{2,1,0:T(8,128)} %get-tuple-element.10.p1_ref), channel_id=1, source_target_pairs={{0,2},{1,3},{2,0},{3,1},{4,6},{5,7},{6,4},{7,5},{8,10},{9,11},{10,... | collective-permute-start | bytes 675848 | tf_op jit(solution)/shard_map/ppermute | solution.py:498
  3.5 11.4 %collective-permute-start.1 = (f32[55,8,128]{2,1,0:T(8,128)}, f32[55,8,128]{2,1,0:T(8,128)S(1)}, u32[]{:S(2)}, u32[]{:S(2)}) collective-permute-start(f32[55,8,128]{2,1,0:T(8,128)} %get-tuple-element.11.p2_ref), channel_id=1, source_target_pairs={{0,30},{1,31},{2,4},{3,5},{4,2},{5,3},{6,8},{7,9},{8,6},{9,7},{10,... | collective-permute-start | bytes 675848 | tf_op jit(solution)/shard_map/ppermute | solution.py:498
  9.1 5.8 %collective-permute-start.2 = (f32[13,24,128]{2,1,0:T(8,128)}, f32[13,24,128]{2,1,0:T(8,128)S(1)}, u32[]{:S(2)}, u32[]{:S(2)}) collective-permute-start(f32[13,24,128]{2,1,0:T(8,128)} %get-tuple-element.12.e_ref), channel_id=1, source_target_pairs={{0,1},{1,0},{2,3},{3,2},{4,5},{5,4},{6,7},{7,6},{8,9},{9,8},{10,11... | collective-permute-start | bytes 479240 | tf_op jit(solution)/shard_map/ppermute | solution.py:498
  10.6 12.2 %collective-permute-start.3 = (f32[7,8,128]{2,1,0:T(8,128)}, f32[7,8,128]{2,1,0:T(8,128)S(1)}, u32[]{:S(2)}, u32[]{:S(2)}) collective-permute-start(f32[7,8,128]{2,1,0:T(8,128)} %get-tuple-element.13), channel_id=1, source_target_pairs={{0,3},{1,2},{2,1},{3,0},{4,7},{5,6},{6,5},{7,4},{8,11},{9,10},{10,... | collective-permute-start | bytes 86024 | tf_op jit(solution)/shard_map/ppermute | solution.py:498
  10.6 13.7 %collective-permute-start.4 = (f32[7,8,128]{2,1,0:T(8,128)}, f32[7,8,128]{2,1,0:T(8,128)S(1)}, u32[]{:S(2)}, u32[]{:S(2)}) collective-permute-start(f32[7,8,128]{2,1,0:T(8,128)} %get-tuple-element.14), channel_id=1, source_target_pairs={{0,31},{1,30},{2,5},{3,4},{4,3},{5,2},{6,9},{7,8},{8,7},{9,6},{10,... | collective-permute-start | bytes 86024 | tf_op jit(solution)/shard_map/ppermute | solution.py:498
  14.8 9.5 %copy-start = (f32[32,24,128]{2,1,0:T(8,128)S(1)}, f32[32,24,128]{2,1,0:T(8,128)}, u32[]{:S(2)}) copy-start(f32[32,24,128]{2,1,0:T(8,128)} %u_ref.5) | copy-start | bytes 1179652
  14.8 9.5 %copy-start.1 = (f32[32,24,128]{2,1,0:T(8,128)S(1)}, f32[32,24,128]{2,1,0:T(8,128)}, u32[]{:S(2)}) copy-start(f32[32,24,128]{2,1,0:T(8,128)} %s_ref.5) | copy-start | bytes 1179652
  14.8 9.6 %copy-start.2 = (f32[32,24,128]{2,1,0:T(8,128)S(1)}, f32[32,24,128]{2,1,0:T(8,128)}, u32[]{:S(2)}) copy-start(f32[32,24,128]{2,1,0:T(8,128)} %c_ref.5) | copy-start | bytes 1179652
  14.8 9.6 %copy-start.10 = (f32[13,24,128]{2,1,0:T(8,128)S(1)}, f32[13,24,128]{2,1,0:T(8,128)}, u32[]{:S(2)}) copy-start(f32[13,24,128]{2,1,0:T(8,128)} %get-tuple-element.12.e_ref) | copy-start | bytes 479236
  14.9 0.7 %copy-start.3 = (f32[13,24,128]{2,1,0:T(8,128)}, f32[13,24,128]{2,1,0:T(8,128)S(1)}, u32[]{:S(2)}) copy-start(f32[13,24,128]{2,1,0:T(8,128)S(1)} %collective-permute-done.2.el_ref.er_ref) | copy-start | bytes 479236
  14.9 0.8 %copy-start.6 = (f32[55,8,128]{2,1,0:T(8,128)}, f32[55,8,128]{2,1,0:T(8,128)S(1)}, u32[]{:S(2)}) copy-start(f32[55,8,128]{2,1,0:T(8,128)S(1)} %collective-permute-done.r1_ref) | copy-start | bytes 675844
  15.7 0.7 %copy-start.8 = (f32[55,8,128]{2,1,0:T(8,128)}, f32[55,8,128]{2,1,0:T(8,128)S(1)}, u32[]{:S(2)}) copy-start(f32[55,8,128]{2,1,0:T(8,128)S(1)} %collective-permute-done.1.r2_ref) | copy-start | bytes 675844
  18.7 14.8 %collective-permute-start.9 = (f32[3,8,128]{2,1,0:T(8,128)}, f32[3,8,128]{2,1,0:T(8,128)S(1)}, u32[]{:S(2)}, u32[]{:S(2)}) collective-permute-start(f32[3,8,128]{2,1,0:T(8,128)} %faces.1.m_ref), channel_id=1, source_target_pairs={{0,31},{1,30},{2,5},{3,4},{4,3},{5,2},{6,9},{7,8},{8,7},{9,6},{10,... | collective-permute-start | bytes 36872 | tf_op jit(solution)/shard_map/ppermute | solution.py:498
  22.3 11.3 %collective-permute-start.8 = (f32[3,8,128]{2,1,0:T(8,128)}, f32[3,8,128]{2,1,0:T(8,128)S(1)}, u32[]{:S(2)}, u32[]{:S(2)}) collective-permute-start(f32[3,8,128]{2,1,0:T(8,128)} %faces.1.m_ref), channel_id=1, source_target_pairs={{0,3},{1,2},{2,1},{3,0},{4,7},{5,6},{6,5},{7,4},{8,11},{9,10},{10,... | collective-permute-start | bytes 36872 | tf_op jit(solution)/shard_map/ppermute | solution.py:498
  22.3 11.3 %collective-permute-start.7 = (f32[3,8,128]{2,1,0:T(8,128)}, f32[3,8,128]{2,1,0:T(8,128)S(1)}, u32[]{:S(2)}, u32[]{:S(2)}) collective-permute-start(f32[3,8,128]{2,1,0:T(8,128)} %faces.1.m_ref), channel_id=1, source_target_pairs={{0,1},{1,0},{2,3},{3,2},{4,5},{5,4},{6,7},{7,6},{8,9},{9,8},{10,11... | collective-permute-start | bytes 36872 | tf_op jit(solution)/shard_map/ppermute | solution.py:498
  22.8 10.8 %collective-permute-start.6 = (f32[3,8,128]{2,1,0:T(8,128)}, f32[3,8,128]{2,1,0:T(8,128)S(1)}, u32[]{:S(2)}, u32[]{:S(2)}) collective-permute-start(f32[3,8,128]{2,1,0:T(8,128)} %faces.1.m_ref), channel_id=1, source_target_pairs={{0,30},{1,31},{2,4},{3,5},{4,2},{5,3},{6,8},{7,9},{8,6},{9,7},{10,... | collective-permute-start | bytes 36872 | tf_op jit(solution)/shard_map/ppermute | solution.py:498
  24.4 9.2 %collective-permute-start.5 = (f32[3,8,128]{2,1,0:T(8,128)}, f32[3,8,128]{2,1,0:T(8,128)S(1)}, u32[]{:S(2)}, u32[]{:S(2)}) collective-permute-start(f32[3,8,128]{2,1,0:T(8,128)} %faces.1.m_ref), channel_id=1, source_target_pairs={{0,2},{1,3},{2,0},{3,1},{4,6},{5,7},{6,4},{7,5},{8,10},{9,11},{10,... | collective-permute-start | bytes 36872 | tf_op jit(solution)/shard_map/ppermute | solution.py:498
  24.4 0.9 %copy-start.4 = (f32[13,24,128]{2,1,0:T(8,128)S(1)}, f32[13,24,128]{2,1,0:T(8,128)}, u32[]{:S(2)}) copy-start(f32[13,24,128]{2,1,0:T(8,128)} %copy-done.3) | copy-start | bytes 479236
  25.3 0.9 %copy-start.7 = (f32[55,8,128]{2,1,0:T(8,128)S(1)}, f32[55,8,128]{2,1,0:T(8,128)}, u32[]{:S(2)}) copy-start(f32[55,8,128]{2,1,0:T(8,128)} %copy-done.6) | copy-start | bytes 675844
  26.3 0.9 %copy-start.9 = (f32[55,8,128]{2,1,0:T(8,128)S(1)}, f32[55,8,128]{2,1,0:T(8,128)}, u32[]{:S(2)}) copy-start(f32[55,8,128]{2,1,0:T(8,128)} %copy-done.8) | copy-start | bytes 675844
  32.8 0.7 %copy-start.5 = (f32[32,24,128]{2,1,0:T(8,128)}, f32[32,24,128]{2,1,0:T(8,128)S(1)}, u32[]{:S(2)}) copy-start(f32[32,24,128]{2,1,0:T(8,128)S(1)} %fine.1.x_ref) | copy-start | bytes 1179652
  33.5 0.6 %copy-start.11 = (f32[3,8,128]{2,1,0:T(8,128)}, f32[3,8,128]{2,1,0:T(8,128)S(1)}, u32[]{:S(2)}) copy-start(f32[3,8,128]{2,1,0:T(8,128)S(1)} %collective-permute-done.9.d2l_ref.d2r_ref) | copy-start | bytes 36868
  33.6 0.6 %copy-start.12 = (f32[3,8,128]{2,1,0:T(8,128)}, f32[3,8,128]{2,1,0:T(8,128)S(1)}, u32[]{:S(2)}) copy-start(f32[3,8,128]{2,1,0:T(8,128)S(1)} %collective-permute-done.8.d1l_ref.d1r_ref) | copy-start | bytes 36868
  33.6 0.6 %copy-start.13 = (f32[3,8,128]{2,1,0:T(8,128)}, f32[3,8,128]{2,1,0:T(8,128)S(1)}, u32[]{:S(2)}) copy-start(f32[3,8,128]{2,1,0:T(8,128)S(1)} %collective-permute-done.7.yl_ref.yr_ref) | copy-start | bytes 36868
  33.6 0.6 %copy-start.14 = (f32[3,8,128]{2,1,0:T(8,128)}, f32[3,8,128]{2,1,0:T(8,128)S(1)}, u32[]{:S(2)}) copy-start(f32[3,8,128]{2,1,0:T(8,128)S(1)} %collective-permute-done.6.r2_ref) | copy-start | bytes 36868
  34.2 0.6 %copy-start.15 = (f32[3,8,128]{2,1,0:T(8,128)}, f32[3,8,128]{2,1,0:T(8,128)S(1)}, u32[]{:S(2)}) copy-start(f32[3,8,128]{2,1,0:T(8,128)S(1)} %collective-permute-done.5.r1_ref) | copy-start | bytes 36868

commit v2 on v1

--- a/solution.py
+++ b/solution.py
@@ -28,6 +28,7 @@
 
 f32 = jnp.float32
 VMEM = pl.BlockSpec(memory_space=pltpu.VMEM)
+SMALL = pltpu.CompilerParams(vmem_limit_bytes=12 * 1024 * 1024)
 
 
 def steps():
@@ -140,6 +141,7 @@
         out_shape=(big, big, strip, small, small),
         in_specs=[VMEM] * 3,
         out_specs=(VMEM,) * 5,
+        compiler_params=SMALL,
         name="pack",
     )(u, s, c)
 
@@ -175,6 +177,7 @@
         in_specs=[VMEM] * 3,
         out_specs=VMEM,
         cost_estimate=pl.CostEstimate(flops=20 * u.size, bytes_accessed=12 * u.size, transcendentals=0),
+        compiler_params=SMALL,
         name="local_part",
     )(u, s, c)
 
@@ -248,6 +251,7 @@
         out_shape=jax.ShapeDtypeStruct((3, SUB, LANES), f32),
         in_specs=[VMEM] * 8,
         out_specs=VMEM,
+        compiler_params=SMALL,
         name="faces",
     )(part, p1, p2, r1, r2, e, el, er)
 
@@ -420,7 +424,7 @@
         in_specs=[VMEM] * 12,
         out_specs=VMEM,
         scratch_shapes=[rim] * 3 + [full] * 7 + [strip] * 5,
-        compiler_params=pltpu.CompilerParams(vmem_limit_bytes=32 * 1024 * 1024),
+        compiler_params=SMALL,
         cost_estimate=pl.CostEstimate(flops=150 * u.size, bytes_accessed=20 * u.size, transcendentals=0),
         name="fine",
     )(u, s, c, r1, r2, e, el, er, d1l, d1r, d2l, d2r)
@@ -482,6 +486,7 @@
         in_specs=[VMEM] * (1 + len(messages)),
         out_specs=VMEM,
         scratch_shapes=[pltpu.VMEM((3, 2 * SUB, LANES), f32)],
+        compiler_params=SMALL,
         name="finish",
     )(x, *messages)
 

time: 37.5 us -> 29.1 us (0.78)
  Pallas kernels: 15.8 us -> 8.95 us
  local copies, waits for them, and re-layouts: 6.15 us -> 3 us
  waiting for transfers between devices: 0.1 us -> 1.71 us
    unnamed x32 -> x12, local copies, waits for them, and re-layouts: 6.15 us -> 3 us
    pallas_call x1, Pallas kernels: 3.03 us -> 0.97 us  [pack(): pl.pallas_call(pack_kernel, out_shape=(big, big, strip, small, small), in...]
    pallas_call x1, Pallas kernels: 2.33 us -> 0.34 us  [faces(): pl.pallas_call(functools.partial(faces_kernel, nz=nz, nx=nx), out_shape=j...]
    pallas_call x1, Pallas kernels: 2.47 us -> 0.65 us  [local(): pl.pallas_call(local_kernel, out_shape=jax.ShapeDtypeStruct((SUB, LANES),...]
    ppermute x10, waiting for transfers between devices: 0.1 us -> 1.71 us  [send(): return lax.ppermute(x, ('gx', 'gy'), pairs)]
    pallas_call x1, Pallas kernels: 2.43 us -> 1.36 us  [finish(): pl.pallas_call(finish_kernel, out_shape=jax.ShapeDtypeStruct(x.shape, f32...]
  transfers between devices with their start and end apart: 10 -> 10, of which waited for: 1 -> 1; matrix products, arithmetic and copies ran while one was open for 0% -> 0% of each run, Pallas kernels for 28% -> 23%
where the time goes in v2:
time: 29.1 us; the launch traced here: 28.9 us
  starting transfers between devices  15.1 us (52%)
  Pallas kernels  8.95 us (31%)
  local copies, waits for them, and re-layouts  3 us (10%)
  waiting for transfers between devices  1.71 us (6%)
    ppermute x10, starting transfers between devices, send(): return lax.ppermute(x, ('gx', 'gy'), pairs)  15.1 us
    pallas_call x1, Pallas kernels, fine(): pl.pallas_call(fine_kernel, out_shape=jax.ShapeDtypeStruct(u.shape, f32),...  5.63 us
    unnamed x12, local copies, waits for them, and re-layouts  3 us
    ppermute x10, waiting for transfers between devices, send(): return lax.ppermute(x, ('gx', 'gy'), pairs)  1.71 us
    pallas_call x1, Pallas kernels, finish(): pl.pallas_call(finish_kernel, out_shape=jax.ShapeDtypeStruct(x.shape, f32...  1.36 us
    pallas_call x1, Pallas kernels, pack(): pl.pallas_call(pack_kernel, out_shape=(big, big, strip, small, small), in...  0.97 us
    pallas_call x1, Pallas kernels, local(): pl.pallas_call(local_kernel, out_shape=jax.ShapeDtypeStruct((SUB, LANES),...  0.65 us
  transfers between devices with their start and end apart: 10, of which 1 were waited for; matrix products, arithmetic and copies ran while one was open for 0% of the time, Pallas kernels for 23%

profile of v2, /device:TPU:0, one launch (start us, length us, event | category | flops | bytes accessed | tf_op | source)
XLA Modules:
  0.0 28.9 jit_solution(5687573295807719098)
XLA Ops:
  0.0 0.0 copy-start
  0.0 1.0 %copy-done = f32[32,24,128]{2,1,0:T(8,128)S(1)} copy-done((f32[32,24,128]{2,1,0:T(8,128)S(1)}, f32[32,24,128]{2,1,0:T(8,128)}, u32[]{:S(2)}) %copy-start) | copy-done | bytes 393240
  1.0 0.0 copy-start.2
  1.0 1.0 %copy-done.2 = f32[32,24,128]{2,1,0:T(8,128)S(1)} copy-done((f32[32,24,128]{2,1,0:T(8,128)S(1)}, f32[32,24,128]{2,1,0:T(8,128)}, u32[]{:S(2)}) %copy-start.2) | copy-done | bytes 393240
  2.0 0.0 copy-start.4
  2.0 1.0 %copy-done.4 = f32[32,24,128]{2,1,0:T(8,128)S(1)} copy-done((f32[32,24,128]{2,1,0:T(8,128)S(1)}, f32[32,24,128]{2,1,0:T(8,128)}, u32[]{:S(2)}) %copy-start.4) | copy-done | bytes 393240
  3.0 1.0 %pack.1 = (f32[55,8,128]{2,1,0:T(8,128)S(1)}, f32[55,8,128]{2,1,0:T(8,128)S(1)}, f32[13,24,128]{2,1,0:T(8,128)S(1)}, f32[7,8,128]{2,1,0:T(8,128)S(1)}, f32[7,8,128]{2,1,0:T(8,128)S(1)}) custom-call(f32[32,24,128]{2,1,0:T(8,128)S(1)} %copy-done, f32[32,24,128]{2,1,0:T(8,128)S(1)} %copy-done.2, f32[32,24,128]{2,1,0:T(8,128)S(1)} %copy-done.4), custom_call_target="tpu_custom_call" | custom-call | tf_op jit(solution)/shard_map/pack/pallas_call | solution.py:139
  4.0 0.5 %collective-permute-start = (f32[55,8,128]{2,1,0:T(8,128)S(1)}, f32[55,8,128]{2,1,0:T(8,128)S(1)}, u32[]{:S(2)}, u32[]{:S(2)}) collective-permute-start(f32[55,8,128]{2,1,0:T(8,128)S(1)} %get-tuple-element.10.p1_ref), channel_id=1, source_target_pairs={{0,2},{1,3},{2,0},{3,1},{4,6},{5,7},{6,4},{7,5},{8,10},{9,11},{10,... | collective-permute-start | bytes 675848 | tf_op jit(solution)/shard_map/ppermute | solution.py:503
  4.5 5.6 %collective-permute-start.1 = (f32[55,8,128]{2,1,0:T(8,128)S(1)}, f32[55,8,128]{2,1,0:T(8,128)S(1)}, u32[]{:S(2)}, u32[]{:S(2)}) collective-permute-start(f32[55,8,128]{2,1,0:T(8,128)S(1)} %get-tuple-element.11.p2_ref), channel_id=1, source_target_pairs={{0,30},{1,31},{2,4},{3,5},{4,2},{5,3},{6,8},{7,9},{8,6},{9,7},{10,... | collective-permute-start | bytes 675848 | tf_op jit(solution)/shard_map/ppermute | solution.py:503
  10.1 1.5 %collective-permute-start.2 = (f32[13,24,128]{2,1,0:T(8,128)S(1)}, f32[13,24,128]{2,1,0:T(8,128)S(1)}, u32[]{:S(2)}, u32[]{:S(2)}) collective-permute-start(f32[13,24,128]{2,1,0:T(8,128)S(1)} %get-tuple-element.12.e_ref), channel_id=1, source_target_pairs={{0,1},{1,0},{2,3},{3,2},{4,5},{5,4},{6,7},{7,6},{8,9},{9,8},{10,11... | collective-permute-start | bytes 479240 | tf_op jit(solution)/shard_map/ppermute | solution.py:503
  11.6 0.0 collective-permute-start.3
  11.7 1.7 %collective-permute-start.4 = (f32[7,8,128]{2,1,0:T(8,128)S(1)}, f32[7,8,128]{2,1,0:T(8,128)S(1)}, u32[]{:S(2)}, u32[]{:S(2)}) collective-permute-start(f32[7,8,128]{2,1,0:T(8,128)S(1)} %get-tuple-element.14), channel_id=1, source_target_pairs={{0,31},{1,30},{2,5},{3,4},{4,3},{5,2},{6,9},{7,8},{8,7},{9,6},{10,... | collective-permute-start | bytes 86024 | tf_op jit(solution)/shard_map/ppermute | solution.py:503
  13.4 0.6 %local_part.1.part_ref = f32[8,128]{1,0:T(8,128)S(1)} custom-call(f32[32,24,128]{2,1,0:T(8,128)S(1)} %copy-done, f32[32,24,128]{2,1,0:T(8,128)S(1)} %copy-done.2, f32[32,24,128]{2,1,0:T(8,128)S(1)} %copy-done.4), custom_call_target="tpu_custom_call" | custom-call | flops 1966080 | bytes 1179648 | tf_op jit(solution)/shard_map/local_part/pallas_call | solution.py:174
  14.0 0.0 copy-start.1
  14.0 0.0 copy-start.3
  14.0 0.0 copy-start.5
  14.0 1.7 %collective-permute-done.2.el_ref.er_ref = f32[13,24,128]{2,1,0:T(8,128)S(1)} collective-permute-done((f32[13,24,128]{2,1,0:T(8,128)S(1)}, f32[13,24,128]{2,1,0:T(8,128)S(1)}, u32[]{:S(2)}, u32[]{:S(2)}) %collective-permute-start.2) | collective-permute-done | bytes 159776 | tf_op jit(solution)/shard_map/ppermute | solution.py:503
  15.7 0.0 collective-permute-done.r1_ref
  15.7 0.0 collective-permute-done.1.r2_ref
  15.7 0.3 %faces.1.m_ref = f32[3,8,128]{2,1,0:T(8,128)S(1)} custom-call(f32[8,128]{1,0:T(8,128)S(1)} %local_part.1.part_ref, f32[55,8,128]{2,1,0:T(8,128)S(1)} %get-tuple-element.10.p1_ref, f32[55,8,128]{2,1,0:T(8,128)S(1)} %get-tuple-element.11.p2_ref, f32[55,8,128]{2,1,0:T(8,128)S(1)} %collective-permute-done.r1_ref, ...), custom_call_target="tpu_custom_call" | custom-call | tf_op jit(solution)/shard_map/faces/pallas_call | solution.py:249
  16.1 3.5 %collective-permute-start.9 = (f32[3,8,128]{2,1,0:T(8,128)S(1)}, f32[3,8,128]{2,1,0:T(8,128)S(1)}, u32[]{:S(2)}, u32[]{:S(2)}) collective-permute-start(f32[3,8,128]{2,1,0:T(8,128)S(1)} %faces.1.m_ref), channel_id=1, source_target_pairs={{0,31},{1,30},{2,5},{3,4},{4,3},{5,2},{6,9},{7,8},{8,7},{9,6},{10,... | collective-permute-start | bytes 36872 | tf_op jit(solution)/shard_map/ppermute | solution.py:503
  19.6 0.0 collective-permute-start.8
  19.6 0.5 %collective-permute-start.7 = (f32[3,8,128]{2,1,0:T(8,128)S(1)}, f32[3,8,128]{2,1,0:T(8,128)S(1)}, u32[]{:S(2)}, u32[]{:S(2)}) collective-permute-start(f32[3,8,128]{2,1,0:T(8,128)S(1)} %faces.1.m_ref), channel_id=1, source_target_pairs={{0,1},{1,0},{2,3},{3,2},{4,5},{5,4},{6,7},{7,6},{8,9},{9,8},{10,11... | collective-permute-start | bytes 36872 | tf_op jit(solution)/shard_map/ppermute | solution.py:503
  20.1 0.0 collective-permute-done.3.d1l_ref.d1r_ref
  20.1 1.7 %collective-permute-start.6 = (f32[3,8,128]{2,1,0:T(8,128)S(1)}, f32[3,8,128]{2,1,0:T(8,128)S(1)}, u32[]{:S(2)}, u32[]{:S(2)}) collective-permute-start(f32[3,8,128]{2,1,0:T(8,128)S(1)} %faces.1.m_ref), channel_id=1, source_target_pairs={{0,30},{1,31},{2,4},{3,5},{4,2},{5,3},{6,8},{7,9},{8,6},{9,7},{10,... | collective-permute-start | bytes 36872 | tf_op jit(solution)/shard_map/ppermute | solution.py:503
  21.8 0.0 collective-permute-done.4.d2l_ref.d2r_ref
  21.8 0.0 collective-permute-start.5
  21.8 0.0 copy-done.1
  21.8 0.0 copy-done.3
  21.8 0.0 copy-done.5
  21.8 5.6 %fine.1.x_ref = f32[32,24,128]{2,1,0:T(8,128)S(1)} custom-call(f32[32,24,128]{2,1,0:T(8,128)S(1)} %copy-done.1, f32[32,24,128]{2,1,0:T(8,128)S(1)} %copy-done.3, f32[32,24,128]{2,1,0:T(8,128)S(1)} %copy-done.5, f32[55,8,128]{2,1,0:T(8,128)S(1)} %collective-permute-done.r1_ref, f32[55,8,128]{2,1,0:T(8,128)S(1)} %collective-permute-done.1.r2_ref, ...), custom_call_target="tpu_custom_call" | custom-call | flops 14745600 | bytes 1966080 | tf_op jit(solution)/shard_map/fine/pallas_call | solution.py:421
  27.4 0.0 collective-permute-done.9.d2l_ref.d2r_ref
  27.5 0.0 collective-permute-done.8.d1l_ref.d1r_ref
  27.5 0.0 collective-permute-done.7.yl_ref.yr_ref
  27.5 0.0 collective-permute-done.6.r2_ref
  27.5 0.0 collective-permute-done.5.r1_ref
  27.5 1.4 %finish.1 = f32[32,24,128]{2,1,0:T(8,128)} custom-call(f32[32,24,128]{2,1,0:T(8,128)S(1)} %fine.1.x_ref, f32[3,8,128]{2,1,0:T(8,128)S(1)} %faces.1.m_ref, f32[3,8,128]{2,1,0:T(8,128)S(1)} %collective-permute-done.5.r1_ref, f32[3,8,128]{2,1,0:T(8,128)S(1)} %collective-permute-done.6.r2_ref, f32[3,8,128]{2,1,0:T(8,128)S(1)} %collective-permute-done.7.yl_ref.yr_ref, ...), custom_call_target="tpu_custom_call" | custom-call | tf_op jit(solution)/shard_map/finish/pallas_call | solution.py:483
Async XLA Ops:
  0.0 1.0 %copy-start = (f32[32,24,128]{2,1,0:T(8,128)S(1)}, f32[32,24,128]{2,1,0:T(8,128)}, u32[]{:S(2)}) copy-start(f32[32,24,128]{2,1,0:T(8,128)} %u_ref.5) | copy-start | bytes 1179652
  1.0 1.0 %copy-start.2 = (f32[32,24,128]{2,1,0:T(8,128)S(1)}, f32[32,24,128]{2,1,0:T(8,128)}, u32[]{:S(2)}) copy-start(f32[32,24,128]{2,1,0:T(8,128)} %s_ref.5) | copy-start | bytes 1179652
  2.0 1.0 %copy-start.4 = (f32[32,24,128]{2,1,0:T(8,128)S(1)}, f32[32,24,128]{2,1,0:T(8,128)}, u32[]{:S(2)}) copy-start(f32[32,24,128]{2,1,0:T(8,128)} %c_ref.5) | copy-start | bytes 1179652
  4.0 11.7 %collective-permute-start = (f32[55,8,128]{2,1,0:T(8,128)S(1)}, f32[55,8,128]{2,1,0:T(8,128)S(1)}, u32[]{:S(2)}, u32[]{:S(2)}) collective-permute-start(f32[55,8,128]{2,1,0:T(8,128)S(1)} %get-tuple-element.10.p1_ref), channel_id=1, source_target_pairs={{0,2},{1,3},{2,0},{3,1},{4,6},{5,7},{6,4},{7,5},{8,10},{9,11},{10,... | collective-permute-start | bytes 675848 | tf_op jit(solution)/shard_map/ppermute | solution.py:503
  4.5 11.2 %collective-permute-start.1 = (f32[55,8,128]{2,1,0:T(8,128)S(1)}, f32[55,8,128]{2,1,0:T(8,128)S(1)}, u32[]{:S(2)}, u32[]{:S(2)}) collective-permute-start(f32[55,8,128]{2,1,0:T(8,128)S(1)} %get-tuple-element.11.p2_ref), channel_id=1, source_target_pairs={{0,30},{1,31},{2,4},{3,5},{4,2},{5,3},{6,8},{7,9},{8,6},{9,7},{10,... | collective-permute-start | bytes 675848 | tf_op jit(solution)/shard_map/ppermute | solution.py:503
  10.1 5.6 %collective-permute-start.2 = (f32[13,24,128]{2,1,0:T(8,128)S(1)}, f32[13,24,128]{2,1,0:T(8,128)S(1)}, u32[]{:S(2)}, u32[]{:S(2)}) collective-permute-start(f32[13,24,128]{2,1,0:T(8,128)S(1)} %get-tuple-element.12.e_ref), channel_id=1, source_target_pairs={{0,1},{1,0},{2,3},{3,2},{4,5},{5,4},{6,7},{7,6},{8,9},{9,8},{10,11... | collective-permute-start | bytes 479240 | tf_op jit(solution)/shard_map/ppermute | solution.py:503
  11.6 8.5 %collective-permute-start.3 = (f32[7,8,128]{2,1,0:T(8,128)S(1)}, f32[7,8,128]{2,1,0:T(8,128)S(1)}, u32[]{:S(2)}, u32[]{:S(2)}) collective-permute-start(f32[7,8,128]{2,1,0:T(8,128)S(1)} %get-tuple-element.13), channel_id=1, source_target_pairs={{0,3},{1,2},{2,1},{3,0},{4,7},{5,6},{6,5},{7,4},{8,11},{9,10},{10,... | collective-permute-start | bytes 86024 | tf_op jit(solution)/shard_map/ppermute | solution.py:503
  11.7 10.1 %collective-permute-start.4 = (f32[7,8,128]{2,1,0:T(8,128)S(1)}, f32[7,8,128]{2,1,0:T(8,128)S(1)}, u32[]{:S(2)}, u32[]{:S(2)}) collective-permute-start(f32[7,8,128]{2,1,0:T(8,128)S(1)} %get-tuple-element.14), channel_id=1, source_target_pairs={{0,31},{1,30},{2,5},{3,4},{4,3},{5,2},{6,9},{7,8},{8,7},{9,6},{10,... | collective-permute-start | bytes 86024 | tf_op jit(solution)/shard_map/ppermute | solution.py:503
  14.0 7.8 %copy-start.1 = (f32[32,24,128]{2,1,0:T(8,128)S(1)}, f32[32,24,128]{2,1,0:T(8,128)}, u32[]{:S(2)}) copy-start(f32[32,24,128]{2,1,0:T(8,128)} %u_ref.5) | copy-start | bytes 1179652
  14.0 7.8 %copy-start.3 = (f32[32,24,128]{2,1,0:T(8,128)S(1)}, f32[32,24,128]{2,1,0:T(8,128)}, u32[]{:S(2)}) copy-start(f32[32,24,128]{2,1,0:T(8,128)} %s_ref.5) | copy-start | bytes 1179652
  14.0 7.8 %copy-start.5 = (f32[32,24,128]{2,1,0:T(8,128)S(1)}, f32[32,24,128]{2,1,0:T(8,128)}, u32[]{:S(2)}) copy-start(f32[32,24,128]{2,1,0:T(8,128)} %c_ref.5) | copy-start | bytes 1179652
  16.1 11.4 %collective-permute-start.9 = (f32[3,8,128]{2,1,0:T(8,128)S(1)}, f32[3,8,128]{2,1,0:T(8,128)S(1)}, u32[]{:S(2)}, u32[]{:S(2)}) collective-permute-start(f32[3,8,128]{2,1,0:T(8,128)S(1)} %faces.1.m_ref), channel_id=1, source_target_pairs={{0,31},{1,30},{2,5},{3,4},{4,3},{5,2},{6,9},{7,8},{8,7},{9,6},{10,... | collective-permute-start | bytes 36872 | tf_op jit(solution)/shard_map/ppermute | solution.py:503
  19.6 7.9 %collective-permute-start.8 = (f32[3,8,128]{2,1,0:T(8,128)S(1)}, f32[3,8,128]{2,1,0:T(8,128)S(1)}, u32[]{:S(2)}, u32[]{:S(2)}) collective-permute-start(f32[3,8,128]{2,1,0:T(8,128)S(1)} %faces.1.m_ref), channel_id=1, source_target_pairs={{0,3},{1,2},{2,1},{3,0},{4,7},{5,6},{6,5},{7,4},{8,11},{9,10},{10,... | collective-permute-start | bytes 36872 | tf_op jit(solution)/shard_map/ppermute | solution.py:503
  19.6 7.9 %collective-permute-start.7 = (f32[3,8,128]{2,1,0:T(8,128)S(1)}, f32[3,8,128]{2,1,0:T(8,128)S(1)}, u32[]{:S(2)}, u32[]{:S(2)}) collective-permute-start(f32[3,8,128]{2,1,0:T(8,128)S(1)} %faces.1.m_ref), channel_id=1, source_target_pairs={{0,1},{1,0},{2,3},{3,2},{4,5},{5,4},{6,7},{7,6},{8,9},{9,8},{10,11... | collective-permute-start | bytes 36872 | tf_op jit(solution)/shard_map/ppermute | solution.py:503
  20.1 7.4 %collective-permute-start.6 = (f32[3,8,128]{2,1,0:T(8,128)S(1)}, f32[3,8,128]{2,1,0:T(8,128)S(1)}, u32[]{:S(2)}, u32[]{:S(2)}) collective-permute-start(f32[3,8,128]{2,1,0:T(8,128)S(1)} %faces.1.m_ref), channel_id=1, source_target_pairs={{0,30},{1,31},{2,4},{3,5},{4,2},{5,3},{6,8},{7,9},{8,6},{9,7},{10,... | collective-permute-start | bytes 36872 | tf_op jit(solution)/shard_map/ppermute | solution.py:503
  21.8 5.7 %collective-permute-start.5 = (f32[3,8,128]{2,1,0:T(8,128)S(1)}, f32[3,8,128]{2,1,0:T(8,128)S(1)}, u32[]{:S(2)}, u32[]{:S(2)}) collective-permute-start(f32[3,8,128]{2,1,0:T(8,128)S(1)} %faces.1.m_ref), channel_id=1, source_target_pairs={{0,2},{1,3},{2,0},{3,1},{4,6},{5,7},{6,4},{7,5},{8,10},{9,11},{10,... | collective-permute-start | bytes 36872 | tf_op jit(solution)/shard_map/ppermute | solution.py:503

commit v3 on v0

v3 whole, which is shorter than its diff:
```python
import functools

import jax
import jax.numpy as jnp
from jax import lax
from jax.experimental import pallas as pl
from jax.experimental.pallas import tpu as pltpu
from jax.sharding import PartitionSpec as P

SWEEPS = 3
COARSE_SWEEPS = 4
COARSEN = 8

SHIFT = 0.1
LMIN = 0.3
LMAX = 2.0
OMEGA = 0.8

THETA = (LMAX + LMIN) / 2.0
DELTA = (LMAX - LMIN) / 2.0
SIGMA = THETA / DELTA

RIM = SWEEPS + 1
SUB = 8
LANES = 128
HALF = LANES // 2
GROUP = 4 * RIM
ZS = LANES // GROUP
WIDTH = LANES // COARSEN
SPREAD = 2 * WIDTH
REACH = (COARSE_SWEEPS - 1) * COARSEN
CELLS = COARSEN**3

f32 = jnp.float32
VMEM = pl.BlockSpec(memory_space=pltpu.VMEM)
SMALL = pltpu.CompilerParams(vmem_limit_bytes=12 * 1024 * 1024)


def steps():
    rho, listed = 1.0 / SIGMA, []
    for _ in range(SWEEPS):
        nxt = 1.0 / (2.0 * SIGMA - rho)
        listed.append((nxt * rho, 2.0 * nxt / DELTA))
        rho = nxt
    return listed


def iota(shape, dim):
    return lax.broadcasted_iota(jnp.int32, shape, dim)


def rolled(x, by, dim):
    return pltpu.roll(x, by % x.shape[dim], dim)


def is_even():
    return lax.axis_index("gx") % 2 == 0


def tiles(count):
    return jax.ShapeDtypeStruct((count * SUB, LANES), f32)


def tile(ref, index):
    return ref[index * SUB : (index + 1) * SUB]


def picked(ref, start, stride):
    return ref[pl.ds(start, SUB, stride=stride), :]


def lane_sums(rows):
    shift = 1
    while shift < COARSEN:
        rows = rows + rolled(rows, -shift, 1)
        shift *= 2
    return rows


def compact(rows, place):
    lane = iota(rows.shape, 1)
    column = lane % SPREAD - RIM
    source = jnp.clip(column * COARSEN, 0, LANES - 1)
    here = (lane // SPREAD == place) & (column >= 0) & (column < WIDTH)
    return jnp.where(here, jnp.take_along_axis(lane_sums(rows), source, axis=1), 0.0)


def block_rows(values):
    sub = iota((SUB, LANES), 0)
    out = jnp.zeros((SUB, LANES), f32)
    for block in range(values.shape[0] // COARSEN):
        part = values[block * COARSEN : (block + 1) * COARSEN]
        out = jnp.where(sub == block, jnp.sum(part, axis=0, keepdims=True), out)
    return out


def all_rows(values):
    return jnp.sum(values, axis=0, keepdims=True)


def pack_kernel(u_hbm, s_hbm, c_hbm, q_ref, a1_ref, a2_ref, r_ref, own_ref, u_ref, s_ref, c_ref, sems, *, nz, nx):
    pieces = sems.shape[1]
    size = nz * nx // pieces
    copies = []
    for k, (source, target) in enumerate(((c_hbm, c_ref), (u_hbm, u_ref), (s_hbm, s_ref))):
        for piece in range(pieces):
            at = pl.ds(piece * size, size)
            copies.append(pltpu.make_async_copy(source.at[at], target.at[at], sems.at[k, piece]))
    for copy in copies:
        copy.start()
    for copy in copies:
        copy.wait()

    even = is_even()
    sub, lane = iota((SUB, LANES), 0), iota((SUB, LANES), 1)
    low = sub < RIM
    row, wide = iota((nx, LANES), 0), iota((nx, LANES), 1)

    def plane(ref, z):
        return ref[z % nz * nx : (z % nz + 1) * nx]

    def up(z):
        return 0.5 * (plane(c_ref, z) + plane(c_ref, z + 1)) * (plane(u_ref, z) - plane(u_ref, z + 1))

    coarse = jnp.zeros((SUB, LANES), f32)
    below = up(nz - 1)
    for Z in range(nz // COARSEN):
        sum_r = sum_c = jnp.zeros((nx, LANES), f32)
        for z in range(Z * COARSEN, (Z + 1) * COARSEN):
            u, c = plane(u_ref, z), plane(c_ref, z)
            above = up(z)
            fx = 0.5 * (c + rolled(c, -1, 0)) * (u - rolled(u, -1, 0))
            fy = 0.5 * (c + rolled(c, -1, 1)) * (u - rolled(u, -1, 1))
            fx = jnp.where(row == nx - 1, 0.0, fx)
            fy = jnp.where(wide == LANES - 1, 0.0, fy)
            r = plane(s_ref, z) - SHIFT * u - (fx - rolled(fx, 1, 0)) - (fy - rolled(fy, 1, 1)) - (above - below)
            below = above
            r_ref[z * nx : (z + 1) * nx] = r
            sum_r = sum_r + r
            sum_c = sum_c + c
            u0, u2, c0, c2 = u[:SUB], u[nx - SUB :], c[:SUB], c[nx - SUB :]
            first = jnp.where(low, c0, jnp.where(sub == SUB - 1, rolled(u0, -1, 0), rolled(r[:SUB], RIM, 0)))
            last = jnp.where(low, jnp.where(sub == 0, rolled(u2, 1, 0), rolled(r[nx - SUB :], RIM, 0)), c2)
            a1_ref[z * SUB : (z + 1) * SUB] = jnp.where(even, last, first)
            a2_ref[z * SUB : (z + 1) * SUB] = jnp.where(even, first, last)
        coarse = coarse + compact(block_rows(sum_r) + rolled(block_rows(sum_c), RIM, 0), Z)
    coarse = coarse * (1.0 / CELLS)

    zs = nz // ZS
    half = zs // 2
    for a, ref in enumerate((u_ref, c_ref, r_ref)):
        for pair in range(half):
            strip = jnp.zeros((nx, LANES), f32)
            for g in range(ZS):
                for second in range(2):
                    at = 2 * g + second
                    moved = rolled(plane(ref, g * zs + pair + second * half), at * 2 * RIM + RIM, 1)
                    strip = jnp.where(wide // (2 * RIM) == at, moved, strip)
            q_ref[(a * half + pair) * nx : (a * half + pair + 1) * nx] = strip

    base = 3 * half * nx
    for a, ref in enumerate((u_ref, c_ref)):
        for Z in range(nz // SUB):
            at = Z * SUB * nx
            first, last = picked(ref, at, nx), picked(ref, at + nx - 1, nx)
            spot = a * nz + Z * SUB
            own_ref[spot : spot + SUB] = first
            own_ref[2 * nz + spot : 2 * nz + spot + SUB] = last
            q_ref[base + spot : base + spot + SUB] = jnp.where(
                lane < HALF, rolled(first, REACH, 1), rolled(last, REACH + HALF, 1)
            )
    q_ref[base + 2 * nz : base + 2 * nz + SUB] = coarse
    a1_ref[nz * SUB :] = coarse


def pack(u, s, c, nz, nx):
    half = nz // ZS // 2
    pieces = 4
    return pl.pallas_call(
        functools.partial(pack_kernel, nz=nz, nx=nx),
        out_shape=(
            tiles(3 * half * nx // SUB + 2 * nz // SUB + 1),
            tiles(nz + 1),
            tiles(nz),
            jax.ShapeDtypeStruct(u.shape, f32),
            tiles(4 * nz // SUB),
        ),
        in_specs=[pl.BlockSpec(memory_space=pltpu.HBM)] * 3,
        out_specs=(VMEM,) * 5,
        scratch_shapes=[pltpu.VMEM(u.shape, f32)] * 3 + [pltpu.SemaphoreType.DMA((3, pieces))],
        compiler_params=SMALL,
        name="pack",
    )(u, s, c)


def facing(own_ref, a, z, nz, last):
    first, second = own_ref[a * nz + z : a * nz + z + SUB], own_ref[(2 + a) * nz + z : (2 + a) * nz + z + SUB]
    return jnp.where(last, second, first)


def opposite(rows_ref, a, z, after):
    first = picked(rows_ref, z * SUB, SUB)
    last = picked(rows_ref, z * SUB + SUB - 1, SUB)
    return jnp.where(after, last, first) if a == 0 else jnp.where(after, first, last)


def flux_between(own_ref, rows_ref, z, nz, after):
    u = facing(own_ref, 0, z, nz, after) - opposite(rows_ref, 0, z, after)
    c = facing(own_ref, 1, z, nz, after) + opposite(rows_ref, 1, z, after)
    return all_rows(0.5 * c * u)


def join_kernel(q_ref, ql_ref, qr_ref, a1_ref, own_ref, b1_ref, b2_ref, strip_ref, *, nz, nx):
    zs = nz // ZS
    half = zs // 2
    even = is_even()
    sub, lane = iota((SUB, LANES), 0), iota((SUB, LANES), 1)
    low = sub < RIM
    spot = iota((nx, LANES), 1) % GROUP
    joined = []
    for a in range(3):
        group = [None] * zs
        for pair in range(half):
            at = slice((a * half + pair) * nx, (a * half + pair + 1) * nx)
            left, own, right = ql_ref[at], q_ref[at], qr_ref[at]
            moved = rolled(jnp.where(spot < RIM, own, right), 2 * RIM, 1)
            one = jnp.where(spot < 2 * RIM, jnp.where(spot < RIM, left, own), moved)
            moved = rolled(jnp.where(spot < 3 * RIM, left, own), -2 * RIM, 1)
            two = jnp.where(spot < 2 * RIM, moved, jnp.where(spot < 3 * RIM, own, right))
            group[pair], group[pair + half] = one, two
            first = jnp.where(low, one[:SUB], rolled(two[:SUB], RIM, 0))
            last = jnp.where(low, rolled(two[nx - SUB :], RIM, 0), one[nx - SUB :])
            to = slice((a * half + pair) * SUB, (a * half + pair + 1) * SUB)
            b1_ref[to] = jnp.where(even, last, first)
            b2_ref[to] = jnp.where(even, first, last)
        for zi in range(zs):
            strip_ref[(a * zs + zi) * nx : (a * zs + zi + 1) * nx] = group[zi]
        joined.append(group)

    source, target = 3 * half * nx, 3 * half * SUB
    for index in range(2 * nz // SUB):
        at = slice(source + index * SUB, source + (index + 1) * SUB)
        both = jnp.where(lane % HALF < REACH, ql_ref[at], qr_ref[at])
        to = slice(target + index * SUB, target + (index + 1) * SUB)
        b1_ref[to] = both
        b2_ref[to] = both

    at = slice(source + 2 * nz, source + 2 * nz + SUB)
    place = lane % SPREAD
    window = jnp.where(
        place < RIM,
        rolled(ql_ref[at], -WIDTH, 1),
        jnp.where(place < RIM + WIDTH, q_ref[at], rolled(qr_ref[at], WIDTH, 1)),
    )
    flux = jnp.zeros((nx, LANES), f32)
    for u, c in zip(joined[0], joined[1]):
        flux = flux + (c + rolled(c, -1, 1)) * (u - rolled(u, -1, 1))
    flux = block_rows((0.5 / CELLS) * flux)
    flux = flux + rolled(flux, -GROUP, 1)
    near, far = RIM - 1, 3 * RIM - 1
    change = jnp.where(place == RIM - 1, -rolled(flux, RIM - 1 - near, 1), 0.0)
    change = jnp.where(place == RIM, rolled(flux, RIM - near, 1), change)
    change = jnp.where(place == RIM + WIDTH - 1, -rolled(flux, RIM + WIDTH - 1 - far, 1), change)
    change = jnp.where(place == RIM + WIDTH, rolled(flux, RIM + WIDTH - far, 1), change)
    rows = nx // COARSEN
    nearest = jnp.where(even, rows - 1, 0)
    for Z in range(nz // COARSEN):
        across = flux_between(own_ref, a1_ref, Z * COARSEN, nz, even) * (1.0 / CELLS)
        change = change - compact(jnp.where(sub == nearest, across, 0.0), Z)
    mate = a1_ref[nz * SUB :]
    mate = jnp.where(even, rolled(mate, rows - RIM, 0), rolled(mate, 1 - RIM, 0))
    cond = jnp.where(sub == rows, mate, rolled(window, -RIM, 0))
    to = target + 2 * nz
    for ref in (b1_ref, b2_ref):
        ref[to : to + SUB] = window + change
        ref[to + SUB : to + 2 * SUB] = cond


def join(q, ql, qr, a1, own, nz, nx):
    zs = nz // ZS
    message = tiles(3 * (zs // 2) + 2 * nz // SUB + 2)
    return pl.pallas_call(
        functools.partial(join_kernel, nz=nz, nx=nx),
        out_shape=(message, message, jax.ShapeDtypeStruct((3 * zs * nx, LANES), f32)),
        in_specs=[VMEM] * 5,
        out_specs=(VMEM,) * 3,
        compiler_params=SMALL,
        name="join",
    )(q, ql, qr, a1, own)


def faces_kernel(own_ref, b_ref, r1_ref, r2_ref, a2_ref, o_ref, *, nz, nx):
    half = nz // ZS // 2
    even = is_even()
    sub, lane = iota((SUB, LANES), 0), iota((SUB, LANES), 1)
    place = lane % SPREAD
    rows = nx // COARSEN
    base = 3 * half * SUB

    outer = REACH // COARSEN
    is_left, is_right = (place >= RIM - outer) & (place < RIM), (place >= RIM + WIDTH) & (place < RIM + WIDTH + outer)
    is_own = (place >= RIM) & (place < RIM + WIDTH)
    source = jnp.where(is_left, place - (RIM - outer), place - (RIM + WIDTH - outer))
    source = jnp.where(sub == 0, place - RIM, source) * COARSEN
    source = jnp.clip(source, 0, LANES - 1)
    valid = ((sub == 0) & is_own) | ((sub > 0) & (is_left | is_right))

    def outside(r_ref, Z, upper):
        def at(ref, a):
            start = base + a * nz + Z * COARSEN
            return ref[start : start + SUB]

        u = at(b_ref, 0) - rolled(at(r_ref, 0), HALF, 1)
        c = at(b_ref, 1) + rolled(at(r_ref, 1), HALF, 1)
        flux = all_rows(0.5 * c * u)
        return jnp.where(upper, rolled(flux, HALF, 1), flux)

    flux = jnp.zeros((SUB, LANES), f32)
    for Z in range(nz // COARSEN):
        one = flux_between(own_ref, a2_ref, Z * COARSEN, nz, jnp.logical_not(even))
        two = outside(r2_ref, Z, jnp.logical_not(even))
        three = outside(r1_ref, Z, even)
        sums = lane_sums(jnp.where(sub == 0, one, jnp.where(sub == 1, two, jnp.where(sub == 2, three, 0.0))))
        here = valid & (lane // SPREAD == Z)
        flux = flux + jnp.where(here, jnp.take_along_axis(sums, source, axis=1), 0.0)
    flux = flux * (1.0 / CELLS)
    far, mate = flux[0:1] + flux[1:2], flux[2:3]

    def stacked(own, other):
        before, after = jnp.where(even, other, own), jnp.where(even, own, other)
        return jnp.where(sub <= rows, rolled(before, 1, 0), rolled(after, rows + 1, 0))

    at = base + 2 * nz
    rhs = stacked(b_ref[at : at + SUB], r2_ref[at : at + SUB])
    sign = jnp.where(even, 1.0, -1.0)
    rhs = rhs + jnp.where(sub == rows, sign * far, jnp.where(sub == rows + 1, -sign * far, 0.0))
    rhs = rhs - jnp.where(sub == jnp.where(even, 2 * rows, 1), mate, 0.0)

    at = at + SUB
    near_c, far_c = r1_ref[at : at + SUB], r2_ref[at : at + SUB]
    cond = stacked(b_ref[at : at + SUB], far_c)
    before = jnp.where(even, rolled(far_c, -rows, 0), rolled(near_c, 1 - rows, 0))
    after = jnp.where(even, rolled(near_c, 2 * rows + 1, 0), rolled(far_c, rows + 1, 0))
    cond = jnp.where(sub == 0, before, jnp.where(sub == 2 * rows + 1, after, cond))
    around = rolled(cond, -1, 0) + rolled(cond, 1, 0) + rolled(cond, -1, 1) + rolled(cond, 1, 1)
    around = around + rolled(cond, -SPREAD, 1) + rolled(cond, SPREAD, 1)
    weight = OMEGA / (SHIFT + (0.5 / COARSEN**2) * (6.0 * cond + around))
    o_ref[0:SUB] = weight * rhs
    o_ref[SUB : 2 * SUB] = weight
    o_ref[2 * SUB :] = cond


def faces(own, b, r1, r2, a2, nz, nx):
    return pl.pallas_call(
        functools.partial(faces_kernel, nz=nz, nx=nx),
        out_shape=tiles(3),
        in_specs=[VMEM] * 5,
        out_specs=VMEM,
        compiler_params=SMALL,
        name="faces",
    )(own, b, r1, r2, a2)


def fine_kernel(
    u_ref, c_ref, r_ref, a1_ref, a2_ref, b1_ref, b2_ref, strip_ref,
    o_ref,
    ch, rh, cx, cy, cz, inv, q, va, vb, acc, wr, w0, w1, w2,
    *, nz, nx,
):
    zs = nz // ZS
    half = zs // 2
    ext = nx + SUB
    even = is_even()
    sub = iota((SUB, LANES), 0)
    low, end = sub < RIM, sub == SUB - 1
    table = steps()

    def sides(one, two):
        return jnp.where(even, one, two), jnp.where(even, two, one)

    for z in range(nz):
        after, before = sides(tile(a1_ref, z), tile(a2_ref, z))
        tile_at = slice(z * SUB, (z + 1) * SUB)
        ch[tile_at] = jnp.where(low, after, before)
        rh[tile_at] = rolled(jnp.where(low, before, after), RIM, 0)

    row, spot = iota((ext, LANES), 0), iota((ext, LANES), 1) % GROUP

    def strips_of(a):
        rims = [None] * zs
        for pair in range(half):
            after, before = sides(tile(b1_ref, a * half + pair), tile(b2_ref, a * half + pair))
            rims[pair] = jnp.where(low, after, before)
            rims[pair + half] = rolled(jnp.where(low, before, after), RIM, 0)
        return [
            jnp.concatenate([strip_ref[(a * zs + zi) * nx : (a * zs + zi + 1) * nx], rims[zi]], axis=0)
            for zi in range(zs)
        ]

    def z_up(x):
        return x[1:] + [rolled(x[0], -GROUP, 1)]

    def z_down(x):
        return [rolled(x[-1], GROUP, 1)] + x[:-1]

    us, cs, rs = strips_of(0), strips_of(1), strips_of(2)
    cxs = [0.5 * (c + rolled(c, -1, 0)) for c in cs]
    cys = [0.5 * (c + rolled(c, -1, 1)) for c in cs]
    czs = [0.5 * (c + d) for c, d in zip(cs, z_up(cs))]
    czds = z_down(czs)
    invs, qs, vs = [], [], []
    for zi in range(zs):
        u = us[zi]
        fx = jnp.where((row == nx - 1) | (row == ext - 1), cxs[zi] * (u - rolled(u, -1, 0)), 0.0)
        fy = jnp.where((spot == RIM - 1) | (spot == 3 * RIM - 1), cys[zi] * (u - rolled(u, -1, 1)), 0.0)
        r = rs[zi] - (fx - rolled(fx, 1, 0)) - (fy - rolled(fy, 1, 1))
        wr[zi * ext : (zi + 1) * ext] = jnp.where(spot == RIM, r, rolled(r, -2 * RIM, 1))
        diag = SHIFT + (cxs[zi] + rolled(cxs[zi], 1, 0)) + (cys[zi] + rolled(cys[zi], 1, 1)) + (czs[zi] + czds[zi])
        invs.append(1.0 / diag)
        qs.append(r * invs[zi])
        vs.append(qs[zi] * (1.0 / THETA))
    for k, w in enumerate((w0, w1, w2)):
        prod = [cys[zi] * vs[zi] for zi in range(zs)]
        for zi in range(zs):
            w[zi * ext : (zi + 1) * ext] = jnp.where(spot == RIM - 1, prod[zi], rolled(vs[zi], -(2 * RIM + 2), 1))
        if k == SWEEPS - 1:
            break
        keep, lift = table[k]
        v_up, v_down = z_up(vs), z_down(vs)
        fresh = []
        for zi in range(zs):
            v = vs[zi]
            near = cxs[zi] * rolled(v, -1, 0) + rolled(cxs[zi] * v, 1, 0)
            near = near + cys[zi] * rolled(v, -1, 1) + rolled(prod[zi], 1, 1)
            near = near + czs[zi] * v_up[zi] + czds[zi] * v_down[zi]
            qs[zi] = qs[zi] - v + near * invs[zi]
            fresh.append(keep * v + lift * qs[zi])
        vs = fresh

    wc = [jnp.where(spot == RIM - 1, c, rolled(c, -(2 * RIM + 2), 1)) for c in cs]

    lane = iota((ext, LANES), 1)
    first_lane, last_lane = lane == 0, lane == LANES - 1
    both_lanes = first_lane | last_lane

    def own(ref, z):
        return ref[z % nz * nx : (z % nz + 1) * nx]

    def long(ref, z):
        return ref[z % nz * ext : (z % nz + 1) * ext]

    def whole(z):
        return jnp.concatenate([own(c_ref, z), tile(ch, z % nz)], axis=0)

    def beside(w, z, column):
        return rolled(w, -column - z // zs * GROUP, 1)

    below = 0.5 * (whole(nz - 1) + whole(0))
    for z in range(nz):
        at = slice(z * ext, (z + 1) * ext)
        c = whole(z)
        edge = beside(wc[z % zs], z, RIM - 1)
        gx = 0.5 * (c + rolled(c, -1, 0))
        gy = 0.5 * (c + jnp.where(last_lane, edge, rolled(c, -1, 1)))
        gyl = 0.5 * (c + jnp.where(first_lane, edge, rolled(c, 1, 1)))
        above = 0.5 * (c + whole(z + 1))
        diag = SHIFT + (gx + rolled(gx, 1, 0)) + (gy + gyl) + (above + below)
        inverse = 1.0 / diag
        r, rim = own(r_ref, z), tile(rh, z)
        u_first, u_last = own(u_ref, z)[:SUB], own(u_ref, z)[nx - SUB :]
        u_rim = jnp.where(sub == 0, rolled(rim, 1 - RIM, 0), rolled(rim, RIM - 1, 0))
        fa = jnp.where(end, gx[nx - SUB : nx] * (u_last - rolled(u_rim, -1, 0)), 0.0)
        fb = jnp.where(end, gx[nx:] * (u_rim - rolled(u_first, -1, 0)), 0.0)
        r = jnp.concatenate(
            [
                r[:SUB] + rolled(fb, 1, 0),
                r[SUB : nx - SUB],
                r[nx - SUB :] - fa,
                rim + rolled(fa, 1, 0) - fb,
            ],
            axis=0,
        )
        zi = z % zs
        r = jnp.where(both_lanes, beside(wr[zi * ext : (zi + 1) * ext], z, RIM), r)
        scaled = r * inverse
        v = scaled * (1.0 / THETA)
        cx[at] = gx
        cy[at] = gy
        cz[at] = above
        inv[at] = inverse
        q[at] = scaled
        va[at] = v
        acc[z * nx : (z + 1) * nx] = v[:nx]
        below = above

    for k, w in enumerate((w0, w1, w2)):
        old, new = (va, vb) if k % 2 == 0 else (vb, va)
        keep, lift = table[k]
        for z in range(nz):
            at = slice(z * ext, (z + 1) * ext)
            zi = z % zs
            v, gx, gy = old[at], cx[at], cy[at]
            edge = beside(w[zi * ext : (zi + 1) * ext], z, RIM - 1)
            near = gx * rolled(v, -1, 0) + rolled(gx * v, 1, 0)
            near = near + gy * jnp.where(last_lane, edge, rolled(v, -1, 1))
            near = near + jnp.where(first_lane, edge, rolled(gy * v, 1, 1))
            near = near + cz[at] * long(old, z + 1) + long(cz, z - 1) * long(old, z - 1)
            scaled = q[at] - v + near * inv[at]
            fresh = keep * v + lift * scaled
            here = slice(z * nx, (z + 1) * nx)
            if k < SWEEPS - 1:
                q[at] = scaled
                new[at] = fresh
                acc[here] = acc[here] + fresh[:nx]
            else:
                o_ref[here] = own(u_ref, z) + (acc[here] + fresh[:nx])


def fine(u, c, r, a1, a2, b1, b2, strips, nz, nx):
    zs = nz // ZS
    ext = nx + SUB
    rim = pltpu.VMEM((nz * SUB, LANES), f32)
    full = pltpu.VMEM((nz * ext, LANES), f32)
    strip = pltpu.VMEM((zs * ext, LANES), f32)
    return pl.pallas_call(
        functools.partial(fine_kernel, nz=nz, nx=nx),
        out_shape=jax.ShapeDtypeStruct(u.shape, f32),
        in_specs=[VMEM] * 8,
        out_specs=VMEM,
        scratch_shapes=[rim] * 2 + [full] * 7 + [pltpu.VMEM(u.shape, f32)] + [strip] * 4,
        compiler_params=SMALL,
        cost_estimate=pl.CostEstimate(flops=150 * u.size, bytes_accessed=20 * u.size, transcendentals=0),
        name="fine",
    )(u, c, r, a1, a2, b1, b2, strips)


def finish_kernel(x_ref, m_ref, r_ref, o_ref, *, nz, nx):
    rows = nx // COARSEN
    even = is_even()
    sub, lane = iota((SUB, LANES), 0), iota((SUB, LANES), 1)
    beyond = sub == jnp.where(even, 2 * rows + 1, 0)
    fields = []
    for a in range(3):
        mine, mate = tile(m_ref, a), tile(r_ref, a)
        mate = jnp.where(even, rolled(mate, 2 * rows, 0), rolled(mate, -2 * rows, 0))
        fields.append(jnp.concatenate([jnp.where(beyond, mate, mine), mate], axis=0))
    start, weight, cond = fields
    scale = 0.5 / COARSEN**2
    gx = scale * (cond + rolled(cond, -1, 0))
    gy = scale * (cond + rolled(cond, -1, 1))
    gz = scale * (cond + rolled(cond, -SPREAD, 1))
    v = start
    for _ in range(COARSE_SWEEPS - 1):
        fx = gx * (v - rolled(v, -1, 0))
        fy = gy * (v - rolled(v, -1, 1))
        fz = gz * (v - rolled(v, -SPREAD, 1))
        image = SHIFT * v + (fx - rolled(fx, 1, 0)) + (fy - rolled(fy, 1, 1)) + (fz - rolled(fz, SPREAD, 1))
        v = v + start - weight * image
    top = v[:SUB]
    top = jnp.where(even, rolled(top, -rows - 1, 0), rolled(top, -1, 0))
    for Z in range(nz // COARSEN):
        spread = jnp.take_along_axis(top, Z * SPREAD + RIM + lane // COARSEN, axis=1)
        for X in range(rows):
            value = jnp.broadcast_to(spread[X : X + 1], (COARSEN, LANES))
            for z in range(Z * COARSEN, (Z + 1) * COARSEN):
                at = slice(z * nx + X * COARSEN, z * nx + (X + 1) * COARSEN)
                o_ref[at] = x_ref[at] + value


def finish(x, m, r, nz, nx):
    return pl.pallas_call(
        functools.partial(finish_kernel, nz=nz, nx=nx),
        out_shape=jax.ShapeDtypeStruct(x.shape, f32),
        in_specs=[VMEM] * 3,
        out_specs=VMEM,
        compiler_params=SMALL,
        name="finish",
    )(x, m, r)


def moves():
    size_x, size_y = lax.axis_size("gx"), lax.axis_size("gy")

    def send(x, go):
        pairs = []
        for i in range(size_x):
            for j in range(size_y):
                k, l = go(i, j)
                pairs.append((i * size_y + j, (k % size_x) * size_y + l % size_y))
        return lax.ppermute(x, ("gx", "gy"), pairs)

    def mate(x):
        return send(x, lambda i, j: (i + 1 if i % 2 == 0 else i - 1, j))

    def far(x):
        return send(x, lambda i, j: (i - 1 if i % 2 == 0 else i + 1, j))

    def sides(x):
        left = send(x, lambda i, j: (i, j + 1))
        if size_y == 2:
            return left, left
        return left, send(x, lambda i, j: (i, j - 1))

    return mate, far, sides


def body(iterate, source, conduct):
    nz, nx, ny = iterate.shape
    if nz != ZS * 4 or ny != LANES or nx != 3 * SUB or lax.axis_size("gx") % 2:
        raise ValueError("shapes")
    mate, far, sides = moves()
    u, s, c = (x.reshape(nz * nx, ny) for x in (iterate, source, conduct))
    q, a1, a2, r, own = pack(u, s, c, nz, nx)
    ql, qr = sides(q)
    ra1 = mate(a1)
    ra2 = far(a2)
    b1, b2, strips = join(q, ql, qr, ra1, own, nz, nx)
    rb2 = far(b2)
    rb1 = mate(b1)
    m = faces(own, b1, rb1, rb2, ra2, nz, nx)
    rm = mate(m)
    x = fine(u, c, r, ra1, ra2, rb1, rb2, strips, nz, nx)
    return finish(x, m, rm, nz, nx).reshape(nz, nx, ny)


def solution(mesh):
    spec = P(None, "gx", "gy")
    return jax.shard_map(body, mesh=mesh, in_specs=(spec,) * 3, out_specs=spec, check_vma=False)
```

time: 122 us -> 26.6 us (0.22)
  local copies, waits for them, and re-layouts: 44.4 us -> 3 us
  other arithmetic: 28.2 us -> 0 us
  waiting for transfers between devices: 26.7 us -> 2.26 us
  starting transfers between devices: 21.8 us -> 11.8 us
  Pallas kernels: 0 us -> 9.25 us
    ppermute x20 -> x6, waiting for transfers between devices: 26.7 us -> 2.26 us  [send(): return lax.ppermute(x, ('gx', 'gy'), pairs)]
    slice x36 -> x0, local copies, waits for them, and re-layouts: 18.6 us -> none  [the longest x7 3.83 us: extended(): last = lax.slice_in_dim(x, length - width, length, axis=dim)]
    reshape x3 -> x0, local copies, waits for them, and re-layouts: 16.1 us -> none  [the longest x2 10.8 us: restrict(): values.reshape(depth // COARSEN, COARSEN, width_x // COARSEN, COARSEN, wi...]
    add x6 -> x0, other arithmetic: 12.6 us -> none  [the longest x2 7.67 us: body(): rho_next * rho_now * crop(direction, 1)]
    ppermute x20 -> x6, starting transfers between devices: 21.8 us -> 11.8 us  [send(): return lax.ppermute(x, ('gx', 'gy'), pairs)]
    pallas_call x0 -> x5, Pallas kernels: none -> 9.25 us  [the longest x1 4.35 us: pack(): pl.pallas_call(functools.partial(pack_kernel, nz=nz, nx=nx), out_shape=(t...]
    reduce_sum x2 -> x0, other arithmetic: 6.64 us -> none  [restrict(): return jnp.mean(blocks, axis=(1, 3, 5))]
    ppermute x2 -> x0, local copies, waits for them, and re-layouts: 4.3 us -> none  [the longest x1 2.73 us: extended(): before = lax.ppermute(last, axis, up)]
  transfers between devices with their start and end apart: 20 -> 6, of which waited for: 14 -> 1; matrix products, arithmetic and copies ran while one was open for 30% -> 0% of each run, Pallas kernels for 0% -> 12%
where the time goes in v3:
time: 26.6 us; the launch traced here: 26.3 us
  starting transfers between devices  11.8 us (44%)
  Pallas kernels  9.25 us (35%)
  local copies, waits for them, and re-layouts  3 us (11%)
  waiting for transfers between devices  2.26 us (8%)
    ppermute x6, starting transfers between devices, send(): return lax.ppermute(x, ('gx', 'gy'), pairs)  11.8 us
    pallas_call x1, Pallas kernels, pack(): pl.pallas_call(functools.partial(pack_kernel, nz=nz, nx=nx), out_shape=(t...  4.35 us
    unnamed x10, local copies, waits for them, and re-layouts  3 us
    pallas_call x1, Pallas kernels, fine(): pl.pallas_call(functools.partial(fine_kernel, nz=nz, nx=nx), out_shape=ja...  2.85 us
    ppermute x6, waiting for transfers between devices, send(): return lax.ppermute(x, ('gx', 'gy'), pairs)  2.26 us
    pallas_call x1, Pallas kernels, finish(): pl.pallas_call(functools.partial(finish_kernel, nz=nz, nx=nx), out_shape=...  1.29 us
  transfers between devices with their start and end apart: 6, of which 1 were waited for; matrix products, arithmetic and copies ran while one was open for 0% of the time, Pallas kernels for 12%

profile of v3, /device:TPU:0, one launch (start us, length us, event | category | flops | bytes accessed | tf_op | source)
XLA Modules:
  0.0 26.3 jit_solution(7255532632458370637)
XLA Ops:
  0.0 0.0 copy-start
  0.0 1.0 %copy-done = f32[32,24,128]{2,1,0:T(8,128)S(1)} copy-done((f32[32,24,128]{2,1,0:T(8,128)S(1)}, f32[32,24,128]{2,1,0:T(8,128)}, u32[]{:S(2)}) %copy-start) | copy-done | bytes 393240
  1.0 0.0 copy-start.2
  1.0 1.0 %copy-done.2 = f32[32,24,128]{2,1,0:T(8,128)S(1)} copy-done((f32[32,24,128]{2,1,0:T(8,128)S(1)}, f32[32,24,128]{2,1,0:T(8,128)}, u32[]{:S(2)}) %copy-start.2) | copy-done | bytes 393240
  2.0 0.0 copy-start.4
  2.0 1.0 %copy-done.4 = f32[32,24,128]{2,1,0:T(8,128)S(1)} copy-done((f32[32,24,128]{2,1,0:T(8,128)S(1)}, f32[32,24,128]{2,1,0:T(8,128)}, u32[]{:S(2)}) %copy-start.4) | copy-done | bytes 393240
  3.0 4.3 %pack.1 = (f32[216,128]{1,0:T(8,128)S(1)}, f32[264,128]{1,0:T(8,128)S(1)}, f32[256,128]{1,0:T(8,128)S(1)}, f32[768,128]{1,0:T(8,128)S(1)}, f32[128,128]{1,0:T(8,128)S(1)}) custom-call(f32[768,128]{1,0:T(8,128)S(1)} %bitcast.4, f32[768,128]{1,0:T(8,128)S(1)} %bitcast.8, f32[768,128]{1,0:T(8,128)S(1)} %bitcast.6), custom_call_target="tpu_custom_call" | custom-call | tf_op jit(solution)/shard_map/pack/pallas_call | solution.py:179
  7.3 0.5 %collective-permute-start = (f32[264,128]{1,0:T(8,128)S(1)}, f32[264,128]{1,0:T(8,128)S(1)}, u32[]{:S(2)}, u32[]{:S(2)}) collective-permute-start(f32[264,128]{1,0:T(8,128)S(1)} %get-tuple-element.14), channel_id=1, source_target_pairs={{0,2},{1,3},{2,0},{3,1},{4,6},{5,7},{6,4},{7,5},{8,10},{9,11},{10,... | collective-permute-start | bytes 405512 | tf_op jit(solution)/shard_map/ppermute | solution.py:590
  7.9 2.6 %collective-permute-start.2 = (f32[216,128]{1,0:T(8,128)S(1)}, f32[216,128]{1,0:T(8,128)S(1)}, u32[]{:S(2)}, u32[]{:S(2)}) collective-permute-start(f32[216,128]{1,0:T(8,128)S(1)} %get-tuple-element.16.q_ref), channel_id=1, source_target_pairs={{0,1},{1,0},{2,3},{3,2},{4,5},{5,4},{6,7},{7,6},{8,9},{9,8},{10,11... | collective-permute-start | bytes 331784 | tf_op jit(solution)/shard_map/ppermute | solution.py:590
  10.5 4.3 %collective-permute-start.1 = (f32[256,128]{1,0:T(8,128)S(1)}, f32[256,128]{1,0:T(8,128)S(1)}, u32[]{:S(2)}, u32[]{:S(2)}) collective-permute-start(f32[256,128]{1,0:T(8,128)S(1)} %get-tuple-element.15), channel_id=1, source_target_pairs={{0,30},{1,31},{2,4},{3,5},{4,2},{5,3},{6,8},{7,9},{8,6},{9,7},{10,... | collective-permute-start | bytes 393224 | tf_op jit(solution)/shard_map/ppermute | solution.py:590
  14.8 0.0 collective-permute-done.2.ql_ref.qr_ref
  14.8 0.0 collective-permute-done.a1_ref
  14.8 0.0 copy-start.1
  14.8 0.0 copy-start.3
  14.8 0.3 %join.1 = (f32[128,128]{1,0:T(8,128)S(1)}, f32[128,128]{1,0:T(8,128)S(1)}, f32[288,128]{1,0:T(8,128)S(1)}) custom-call(f32[216,128]{1,0:T(8,128)S(1)} %get-tuple-element.16.q_ref, f32[216,128]{1,0:T(8,128)S(1)} %collective-permute-done.2.ql_ref.qr_ref, f32[216,128]{1,0:T(8,128)S(1)} %collective-permute-done.2.ql_ref.qr_ref, ...), custom_call_target="tpu_custom_call" | custom-call | tf_op jit(solution)/shard_map/join/pallas_call | solution.py:282
  15.1 0.1 collective-permute-start.3
  15.2 4.2 %collective-permute-start.4 = (f32[128,128]{1,0:T(8,128)S(1)}, f32[128,128]{1,0:T(8,128)S(1)}, u32[]{:S(2)}, u32[]{:S(2)}) collective-permute-start(f32[128,128]{1,0:T(8,128)S(1)} %get-tuple-element.19), channel_id=1, source_target_pairs={{0,30},{1,31},{2,4},{3,5},{4,2},{5,3},{6,8},{7,9},{8,6},{9,7},{10,... | collective-permute-start | bytes 196616 | tf_op jit(solution)/shard_map/ppermute | solution.py:590
  19.4 0.0 collective-permute-done.1.a2_ref
  19.4 0.0 collective-permute-done.3.b1_ref.r1_ref
  19.4 2.2 %collective-permute-done.4.b2_ref.r2_ref = f32[128,128]{1,0:T(8,128)S(1)} collective-permute-done((f32[128,128]{1,0:T(8,128)S(1)}, f32[128,128]{1,0:T(8,128)S(1)}, u32[]{:S(2)}, u32[]{:S(2)}) %collective-permute-start.4) | collective-permute-done | bytes 65568 | tf_op jit(solution)/shard_map/ppermute | solution.py:590
  21.6 0.4 %faces.1.m_ref = f32[24,128]{1,0:T(8,128)S(1)} custom-call(f32[128,128]{1,0:T(8,128)S(1)} %get-tuple-element.17.own_ref, f32[128,128]{1,0:T(8,128)S(1)} %get-tuple-element.18.b_ref, f32[128,128]{1,0:T(8,128)S(1)} %collective-permute-done.3.b1_ref.r1_ref, f32[128,128]{1,0:T(8,128)S(1)} %collective-permute-done.4.b2_ref.r2_ref, ...), custom_call_target="tpu_custom_call" | custom-call | tf_op jit(solution)/shard_map/faces/pallas_call | solution.py:354
  22.1 0.1 collective-permute-start.5
  22.2 0.0 copy-done.1
  22.2 0.0 copy-done.3
  22.2 2.8 %fine.1.x_ref = f32[768,128]{1,0:T(8,128)S(1)} custom-call(f32[768,128]{1,0:T(8,128)S(1)} %bitcast.5, f32[768,128]{1,0:T(8,128)S(1)} %bitcast.7, f32[768,128]{1,0:T(8,128)S(1)} %get-tuple-element.13.r_ref, f32[264,128]{1,0:T(8,128)S(1)} %collective-permute-done.a1_ref, f32[256,128]{1,0:T(8,128)S(1)} %collective-permute-done.1.a2_ref, ...), custom_call_target="tpu_custom_call" | custom-call | flops 14745600 | bytes 1966080 | tf_op jit(solution)/shard_map/fine/pallas_call | solution.py:525
  25.0 0.0 collective-permute-done.5.r_ref
  25.1 1.3 %finish.1 = f32[768,128]{1,0:T(8,128)} custom-call(f32[768,128]{1,0:T(8,128)S(1)} %fine.1.x_ref, f32[24,128]{1,0:T(8,128)S(1)} %faces.1.m_ref, f32[24,128]{1,0:T(8,128)S(1)} %collective-permute-done.5.r_ref), custom_call_target="tpu_custom_call" | custom-call | tf_op jit(solution)/shard_map/finish/pallas_call | solution.py:571
Async XLA Ops:
  0.0 1.0 %copy-start = (f32[32,24,128]{2,1,0:T(8,128)S(1)}, f32[32,24,128]{2,1,0:T(8,128)}, u32[]{:S(2)}) copy-start(f32[32,24,128]{2,1,0:T(8,128)} %param.3) | copy-start | bytes 1179652
  1.0 1.0 %copy-start.2 = (f32[32,24,128]{2,1,0:T(8,128)S(1)}, f32[32,24,128]{2,1,0:T(8,128)}, u32[]{:S(2)}) copy-start(f32[32,24,128]{2,1,0:T(8,128)} %param.5) | copy-start | bytes 1179652
  2.0 1.0 %copy-start.4 = (f32[32,24,128]{2,1,0:T(8,128)S(1)}, f32[32,24,128]{2,1,0:T(8,128)}, u32[]{:S(2)}) copy-start(f32[32,24,128]{2,1,0:T(8,128)} %param.4) | copy-start | bytes 1179652
  7.3 7.4 %collective-permute-start = (f32[264,128]{1,0:T(8,128)S(1)}, f32[264,128]{1,0:T(8,128)S(1)}, u32[]{:S(2)}, u32[]{:S(2)}) collective-permute-start(f32[264,128]{1,0:T(8,128)S(1)} %get-tuple-element.14), channel_id=1, source_target_pairs={{0,2},{1,3},{2,0},{3,1},{4,6},{5,7},{6,4},{7,5},{8,10},{9,11},{10,... | collective-permute-start | bytes 405512 | tf_op jit(solution)/shard_map/ppermute | solution.py:590
  7.9 6.9 %collective-permute-start.2 = (f32[216,128]{1,0:T(8,128)S(1)}, f32[216,128]{1,0:T(8,128)S(1)}, u32[]{:S(2)}, u32[]{:S(2)}) collective-permute-start(f32[216,128]{1,0:T(8,128)S(1)} %get-tuple-element.16.q_ref), channel_id=1, source_target_pairs={{0,1},{1,0},{2,3},{3,2},{4,5},{5,4},{6,7},{7,6},{8,9},{9,8},{10,11... | collective-permute-start | bytes 331784 | tf_op jit(solution)/shard_map/ppermute | solution.py:590
  10.5 8.9 %collective-permute-start.1 = (f32[256,128]{1,0:T(8,128)S(1)}, f32[256,128]{1,0:T(8,128)S(1)}, u32[]{:S(2)}, u32[]{:S(2)}) collective-permute-start(f32[256,128]{1,0:T(8,128)S(1)} %get-tuple-element.15), channel_id=1, source_target_pairs={{0,30},{1,31},{2,4},{3,5},{4,2},{5,3},{6,8},{7,9},{8,6},{9,7},{10,... | collective-permute-start | bytes 393224 | tf_op jit(solution)/shard_map/ppermute | solution.py:590
  14.8 7.4 %copy-start.1 = (f32[32,24,128]{2,1,0:T(8,128)S(1)}, f32[32,24,128]{2,1,0:T(8,128)}, u32[]{:S(2)}) copy-start(f32[32,24,128]{2,1,0:T(8,128)} %param.3) | copy-start | bytes 1179652
  14.8 7.4 %copy-start.3 = (f32[32,24,128]{2,1,0:T(8,128)S(1)}, f32[32,24,128]{2,1,0:T(8,128)}, u32[]{:S(2)}) copy-start(f32[32,24,128]{2,1,0:T(8,128)} %param.5) | copy-start | bytes 1179652
  15.1 4.3 %collective-permute-start.3 = (f32[128,128]{1,0:T(8,128)S(1)}, f32[128,128]{1,0:T(8,128)S(1)}, u32[]{:S(2)}, u32[]{:S(2)}) collective-permute-start(f32[128,128]{1,0:T(8,128)S(1)} %get-tuple-element.18.b_ref), channel_id=1, source_target_pairs={{0,2},{1,3},{2,0},{3,1},{4,6},{5,7},{6,4},{7,5},{8,10},{9,11},{10,... | collective-permute-start | bytes 196616 | tf_op jit(solution)/shard_map/ppermute | solution.py:590
  15.2 6.5 %collective-permute-start.4 = (f32[128,128]{1,0:T(8,128)S(1)}, f32[128,128]{1,0:T(8,128)S(1)}, u32[]{:S(2)}, u32[]{:S(2)}) collective-permute-start(f32[128,128]{1,0:T(8,128)S(1)} %get-tuple-element.19), channel_id=1, source_target_pairs={{0,30},{1,31},{2,4},{3,5},{4,2},{5,3},{6,8},{7,9},{8,6},{9,7},{10,... | collective-permute-start | bytes 196616 | tf_op jit(solution)/shard_map/ppermute | solution.py:590
  22.1 3.0 %collective-permute-start.5 = (f32[24,128]{1,0:T(8,128)S(1)}, f32[24,128]{1,0:T(8,128)S(1)}, u32[]{:S(2)}, u32[]{:S(2)}) collective-permute-start(f32[24,128]{1,0:T(8,128)S(1)} %faces.1.m_ref), channel_id=1, source_target_pairs={{0,2},{1,3},{2,0},{3,1},{4,6},{5,7},{6,4},{7,5},{8,10},{9,11},{10,... | collective-permute-start | bytes 36872 | tf_op jit(solution)/shard_map/ppermute | solution.py:590

commit v4 on v3

--- a/solution.py
+++ b/solution.py
@@ -49,6 +49,10 @@
     return lax.broadcasted_iota(jnp.int32, shape, dim)
 
 
+def part(index, size):
+    return lax.shift_right_logical(index, size.bit_length() - 1), lax.bitwise_and(index, size - 1)
+
+
 def rolled(x, by, dim):
     return pltpu.roll(x, by % x.shape[dim], dim)
 
@@ -78,11 +82,15 @@
 
 
 def compact(rows, place):
-    lane = iota(rows.shape, 1)
-    column = lane % SPREAD - RIM
+    plane, column = part(iota(rows.shape, 1), SPREAD)
+    column = column - RIM
     source = jnp.clip(column * COARSEN, 0, LANES - 1)
-    here = (lane // SPREAD == place) & (column >= 0) & (column < WIDTH)
+    here = (plane == place) & (column >= 0) & (column < WIDTH)
     return jnp.where(here, jnp.take_along_axis(lane_sums(rows), source, axis=1), 0.0)
+
+
+def section(run):
+    pl.when(lax.axis_index("gx") >= 0)(run)
 
 
 def block_rows(values):
@@ -98,7 +106,7 @@
     return jnp.sum(values, axis=0, keepdims=True)
 
 
-def pack_kernel(u_hbm, s_hbm, c_hbm, q_ref, a1_ref, a2_ref, r_ref, own_ref, u_ref, s_ref, c_ref, sems, *, nz, nx):
+def pack_kernel(u_hbm, s_hbm, c_hbm, q_ref, f1_ref, a1_ref, a2_ref, r_ref, own_ref, u_ref, s_ref, c_ref, sems, *, nz, nx):
     pieces = sems.shape[1]
     size = nz * nx // pieces
     copies = []
@@ -115,6 +123,7 @@
     sub, lane = iota((SUB, LANES), 0), iota((SUB, LANES), 1)
     low = sub < RIM
     row, wide = iota((nx, LANES), 0), iota((nx, LANES), 1)
+    slot = part(wide, 2 * RIM)[0]
 
     def plane(ref, z):
         return ref[z % nz * nx : (z % nz + 1) * nx]
@@ -148,15 +157,18 @@
 
     zs = nz // ZS
     half = zs // 2
-    for a, ref in enumerate((u_ref, c_ref, r_ref)):
-        for pair in range(half):
-            strip = jnp.zeros((nx, LANES), f32)
-            for g in range(ZS):
-                for second in range(2):
-                    at = 2 * g + second
-                    moved = rolled(plane(ref, g * zs + pair + second * half), at * 2 * RIM + RIM, 1)
-                    strip = jnp.where(wide // (2 * RIM) == at, moved, strip)
-            q_ref[(a * half + pair) * nx : (a * half + pair + 1) * nx] = strip
+    def strips():
+        for a, ref in enumerate((u_ref, c_ref, r_ref)):
+            for pair in range(half):
+                strip = jnp.zeros((nx, LANES), f32)
+                for g in range(ZS):
+                    for second in range(2):
+                        at = 2 * g + second
+                        moved = rolled(plane(ref, g * zs + pair + second * half), at * 2 * RIM + RIM, 1)
+                        strip = jnp.where(slot == at, moved, strip)
+                q_ref[(a * half + pair) * nx : (a * half + pair + 1) * nx] = strip
+
+    section(strips)
 
     base = 3 * half * nx
     for a, ref in enumerate((u_ref, c_ref)):
@@ -166,11 +178,12 @@
             spot = a * nz + Z * SUB
             own_ref[spot : spot + SUB] = first
             own_ref[2 * nz + spot : 2 * nz + spot + SUB] = last
+            f1_ref[spot : spot + SUB] = jnp.where(even, last, first)
             q_ref[base + spot : base + spot + SUB] = jnp.where(
                 lane < HALF, rolled(first, REACH, 1), rolled(last, REACH + HALF, 1)
             )
     q_ref[base + 2 * nz : base + 2 * nz + SUB] = coarse
-    a1_ref[nz * SUB :] = coarse
+    f1_ref[2 * nz :] = coarse
 
 
 def pack(u, s, c, nz, nx):
@@ -180,17 +193,18 @@
         functools.partial(pack_kernel, nz=nz, nx=nx),
         out_shape=(
             tiles(3 * half * nx // SUB + 2 * nz // SUB + 1),
-            tiles(nz + 1),
+            tiles(2 * nz // SUB + 1),
+            tiles(nz),
             tiles(nz),
             jax.ShapeDtypeStruct(u.shape, f32),
             tiles(4 * nz // SUB),
         ),
         in_specs=[pl.BlockSpec(memory_space=pltpu.HBM)] * 3,
-        out_specs=(VMEM,) * 5,
+        out_specs=(VMEM,) * 6,
         scratch_shapes=[pltpu.VMEM(u.shape, f32)] * 3 + [pltpu.SemaphoreType.DMA((3, pieces))],
         compiler_params=SMALL,
         name="pack",
-    )(u, s, c)
+    )(*(pltpu.with_memory_space_constraint(x, pltpu.HBM) for x in (u, s, c)))
 
 
 def facing(own_ref, a, z, nz, last):
@@ -204,19 +218,13 @@
     return jnp.where(after, last, first) if a == 0 else jnp.where(after, first, last)
 
 
-def flux_between(own_ref, rows_ref, z, nz, after):
-    u = facing(own_ref, 0, z, nz, after) - opposite(rows_ref, 0, z, after)
-    c = facing(own_ref, 1, z, nz, after) + opposite(rows_ref, 1, z, after)
-    return all_rows(0.5 * c * u)
-
-
-def join_kernel(q_ref, ql_ref, qr_ref, a1_ref, own_ref, b1_ref, b2_ref, strip_ref, *, nz, nx):
+def join_kernel(q_ref, ql_ref, qr_ref, f1_ref, own_ref, b1_ref, b2_ref, strip_ref, *, nz, nx):
     zs = nz // ZS
     half = zs // 2
     even = is_even()
     sub, lane = iota((SUB, LANES), 0), iota((SUB, LANES), 1)
     low = sub < RIM
-    spot = iota((nx, LANES), 1) % GROUP
+    spot = part(iota((nx, LANES), 1), GROUP)[1]
     joined = []
     for a in range(3):
         group = [None] * zs
@@ -240,13 +248,13 @@
     source, target = 3 * half * nx, 3 * half * SUB
     for index in range(2 * nz // SUB):
         at = slice(source + index * SUB, source + (index + 1) * SUB)
-        both = jnp.where(lane % HALF < REACH, ql_ref[at], qr_ref[at])
+        both = jnp.where(part(lane, HALF)[1] < REACH, ql_ref[at], qr_ref[at])
         to = slice(target + index * SUB, target + (index + 1) * SUB)
         b1_ref[to] = both
         b2_ref[to] = both
 
     at = slice(source + 2 * nz, source + 2 * nz + SUB)
-    place = lane % SPREAD
+    place = part(lane, SPREAD)[1]
     window = jnp.where(
         place < RIM,
         rolled(ql_ref[at], -WIDTH, 1),
@@ -265,35 +273,37 @@
     rows = nx // COARSEN
     nearest = jnp.where(even, rows - 1, 0)
     for Z in range(nz // COARSEN):
-        across = flux_between(own_ref, a1_ref, Z * COARSEN, nz, even) * (1.0 / CELLS)
+        u, c = facing(own_ref, 0, Z * SUB, nz, even) - tile(f1_ref, Z), facing(own_ref, 1, Z * SUB, nz, even)
+        across = all_rows((0.5 / CELLS) * (c + tile(f1_ref, nz // SUB + Z)) * u)
         change = change - compact(jnp.where(sub == nearest, across, 0.0), Z)
-    mate = a1_ref[nz * SUB :]
+    mate = f1_ref[2 * nz :]
     mate = jnp.where(even, rolled(mate, rows - RIM, 0), rolled(mate, 1 - RIM, 0))
     cond = jnp.where(sub == rows, mate, rolled(window, -RIM, 0))
     to = target + 2 * nz
     for ref in (b1_ref, b2_ref):
-        ref[to : to + SUB] = window + change
-        ref[to + SUB : to + 2 * SUB] = cond
-
-
-def join(q, ql, qr, a1, own, nz, nx):
+        ref[to : to + SUB] = cond
+    b2_ref[to + SUB : to + 2 * SUB] = window + change
+
+
+def join(q, ql, qr, f1, own, nz, nx):
     zs = nz // ZS
-    message = tiles(3 * (zs // 2) + 2 * nz // SUB + 2)
+    size = 3 * (zs // 2) + 2 * nz // SUB + 1
     return pl.pallas_call(
         functools.partial(join_kernel, nz=nz, nx=nx),
-        out_shape=(message, message, jax.ShapeDtypeStruct((3 * zs * nx, LANES), f32)),
+        out_shape=(tiles(size), tiles(size + 1), jax.ShapeDtypeStruct((3 * zs * nx, LANES), f32)),
         in_specs=[VMEM] * 5,
         out_specs=(VMEM,) * 3,
         compiler_params=SMALL,
         name="join",
-    )(q, ql, qr, a1, own)
-
-
-def faces_kernel(own_ref, b_ref, r1_ref, r2_ref, a2_ref, o_ref, *, nz, nx):
+    )(q, ql, qr, f1, own)
+
+
+def faces_kernel(own_ref, b_ref, r2_ref, r1_ref, a2_ref, after_ref, o_ref, *, nz, nx):
+    del after_ref
     half = nz // ZS // 2
     even = is_even()
     sub, lane = iota((SUB, LANES), 0), iota((SUB, LANES), 1)
-    place = lane % SPREAD
+    plane, place = part(lane, SPREAD)
     rows = nx // COARSEN
     base = 3 * half * SUB
 
@@ -317,11 +327,14 @@
 
     flux = jnp.zeros((SUB, LANES), f32)
     for Z in range(nz // COARSEN):
-        one = flux_between(own_ref, a2_ref, Z * COARSEN, nz, jnp.logical_not(even))
+        after = jnp.logical_not(even)
+        u = facing(own_ref, 0, Z * SUB, nz, after) - opposite(a2_ref, 0, Z * SUB, after)
+        c = facing(own_ref, 1, Z * SUB, nz, after) + opposite(a2_ref, 1, Z * SUB, after)
+        one = all_rows(0.5 * c * u)
         two = outside(r2_ref, Z, jnp.logical_not(even))
         three = outside(r1_ref, Z, even)
         sums = lane_sums(jnp.where(sub == 0, one, jnp.where(sub == 1, two, jnp.where(sub == 2, three, 0.0))))
-        here = valid & (lane // SPREAD == Z)
+        here = valid & (plane == Z)
         flux = flux + jnp.where(here, jnp.take_along_axis(sums, source, axis=1), 0.0)
     flux = flux * (1.0 / CELLS)
     far, mate = flux[0:1] + flux[1:2], flux[2:3]
@@ -330,13 +343,13 @@
         before, after = jnp.where(even, other, own), jnp.where(even, own, other)
         return jnp.where(sub <= rows, rolled(before, 1, 0), rolled(after, rows + 1, 0))
 
-    at = base + 2 * nz
+    at = base + 2 * nz + SUB
     rhs = stacked(b_ref[at : at + SUB], r2_ref[at : at + SUB])
     sign = jnp.where(even, 1.0, -1.0)
     rhs = rhs + jnp.where(sub == rows, sign * far, jnp.where(sub == rows + 1, -sign * far, 0.0))
     rhs = rhs - jnp.where(sub == jnp.where(even, 2 * rows, 1), mate, 0.0)
 
-    at = at + SUB
+    at = at - SUB
     near_c, far_c = r1_ref[at : at + SUB], r2_ref[at : at + SUB]
     cond = stacked(b_ref[at : at + SUB], far_c)
     before = jnp.where(even, rolled(far_c, -rows, 0), rolled(near_c, 1 - rows, 0))
@@ -350,21 +363,115 @@
     o_ref[2 * SUB :] = cond
 
 
-def faces(own, b, r1, r2, a2, nz, nx):
+def faces(own, b, r2, r1, a2, after, nz, nx):
     return pl.pallas_call(
         functools.partial(faces_kernel, nz=nz, nx=nx),
         out_shape=tiles(3),
-        in_specs=[VMEM] * 5,
+        in_specs=[VMEM] * 5 + [pl.BlockSpec(memory_space=pl.ANY)],
         out_specs=VMEM,
         compiler_params=SMALL,
         name="faces",
-    )(own, b, r1, r2, a2)
+    )(own, b, r2, r1, a2, after)
+
+
+def sides(even, one, two):
+    return jnp.where(even, one, two), jnp.where(even, two, one)
+
+
+def rim_of(even, low, one, two):
+    after, before = sides(even, one, two)
+    return jnp.where(low, after, before), rolled(jnp.where(low, before, after), RIM, 0)
+
+
+def rim_faces(sub, face, rim_face, u_first, u_last, rim):
+    u_rim = jnp.where(sub == 0, rolled(rim, 1 - RIM, 0), rolled(rim, RIM - 1, 0))
+    end = sub == SUB - 1
+    after = jnp.where(end, face * (u_last - rolled(u_rim, -1, 0)), 0.0)
+    before = jnp.where(end, rim_face * (u_rim - rolled(u_first, -1, 0)), 0.0)
+    return after, before
+
+
+def beside(w, z, zs, column):
+    return rolled(w, -column - z // zs * GROUP, 1)
+
+
+def window(spot, left, right, column):
+    return jnp.where(spot == RIM - 1, left, rolled(right, RIM - 2 - column, 1))
+
+
+def begin_kernel(
+    strip_ref, a1_ref, a2_ref, u_ref, c_ref, r_ref, cx_ref, cy_ref, cz_ref, inv_ref, q_ref, v_ref, ch, *, nz, nx
+):
+    zs = nz // ZS
+    even = is_even()
+    sub = iota((SUB, LANES), 0)
+    low = sub < RIM
+    spot = part(iota((nx, LANES), 1), GROUP)[1]
+    lane = iota((nx, LANES), 1)
+    first_lane, last_lane = lane == 0, lane == LANES - 1
+    rims = []
+    for z in range(nz):
+        cond, rim = rim_of(even, low, tile(a1_ref, z), tile(a2_ref, z))
+        ch[z * SUB : (z + 1) * SUB] = cond
+        rims.append(rim)
+
+    def strip(a, zi):
+        return strip_ref[(a * zs + zi) * nx : (a * zs + zi + 1) * nx]
+
+    edge_c, edge_f = [], []
+    for zi in range(zs):
+        u, c = strip(0, zi), strip(1, zi)
+        flux = 0.5 * (c + rolled(c, -1, 1)) * (u - rolled(u, -1, 1))
+        edge_c.append(window(spot, c, c, 3 * RIM))
+        edge_f.append(window(spot, flux, flux, 3 * RIM - 1))
+
+    def own(ref, z):
+        return ref[z % nz * nx : (z % nz + 1) * nx]
+
+    below = 0.5 * (own(c_ref, -1) + own(c_ref, 0))
+    for z in range(nz):
+        at = slice(z * nx, (z + 1) * nx)
+        u, c = own(u_ref, z), own(c_ref, z)
+        whole = jnp.concatenate([c, tile(ch, z)], axis=0)
+        gx = 0.5 * (whole + rolled(whole, -1, 0))
+        gxl = rolled(gx, 1, 0)[:nx]
+        edge = beside(edge_c[z % zs], z, zs, RIM - 1)
+        gy = 0.5 * (c + jnp.where(last_lane, edge, rolled(c, -1, 1)))
+        gyl = 0.5 * (c + jnp.where(first_lane, edge, rolled(c, 1, 1)))
+        above = 0.5 * (c + own(c_ref, z + 1))
+        inverse = 1.0 / (SHIFT + (gx[:nx] + gxl) + (gy + gyl) + (above + below))
+        after, before = rim_faces(sub, gx[nx - SUB : nx], gx[nx:], u[:SUB], u[nx - SUB :], rims[z])
+        r = own(r_ref, z)
+        r = jnp.concatenate([r[:SUB] + rolled(before, 1, 0), r[SUB : nx - SUB], r[nx - SUB :] - after], axis=0)
+        edge = beside(edge_f[z % zs], z, zs, RIM - 1)
+        r = r + jnp.where(first_lane, edge, jnp.where(last_lane, -edge, 0.0))
+        scaled = r * inverse
+        cx_ref[at] = gx[:nx]
+        cy_ref[at] = gy
+        cz_ref[at] = above
+        inv_ref[at] = inverse
+        q_ref[at] = scaled
+        v_ref[at] = scaled * (1.0 / THETA)
+        below = above
+
+
+def begin(strips, a1, a2, u, c, r, nz, nx):
+    return pl.pallas_call(
+        functools.partial(begin_kernel, nz=nz, nx=nx),
+        out_shape=(jax.ShapeDtypeStruct(u.shape, f32),) * 6,
+        in_specs=[VMEM] * 6,
+        out_specs=(VMEM,) * 6,
+        scratch_shapes=[pltpu.VMEM((nz * SUB, LANES), f32)],
+        compiler_params=SMALL,
+        cost_estimate=pl.CostEstimate(flops=40 * u.size, bytes_accessed=40 * u.size, transcendentals=0),
+        name="begin",
+    )(strips, a1, a2, u, c, r)
 
 
 def fine_kernel(
-    u_ref, c_ref, r_ref, a1_ref, a2_ref, b1_ref, b2_ref, strip_ref,
+    strip_ref, b2_ref, b1_ref, a1_ref, a2_ref, u_ref, c_ref, cx_ref, cy_ref, cz_ref, inv_ref, q_ref, v_ref,
     o_ref,
-    ch, rh, cx, cy, cz, inv, q, va, vb, acc, wr, w0, w1, w2,
+    ch, cxh, cyh, czh, invh, qh, vh, q, va, vb, acc, wr, w0, w1, w2,
     *, nz, nx,
 ):
     zs = nz // ZS
@@ -375,25 +482,21 @@
     low, end = sub < RIM, sub == SUB - 1
     table = steps()
 
-    def sides(one, two):
-        return jnp.where(even, one, two), jnp.where(even, two, one)
-
+    rims = []
     for z in range(nz):
-        after, before = sides(tile(a1_ref, z), tile(a2_ref, z))
-        tile_at = slice(z * SUB, (z + 1) * SUB)
-        ch[tile_at] = jnp.where(low, after, before)
-        rh[tile_at] = rolled(jnp.where(low, before, after), RIM, 0)
-
-    row, spot = iota((ext, LANES), 0), iota((ext, LANES), 1) % GROUP
+        cond, rim = rim_of(even, low, tile(a1_ref, z), tile(a2_ref, z))
+        ch[z * SUB : (z + 1) * SUB] = cond
+        rims.append(rim)
+
+    row, spot = iota((ext, LANES), 0), part(iota((ext, LANES), 1), GROUP)[1]
 
     def strips_of(a):
-        rims = [None] * zs
+        ends = [None] * zs
         for pair in range(half):
-            after, before = sides(tile(b1_ref, a * half + pair), tile(b2_ref, a * half + pair))
-            rims[pair] = jnp.where(low, after, before)
-            rims[pair + half] = rolled(jnp.where(low, before, after), RIM, 0)
+            index = a * half + pair
+            ends[pair], ends[pair + half] = rim_of(even, low, tile(b1_ref, index), tile(b2_ref, index))
         return [
-            jnp.concatenate([strip_ref[(a * zs + zi) * nx : (a * zs + zi + 1) * nx], rims[zi]], axis=0)
+            jnp.concatenate([strip_ref[(a * zs + zi) * nx : (a * zs + zi + 1) * nx], ends[zi]], axis=0)
             for zi in range(zs)
         ]
 
@@ -414,7 +517,7 @@
         fx = jnp.where((row == nx - 1) | (row == ext - 1), cxs[zi] * (u - rolled(u, -1, 0)), 0.0)
         fy = jnp.where((spot == RIM - 1) | (spot == 3 * RIM - 1), cys[zi] * (u - rolled(u, -1, 1)), 0.0)
         r = rs[zi] - (fx - rolled(fx, 1, 0)) - (fy - rolled(fy, 1, 1))
-        wr[zi * ext : (zi + 1) * ext] = jnp.where(spot == RIM, r, rolled(r, -2 * RIM, 1))
+        wr[zi * SUB : (zi + 1) * SUB] = jnp.where(spot == RIM, r, rolled(r, -2 * RIM, 1))[nx:]
         diag = SHIFT + (cxs[zi] + rolled(cxs[zi], 1, 0)) + (cys[zi] + rolled(cys[zi], 1, 1)) + (czs[zi] + czds[zi])
         invs.append(1.0 / diag)
         qs.append(r * invs[zi])
@@ -422,7 +525,7 @@
     for k, w in enumerate((w0, w1, w2)):
         prod = [cys[zi] * vs[zi] for zi in range(zs)]
         for zi in range(zs):
-            w[zi * ext : (zi + 1) * ext] = jnp.where(spot == RIM - 1, prod[zi], rolled(vs[zi], -(2 * RIM + 2), 1))
+            w[zi * ext : (zi + 1) * ext] = window(spot, prod[zi], vs[zi], 3 * RIM)
         if k == SWEEPS - 1:
             break
         keep, lift = table[k]
@@ -436,87 +539,79 @@
             qs[zi] = qs[zi] - v + near * invs[zi]
             fresh.append(keep * v + lift * qs[zi])
         vs = fresh
-
-    wc = [jnp.where(spot == RIM - 1, c, rolled(c, -(2 * RIM + 2), 1)) for c in cs]
+    edge_c = [window(spot, c, c, 3 * RIM)[nx:] for c in cs]
+
+    lane = iota((SUB, LANES), 1)
+    first_lane, last_lane = lane == 0, lane == LANES - 1
+
+    def own(ref, z):
+        return ref[z % nz * nx : (z % nz + 1) * nx]
+
+    def rim_at(ref, z):
+        return tile(ref, z % nz)
+
+    below = 0.5 * (rim_at(ch, -1) + rim_at(ch, 0))
+    for z in range(nz):
+        at = slice(z * SUB, (z + 1) * SUB)
+        u, c = own(u_ref, z), tile(ch, z)
+        zi = z % zs
+        face = own(cx_ref, z)[nx - SUB :]
+        gx = 0.5 * (c + jnp.where(end, rolled(own(c_ref, z)[:SUB], -1, 0), rolled(c, -1, 0)))
+        gxl = jnp.where(sub == 0, rolled(face, 1, 0), rolled(gx, 1, 0))
+        edge = beside(edge_c[zi], z, zs, RIM - 1)
+        gy = 0.5 * (c + jnp.where(last_lane, edge, rolled(c, -1, 1)))
+        gyl = 0.5 * (c + jnp.where(first_lane, edge, rolled(c, 1, 1)))
+        above = 0.5 * (c + rim_at(ch, z + 1))
+        inverse = 1.0 / (SHIFT + (gx + gxl) + (gy + gyl) + (above + below))
+        after, before = rim_faces(sub, face, gx, u[:SUB], u[nx - SUB :], rims[z])
+        r = rims[z] + rolled(after, 1, 0) - before
+        r = jnp.where(first_lane | last_lane, beside(wr[zi * SUB : (zi + 1) * SUB], z, zs, RIM), r)
+        scaled = r * inverse
+        cxh[at] = gx
+        cyh[at] = gy
+        czh[at] = above
+        invh[at] = inverse
+        qh[at] = scaled
+        vh[at] = scaled * (1.0 / THETA)
+        below = above
 
     lane = iota((ext, LANES), 1)
     first_lane, last_lane = lane == 0, lane == LANES - 1
-    both_lanes = first_lane | last_lane
-
-    def own(ref, z):
-        return ref[z % nz * nx : (z % nz + 1) * nx]
+
+    def whole(ref, rim, z):
+        return jnp.concatenate([own(ref, z), rim_at(rim, z)], axis=0)
 
     def long(ref, z):
         return ref[z % nz * ext : (z % nz + 1) * ext]
 
-    def whole(z):
-        return jnp.concatenate([own(c_ref, z), tile(ch, z % nz)], axis=0)
-
-    def beside(w, z, column):
-        return rolled(w, -column - z // zs * GROUP, 1)
-
-    below = 0.5 * (whole(nz - 1) + whole(0))
-    for z in range(nz):
-        at = slice(z * ext, (z + 1) * ext)
-        c = whole(z)
-        edge = beside(wc[z % zs], z, RIM - 1)
-        gx = 0.5 * (c + rolled(c, -1, 0))
-        gy = 0.5 * (c + jnp.where(last_lane, edge, rolled(c, -1, 1)))
-        gyl = 0.5 * (c + jnp.where(first_lane, edge, rolled(c, 1, 1)))
-        above = 0.5 * (c + whole(z + 1))
-        diag = SHIFT + (gx + rolled(gx, 1, 0)) + (gy + gyl) + (above + below)
-        inverse = 1.0 / diag
-        r, rim = own(r_ref, z), tile(rh, z)
-        u_first, u_last = own(u_ref, z)[:SUB], own(u_ref, z)[nx - SUB :]
-        u_rim = jnp.where(sub == 0, rolled(rim, 1 - RIM, 0), rolled(rim, RIM - 1, 0))
-        fa = jnp.where(end, gx[nx - SUB : nx] * (u_last - rolled(u_rim, -1, 0)), 0.0)
-        fb = jnp.where(end, gx[nx:] * (u_rim - rolled(u_first, -1, 0)), 0.0)
-        r = jnp.concatenate(
-            [
-                r[:SUB] + rolled(fb, 1, 0),
-                r[SUB : nx - SUB],
-                r[nx - SUB :] - fa,
-                rim + rolled(fa, 1, 0) - fb,
-            ],
-            axis=0,
-        )
-        zi = z % zs
-        r = jnp.where(both_lanes, beside(wr[zi * ext : (zi + 1) * ext], z, RIM), r)
-        scaled = r * inverse
-        v = scaled * (1.0 / THETA)
-        cx[at] = gx
-        cy[at] = gy
-        cz[at] = above
-        inv[at] = inverse
-        q[at] = scaled
-        va[at] = v
-        acc[z * nx : (z + 1) * nx] = v[:nx]
-        below = above
-
     for k, w in enumerate((w0, w1, w2)):
-        old, new = (va, vb) if k % 2 == 0 else (vb, va)
+        old, new = (va, vb) if k % 2 else (vb, va)
         keep, lift = table[k]
+
+        def at_z(z, k=k, old=old):
+            return whole(v_ref, vh, z) if k == 0 else long(old, z)
+
         for z in range(nz):
-            at = slice(z * ext, (z + 1) * ext)
+            at, here = slice(z * ext, (z + 1) * ext), slice(z * nx, (z + 1) * nx)
             zi = z % zs
-            v, gx, gy = old[at], cx[at], cy[at]
-            edge = beside(w[zi * ext : (zi + 1) * ext], z, RIM - 1)
+            v, gx, gy = at_z(z), whole(cx_ref, cxh, z), whole(cy_ref, cyh, z)
+            edge = beside(w[zi * ext : (zi + 1) * ext], z, zs, RIM - 1)
             near = gx * rolled(v, -1, 0) + rolled(gx * v, 1, 0)
             near = near + gy * jnp.where(last_lane, edge, rolled(v, -1, 1))
             near = near + jnp.where(first_lane, edge, rolled(gy * v, 1, 1))
-            near = near + cz[at] * long(old, z + 1) + long(cz, z - 1) * long(old, z - 1)
-            scaled = q[at] - v + near * inv[at]
+            near = near + whole(cz_ref, czh, z) * at_z(z + 1) + whole(cz_ref, czh, z - 1) * at_z(z - 1)
+            scaled = (whole(q_ref, qh, z) if k == 0 else q[at]) - v + near * whole(inv_ref, invh, z)
             fresh = keep * v + lift * scaled
-            here = slice(z * nx, (z + 1) * nx)
+            total = (v[:nx] if k == 0 else acc[here]) + fresh[:nx]
             if k < SWEEPS - 1:
                 q[at] = scaled
                 new[at] = fresh
-                acc[here] = acc[here] + fresh[:nx]
+                acc[here] = total
             else:
-                o_ref[here] = own(u_ref, z) + (acc[here] + fresh[:nx])
-
-
-def fine(u, c, r, a1, a2, b1, b2, strips, nz, nx):
+                o_ref[here] = own(u_ref, z) + total
+
+
+def fine(strips, b2, b1, a1, a2, u, c, begun, nz, nx):
     zs = nz // ZS
     ext = nx + SUB
     rim = pltpu.VMEM((nz * SUB, LANES), f32)
@@ -525,13 +620,13 @@
     return pl.pallas_call(
         functools.partial(fine_kernel, nz=nz, nx=nx),
         out_shape=jax.ShapeDtypeStruct(u.shape, f32),
-        in_specs=[VMEM] * 8,
+        in_specs=[VMEM] * 13,
         out_specs=VMEM,
-        scratch_shapes=[rim] * 2 + [full] * 7 + [pltpu.VMEM(u.shape, f32)] + [strip] * 4,
+        scratch_shapes=[rim] * 7 + [full] * 3 + [pltpu.VMEM(u.shape, f32), pltpu.VMEM((zs * SUB, LANES), f32)] + [strip] * 3,
         compiler_params=SMALL,
-        cost_estimate=pl.CostEstimate(flops=150 * u.size, bytes_accessed=20 * u.size, transcendentals=0),
+        cost_estimate=pl.CostEstimate(flops=100 * u.size, bytes_accessed=40 * u.size, transcendentals=0),
         name="fine",
-    )(u, c, r, a1, a2, b1, b2, strips)
+    )(strips, b2, b1, a1, a2, u, c, *begun)
 
 
 def finish_kernel(x_ref, m_ref, r_ref, o_ref, *, nz, nx):
@@ -559,7 +654,7 @@
     top = v[:SUB]
     top = jnp.where(even, rolled(top, -rows - 1, 0), rolled(top, -1, 0))
     for Z in range(nz // COARSEN):
-        spread = jnp.take_along_axis(top, Z * SPREAD + RIM + lane // COARSEN, axis=1)
+        spread = jnp.take_along_axis(top, Z * SPREAD + RIM + part(lane, COARSEN)[0], axis=1)
         for X in range(rows):
             value = jnp.broadcast_to(spread[X : X + 1], (COARSEN, LANES))
             for z in range(Z * COARSEN, (Z + 1) * COARSEN):
@@ -595,31 +690,33 @@
     def far(x):
         return send(x, lambda i, j: (i - 1 if i % 2 == 0 else i + 1, j))
 
-    def sides(x):
+    def beside_y(x):
         left = send(x, lambda i, j: (i, j + 1))
         if size_y == 2:
             return left, left
         return left, send(x, lambda i, j: (i, j - 1))
 
-    return mate, far, sides
+    return mate, far, beside_y
 
 
 def body(iterate, source, conduct):
     nz, nx, ny = iterate.shape
     if nz != ZS * 4 or ny != LANES or nx != 3 * SUB or lax.axis_size("gx") % 2:
         raise ValueError("shapes")
-    mate, far, sides = moves()
+    mate, far, beside_y = moves()
     u, s, c = (x.reshape(nz * nx, ny) for x in (iterate, source, conduct))
-    q, a1, a2, r, own = pack(u, s, c, nz, nx)
-    ql, qr = sides(q)
+    q, f1, a1, a2, r, own = pack(u, s, c, nz, nx)
+    ql, qr = beside_y(q)
+    rf1 = mate(f1)
+    ra2 = far(a2)
     ra1 = mate(a1)
-    ra2 = far(a2)
-    b1, b2, strips = join(q, ql, qr, ra1, own, nz, nx)
+    b1, b2, strips = join(q, ql, qr, rf1, own, nz, nx)
     rb2 = far(b2)
     rb1 = mate(b1)
-    m = faces(own, b1, rb1, rb2, ra2, nz, nx)
+    begun = begin(strips, ra1, ra2, u, c, r, nz, nx)
+    m = faces(own, b2, rb2, rb1, ra2, begun[0], nz, nx)
     rm = mate(m)
-    x = fine(u, c, r, ra1, ra2, rb1, rb2, strips, nz, nx)
+    x = fine(strips, rb2, rb1, ra1, ra2, u, c, begun, nz, nx)
     return finish(x, m, rm, nz, nx).reshape(nz, nx, ny)
 
 

time: 26.6 us -> 21.9 us (0.82)
  starting transfers between devices: 11.8 us -> 8.65 us
  waiting for transfers between devices: 2.26 us -> 5.34 us
  local copies, waits for them, and re-layouts: 3 us -> 0.01 us
  Pallas kernels: 9.25 us -> 7.64 us
    ppermute x6 -> x7, starting transfers between devices: 11.8 us -> 8.65 us  [send(): return lax.ppermute(x, ('gx', 'gy'), pairs)]
    ppermute x6 -> x7, waiting for transfers between devices: 2.26 us -> 5.34 us  [send(): return lax.ppermute(x, ('gx', 'gy'), pairs)]
    unnamed x10 -> x4, local copies, waits for them, and re-layouts: 3 us -> 0.01 us
    pallas_call x1, Pallas kernels: 4.35 us -> 2.8 us  [pack(): pl.pallas_call(functools.partial(pack_kernel, nz=nz, nx=nx), out_shape=(t...]
    pallas_call x1, Pallas kernels: 2.85 us -> 2.14 us  [fine(): pl.pallas_call(functools.partial(fine_kernel, nz=nz, nx=nx), out_shape=ja...]
    pallas_call x1 -> x2, Pallas kernels: 0.32 us -> 0.97 us  [the longest x1 0.64 us: begin(): pl.pallas_call(functools.partial(begin_kernel, nz=nz, nx=nx), out_shape=(...]
  transfers between devices with their start and end apart: 6 -> 7, of which waited for: 1 -> 4; matrix products, arithmetic and copies ran while one was open for 0% -> 0% of each run, Pallas kernels for 12% -> 14%
where the time goes in v4:
time: 21.9 us; the launch traced here: 21.7 us
  starting transfers between devices  8.65 us (39%)
  Pallas kernels  7.64 us (35%)
  waiting for transfers between devices  5.34 us (24%)
    ppermute x7, starting transfers between devices, send(): return lax.ppermute(x, ('gx', 'gy'), pairs)  8.65 us
    ppermute x7, waiting for transfers between devices, send(): return lax.ppermute(x, ('gx', 'gy'), pairs)  5.34 us
    pallas_call x1, Pallas kernels, pack(): pl.pallas_call(functools.partial(pack_kernel, nz=nz, nx=nx), out_shape=(t...  2.8 us
    pallas_call x1, Pallas kernels, fine(): pl.pallas_call(functools.partial(fine_kernel, nz=nz, nx=nx), out_shape=ja...  2.14 us
    pallas_call x1, Pallas kernels, finish(): pl.pallas_call(functools.partial(finish_kernel, nz=nz, nx=nx), out_shape=...  1.29 us
    pallas_call x1, Pallas kernels, begin(): pl.pallas_call(functools.partial(begin_kernel, nz=nz, nx=nx), out_shape=(...  0.64 us
    pallas_call x1, Pallas kernels, faces(): pl.pallas_call(functools.partial(faces_kernel, nz=nz, nx=nx), out_shape=t...  0.44 us
  transfers between devices with their start and end apart: 7, of which 4 were waited for; matrix products, arithmetic and copies ran while one was open for 0% of the time, Pallas kernels for 14%

profile of v4, /device:TPU:0, one launch (start us, length us, event | category | flops | bytes accessed | tf_op | source)
XLA Modules:
  0.0 21.7 jit_solution(9400199710737602360)
XLA Ops:
  0.0 0.0 copy-start.1
  0.0 2.8 %pack.1 = (f32[216,128]{1,0:T(8,128)S(1)}, f32[72,128]{1,0:T(8,128)S(1)}, f32[256,128]{1,0:T(8,128)S(1)}, f32[256,128]{1,0:T(8,128)S(1)}, f32[768,128]{1,0:T(8,128)S(1)}, /*index=5*/f32[128,128]{1,0:T(8,128)S(1)}) custom-call(f32[768,128]{1,0:T(8,128)} %bitcast.4, f32[768,128]{1,0:T(8,128)} %bitcast.10, f32[768,128]{1,0:T(8,128)} %bitcast.7), custom_call_target="tpu_custom_call" | custom-call | tf_op jit(solution)/shard_map/pack/pallas_call | solution.py:192
  2.8 0.0 copy-start
  2.8 3.0 %collective-permute-start = (f32[216,128]{1,0:T(8,128)S(1)}, f32[216,128]{1,0:T(8,128)S(1)}, u32[]{:S(2)}, u32[]{:S(2)}) collective-permute-start(f32[216,128]{1,0:T(8,128)S(1)} %get-tuple-element.20.q_ref), channel_id=1, source_target_pairs={{0,1},{1,0},{2,3},{3,2},{4,5},{5,4},{6,7},{7,6},{8,9},{9,8},{10,11... | collective-permute-start | bytes 331784 | tf_op jit(solution)/shard_map/ppermute | solution.py:685
  5.9 3.7 %collective-permute-start.5 = (f32[256,128]{1,0:T(8,128)S(1)}, f32[256,128]{1,0:T(8,128)S(1)}, u32[]{:S(2)}, u32[]{:S(2)}) collective-permute-start(f32[256,128]{1,0:T(8,128)S(1)} %get-tuple-element.27), channel_id=1, source_target_pairs={{0,30},{1,31},{2,4},{3,5},{4,2},{5,3},{6,8},{7,9},{8,6},{9,7},{10,... | collective-permute-start | bytes 393224 | tf_op jit(solution)/shard_map/ppermute | solution.py:685
  9.5 0.0 collective-permute-start.4
  9.5 0.5 %collective-permute-start.1 = (f32[72,128]{1,0:T(8,128)S(1)}, f32[72,128]{1,0:T(8,128)S(1)}, u32[]{:S(2)}, u32[]{:S(2)}) collective-permute-start(f32[72,128]{1,0:T(8,128)S(1)} %get-tuple-element.21), channel_id=1, source_target_pairs={{0,2},{1,3},{2,0},{3,1},{4,6},{5,7},{6,4},{7,5},{8,10},{9,11},{10,... | collective-permute-start | bytes 110600 | tf_op jit(solution)/shard_map/ppermute | solution.py:685
  10.1 0.9 %collective-permute-done.1.f1_ref = f32[72,128]{1,0:T(8,128)S(1)} collective-permute-done((f32[72,128]{1,0:T(8,128)S(1)}, f32[72,128]{1,0:T(8,128)S(1)}, u32[]{:S(2)}, u32[]{:S(2)}) %collective-permute-start.1) | collective-permute-done | bytes 36896 | tf_op jit(solution)/shard_map/ppermute | solution.py:685
  10.9 0.0 collective-permute-done.ql_ref.qr_ref
  11.0 0.3 %join.1 = (f32[120,128]{1,0:T(8,128)S(1)}, f32[128,128]{1,0:T(8,128)S(1)}, f32[288,128]{1,0:T(8,128)S(1)}) custom-call(f32[216,128]{1,0:T(8,128)S(1)} %get-tuple-element.20.q_ref, f32[216,128]{1,0:T(8,128)S(1)} %collective-permute-done.ql_ref.qr_ref, f32[216,128]{1,0:T(8,128)S(1)} %collective-permute-done.ql_ref.qr_ref, ...), custom_call_target="tpu_custom_call" | custom-call | tf_op jit(solution)/shard_map/join/pallas_call | solution.py:291
  11.3 1.3 %collective-permute-start.2 = (f32[128,128]{1,0:T(8,128)S(1)}, f32[128,128]{1,0:T(8,128)S(1)}, u32[]{:S(2)}, u32[]{:S(2)}) collective-permute-start(f32[128,128]{1,0:T(8,128)S(1)} %get-tuple-element.24.b_ref), channel_id=1, source_target_pairs={{0,30},{1,31},{2,4},{3,5},{4,2},{5,3},{6,8},{7,9},{8,6},{9,7},{10,... | collective-permute-start | bytes 196616 | tf_op jit(solution)/shard_map/ppermute | solution.py:685
  12.6 0.0 collective-permute-start.3
  12.6 0.3 %collective-permute-done.5.a2_ref = f32[256,128]{1,0:T(8,128)S(1)} collective-permute-done((f32[256,128]{1,0:T(8,128)S(1)}, f32[256,128]{1,0:T(8,128)S(1)}, u32[]{:S(2)}, u32[]{:S(2)}) %collective-permute-start.5) | collective-permute-done | bytes 131104 | tf_op jit(solution)/shard_map/ppermute | solution.py:685
  12.9 0.0 collective-permute-done.4.a1_ref
  13.0 0.0 copy-done.1
  13.0 0.0 copy-done
  13.0 0.6 %begin.1 = (f32[768,128]{1,0:T(8,128)S(1)}, f32[768,128]{1,0:T(8,128)S(1)}, f32[768,128]{1,0:T(8,128)S(1)}, f32[768,128]{1,0:T(8,128)S(1)}, f32[768,128]{1,0:T(8,128)S(1)}, /*index=5*/f32[768,128]{1,0:T(8,128)S(1)}) custom-call(f32[288,128]{1,0:T(8,128)S(1)} %get-tuple-element.23.strip_ref, f32[256,128]{1,0:T(8,128)S(1)} %collective-permute-done.4.a1_ref, ...), custom_call_target="tpu_custom_call" | custom-call | flops 3932160 | bytes 3932160 | tf_op jit(solution)/shard_map/begin/pallas_call | solution.py:459
  13.6 0.3 %collective-permute-done.3.b1_ref.r1_ref = f32[120,128]{1,0:T(8,128)S(1)} collective-permute-done((f32[120,128]{1,0:T(8,128)S(1)}, f32[120,128]{1,0:T(8,128)S(1)}, u32[]{:S(2)}, u32[]{:S(2)}) %collective-permute-start.3) | collective-permute-done | bytes 61472 | tf_op jit(solution)/shard_map/ppermute | solution.py:685
  13.9 3.9 %collective-permute-done.2.b2_ref.r2_ref = f32[128,128]{1,0:T(8,128)S(1)} collective-permute-done((f32[128,128]{1,0:T(8,128)S(1)}, f32[128,128]{1,0:T(8,128)S(1)}, u32[]{:S(2)}, u32[]{:S(2)}) %collective-permute-start.2) | collective-permute-done | bytes 65568 | tf_op jit(solution)/shard_map/ppermute | solution.py:685
  17.7 0.4 %faces.1.m_ref = f32[24,128]{1,0:T(8,128)S(1)} custom-call(f32[128,128]{1,0:T(8,128)S(1)} %get-tuple-element.22.own_ref, f32[128,128]{1,0:T(8,128)S(1)} %get-tuple-element.24.b_ref, f32[128,128]{1,0:T(8,128)S(1)} %collective-permute-done.2.b2_ref.r2_ref, f32[120,128]{1,0:T(8,128)S(1)} %collective-permute-done.3.b1_ref.r1_ref, ...), custom_call_target="tpu_custom_call" | custom-call | tf_op jit(solution)/shard_map/faces/pallas_call | solution.py:367
  18.2 0.1 collective-permute-start.6
  18.3 2.1 %fine.1.x_ref = f32[768,128]{1,0:T(8,128)S(1)} custom-call(f32[288,128]{1,0:T(8,128)S(1)} %get-tuple-element.23.strip_ref, f32[128,128]{1,0:T(8,128)S(1)} %collective-permute-done.2.b2_ref.r2_ref, f32[120,128]{1,0:T(8,128)S(1)} %collective-permute-done.3.b1_ref.r1_ref, f32[256,128]{1,0:T(8,128)S(1)} %collective-permute-done.4.a1_ref, ...), custom_call_target="tpu_custom_call" | custom-call | flops 9830400 | bytes 3932160 | tf_op jit(solution)/shard_map/fine/pallas_call | solution.py:620
  20.4 0.0 collective-permute-done.6.r_ref
  20.4 1.3 %finish.1 = f32[768,128]{1,0:T(8,128)} custom-call(f32[768,128]{1,0:T(8,128)S(1)} %fine.1.x_ref, f32[24,128]{1,0:T(8,128)S(1)} %faces.1.m_ref, f32[24,128]{1,0:T(8,128)S(1)} %collective-permute-done.6.r_ref), custom_call_target="tpu_custom_call" | custom-call | tf_op jit(solution)/shard_map/finish/pallas_call | solution.py:666
Async XLA Ops:
  0.0 13.0 %copy-start.1 = (f32[32,24,128]{2,1,0:T(8,128)S(1)}, f32[32,24,128]{2,1,0:T(8,128)}, u32[]{:S(2)}) copy-start(f32[32,24,128]{2,1,0:T(8,128)} %param.5) | copy-start | bytes 1179652
  2.8 10.1 %copy-start = (f32[32,24,128]{2,1,0:T(8,128)S(1)}, f32[32,24,128]{2,1,0:T(8,128)}, u32[]{:S(2)}) copy-start(f32[32,24,128]{2,1,0:T(8,128)} %param.3) | copy-start | bytes 1179652
  2.8 8.1 %collective-permute-start = (f32[216,128]{1,0:T(8,128)S(1)}, f32[216,128]{1,0:T(8,128)S(1)}, u32[]{:S(2)}, u32[]{:S(2)}) collective-permute-start(f32[216,128]{1,0:T(8,128)S(1)} %get-tuple-element.20.q_ref), channel_id=1, source_target_pairs={{0,1},{1,0},{2,3},{3,2},{4,5},{5,4},{6,7},{7,6},{8,9},{9,8},{10,11... | collective-permute-start | bytes 331784 | tf_op jit(solution)/shard_map/ppermute | solution.py:685
  5.9 7.1 %collective-permute-start.5 = (f32[256,128]{1,0:T(8,128)S(1)}, f32[256,128]{1,0:T(8,128)S(1)}, u32[]{:S(2)}, u32[]{:S(2)}) collective-permute-start(f32[256,128]{1,0:T(8,128)S(1)} %get-tuple-element.27), channel_id=1, source_target_pairs={{0,30},{1,31},{2,4},{3,5},{4,2},{5,3},{6,8},{7,9},{8,6},{9,7},{10,... | collective-permute-start | bytes 393224 | tf_op jit(solution)/shard_map/ppermute | solution.py:685
  9.5 3.4 %collective-permute-start.4 = (f32[256,128]{1,0:T(8,128)S(1)}, f32[256,128]{1,0:T(8,128)S(1)}, u32[]{:S(2)}, u32[]{:S(2)}) collective-permute-start(f32[256,128]{1,0:T(8,128)S(1)} %get-tuple-element.26), channel_id=1, source_target_pairs={{0,2},{1,3},{2,0},{3,1},{4,6},{5,7},{6,4},{7,5},{8,10},{9,11},{10,... | collective-permute-start | bytes 393224 | tf_op jit(solution)/shard_map/ppermute | solution.py:685
  9.5 1.4 %collective-permute-start.1 = (f32[72,128]{1,0:T(8,128)S(1)}, f32[72,128]{1,0:T(8,128)S(1)}, u32[]{:S(2)}, u32[]{:S(2)}) collective-permute-start(f32[72,128]{1,0:T(8,128)S(1)} %get-tuple-element.21), channel_id=1, source_target_pairs={{0,2},{1,3},{2,0},{3,1},{4,6},{5,7},{6,4},{7,5},{8,10},{9,11},{10,... | collective-permute-start | bytes 110600 | tf_op jit(solution)/shard_map/ppermute | solution.py:685
  11.3 6.5 %collective-permute-start.2 = (f32[128,128]{1,0:T(8,128)S(1)}, f32[128,128]{1,0:T(8,128)S(1)}, u32[]{:S(2)}, u32[]{:S(2)}) collective-permute-start(f32[128,128]{1,0:T(8,128)S(1)} %get-tuple-element.24.b_ref), channel_id=1, source_target_pairs={{0,30},{1,31},{2,4},{3,5},{4,2},{5,3},{6,8},{7,9},{8,6},{9,7},{10,... | collective-permute-start | bytes 196616 | tf_op jit(solution)/shard_map/ppermute | solution.py:685
  12.6 1.2 %collective-permute-start.3 = (f32[120,128]{1,0:T(8,128)S(1)}, f32[120,128]{1,0:T(8,128)S(1)}, u32[]{:S(2)}, u32[]{:S(2)}) collective-permute-start(f32[120,128]{1,0:T(8,128)S(1)} %get-tuple-element.25), channel_id=1, source_target_pairs={{0,2},{1,3},{2,0},{3,1},{4,6},{5,7},{6,4},{7,5},{8,10},{9,11},{10,... | collective-permute-start | bytes 184328 | tf_op jit(solution)/shard_map/ppermute | solution.py:685
  18.2 2.2 %collective-permute-start.6 = (f32[24,128]{1,0:T(8,128)S(1)}, f32[24,128]{1,0:T(8,128)S(1)}, u32[]{:S(2)}, u32[]{:S(2)}) collective-permute-start(f32[24,128]{1,0:T(8,128)S(1)} %faces.1.m_ref), channel_id=1, source_target_pairs={{0,2},{1,3},{2,0},{3,1},{4,6},{5,7},{6,4},{7,5},{8,10},{9,11},{10,... | collective-permute-start | bytes 36872 | tf_op jit(solution)/shard_map/ppermute | solution.py:685

commit v5 on v4

--- a/solution.py
+++ b/solution.py
@@ -106,7 +106,9 @@
     return jnp.sum(values, axis=0, keepdims=True)
 
 
-def pack_kernel(u_hbm, s_hbm, c_hbm, q_ref, f1_ref, a1_ref, a2_ref, r_ref, own_ref, u_ref, s_ref, c_ref, sems, *, nz, nx):
+def pack_kernel(
+    u_hbm, s_hbm, c_hbm, q_ref, f1_ref, last_ref, one_ref, two_ref, r_ref, own_ref, u_ref, s_ref, c_ref, sems, *, nz, nx
+):
     pieces = sems.shape[1]
     size = nz * nx // pieces
     copies = []
@@ -150,8 +152,9 @@
             u0, u2, c0, c2 = u[:SUB], u[nx - SUB :], c[:SUB], c[nx - SUB :]
             first = jnp.where(low, c0, jnp.where(sub == SUB - 1, rolled(u0, -1, 0), rolled(r[:SUB], RIM, 0)))
             last = jnp.where(low, jnp.where(sub == 0, rolled(u2, 1, 0), rolled(r[nx - SUB :], RIM, 0)), c2)
-            a1_ref[z * SUB : (z + 1) * SUB] = jnp.where(even, last, first)
-            a2_ref[z * SUB : (z + 1) * SUB] = jnp.where(even, first, last)
+            last_ref[z * SUB : (z + 1) * SUB] = last
+            to = z % (nz // 2) * SUB
+            (one_ref if z < nz // 2 else two_ref)[to : to + SUB] = first
         coarse = coarse + compact(block_rows(sum_r) + rolled(block_rows(sum_c), RIM, 0), Z)
     coarse = coarse * (1.0 / CELLS)
 
@@ -195,12 +198,13 @@
             tiles(3 * half * nx // SUB + 2 * nz // SUB + 1),
             tiles(2 * nz // SUB + 1),
             tiles(nz),
-            tiles(nz),
+            tiles(nz // 2),
+            tiles(nz // 2),
             jax.ShapeDtypeStruct(u.shape, f32),
             tiles(4 * nz // SUB),
         ),
         in_specs=[pl.BlockSpec(memory_space=pltpu.HBM)] * 3,
-        out_specs=(VMEM,) * 6,
+        out_specs=(VMEM,) * 7,
         scratch_shapes=[pltpu.VMEM(u.shape, f32)] * 3 + [pltpu.SemaphoreType.DMA((3, pieces))],
         compiler_params=SMALL,
         name="pack",
@@ -212,13 +216,7 @@
     return jnp.where(last, second, first)
 
 
-def opposite(rows_ref, a, z, after):
-    first = picked(rows_ref, z * SUB, SUB)
-    last = picked(rows_ref, z * SUB + SUB - 1, SUB)
-    return jnp.where(after, last, first) if a == 0 else jnp.where(after, first, last)
-
-
-def join_kernel(q_ref, ql_ref, qr_ref, f1_ref, own_ref, b1_ref, b2_ref, strip_ref, *, nz, nx):
+def join_kernel(q_ref, ql_ref, qr_ref, f1_ref, own_ref, b1_ref, b2_ref, strip_ref, kept_ref, *, nz, nx):
     zs = nz // ZS
     half = zs // 2
     even = is_even()
@@ -246,12 +244,18 @@
         joined.append(group)
 
     source, target = 3 * half * nx, 3 * half * SUB
-    for index in range(2 * nz // SUB):
-        at = slice(source + index * SUB, source + (index + 1) * SUB)
-        both = jnp.where(part(lane, HALF)[1] < REACH, ql_ref[at], qr_ref[at])
-        to = slice(target + index * SUB, target + (index + 1) * SUB)
-        b1_ref[to] = both
-        b2_ref[to] = both
+    lower, outer = lane < HALF, part(lane, HALF)[1] < REACH
+    for Z in range(nz // SUB):
+        u, c = (
+            jnp.where(outer, ql_ref[at : at + SUB], qr_ref[at : at + SUB])
+            for at in (source + Z * SUB, source + nz + Z * SUB)
+        )
+        kept_ref[Z * SUB : (Z + 1) * SUB] = u
+        kept_ref[nz + Z * SUB : nz + (Z + 1) * SUB] = c
+        first, last = jnp.where(lower, u, rolled(c, HALF, 1)), jnp.where(lower, rolled(u, HALF, 1), c)
+        to = slice(target + Z * SUB, target + (Z + 1) * SUB)
+        b1_ref[to] = jnp.where(even, last, first)
+        b2_ref[to] = jnp.where(even, first, last)
 
     at = slice(source + 2 * nz, source + 2 * nz + SUB)
     place = part(lane, SPREAD)[1]
@@ -276,29 +280,42 @@
         u, c = facing(own_ref, 0, Z * SUB, nz, even) - tile(f1_ref, Z), facing(own_ref, 1, Z * SUB, nz, even)
         across = all_rows((0.5 / CELLS) * (c + tile(f1_ref, nz // SUB + Z)) * u)
         change = change - compact(jnp.where(sub == nearest, across, 0.0), Z)
-    mate = f1_ref[2 * nz :]
+    mate = f1_ref[2 * nz : 2 * nz + SUB]
     mate = jnp.where(even, rolled(mate, rows - RIM, 0), rolled(mate, 1 - RIM, 0))
     cond = jnp.where(sub == rows, mate, rolled(window, -RIM, 0))
-    to = target + 2 * nz
-    for ref in (b1_ref, b2_ref):
-        ref[to : to + SUB] = cond
-    b2_ref[to + SUB : to + 2 * SUB] = window + change
+    rhs = window + change
+    kept_ref[2 * nz : 2 * nz + SUB] = cond
+    kept_ref[2 * nz + SUB :] = rhs
+    to = target + nz
+    b1_ref[to:] = cond
+    b2_ref[to : to + SUB] = cond
+    b2_ref[to + SUB : to + 2 * SUB] = rhs
+    to = to + 2 * SUB
+    for a in range(2):
+        for Z in range(nz // SUB):
+            at = to + a * nz + Z * SUB
+            b2_ref[at : at + SUB] = facing(own_ref, a, Z * SUB, nz, jnp.logical_not(even))
 
 
 def join(q, ql, qr, f1, own, nz, nx):
     zs = nz // ZS
-    size = 3 * (zs // 2) + 2 * nz // SUB + 1
+    size = 3 * (zs // 2) + nz // SUB + 1
     return pl.pallas_call(
         functools.partial(join_kernel, nz=nz, nx=nx),
-        out_shape=(tiles(size), tiles(size + 1), jax.ShapeDtypeStruct((3 * zs * nx, LANES), f32)),
+        out_shape=(
+            tiles(size),
+            tiles(size + 1 + 2 * nz // SUB),
+            jax.ShapeDtypeStruct((3 * zs * nx, LANES), f32),
+            tiles(2 * nz // SUB + 2),
+        ),
         in_specs=[VMEM] * 5,
-        out_specs=(VMEM,) * 3,
+        out_specs=(VMEM,) * 4,
         compiler_params=SMALL,
         name="join",
     )(q, ql, qr, f1, own)
 
 
-def faces_kernel(own_ref, b_ref, r2_ref, r1_ref, a2_ref, after_ref, o_ref, *, nz, nx):
+def faces_kernel(own_ref, kept_ref, r2_ref, r1_ref, after_ref, o_ref, *, nz, nx):
     del after_ref
     half = nz // ZS // 2
     even = is_even()
@@ -316,22 +333,23 @@
     valid = ((sub == 0) & is_own) | ((sub > 0) & (is_left | is_right))
 
     def outside(r_ref, Z, upper):
-        def at(ref, a):
-            start = base + a * nz + Z * COARSEN
-            return ref[start : start + SUB]
-
-        u = at(b_ref, 0) - rolled(at(r_ref, 0), HALF, 1)
-        c = at(b_ref, 1) + rolled(at(r_ref, 1), HALF, 1)
-        flux = all_rows(0.5 * c * u)
-        return jnp.where(upper, rolled(flux, HALF, 1), flux)
-
+        def mine(at):
+            tile_at = kept_ref[at + Z * SUB : at + (Z + 1) * SUB]
+            return jnp.where(upper, rolled(tile_at, HALF, 1), tile_at)
+
+        other = r_ref[base + Z * SUB : base + (Z + 1) * SUB]
+        return all_rows(0.5 * (mine(nz) + rolled(other, HALF, 1)) * (mine(0) - other))
+
+    odd = jnp.logical_not(even)
+    far_rows = base + nz + 2 * SUB
     flux = jnp.zeros((SUB, LANES), f32)
     for Z in range(nz // COARSEN):
-        after = jnp.logical_not(even)
-        u = facing(own_ref, 0, Z * SUB, nz, after) - opposite(a2_ref, 0, Z * SUB, after)
-        c = facing(own_ref, 1, Z * SUB, nz, after) + opposite(a2_ref, 1, Z * SUB, after)
-        one = all_rows(0.5 * c * u)
-        two = outside(r2_ref, Z, jnp.logical_not(even))
+        u, c = (
+            (facing(own_ref, a, Z * SUB, nz, odd), r2_ref[at : at + SUB])
+            for a, at in ((0, far_rows + Z * SUB), (1, far_rows + nz + Z * SUB))
+        )
+        one = all_rows(0.5 * (c[0] + c[1]) * (u[0] - u[1]))
+        two = outside(r2_ref, Z, odd)
         three = outside(r1_ref, Z, even)
         sums = lane_sums(jnp.where(sub == 0, one, jnp.where(sub == 1, two, jnp.where(sub == 2, three, 0.0))))
         here = valid & (plane == Z)
@@ -343,15 +361,15 @@
         before, after = jnp.where(even, other, own), jnp.where(even, own, other)
         return jnp.where(sub <= rows, rolled(before, 1, 0), rolled(after, rows + 1, 0))
 
-    at = base + 2 * nz + SUB
-    rhs = stacked(b_ref[at : at + SUB], r2_ref[at : at + SUB])
+    at = base + nz + SUB
+    rhs = stacked(kept_ref[2 * nz + SUB :], r2_ref[at : at + SUB])
     sign = jnp.where(even, 1.0, -1.0)
     rhs = rhs + jnp.where(sub == rows, sign * far, jnp.where(sub == rows + 1, -sign * far, 0.0))
     rhs = rhs - jnp.where(sub == jnp.where(even, 2 * rows, 1), mate, 0.0)
 
     at = at - SUB
     near_c, far_c = r1_ref[at : at + SUB], r2_ref[at : at + SUB]
-    cond = stacked(b_ref[at : at + SUB], far_c)
+    cond = stacked(kept_ref[2 * nz : 2 * nz + SUB], far_c)
     before = jnp.where(even, rolled(far_c, -rows, 0), rolled(near_c, 1 - rows, 0))
     after = jnp.where(even, rolled(near_c, 2 * rows + 1, 0), rolled(far_c, rows + 1, 0))
     cond = jnp.where(sub == 0, before, jnp.where(sub == 2 * rows + 1, after, cond))
@@ -363,24 +381,29 @@
     o_ref[2 * SUB :] = cond
 
 
-def faces(own, b, r2, r1, a2, after, nz, nx):
+def faces(own, kept, r2, r1, after, nz, nx):
     return pl.pallas_call(
         functools.partial(faces_kernel, nz=nz, nx=nx),
         out_shape=tiles(3),
-        in_specs=[VMEM] * 5 + [pl.BlockSpec(memory_space=pl.ANY)],
+        in_specs=[VMEM] * 4 + [pl.BlockSpec(memory_space=pl.ANY)],
         out_specs=VMEM,
         compiler_params=SMALL,
         name="faces",
-    )(own, b, r2, r1, a2, after)
+    )(own, kept, r2, r1, after)
 
 
 def sides(even, one, two):
     return jnp.where(even, one, two), jnp.where(even, two, one)
 
 
-def rim_of(even, low, one, two):
-    after, before = sides(even, one, two)
+def rim_of(low, after, before):
     return jnp.where(low, after, before), rolled(jnp.where(low, before, after), RIM, 0)
+
+
+def rims_of(low, one_ref, two_ref, last_ref, nz):
+    half = nz // 2
+    for z in range(nz):
+        yield rim_of(low, tile(one_ref if z < half else two_ref, z % half), tile(last_ref, z))
 
 
 def rim_faces(sub, face, rim_face, u_first, u_last, rim):
@@ -400,20 +423,12 @@
 
 
 def begin_kernel(
-    strip_ref, a1_ref, a2_ref, u_ref, c_ref, r_ref, cx_ref, cy_ref, cz_ref, inv_ref, q_ref, v_ref, ch, *, nz, nx
+    strip_ref, u_ref, c_ref, r_ref, cx_ref, cy_ref, cz_ref, diag_ref, inv_ref, q_ref, v_ref, *, nz, nx
 ):
     zs = nz // ZS
-    even = is_even()
-    sub = iota((SUB, LANES), 0)
-    low = sub < RIM
     spot = part(iota((nx, LANES), 1), GROUP)[1]
-    lane = iota((nx, LANES), 1)
+    row, lane = iota((nx, LANES), 0), iota((nx, LANES), 1)
     first_lane, last_lane = lane == 0, lane == LANES - 1
-    rims = []
-    for z in range(nz):
-        cond, rim = rim_of(even, low, tile(a1_ref, z), tile(a2_ref, z))
-        ch[z * SUB : (z + 1) * SUB] = cond
-        rims.append(rim)
 
     def strip(a, zi):
         return strip_ref[(a * zs + zi) * nx : (a * zs + zi + 1) * nx]
@@ -431,47 +446,46 @@
     below = 0.5 * (own(c_ref, -1) + own(c_ref, 0))
     for z in range(nz):
         at = slice(z * nx, (z + 1) * nx)
-        u, c = own(u_ref, z), own(c_ref, z)
-        whole = jnp.concatenate([c, tile(ch, z)], axis=0)
-        gx = 0.5 * (whole + rolled(whole, -1, 0))
-        gxl = rolled(gx, 1, 0)[:nx]
+        c = own(c_ref, z)
+        gx = jnp.where(row == nx - 1, 0.0, 0.5 * (c + rolled(c, -1, 0)))
         edge = beside(edge_c[z % zs], z, zs, RIM - 1)
         gy = 0.5 * (c + jnp.where(last_lane, edge, rolled(c, -1, 1)))
         gyl = 0.5 * (c + jnp.where(first_lane, edge, rolled(c, 1, 1)))
         above = 0.5 * (c + own(c_ref, z + 1))
-        inverse = 1.0 / (SHIFT + (gx[:nx] + gxl) + (gy + gyl) + (above + below))
-        after, before = rim_faces(sub, gx[nx - SUB : nx], gx[nx:], u[:SUB], u[nx - SUB :], rims[z])
-        r = own(r_ref, z)
-        r = jnp.concatenate([r[:SUB] + rolled(before, 1, 0), r[SUB : nx - SUB], r[nx - SUB :] - after], axis=0)
+        diag = SHIFT + (gx + rolled(gx, 1, 0)) + (gy + gyl) + (above + below)
         edge = beside(edge_f[z % zs], z, zs, RIM - 1)
-        r = r + jnp.where(first_lane, edge, jnp.where(last_lane, -edge, 0.0))
-        scaled = r * inverse
-        cx_ref[at] = gx[:nx]
+        r = own(r_ref, z) + jnp.where(first_lane, edge, jnp.where(last_lane, -edge, 0.0))
+        inner = slice(SUB, nx - SUB)
+        inverse = 1.0 / diag[inner]
+        scaled = r[inner] * inverse
+        cx_ref[at] = gx
         cy_ref[at] = gy
         cz_ref[at] = above
-        inv_ref[at] = inverse
-        q_ref[at] = scaled
-        v_ref[at] = scaled * (1.0 / THETA)
+        diag_ref[at] = diag
+        q_ref[at] = jnp.concatenate([r[:SUB], scaled, r[nx - SUB :]], axis=0)
+        to = slice(z * (nx - 2 * SUB), (z + 1) * (nx - 2 * SUB))
+        inv_ref[to] = inverse
+        v_ref[to] = scaled * (1.0 / THETA)
         below = above
 
 
-def begin(strips, a1, a2, u, c, r, nz, nx):
+def begin(strips, u, c, r, nz, nx):
+    inner = jax.ShapeDtypeStruct((nz * (nx - 2 * SUB), LANES), f32)
     return pl.pallas_call(
         functools.partial(begin_kernel, nz=nz, nx=nx),
-        out_shape=(jax.ShapeDtypeStruct(u.shape, f32),) * 6,
-        in_specs=[VMEM] * 6,
-        out_specs=(VMEM,) * 6,
-        scratch_shapes=[pltpu.VMEM((nz * SUB, LANES), f32)],
+        out_shape=(jax.ShapeDtypeStruct(u.shape, f32),) * 4 + (inner, jax.ShapeDtypeStruct(u.shape, f32), inner),
+        in_specs=[VMEM] * 4,
+        out_specs=(VMEM,) * 7,
         compiler_params=SMALL,
         cost_estimate=pl.CostEstimate(flops=40 * u.size, bytes_accessed=40 * u.size, transcendentals=0),
         name="begin",
-    )(strips, a1, a2, u, c, r)
+    )(strips, u, c, r)
 
 
 def fine_kernel(
-    strip_ref, b2_ref, b1_ref, a1_ref, a2_ref, u_ref, c_ref, cx_ref, cy_ref, cz_ref, inv_ref, q_ref, v_ref,
+    strip_ref, b2_ref, b1_ref, one_ref, two_ref, last_ref, u_ref, c_ref, cx_ref, cy_ref, cz_ref, diag_ref, inv_ref, q_ref, v_ref,
     o_ref,
-    ch, cxh, cyh, czh, invh, qh, vh, q, va, vb, acc, wr, w0, w1, w2,
+    ch, cyh, czh, cx, inv, q, va, vb, acc, wr, w0, w1, w2,
     *, nz, nx,
 ):
     zs = nz // ZS
@@ -483,8 +497,7 @@
     table = steps()
 
     rims = []
-    for z in range(nz):
-        cond, rim = rim_of(even, low, tile(a1_ref, z), tile(a2_ref, z))
+    for z, (cond, rim) in enumerate(rims_of(low, one_ref, two_ref, last_ref, nz)):
         ch[z * SUB : (z + 1) * SUB] = cond
         rims.append(rim)
 
@@ -494,7 +507,7 @@
         ends = [None] * zs
         for pair in range(half):
             index = a * half + pair
-            ends[pair], ends[pair + half] = rim_of(even, low, tile(b1_ref, index), tile(b2_ref, index))
+            ends[pair], ends[pair + half] = rim_of(low, *sides(even, tile(b1_ref, index), tile(b2_ref, index)))
         return [
             jnp.concatenate([strip_ref[(a * zs + zi) * nx : (a * zs + zi + 1) * nx], ends[zi]], axis=0)
             for zi in range(zs)
@@ -554,25 +567,38 @@
     for z in range(nz):
         at = slice(z * SUB, (z + 1) * SUB)
         u, c = own(u_ref, z), tile(ch, z)
+        c_first, c_last = own(c_ref, z)[:SUB], own(c_ref, z)[nx - SUB :]
         zi = z % zs
-        face = own(cx_ref, z)[nx - SUB :]
-        gx = 0.5 * (c + jnp.where(end, rolled(own(c_ref, z)[:SUB], -1, 0), rolled(c, -1, 0)))
-        gxl = jnp.where(sub == 0, rolled(face, 1, 0), rolled(gx, 1, 0))
+        face = jnp.where(end, 0.5 * (c_last + rolled(c, -1, 0)), 0.0)
+        gx = 0.5 * (c + jnp.where(end, rolled(c_first, -1, 0), rolled(c, -1, 0)))
+        gxl = rolled(gx, 1, 0)
         edge = beside(edge_c[zi], z, zs, RIM - 1)
         gy = 0.5 * (c + jnp.where(last_lane, edge, rolled(c, -1, 1)))
         gyl = 0.5 * (c + jnp.where(first_lane, edge, rolled(c, 1, 1)))
         above = 0.5 * (c + rim_at(ch, z + 1))
-        inverse = 1.0 / (SHIFT + (gx + gxl) + (gy + gyl) + (above + below))
+        diag = SHIFT + (gx + jnp.where(sub == 0, rolled(face, 1, 0), gxl)) + (gy + gyl) + (above + below)
         after, before = rim_faces(sub, face, gx, u[:SUB], u[nx - SUB :], rims[z])
         r = rims[z] + rolled(after, 1, 0) - before
         r = jnp.where(first_lane | last_lane, beside(wr[zi * SUB : (zi + 1) * SUB], z, zs, RIM), r)
-        scaled = r * inverse
-        cxh[at] = gx
+        own_diag, own_q = own(diag_ref, z), own(q_ref, z)
+        long_at = slice(z * ext, (z + 1) * ext)
+        parts = []
+        for this_diag, this_r in (
+            (own_diag[:SUB] + jnp.where(sub == 0, gxl, 0.0), own_q[:SUB] + rolled(before, 1, 0)),
+            (own_diag[nx - SUB :] + face, own_q[nx - SUB :] - after),
+            (diag, r),
+        ):
+            inverse = 1.0 / this_diag
+            scaled = this_r * inverse
+            parts.append((inverse, scaled, scaled * (1.0 / THETA)))
+        inner = slice(z * (nx - 2 * SUB), (z + 1) * (nx - 2 * SUB))
+        middle = (inv_ref[inner], own_q[SUB : nx - SUB], v_ref[inner])
+        for ref, one, two, three, four in zip((inv, q, va), parts[0], middle, parts[1], parts[2]):
+            ref[long_at] = jnp.concatenate([one, two, three, four], axis=0)
+        own_cx = own(cx_ref, z)
+        cx[long_at] = jnp.concatenate([own_cx[: nx - SUB], own_cx[nx - SUB :] + face, gx], axis=0)
         cyh[at] = gy
         czh[at] = above
-        invh[at] = inverse
-        qh[at] = scaled
-        vh[at] = scaled * (1.0 / THETA)
         below = above
 
     lane = iota((ext, LANES), 1)
@@ -585,22 +611,18 @@
         return ref[z % nz * ext : (z % nz + 1) * ext]
 
     for k, w in enumerate((w0, w1, w2)):
-        old, new = (va, vb) if k % 2 else (vb, va)
+        old, new = (va, vb) if k % 2 == 0 else (vb, va)
         keep, lift = table[k]
-
-        def at_z(z, k=k, old=old):
-            return whole(v_ref, vh, z) if k == 0 else long(old, z)
-
         for z in range(nz):
             at, here = slice(z * ext, (z + 1) * ext), slice(z * nx, (z + 1) * nx)
             zi = z % zs
-            v, gx, gy = at_z(z), whole(cx_ref, cxh, z), whole(cy_ref, cyh, z)
+            v, gx, gy = old[at], cx[at], whole(cy_ref, cyh, z)
             edge = beside(w[zi * ext : (zi + 1) * ext], z, zs, RIM - 1)
             near = gx * rolled(v, -1, 0) + rolled(gx * v, 1, 0)
             near = near + gy * jnp.where(last_lane, edge, rolled(v, -1, 1))
             near = near + jnp.where(first_lane, edge, rolled(gy * v, 1, 1))
-            near = near + whole(cz_ref, czh, z) * at_z(z + 1) + whole(cz_ref, czh, z - 1) * at_z(z - 1)
-            scaled = (whole(q_ref, qh, z) if k == 0 else q[at]) - v + near * whole(inv_ref, invh, z)
+            near = near + whole(cz_ref, czh, z) * long(old, z + 1) + whole(cz_ref, czh, z - 1) * long(old, z - 1)
+            scaled = q[at] - v + near * inv[at]
             fresh = keep * v + lift * scaled
             total = (v[:nx] if k == 0 else acc[here]) + fresh[:nx]
             if k < SWEEPS - 1:
@@ -611,7 +633,7 @@
                 o_ref[here] = own(u_ref, z) + total
 
 
-def fine(strips, b2, b1, a1, a2, u, c, begun, nz, nx):
+def fine(strips, b2, b1, one, two, last, u, c, begun, nz, nx):
     zs = nz // ZS
     ext = nx + SUB
     rim = pltpu.VMEM((nz * SUB, LANES), f32)
@@ -620,13 +642,13 @@
     return pl.pallas_call(
         functools.partial(fine_kernel, nz=nz, nx=nx),
         out_shape=jax.ShapeDtypeStruct(u.shape, f32),
-        in_specs=[VMEM] * 13,
+        in_specs=[VMEM] * 15,
         out_specs=VMEM,
-        scratch_shapes=[rim] * 7 + [full] * 3 + [pltpu.VMEM(u.shape, f32), pltpu.VMEM((zs * SUB, LANES), f32)] + [strip] * 3,
+        scratch_shapes=[rim] * 3 + [full] * 5 + [pltpu.VMEM(u.shape, f32), pltpu.VMEM((zs * SUB, LANES), f32)] + [strip] * 3,
         compiler_params=SMALL,
         cost_estimate=pl.CostEstimate(flops=100 * u.size, bytes_accessed=40 * u.size, transcendentals=0),
         name="fine",
-    )(strips, b2, b1, a1, a2, u, c, *begun)
+    )(strips, b2, b1, one, two, last, u, c, *begun)
 
 
 def finish_kernel(x_ref, m_ref, r_ref, o_ref, *, nz, nx):
@@ -687,6 +709,9 @@
     def mate(x):
         return send(x, lambda i, j: (i + 1 if i % 2 == 0 else i - 1, j))
 
+    def shift(x, by):
+        return send(x, lambda i, j: (i + by, j))
+
     def far(x):
         return send(x, lambda i, j: (i - 1 if i % 2 == 0 else i + 1, j))
 
@@ -696,27 +721,28 @@
             return left, left
         return left, send(x, lambda i, j: (i, j - 1))
 
-    return mate, far, beside_y
+    return mate, far, shift, beside_y
 
 
 def body(iterate, source, conduct):
     nz, nx, ny = iterate.shape
     if nz != ZS * 4 or ny != LANES or nx != 3 * SUB or lax.axis_size("gx") % 2:
         raise ValueError("shapes")
-    mate, far, beside_y = moves()
+    mate, far, shift, beside_y = moves()
     u, s, c = (x.reshape(nz * nx, ny) for x in (iterate, source, conduct))
-    q, f1, a1, a2, r, own = pack(u, s, c, nz, nx)
+    q, f1, last, one, two, r, own = pack(u, s, c, nz, nx)
     ql, qr = beside_y(q)
     rf1 = mate(f1)
-    ra2 = far(a2)
-    ra1 = mate(a1)
-    b1, b2, strips = join(q, ql, qr, rf1, own, nz, nx)
+    before = shift(last, 1)
+    b1, b2, strips, kept = join(q, ql, qr, rf1, own, nz, nx)
     rb2 = far(b2)
     rb1 = mate(b1)
-    begun = begin(strips, ra1, ra2, u, c, r, nz, nx)
-    m = faces(own, b2, rb2, rb1, ra2, begun[0], nz, nx)
+    one, two, strips = lax.optimization_barrier((one, two, strips))
+    after = shift(one, -1), shift(two, -1)
+    begun = begin(strips, u, c, r, nz, nx)
+    m = faces(own, kept, rb2, rb1, begun[0], nz, nx)
     rm = mate(m)
-    x = fine(strips, rb2, rb1, ra1, ra2, u, c, begun, nz, nx)
+    x = fine(strips, rb2, rb1, *after, before, u, c, begun, nz, nx)
     return finish(x, m, rm, nz, nx).reshape(nz, nx, ny)
 
 

time: 21.9 us -> 20.1 us (0.918)
  waiting for transfers between devices: 5.34 us -> 2.49 us
  starting transfers between devices: 8.65 us -> 9.73 us
    ppermute x7 -> x8, waiting for transfers between devices: 5.34 us -> 2.49 us  [send(): return lax.ppermute(x, ('gx', 'gy'), pairs)]
    ppermute x7 -> x8, starting transfers between devices: 8.65 us -> 9.73 us  [send(): return lax.ppermute(x, ('gx', 'gy'), pairs)]
  transfers between devices with their start and end apart: 7 -> 8, of which waited for: 4 -> 4; matrix products, arithmetic and copies ran while one was open for 0% -> 0% of each run, Pallas kernels for 14% -> 18%
where the time goes in v5:
time: 20.1 us; the launch traced here: 19.9 us
  starting transfers between devices  9.73 us (48%)
  Pallas kernels  7.58 us (38%)
  waiting for transfers between devices  2.49 us (12%)
    ppermute x8, starting transfers between devices, send(): return lax.ppermute(x, ('gx', 'gy'), pairs)  9.73 us
    pallas_call x1, Pallas kernels, pack(): pl.pallas_call(functools.partial(pack_kernel, nz=nz, nx=nx), out_shape=(t...  2.79 us
    ppermute x8, waiting for transfers between devices, send(): return lax.ppermute(x, ('gx', 'gy'), pairs)  2.49 us
    pallas_call x1, Pallas kernels, fine(): pl.pallas_call(functools.partial(fine_kernel, nz=nz, nx=nx), out_shape=ja...  2.22 us
    pallas_call x1, Pallas kernels, finish(): pl.pallas_call(functools.partial(finish_kernel, nz=nz, nx=nx), out_shape=...  1.29 us
    pallas_call x1, Pallas kernels, begin(): pl.pallas_call(functools.partial(begin_kernel, nz=nz, nx=nx), out_shape=(...  0.58 us
  transfers between devices with their start and end apart: 8, of which 4 were waited for; matrix products, arithmetic and copies ran while one was open for 0% of the time, Pallas kernels for 18%

profile of v5, /device:TPU:0, one launch (start us, length us, event | category | flops | bytes accessed | tf_op | source)
XLA Modules:
  0.0 19.9 jit_solution(10606667641341885332)
XLA Ops:
  0.0 0.0 copy-start.1
  0.0 2.8 %pack.1 = (f32[216,128]{1,0:T(8,128)S(1)}, f32[72,128]{1,0:T(8,128)S(1)}, f32[256,128]{1,0:T(8,128)S(1)}, f32[128,128]{1,0:T(8,128)S(1)}, f32[128,128]{1,0:T(8,1...) custom-call(f32[768,128]{1,0:T(8,128)} %bitcast.4, f32[768,128]{1,0:T(8,128)} %bitcast.10, f32[768,128]{1,0:T(8,128)} %bitcast.7), custom_call_target="tpu_custom_call" | custom-call | tf_op jit(solution)/shard_map/pack/pallas_call | solution.py:195
  2.8 0.0 copy-start
  2.8 3.0 %collective-permute-start = (f32[216,128]{1,0:T(8,128)S(1)}, f32[216,128]{1,0:T(8,128)S(1)}, u32[]{:S(2)}, u32[]{:S(2)}) collective-permute-start(f32[216,128]{1,0:T(8,128)S(1)} %get-tuple-element.28.q_ref), channel_id=1, source_target_pairs={{0,1},{1,0},{2,3},{3,2},{4,5},{5,4},{6,7},{7,6},{8,9},{9,8},{10,11... | collective-permute-start | bytes 331784 | tf_op jit(solution)/shard_map/ppermute | solution.py:707
  5.8 0.0 collective-permute-start.6
  5.8 1.6 %collective-permute-start.1 = (f32[72,128]{1,0:T(8,128)S(1)}, f32[72,128]{1,0:T(8,128)S(1)}, u32[]{:S(2)}, u32[]{:S(2)}) collective-permute-start(f32[72,128]{1,0:T(8,128)S(1)} %get-tuple-element.29), channel_id=1, source_target_pairs={{0,2},{1,3},{2,0},{3,1},{4,6},{5,7},{6,4},{7,5},{8,10},{9,11},{10,... | collective-permute-start | bytes 110600 | tf_op jit(solution)/shard_map/ppermute | solution.py:707
  7.5 0.9 %collective-permute-done.1.f1_ref = f32[72,128]{1,0:T(8,128)S(1)} collective-permute-done((f32[72,128]{1,0:T(8,128)S(1)}, f32[72,128]{1,0:T(8,128)S(1)}, u32[]{:S(2)}, u32[]{:S(2)}) %collective-permute-start.1) | collective-permute-done | bytes 36896 | tf_op jit(solution)/shard_map/ppermute | solution.py:707
  8.3 0.6 %collective-permute-done.ql_ref.qr_ref = f32[216,128]{1,0:T(8,128)S(1)} collective-permute-done((f32[216,128]{1,0:T(8,128)S(1)}, f32[216,128]{1,0:T(8,128)S(1)}, u32[]{:S(2)}, u32[]{:S(2)}) %collective-permute-start) | collective-permute-done | bytes 110624 | tf_op jit(solution)/shard_map/ppermute | solution.py:707
  8.9 0.3 %join.1 = (f32[88,128]{1,0:T(8,128)S(1)}, f32[160,128]{1,0:T(8,128)S(1)}, f32[288,128]{1,0:T(8,128)S(1)}, f32[80,128]{1,0:T(8,128)S(1)}) custom-call(f32[216,128]{1,0:T(8,128)S(1)} %get-tuple-element.28.q_ref, f32[216,128]{1,0:T(8,128)S(1)} %collective-permute-done.ql_ref.qr_ref, f32[216,128]{1,0:T(8,128)S(1)} %collective-permute-done.ql_ref.qr_ref, ...), custom_call_target="tpu_custom_call" | custom-call | tf_op jit(solution)/shard_map/join/pallas_call | solution.py:303
  9.2 3.4 %collective-permute-start.2 = (f32[160,128]{1,0:T(8,128)S(1)}, f32[160,128]{1,0:T(8,128)S(1)}, u32[]{:S(2)}, u32[]{:S(2)}) collective-permute-start(f32[160,128]{1,0:T(8,128)S(1)} %get-tuple-element.33), channel_id=1, source_target_pairs={{0,30},{1,31},{2,4},{3,5},{4,2},{5,3},{6,8},{7,9},{8,6},{9,7},{10,... | collective-permute-start | bytes 245768 | tf_op jit(solution)/shard_map/ppermute | solution.py:707
  12.6 1.1 %collective-permute-start.4 = (f32[128,128]{1,0:T(8,128)S(1)}, f32[128,128]{1,0:T(8,128)S(1)}, u32[]{:S(2)}, u32[]{:S(2)}) collective-permute-start(f32[128,128]{1,0:T(8,128)S(1)} %get-tuple-element.35), channel_id=1, source_target_pairs={{0,30},{1,31},{2,0},{3,1},{4,2},{5,3},{6,4},{7,5},{8,6},{9,7},{10,... | collective-permute-start | bytes 196616 | tf_op jit(solution)/shard_map/ppermute | solution.py:707
  13.7 0.5 %collective-permute-start.5 = (f32[128,128]{1,0:T(8,128)S(1)}, f32[128,128]{1,0:T(8,128)S(1)}, u32[]{:S(2)}, u32[]{:S(2)}) collective-permute-start(f32[128,128]{1,0:T(8,128)S(1)} %get-tuple-element.36), channel_id=1, source_target_pairs={{0,30},{1,31},{2,0},{3,1},{4,2},{5,3},{6,4},{7,5},{8,6},{9,7},{10,... | collective-permute-start | bytes 196616 | tf_op jit(solution)/shard_map/ppermute | solution.py:707
  14.2 0.0 collective-permute-start.3
  14.3 0.0 copy-done.1
  14.3 0.0 copy-done
  14.3 0.6 %begin.1 = (f32[768,128]{1,0:T(8,128)S(1)}, f32[768,128]{1,0:T(8,128)S(1)}, f32[768,128]{1,0:T(8,128)S(1)}, f32[768,128]{1,0:T(8,128)S(1)}, f32[256,128]{1,0:T(8...) custom-call(f32[288,128]{1,0:T(8,128)S(1)} %get-tuple-element.32.strip_ref, f32[768,128]{1,0:T(8,128)S(1)} %bitcast.5, ...), custom_call_target="tpu_custom_call" | custom-call | flops 3932160 | bytes 3932160 | tf_op jit(solution)/shard_map/begin/pallas_call | solution.py:474
  14.8 0.6 %collective-permute-done.3.b1_ref.r1_ref = f32[88,128]{1,0:T(8,128)S(1)} collective-permute-done((f32[88,128]{1,0:T(8,128)S(1)}, f32[88,128]{1,0:T(8,128)S(1)}, u32[]{:S(2)}, u32[]{:S(2)}) %collective-permute-start.3) | collective-permute-done | bytes 45088 | tf_op jit(solution)/shard_map/ppermute | solution.py:707
  15.5 0.4 %collective-permute-done.2.b2_ref.r2_ref = f32[160,128]{1,0:T(8,128)S(1)} collective-permute-done((f32[160,128]{1,0:T(8,128)S(1)}, f32[160,128]{1,0:T(8,128)S(1)}, u32[]{:S(2)}, u32[]{:S(2)}) %collective-permute-start.2) | collective-permute-done | bytes 81952 | tf_op jit(solution)/shard_map/ppermute | solution.py:707
  15.9 0.4 %faces.1.m_ref = f32[24,128]{1,0:T(8,128)S(1)} custom-call(f32[128,128]{1,0:T(8,128)S(1)} %get-tuple-element.30.own_ref, f32[80,128]{1,0:T(8,128)S(1)} %get-tuple-element.46.kept_ref, f32[160,128]{1,0:T(8,128)S(1)} %collective-permute-done.2.b2_ref.r2_ref, f32[88,128]{1,0:T(8,128)S(1)} %collective-permute-done.3.b1_ref.r1_ref, ...), custom_call_target="tpu_custom_call" | custom-call | tf_op jit(solution)/shard_map/faces/pallas_call | solution.py:385
  16.3 0.1 collective-permute-start.7
  16.3 0.0 collective-permute-done.6.last_ref
  16.3 0.0 collective-permute-done.4.one_ref
  16.4 0.0 collective-permute-done.5.two_ref
  16.4 2.2 %fine.1.x_ref = f32[768,128]{1,0:T(8,128)S(1)} custom-call(f32[288,128]{1,0:T(8,128)S(1)} %get-tuple-element.32.strip_ref, f32[160,128]{1,0:T(8,128)S(1)} %collective-permute-done.2.b2_ref.r2_ref, f32[88,128]{1,0:T(8,128)S(1)} %collective-permute-done.3.b1_ref.r1_ref, f32[128,128]{1,0:T(8,128)S(1)} %collective-permute-done.4.one_ref, ...), custom_call_target="tpu_custom_call" | custom-call | flops 9830400 | bytes 3932160 | tf_op jit(solution)/shard_map/fine/pallas_call | solution.py:642
  18.6 0.0 collective-permute-done.7.r_ref
  18.6 1.3 %finish.1 = f32[768,128]{1,0:T(8,128)} custom-call(f32[768,128]{1,0:T(8,128)S(1)} %fine.1.x_ref, f32[24,128]{1,0:T(8,128)S(1)} %faces.1.m_ref, f32[24,128]{1,0:T(8,128)S(1)} %collective-permute-done.7.r_ref), custom_call_target="tpu_custom_call" | custom-call | tf_op jit(solution)/shard_map/finish/pallas_call | solution.py:688
Async XLA Ops:
  0.0 14.3 %copy-start.1 = (f32[32,24,128]{2,1,0:T(8,128)S(1)}, f32[32,24,128]{2,1,0:T(8,128)}, u32[]{:S(2)}) copy-start(f32[32,24,128]{2,1,0:T(8,128)} %param.5) | copy-start | bytes 1179652
  2.8 11.5 %copy-start = (f32[32,24,128]{2,1,0:T(8,128)S(1)}, f32[32,24,128]{2,1,0:T(8,128)}, u32[]{:S(2)}) copy-start(f32[32,24,128]{2,1,0:T(8,128)} %param.3) | copy-start | bytes 1179652
  2.8 6.1 %collective-permute-start = (f32[216,128]{1,0:T(8,128)S(1)}, f32[216,128]{1,0:T(8,128)S(1)}, u32[]{:S(2)}, u32[]{:S(2)}) collective-permute-start(f32[216,128]{1,0:T(8,128)S(1)} %get-tuple-element.28.q_ref), channel_id=1, source_target_pairs={{0,1},{1,0},{2,3},{3,2},{4,5},{5,4},{6,7},{7,6},{8,9},{9,8},{10,11... | collective-permute-start | bytes 331784 | tf_op jit(solution)/shard_map/ppermute | solution.py:707
  5.8 10.5 %collective-permute-start.6 = (f32[256,128]{1,0:T(8,128)S(1)}, f32[256,128]{1,0:T(8,128)S(1)}, u32[]{:S(2)}, u32[]{:S(2)}) collective-permute-start(f32[256,128]{1,0:T(8,128)S(1)} %get-tuple-element.37), channel_id=1, source_target_pairs={{0,2},{1,3},{2,4},{3,5},{4,6},{5,7},{6,8},{7,9},{8,10},{9,11},{10,... | collective-permute-start | bytes 393224 | tf_op jit(solution)/shard_map/ppermute | solution.py:707
  5.8 2.5 %collective-permute-start.1 = (f32[72,128]{1,0:T(8,128)S(1)}, f32[72,128]{1,0:T(8,128)S(1)}, u32[]{:S(2)}, u32[]{:S(2)}) collective-permute-start(f32[72,128]{1,0:T(8,128)S(1)} %get-tuple-element.29), channel_id=1, source_target_pairs={{0,2},{1,3},{2,0},{3,1},{4,6},{5,7},{6,4},{7,5},{8,10},{9,11},{10,... | collective-permute-start | bytes 110600 | tf_op jit(solution)/shard_map/ppermute | solution.py:707
  9.2 6.6 %collective-permute-start.2 = (f32[160,128]{1,0:T(8,128)S(1)}, f32[160,128]{1,0:T(8,128)S(1)}, u32[]{:S(2)}, u32[]{:S(2)}) collective-permute-start(f32[160,128]{1,0:T(8,128)S(1)} %get-tuple-element.33), channel_id=1, source_target_pairs={{0,30},{1,31},{2,4},{3,5},{4,2},{5,3},{6,8},{7,9},{8,6},{9,7},{10,... | collective-permute-start | bytes 245768 | tf_op jit(solution)/shard_map/ppermute | solution.py:707
  12.6 3.7 %collective-permute-start.4 = (f32[128,128]{1,0:T(8,128)S(1)}, f32[128,128]{1,0:T(8,128)S(1)}, u32[]{:S(2)}, u32[]{:S(2)}) collective-permute-start(f32[128,128]{1,0:T(8,128)S(1)} %get-tuple-element.35), channel_id=1, source_target_pairs={{0,30},{1,31},{2,0},{3,1},{4,2},{5,3},{6,4},{7,5},{8,6},{9,7},{10,... | collective-permute-start | bytes 196616 | tf_op jit(solution)/shard_map/ppermute | solution.py:707
  13.7 2.6 %collective-permute-start.5 = (f32[128,128]{1,0:T(8,128)S(1)}, f32[128,128]{1,0:T(8,128)S(1)}, u32[]{:S(2)}, u32[]{:S(2)}) collective-permute-start(f32[128,128]{1,0:T(8,128)S(1)} %get-tuple-element.36), channel_id=1, source_target_pairs={{0,30},{1,31},{2,0},{3,1},{4,2},{5,3},{6,4},{7,5},{8,6},{9,7},{10,... | collective-permute-start | bytes 196616 | tf_op jit(solution)/shard_map/ppermute | solution.py:707
  14.2 1.2 %collective-permute-start.3 = (f32[88,128]{1,0:T(8,128)S(1)}, f32[88,128]{1,0:T(8,128)S(1)}, u32[]{:S(2)}, u32[]{:S(2)}) collective-permute-start(f32[88,128]{1,0:T(8,128)S(1)} %get-tuple-element.34), channel_id=1, source_target_pairs={{0,2},{1,3},{2,0},{3,1},{4,6},{5,7},{6,4},{7,5},{8,10},{9,11},{10,... | collective-permute-start | bytes 135176 | tf_op jit(solution)/shard_map/ppermute | solution.py:707
  16.3 2.3 %collective-permute-start.7 = (f32[24,128]{1,0:T(8,128)S(1)}, f32[24,128]{1,0:T(8,128)S(1)}, u32[]{:S(2)}, u32[]{:S(2)}) collective-permute-start(f32[24,128]{1,0:T(8,128)S(1)} %faces.1.m_ref), channel_id=1, source_target_pairs={{0,2},{1,3},{2,0},{3,1},{4,6},{5,7},{6,4},{7,5},{8,10},{9,11},{10,... | collective-permute-start | bytes 36872 | tf_op jit(solution)/shard_map/ppermute | solution.py:707

commit v6 on v5

--- a/solution.py
+++ b/solution.py
@@ -107,7 +107,7 @@
 
 
 def pack_kernel(
-    u_hbm, s_hbm, c_hbm, q_ref, f1_ref, last_ref, one_ref, two_ref, r_ref, own_ref, u_ref, s_ref, c_ref, sems, *, nz, nx
+    u_hbm, s_hbm, c_hbm, q_ref, f1_ref, last_ref, one_ref, two_ref, r_ref, own_ref, u_ref, s_ref, c_ref, sums_ref, sems, *, nz, nx
 ):
     pieces = sems.shape[1]
     size = nz * nx // pieces
@@ -133,7 +133,10 @@
     def up(z):
         return 0.5 * (plane(c_ref, z) + plane(c_ref, z + 1)) * (plane(u_ref, z) - plane(u_ref, z + 1))
 
-    coarse = jnp.zeros((SUB, LANES), f32)
+    for z in range(nz):
+        u, c = plane(u_ref, z), plane(c_ref, z)
+        fy = 0.5 * (c + rolled(c, -1, 1)) * (u - rolled(u, -1, 1))
+        r_ref[z * nx : (z + 1) * nx] = jnp.where(wide == LANES - 1, 0.0, fy)
     below = up(nz - 1)
     for Z in range(nz // COARSEN):
         sum_r = sum_c = jnp.zeros((nx, LANES), f32)
@@ -141,9 +144,8 @@
             u, c = plane(u_ref, z), plane(c_ref, z)
             above = up(z)
             fx = 0.5 * (c + rolled(c, -1, 0)) * (u - rolled(u, -1, 0))
-            fy = 0.5 * (c + rolled(c, -1, 1)) * (u - rolled(u, -1, 1))
+            fy = plane(r_ref, z)
             fx = jnp.where(row == nx - 1, 0.0, fx)
-            fy = jnp.where(wide == LANES - 1, 0.0, fy)
             r = plane(s_ref, z) - SHIFT * u - (fx - rolled(fx, 1, 0)) - (fy - rolled(fy, 1, 1)) - (above - below)
             below = above
             r_ref[z * nx : (z + 1) * nx] = r
@@ -155,8 +157,8 @@
             last_ref[z * SUB : (z + 1) * SUB] = last
             to = z % (nz // 2) * SUB
             (one_ref if z < nz // 2 else two_ref)[to : to + SUB] = first
-        coarse = coarse + compact(block_rows(sum_r) + rolled(block_rows(sum_c), RIM, 0), Z)
-    coarse = coarse * (1.0 / CELLS)
+        sums_ref[Z * nx : (Z + 1) * nx] = sum_r
+        sums_ref[(Z + nz // COARSEN) * nx : (Z + nz // COARSEN + 1) * nx] = sum_c
 
     zs = nz // ZS
     half = zs // 2
@@ -171,22 +173,31 @@
                         strip = jnp.where(slot == at, moved, strip)
                 q_ref[(a * half + pair) * nx : (a * half + pair + 1) * nx] = strip
 
-    section(strips)
-
-    base = 3 * half * nx
-    for a, ref in enumerate((u_ref, c_ref)):
-        for Z in range(nz // SUB):
-            at = Z * SUB * nx
-            first, last = picked(ref, at, nx), picked(ref, at + nx - 1, nx)
-            spot = a * nz + Z * SUB
-            own_ref[spot : spot + SUB] = first
-            own_ref[2 * nz + spot : 2 * nz + spot + SUB] = last
-            f1_ref[spot : spot + SUB] = jnp.where(even, last, first)
-            q_ref[base + spot : base + spot + SUB] = jnp.where(
-                lane < HALF, rolled(first, REACH, 1), rolled(last, REACH + HALF, 1)
-            )
-    q_ref[base + 2 * nz : base + 2 * nz + SUB] = coarse
-    f1_ref[2 * nz :] = coarse
+    def finish():
+        coarse = jnp.zeros((SUB, LANES), f32)
+        planes = nz // COARSEN
+        for Z in range(planes):
+            sum_r, sum_c = (sums_ref[(Z + k * planes) * nx : (Z + k * planes + 1) * nx] for k in range(2))
+            coarse = coarse + compact(block_rows(sum_r) + rolled(block_rows(sum_c), RIM, 0), Z)
+        coarse = coarse * (1.0 / CELLS)
+        strips()
+
+        base = 3 * half * nx
+        for a, ref in enumerate((u_ref, c_ref)):
+            for Z in range(nz // SUB):
+                at = Z * SUB * nx
+                first, last = picked(ref, at, nx), picked(ref, at + nx - 1, nx)
+                spot = a * nz + Z * SUB
+                own_ref[spot : spot + SUB] = first
+                own_ref[2 * nz + spot : 2 * nz + spot + SUB] = last
+                f1_ref[spot : spot + SUB] = jnp.where(even, last, first)
+                q_ref[base + spot : base + spot + SUB] = jnp.where(
+                    lane < HALF, rolled(first, REACH, 1), rolled(last, REACH + HALF, 1)
+                )
+        q_ref[base + 2 * nz : base + 2 * nz + SUB] = coarse
+        f1_ref[2 * nz :] = coarse
+
+    section(finish)
 
 
 def pack(u, s, c, nz, nx):
@@ -205,7 +216,8 @@
         ),
         in_specs=[pl.BlockSpec(memory_space=pltpu.HBM)] * 3,
         out_specs=(VMEM,) * 7,
-        scratch_shapes=[pltpu.VMEM(u.shape, f32)] * 3 + [pltpu.SemaphoreType.DMA((3, pieces))],
+        scratch_shapes=[pltpu.VMEM(u.shape, f32)] * 3
+        + [pltpu.VMEM((2 * nz // COARSEN * nx, LANES), f32), pltpu.SemaphoreType.DMA((3, pieces))],
         compiler_params=SMALL,
         name="pack",
     )(*(pltpu.with_memory_space_constraint(x, pltpu.HBM) for x in (u, s, c)))
@@ -663,16 +675,14 @@
         fields.append(jnp.concatenate([jnp.where(beyond, mate, mine), mate], axis=0))
     start, weight, cond = fields
     scale = 0.5 / COARSEN**2
-    gx = scale * (cond + rolled(cond, -1, 0))
-    gy = scale * (cond + rolled(cond, -1, 1))
-    gz = scale * (cond + rolled(cond, -SPREAD, 1))
+    turns = (-1, 0), (1, 0), (-1, 1), (1, 1), (-SPREAD, 1), (SPREAD, 1)
+    shares = [scale * (cond + rolled(cond, *turn)) for turn in turns]
+    keep = 1.0 - weight * (SHIFT + sum(shares))
+    shares = [weight * share for share in shares]
     v = start
     for _ in range(COARSE_SWEEPS - 1):
-        fx = gx * (v - rolled(v, -1, 0))
-        fy = gy * (v - rolled(v, -1, 1))
-        fz = gz * (v - rolled(v, -SPREAD, 1))
-        image = SHIFT * v + (fx - rolled(fx, 1, 0)) + (fy - rolled(fy, 1, 1)) + (fz - rolled(fz, SPREAD, 1))
-        v = v + start - weight * image
+        terms = [share * rolled(v, *turn) for share, turn in zip(shares, turns)]
+        v = (start + keep * v) + ((terms[0] + terms[1]) + (terms[2] + terms[3]) + (terms[4] + terms[5]))
     top = v[:SUB]
     top = jnp.where(even, rolled(top, -rows - 1, 0), rolled(top, -1, 0))
     for Z in range(nz // COARSEN):

time: 20.1 us -> 19.5 us (0.970)
  Pallas kernels: 7.58 us -> 7.07 us
    pallas_call x1, Pallas kernels: 2.79 us -> 2.47 us  [pack(): pl.pallas_call(functools.partial(pack_kernel, nz=nz, nx=nx), out_shape=(t...]
where the time goes in v6:
time: 19.5 us; the launch traced here: 19.4 us
  starting transfers between devices  9.73 us (50%)
  Pallas kernels  7.07 us (36%)
  waiting for transfers between devices  2.49 us (13%)
    ppermute x8, starting transfers between devices, send(): return lax.ppermute(x, ('gx', 'gy'), pairs)  9.73 us
    ppermute x8, waiting for transfers between devices, send(): return lax.ppermute(x, ('gx', 'gy'), pairs)  2.49 us
    pallas_call x1, Pallas kernels, pack(): pl.pallas_call(functools.partial(pack_kernel, nz=nz, nx=nx), out_shape=(t...  2.47 us
    pallas_call x1, Pallas kernels, fine(): pl.pallas_call(functools.partial(fine_kernel, nz=nz, nx=nx), out_shape=ja...  2.22 us
    pallas_call x1, Pallas kernels, finish(): pl.pallas_call(functools.partial(finish_kernel, nz=nz, nx=nx), out_shape=...  1.09 us
    pallas_call x1, Pallas kernels, begin(): pl.pallas_call(functools.partial(begin_kernel, nz=nz, nx=nx), out_shape=(...  0.58 us
  transfers between devices with their start and end apart: 8, of which 4 were waited for; matrix products, arithmetic and copies ran while one was open for 0% of the time, Pallas kernels for 18%

profile of v6, /device:TPU:0, one launch (start us, length us, event | category | flops | bytes accessed | tf_op | source)
XLA Modules:
  0.0 19.4 jit_solution(5295205316552070877)
XLA Ops:
  0.0 0.0 copy-start.1
  0.0 2.5 %pack.1 = (f32[216,128]{1,0:T(8,128)S(1)}, f32[72,128]{1,0:T(8,128)S(1)}, f32[256,128]{1,0:T(8,128)S(1)}, f32[128,128]{1,0:T(8,128)S(1)}, f32[128,128]{1,0:T(8,1...) custom-call(f32[768,128]{1,0:T(8,128)} %bitcast.4, f32[768,128]{1,0:T(8,128)} %bitcast.10, f32[768,128]{1,0:T(8,128)} %bitcast.7), custom_call_target="tpu_custom_call" | custom-call | tf_op jit(solution)/shard_map/pack/pallas_call | solution.py:206
  2.5 0.0 copy-start
  2.5 3.0 %collective-permute-start = (f32[216,128]{1,0:T(8,128)S(1)}, f32[216,128]{1,0:T(8,128)S(1)}, u32[]{:S(2)}, u32[]{:S(2)}) collective-permute-start(f32[216,128]{1,0:T(8,128)S(1)} %get-tuple-element.28.q_ref), channel_id=1, source_target_pairs={{0,1},{1,0},{2,3},{3,2},{4,5},{5,4},{6,7},{7,6},{8,9},{9,8},{10,11... | collective-permute-start | bytes 331784 | tf_op jit(solution)/shard_map/ppermute | solution.py:717
  5.5 0.0 collective-permute-start.6
  5.5 1.6 %collective-permute-start.1 = (f32[72,128]{1,0:T(8,128)S(1)}, f32[72,128]{1,0:T(8,128)S(1)}, u32[]{:S(2)}, u32[]{:S(2)}) collective-permute-start(f32[72,128]{1,0:T(8,128)S(1)} %get-tuple-element.29), channel_id=1, source_target_pairs={{0,2},{1,3},{2,0},{3,1},{4,6},{5,7},{6,4},{7,5},{8,10},{9,11},{10,... | collective-permute-start | bytes 110600 | tf_op jit(solution)/shard_map/ppermute | solution.py:717
  7.1 0.9 %collective-permute-done.1.f1_ref = f32[72,128]{1,0:T(8,128)S(1)} collective-permute-done((f32[72,128]{1,0:T(8,128)S(1)}, f32[72,128]{1,0:T(8,128)S(1)}, u32[]{:S(2)}, u32[]{:S(2)}) %collective-permute-start.1) | collective-permute-done | bytes 36896 | tf_op jit(solution)/shard_map/ppermute | solution.py:717
  8.0 0.6 %collective-permute-done.ql_ref.qr_ref = f32[216,128]{1,0:T(8,128)S(1)} collective-permute-done((f32[216,128]{1,0:T(8,128)S(1)}, f32[216,128]{1,0:T(8,128)S(1)}, u32[]{:S(2)}, u32[]{:S(2)}) %collective-permute-start) | collective-permute-done | bytes 110624 | tf_op jit(solution)/shard_map/ppermute | solution.py:717
  8.6 0.3 %join.1 = (f32[88,128]{1,0:T(8,128)S(1)}, f32[160,128]{1,0:T(8,128)S(1)}, f32[288,128]{1,0:T(8,128)S(1)}, f32[80,128]{1,0:T(8,128)S(1)}) custom-call(f32[216,128]{1,0:T(8,128)S(1)} %get-tuple-element.28.q_ref, f32[216,128]{1,0:T(8,128)S(1)} %collective-permute-done.ql_ref.qr_ref, f32[216,128]{1,0:T(8,128)S(1)} %collective-permute-done.ql_ref.qr_ref, ...), custom_call_target="tpu_custom_call" | custom-call | tf_op jit(solution)/shard_map/join/pallas_call | solution.py:315
  8.9 3.4 %collective-permute-start.2 = (f32[160,128]{1,0:T(8,128)S(1)}, f32[160,128]{1,0:T(8,128)S(1)}, u32[]{:S(2)}, u32[]{:S(2)}) collective-permute-start(f32[160,128]{1,0:T(8,128)S(1)} %get-tuple-element.33), channel_id=1, source_target_pairs={{0,30},{1,31},{2,4},{3,5},{4,2},{5,3},{6,8},{7,9},{8,6},{9,7},{10,... | collective-permute-start | bytes 245768 | tf_op jit(solution)/shard_map/ppermute | solution.py:717
  12.3 1.1 %collective-permute-start.4 = (f32[128,128]{1,0:T(8,128)S(1)}, f32[128,128]{1,0:T(8,128)S(1)}, u32[]{:S(2)}, u32[]{:S(2)}) collective-permute-start(f32[128,128]{1,0:T(8,128)S(1)} %get-tuple-element.35), channel_id=1, source_target_pairs={{0,30},{1,31},{2,0},{3,1},{4,2},{5,3},{6,4},{7,5},{8,6},{9,7},{10,... | collective-permute-start | bytes 196616 | tf_op jit(solution)/shard_map/ppermute | solution.py:717
  13.4 0.5 %collective-permute-start.5 = (f32[128,128]{1,0:T(8,128)S(1)}, f32[128,128]{1,0:T(8,128)S(1)}, u32[]{:S(2)}, u32[]{:S(2)}) collective-permute-start(f32[128,128]{1,0:T(8,128)S(1)} %get-tuple-element.36), channel_id=1, source_target_pairs={{0,30},{1,31},{2,0},{3,1},{4,2},{5,3},{6,4},{7,5},{8,6},{9,7},{10,... | collective-permute-start | bytes 196616 | tf_op jit(solution)/shard_map/ppermute | solution.py:717
  13.9 0.0 collective-permute-start.3
  13.9 0.0 copy-done.1
  13.9 0.0 copy-done
  13.9 0.6 %begin.1 = (f32[768,128]{1,0:T(8,128)S(1)}, f32[768,128]{1,0:T(8,128)S(1)}, f32[768,128]{1,0:T(8,128)S(1)}, f32[768,128]{1,0:T(8,128)S(1)}, f32[256,128]{1,0:T(8...) custom-call(f32[288,128]{1,0:T(8,128)S(1)} %get-tuple-element.32.strip_ref, f32[768,128]{1,0:T(8,128)S(1)} %bitcast.5, ...), custom_call_target="tpu_custom_call" | custom-call | flops 3932160 | bytes 3932160 | tf_op jit(solution)/shard_map/begin/pallas_call | solution.py:486
  14.5 0.6 %collective-permute-done.3.b1_ref.r1_ref = f32[88,128]{1,0:T(8,128)S(1)} collective-permute-done((f32[88,128]{1,0:T(8,128)S(1)}, f32[88,128]{1,0:T(8,128)S(1)}, u32[]{:S(2)}, u32[]{:S(2)}) %collective-permute-start.3) | collective-permute-done | bytes 45088 | tf_op jit(solution)/shard_map/ppermute | solution.py:717
  15.1 0.4 %collective-permute-done.2.b2_ref.r2_ref = f32[160,128]{1,0:T(8,128)S(1)} collective-permute-done((f32[160,128]{1,0:T(8,128)S(1)}, f32[160,128]{1,0:T(8,128)S(1)}, u32[]{:S(2)}, u32[]{:S(2)}) %collective-permute-start.2) | collective-permute-done | bytes 81952 | tf_op jit(solution)/shard_map/ppermute | solution.py:717
  15.6 0.4 %faces.1.m_ref = f32[24,128]{1,0:T(8,128)S(1)} custom-call(f32[128,128]{1,0:T(8,128)S(1)} %get-tuple-element.30.own_ref, f32[80,128]{1,0:T(8,128)S(1)} %get-tuple-element.46.kept_ref, f32[160,128]{1,0:T(8,128)S(1)} %collective-permute-done.2.b2_ref.r2_ref, f32[88,128]{1,0:T(8,128)S(1)} %collective-permute-done.3.b1_ref.r1_ref, ...), custom_call_target="tpu_custom_call" | custom-call | tf_op jit(solution)/shard_map/faces/pallas_call | solution.py:397
  15.9 0.1 collective-permute-start.7
  16.0 0.0 collective-permute-done.6.last_ref
  16.0 0.0 collective-permute-done.4.one_ref
  16.0 0.0 collective-permute-done.5.two_ref
  16.0 2.2 %fine.1.x_ref = f32[768,128]{1,0:T(8,128)S(1)} custom-call(f32[288,128]{1,0:T(8,128)S(1)} %get-tuple-element.32.strip_ref, f32[160,128]{1,0:T(8,128)S(1)} %collective-permute-done.2.b2_ref.r2_ref, f32[88,128]{1,0:T(8,128)S(1)} %collective-permute-done.3.b1_ref.r1_ref, f32[128,128]{1,0:T(8,128)S(1)} %collective-permute-done.4.one_ref, ...), custom_call_target="tpu_custom_call" | custom-call | flops 9830400 | bytes 3932160 | tf_op jit(solution)/shard_map/fine/pallas_call | solution.py:654
  18.3 0.0 collective-permute-done.7.r_ref
  18.3 1.1 %finish.1 = f32[768,128]{1,0:T(8,128)} custom-call(f32[768,128]{1,0:T(8,128)S(1)} %fine.1.x_ref, f32[24,128]{1,0:T(8,128)S(1)} %faces.1.m_ref, f32[24,128]{1,0:T(8,128)S(1)} %collective-permute-done.7.r_ref), custom_call_target="tpu_custom_call" | custom-call | tf_op jit(solution)/shard_map/finish/pallas_call | solution.py:698
Async XLA Ops:
  0.0 13.9 %copy-start.1 = (f32[32,24,128]{2,1,0:T(8,128)S(1)}, f32[32,24,128]{2,1,0:T(8,128)}, u32[]{:S(2)}) copy-start(f32[32,24,128]{2,1,0:T(8,128)} %param.5) | copy-start | bytes 1179652
  2.5 11.5 %copy-start = (f32[32,24,128]{2,1,0:T(8,128)S(1)}, f32[32,24,128]{2,1,0:T(8,128)}, u32[]{:S(2)}) copy-start(f32[32,24,128]{2,1,0:T(8,128)} %param.3) | copy-start | bytes 1179652
  2.5 6.1 %collective-permute-start = (f32[216,128]{1,0:T(8,128)S(1)}, f32[216,128]{1,0:T(8,128)S(1)}, u32[]{:S(2)}, u32[]{:S(2)}) collective-permute-start(f32[216,128]{1,0:T(8,128)S(1)} %get-tuple-element.28.q_ref), channel_id=1, source_target_pairs={{0,1},{1,0},{2,3},{3,2},{4,5},{5,4},{6,7},{7,6},{8,9},{9,8},{10,11... | collective-permute-start | bytes 331784 | tf_op jit(solution)/shard_map/ppermute | solution.py:717
  5.5 10.5 %collective-permute-start.6 = (f32[256,128]{1,0:T(8,128)S(1)}, f32[256,128]{1,0:T(8,128)S(1)}, u32[]{:S(2)}, u32[]{:S(2)}) collective-permute-start(f32[256,128]{1,0:T(8,128)S(1)} %get-tuple-element.37), channel_id=1, source_target_pairs={{0,2},{1,3},{2,4},{3,5},{4,6},{5,7},{6,8},{7,9},{8,10},{9,11},{10,... | collective-permute-start | bytes 393224 | tf_op jit(solution)/shard_map/ppermute | solution.py:717
  5.5 2.5 %collective-permute-start.1 = (f32[72,128]{1,0:T(8,128)S(1)}, f32[72,128]{1,0:T(8,128)S(1)}, u32[]{:S(2)}, u32[]{:S(2)}) collective-permute-start(f32[72,128]{1,0:T(8,128)S(1)} %get-tuple-element.29), channel_id=1, source_target_pairs={{0,2},{1,3},{2,0},{3,1},{4,6},{5,7},{6,4},{7,5},{8,10},{9,11},{10,... | collective-permute-start | bytes 110600 | tf_op jit(solution)/shard_map/ppermute | solution.py:717
  8.9 6.6 %collective-permute-start.2 = (f32[160,128]{1,0:T(8,128)S(1)}, f32[160,128]{1,0:T(8,128)S(1)}, u32[]{:S(2)}, u32[]{:S(2)}) collective-permute-start(f32[160,128]{1,0:T(8,128)S(1)} %get-tuple-element.33), channel_id=1, source_target_pairs={{0,30},{1,31},{2,4},{3,5},{4,2},{5,3},{6,8},{7,9},{8,6},{9,7},{10,... | collective-permute-start | bytes 245768 | tf_op jit(solution)/shard_map/ppermute | solution.py:717
  12.3 3.7 %collective-permute-start.4 = (f32[128,128]{1,0:T(8,128)S(1)}, f32[128,128]{1,0:T(8,128)S(1)}, u32[]{:S(2)}, u32[]{:S(2)}) collective-permute-start(f32[128,128]{1,0:T(8,128)S(1)} %get-tuple-element.35), channel_id=1, source_target_pairs={{0,30},{1,31},{2,0},{3,1},{4,2},{5,3},{6,4},{7,5},{8,6},{9,7},{10,... | collective-permute-start | bytes 196616 | tf_op jit(solution)/shard_map/ppermute | solution.py:717
  13.4 2.6 %collective-permute-start.5 = (f32[128,128]{1,0:T(8,128)S(1)}, f32[128,128]{1,0:T(8,128)S(1)}, u32[]{:S(2)}, u32[]{:S(2)}) collective-permute-start(f32[128,128]{1,0:T(8,128)S(1)} %get-tuple-element.36), channel_id=1, source_target_pairs={{0,30},{1,31},{2,0},{3,1},{4,2},{5,3},{6,4},{7,5},{8,6},{9,7},{10,... | collective-permute-start | bytes 196616 | tf_op jit(solution)/shard_map/ppermute | solution.py:717
  13.9 1.2 %collective-permute-start.3 = (f32[88,128]{1,0:T(8,128)S(1)}, f32[88,128]{1,0:T(8,128)S(1)}, u32[]{:S(2)}, u32[]{:S(2)}) collective-permute-start(f32[88,128]{1,0:T(8,128)S(1)} %get-tuple-element.34), channel_id=1, source_target_pairs={{0,2},{1,3},{2,0},{3,1},{4,6},{5,7},{6,4},{7,5},{8,10},{9,11},{10,... | collective-permute-start | bytes 135176 | tf_op jit(solution)/shard_map/ppermute | solution.py:717
  15.9 2.3 %collective-permute-start.7 = (f32[24,128]{1,0:T(8,128)S(1)}, f32[24,128]{1,0:T(8,128)S(1)}, u32[]{:S(2)}, u32[]{:S(2)}) collective-permute-start(f32[24,128]{1,0:T(8,128)S(1)} %faces.1.m_ref), channel_id=1, source_target_pairs={{0,2},{1,3},{2,0},{3,1},{4,6},{5,7},{6,4},{7,5},{8,10},{9,11},{10,... | collective-permute-start | bytes 36872 | tf_op jit(solution)/shard_map/ppermute | solution.py:717

commit v7 on v6

--- a/solution.py
+++ b/solution.py
@@ -73,20 +73,19 @@
     return ref[pl.ds(start, SUB, stride=stride), :]
 
 
-def lane_sums(rows):
-    shift = 1
-    while shift < COARSEN:
-        rows = rows + rolled(rows, -shift, 1)
-        shift *= 2
-    return rows
+def gathered(rows, source):
+    parts = [jnp.take_along_axis(rows, source + k, axis=1) for k in range(COARSEN)]
+    while len(parts) > 1:
+        parts = [a + b for a, b in zip(parts[::2], parts[1::2])]
+    return parts[0]
 
 
 def compact(rows, place):
     plane, column = part(iota(rows.shape, 1), SPREAD)
     column = column - RIM
-    source = jnp.clip(column * COARSEN, 0, LANES - 1)
+    source = jnp.clip(column * COARSEN, 0, LANES - COARSEN)
     here = (plane == place) & (column >= 0) & (column < WIDTH)
-    return jnp.where(here, jnp.take_along_axis(lane_sums(rows), source, axis=1), 0.0)
+    return jnp.where(here, gathered(rows, source), 0.0)
 
 
 def section(run):
@@ -118,7 +117,7 @@
             copies.append(pltpu.make_async_copy(source.at[at], target.at[at], sems.at[k, piece]))
     for copy in copies:
         copy.start()
-    for copy in copies:
+    for copy in copies[: 2 * pieces]:
         copy.wait()
 
     even = is_even()
@@ -137,6 +136,8 @@
         u, c = plane(u_ref, z), plane(c_ref, z)
         fy = 0.5 * (c + rolled(c, -1, 1)) * (u - rolled(u, -1, 1))
         r_ref[z * nx : (z + 1) * nx] = jnp.where(wide == LANES - 1, 0.0, fy)
+    for copy in copies[2 * pieces :]:
+        copy.wait()
     below = up(nz - 1)
     for Z in range(nz // COARSEN):
         sum_r = sum_c = jnp.zeros((nx, LANES), f32)
@@ -341,7 +342,7 @@
     is_own = (place >= RIM) & (place < RIM + WIDTH)
     source = jnp.where(is_left, place - (RIM - outer), place - (RIM + WIDTH - outer))
     source = jnp.where(sub == 0, place - RIM, source) * COARSEN
-    source = jnp.clip(source, 0, LANES - 1)
+    source = jnp.clip(source, 0, LANES - COARSEN)
     valid = ((sub == 0) & is_own) | ((sub > 0) & (is_left | is_right))
 
     def outside(r_ref, Z, upper):
@@ -363,9 +364,9 @@
         one = all_rows(0.5 * (c[0] + c[1]) * (u[0] - u[1]))
         two = outside(r2_ref, Z, odd)
         three = outside(r1_ref, Z, even)
-        sums = lane_sums(jnp.where(sub == 0, one, jnp.where(sub == 1, two, jnp.where(sub == 2, three, 0.0))))
+        sums = jnp.where(sub == 0, one, jnp.where(sub == 1, two, jnp.where(sub == 2, three, 0.0)))
         here = valid & (plane == Z)
-        flux = flux + jnp.where(here, jnp.take_along_axis(sums, source, axis=1), 0.0)
+        flux = flux + jnp.where(here, gathered(sums, source), 0.0)
     flux = flux * (1.0 / CELLS)
     far, mate = flux[0:1] + flux[1:2], flux[2:3]
 
@@ -496,8 +497,8 @@
 
 def fine_kernel(
     strip_ref, b2_ref, b1_ref, one_ref, two_ref, last_ref, u_ref, c_ref, cx_ref, cy_ref, cz_ref, diag_ref, inv_ref, q_ref, v_ref,
-    o_ref,
-    ch, cyh, czh, cx, inv, q, va, vb, acc, wr, w0, w1, w2,
+    cx, inv, q, va, acc, w2,
+    ch, cyh, czh, vb, wr, w0, w1,
     *, nz, nx,
 ):
     zs = nz // ZS
@@ -622,7 +623,7 @@
     def long(ref, z):
         return ref[z % nz * ext : (z % nz + 1) * ext]
 
-    for k, w in enumerate((w0, w1, w2)):
+    for k, w in enumerate((w0, w1)):
         old, new = (va, vb) if k % 2 == 0 else (vb, va)
         keep, lift = table[k]
         for z in range(nz):
@@ -636,34 +637,34 @@
             near = near + whole(cz_ref, czh, z) * long(old, z + 1) + whole(cz_ref, czh, z - 1) * long(old, z - 1)
             scaled = q[at] - v + near * inv[at]
             fresh = keep * v + lift * scaled
-            total = (v[:nx] if k == 0 else acc[here]) + fresh[:nx]
-            if k < SWEEPS - 1:
-                q[at] = scaled
-                new[at] = fresh
-                acc[here] = total
-            else:
-                o_ref[here] = own(u_ref, z) + total
+            q[at] = scaled
+            new[at] = fresh
+            acc[here] = (own(u_ref, z) + v[:nx] if k == 0 else acc[here]) + fresh[:nx]
 
 
 def fine(strips, b2, b1, one, two, last, u, c, begun, nz, nx):
     zs = nz // ZS
     ext = nx + SUB
     rim = pltpu.VMEM((nz * SUB, LANES), f32)
-    full = pltpu.VMEM((nz * ext, LANES), f32)
+    full = jax.ShapeDtypeStruct((nz * ext, LANES), f32)
     strip = pltpu.VMEM((zs * ext, LANES), f32)
     return pl.pallas_call(
         functools.partial(fine_kernel, nz=nz, nx=nx),
-        out_shape=jax.ShapeDtypeStruct(u.shape, f32),
+        out_shape=(full,) * 4 + (jax.ShapeDtypeStruct(u.shape, f32), jax.ShapeDtypeStruct((zs * ext, LANES), f32)),
         in_specs=[VMEM] * 15,
-        out_specs=VMEM,
-        scratch_shapes=[rim] * 3 + [full] * 5 + [pltpu.VMEM(u.shape, f32), pltpu.VMEM((zs * SUB, LANES), f32)] + [strip] * 3,
+        out_specs=(VMEM,) * 6,
+        scratch_shapes=[rim] * 3 + [pltpu.VMEM((nz * ext, LANES), f32), pltpu.VMEM((zs * SUB, LANES), f32)] + [strip] * 2,
         compiler_params=SMALL,
         cost_estimate=pl.CostEstimate(flops=100 * u.size, bytes_accessed=40 * u.size, transcendentals=0),
         name="fine",
     )(strips, b2, b1, one, two, last, u, c, *begun)
 
 
-def finish_kernel(x_ref, m_ref, r_ref, o_ref, *, nz, nx):
+def finish_kernel(
+    cx_ref, inv_ref, q_ref, v_ref, sum_ref, w_ref, cy_ref, cz_ref, m_ref, r_ref, o_ref, out, sems, *, nz, nx
+):
+    zs = nz // ZS
+    ext = nx + SUB
     rows = nx // COARSEN
     even = is_even()
     sub, lane = iota((SUB, LANES), 0), iota((SUB, LANES), 1)
@@ -685,24 +686,52 @@
         v = (start + keep * v) + ((terms[0] + terms[1]) + (terms[2] + terms[3]) + (terms[4] + terms[5]))
     top = v[:SUB]
     top = jnp.where(even, rolled(top, -rows - 1, 0), rolled(top, -1, 0))
+
+    wide = iota((nx, LANES), 1)
+    first_lane, last_lane = wide == 0, wide == LANES - 1
+    keep, lift = steps()[-1]
+
+    def own(ref, z):
+        return ref[z % nz * nx : (z % nz + 1) * nx]
+
+    def long(ref, z):
+        return ref[z % nz * ext : z % nz * ext + nx]
+
+    copies = []
+    size = COARSEN * nx
     for Z in range(nz // COARSEN):
         spread = jnp.take_along_axis(top, Z * SPREAD + RIM + part(lane, COARSEN)[0], axis=1)
-        for X in range(rows):
-            value = jnp.broadcast_to(spread[X : X + 1], (COARSEN, LANES))
-            for z in range(Z * COARSEN, (Z + 1) * COARSEN):
-                at = slice(z * nx + X * COARSEN, z * nx + (X + 1) * COARSEN)
-                o_ref[at] = x_ref[at] + value
-
-
-def finish(x, m, r, nz, nx):
+        value = jnp.concatenate([jnp.broadcast_to(spread[X : X + 1], (COARSEN, LANES)) for X in range(rows)], axis=0)
+        for z in range(Z * COARSEN, (Z + 1) * COARSEN):
+            at = slice(z * ext, (z + 1) * ext)
+            v, gx = v_ref[at], cx_ref[at]
+            near = (gx * rolled(v, -1, 0) + rolled(gx * v, 1, 0))[:nx]
+            v, gy, zi = v[:nx], own(cy_ref, z), z % zs
+            edge = beside(w_ref[zi * ext : zi * ext + nx], z, zs, RIM - 1)
+            near = near + gy * jnp.where(last_lane, edge, rolled(v, -1, 1))
+            near = near + jnp.where(first_lane, edge, rolled(gy * v, 1, 1))
+            near = near + own(cz_ref, z) * long(v_ref, z + 1) + own(cz_ref, z - 1) * long(v_ref, z - 1)
+            scaled = long(q_ref, z) - v + near * long(inv_ref, z)
+            here = slice(z * nx, (z + 1) * nx)
+            out[here] = (own(sum_ref, z) + (keep * v + lift * scaled)) + value
+        here = pl.ds(Z * size, size)
+        copies.append(pltpu.make_async_copy(out.at[here], o_ref.at[here], sems.at[Z]))
+        copies[-1].start()
+    for copy in copies:
+        copy.wait()
+
+
+def finish(passed, cy, cz, m, r, nz, nx):
+    shape = (nz * nx, LANES)
     return pl.pallas_call(
         functools.partial(finish_kernel, nz=nz, nx=nx),
-        out_shape=jax.ShapeDtypeStruct(x.shape, f32),
-        in_specs=[VMEM] * 3,
-        out_specs=VMEM,
+        out_shape=jax.ShapeDtypeStruct(shape, f32),
+        in_specs=[VMEM] * 10,
+        out_specs=pl.BlockSpec(memory_space=pltpu.HBM),
+        scratch_shapes=[pltpu.VMEM(shape, f32), pltpu.SemaphoreType.DMA((nz // COARSEN,))],
         compiler_params=SMALL,
         name="finish",
-    )(x, m, r)
+    )(*passed, cy, cz, m, r)
 
 
 def moves():
@@ -752,8 +781,8 @@
     begun = begin(strips, u, c, r, nz, nx)
     m = faces(own, kept, rb2, rb1, begun[0], nz, nx)
     rm = mate(m)
-    x = fine(strips, rb2, rb1, *after, before, u, c, begun, nz, nx)
-    return finish(x, m, rm, nz, nx).reshape(nz, nx, ny)
+    passed = fine(strips, rb2, rb1, *after, before, u, c, begun, nz, nx)
+    return finish(passed, begun[1], begun[2], m, rm, nz, nx).reshape(nz, nx, ny)
 
 
 def solution(mesh):

time: 19.5 us -> 19.3 us (0.990)
  Pallas kernels: 7.07 us -> 6.73 us
    pallas_call x1, Pallas kernels: 2.22 us -> 1.84 us  [fine(): pl.pallas_call(functools.partial(fine_kernel, nz=nz, nx=nx), out_shape=(f...]
  transfers between devices with their start and end apart: 8 -> 8, of which waited for: 4 -> 4; matrix products, arithmetic and copies ran while one was open for 0% -> 0% of each run, Pallas kernels for 18% -> 16%
where the time goes in v7:
time: 19.3 us; the launch traced here: 19.1 us
  starting transfers between devices  9.73 us (50%)
  Pallas kernels  6.73 us (35%)
  waiting for transfers between devices  2.52 us (13%)
    ppermute x8, starting transfers between devices, send(): return lax.ppermute(x, ('gx', 'gy'), pairs)  9.73 us
    ppermute x8, waiting for transfers between devices, send(): return lax.ppermute(x, ('gx', 'gy'), pairs)  2.52 us
    pallas_call x1, Pallas kernels, pack(): pl.pallas_call(functools.partial(pack_kernel, nz=nz, nx=nx), out_shape=(t...  2.48 us
    pallas_call x1, Pallas kernels, fine(): pl.pallas_call(functools.partial(fine_kernel, nz=nz, nx=nx), out_shape=(f...  1.84 us
    pallas_call x1, Pallas kernels, finish(): pl.pallas_call(functools.partial(finish_kernel, nz=nz, nx=nx), out_shape=...  1.28 us
    pallas_call x1, Pallas kernels, begin(): pl.pallas_call(functools.partial(begin_kernel, nz=nz, nx=nx), out_shape=(...  0.58 us
  transfers between devices with their start and end apart: 8, of which 4 were waited for; matrix products, arithmetic and copies ran while one was open for 0% of the time, Pallas kernels for 16%

profile of v7, /device:TPU:0, one launch (start us, length us, event | category | flops | bytes accessed | tf_op | source)
XLA Modules:
  0.0 19.1 jit_solution(11225505337047764505)
XLA Ops:
  0.0 0.0 copy-start.1
  0.0 2.5 %pack.1 = (f32[216,128]{1,0:T(8,128)S(1)}, f32[72,128]{1,0:T(8,128)S(1)}, f32[256,128]{1,0:T(8,128)S(1)}, f32[128,128]{1,0:T(8,128)S(1)}, f32[128,128]{1,0:T(8,1...) custom-call(f32[768,128]{1,0:T(8,128)} %bitcast.4, f32[768,128]{1,0:T(8,128)} %bitcast.10, f32[768,128]{1,0:T(8,128)} %bitcast.7), custom_call_target="tpu_custom_call" | custom-call | tf_op jit(solution)/shard_map/pack/pallas_call | solution.py:207
  2.5 0.0 copy-start
  2.5 3.0 %collective-permute-start = (f32[216,128]{1,0:T(8,128)S(1)}, f32[216,128]{1,0:T(8,128)S(1)}, u32[]{:S(2)}, u32[]{:S(2)}) collective-permute-start(f32[216,128]{1,0:T(8,128)S(1)} %get-tuple-element.34.q_ref), channel_id=1, source_target_pairs={{0,1},{1,0},{2,3},{3,2},{4,5},{5,4},{6,7},{7,6},{8,9},{9,8},{10,11... | collective-permute-start | bytes 331784 | tf_op jit(solution)/shard_map/ppermute | solution.py:746
  5.5 0.0 collective-permute-start.6
  5.5 1.6 %collective-permute-start.1 = (f32[72,128]{1,0:T(8,128)S(1)}, f32[72,128]{1,0:T(8,128)S(1)}, u32[]{:S(2)}, u32[]{:S(2)}) collective-permute-start(f32[72,128]{1,0:T(8,128)S(1)} %get-tuple-element.35), channel_id=1, source_target_pairs={{0,2},{1,3},{2,0},{3,1},{4,6},{5,7},{6,4},{7,5},{8,10},{9,11},{10,... | collective-permute-start | bytes 110600 | tf_op jit(solution)/shard_map/ppermute | solution.py:746
  7.1 0.9 %collective-permute-done.1.f1_ref = f32[72,128]{1,0:T(8,128)S(1)} collective-permute-done((f32[72,128]{1,0:T(8,128)S(1)}, f32[72,128]{1,0:T(8,128)S(1)}, u32[]{:S(2)}, u32[]{:S(2)}) %collective-permute-start.1) | collective-permute-done | bytes 36896 | tf_op jit(solution)/shard_map/ppermute | solution.py:746
  8.0 0.6 %collective-permute-done.ql_ref.qr_ref = f32[216,128]{1,0:T(8,128)S(1)} collective-permute-done((f32[216,128]{1,0:T(8,128)S(1)}, f32[216,128]{1,0:T(8,128)S(1)}, u32[]{:S(2)}, u32[]{:S(2)}) %collective-permute-start) | collective-permute-done | bytes 110624 | tf_op jit(solution)/shard_map/ppermute | solution.py:746
  8.6 0.3 %join.1 = (f32[88,128]{1,0:T(8,128)S(1)}, f32[160,128]{1,0:T(8,128)S(1)}, f32[288,128]{1,0:T(8,128)S(1)}, f32[80,128]{1,0:T(8,128)S(1)}) custom-call(f32[216,128]{1,0:T(8,128)S(1)} %get-tuple-element.34.q_ref, f32[216,128]{1,0:T(8,128)S(1)} %collective-permute-done.ql_ref.qr_ref, f32[216,128]{1,0:T(8,128)S(1)} %collective-permute-done.ql_ref.qr_ref, ...), custom_call_target="tpu_custom_call" | custom-call | tf_op jit(solution)/shard_map/join/pallas_call | solution.py:316
  8.9 3.4 %collective-permute-start.2 = (f32[160,128]{1,0:T(8,128)S(1)}, f32[160,128]{1,0:T(8,128)S(1)}, u32[]{:S(2)}, u32[]{:S(2)}) collective-permute-start(f32[160,128]{1,0:T(8,128)S(1)} %get-tuple-element.39), channel_id=1, source_target_pairs={{0,30},{1,31},{2,4},{3,5},{4,2},{5,3},{6,8},{7,9},{8,6},{9,7},{10,... | collective-permute-start | bytes 245768 | tf_op jit(solution)/shard_map/ppermute | solution.py:746
  12.3 1.1 %collective-permute-start.4 = (f32[128,128]{1,0:T(8,128)S(1)}, f32[128,128]{1,0:T(8,128)S(1)}, u32[]{:S(2)}, u32[]{:S(2)}) collective-permute-start(f32[128,128]{1,0:T(8,128)S(1)} %get-tuple-element.41), channel_id=1, source_target_pairs={{0,30},{1,31},{2,0},{3,1},{4,2},{5,3},{6,4},{7,5},{8,6},{9,7},{10,... | collective-permute-start | bytes 196616 | tf_op jit(solution)/shard_map/ppermute | solution.py:746
  13.4 0.5 %collective-permute-start.5 = (f32[128,128]{1,0:T(8,128)S(1)}, f32[128,128]{1,0:T(8,128)S(1)}, u32[]{:S(2)}, u32[]{:S(2)}) collective-permute-start(f32[128,128]{1,0:T(8,128)S(1)} %get-tuple-element.42), channel_id=1, source_target_pairs={{0,30},{1,31},{2,0},{3,1},{4,2},{5,3},{6,4},{7,5},{8,6},{9,7},{10,... | collective-permute-start | bytes 196616 | tf_op jit(solution)/shard_map/ppermute | solution.py:746
  13.9 0.0 collective-permute-start.3
  13.9 0.0 copy-done.1
  13.9 0.0 copy-done
  13.9 0.6 %begin.1 = (f32[768,128]{1,0:T(8,128)S(1)}, f32[768,128]{1,0:T(8,128)S(1)}, f32[768,128]{1,0:T(8,128)S(1)}, f32[768,128]{1,0:T(8,128)S(1)}, f32[256,128]{1,0:T(8...) custom-call(f32[288,128]{1,0:T(8,128)S(1)} %get-tuple-element.38.strip_ref, f32[768,128]{1,0:T(8,128)S(1)} %bitcast.5, ...), custom_call_target="tpu_custom_call" | custom-call | flops 3932160 | bytes 3932160 | tf_op jit(solution)/shard_map/begin/pallas_call | solution.py:487
  14.5 0.6 %collective-permute-done.3.b1_ref.r1_ref = f32[88,128]{1,0:T(8,128)S(1)} collective-permute-done((f32[88,128]{1,0:T(8,128)S(1)}, f32[88,128]{1,0:T(8,128)S(1)}, u32[]{:S(2)}, u32[]{:S(2)}) %collective-permute-start.3) | collective-permute-done | bytes 45088 | tf_op jit(solution)/shard_map/ppermute | solution.py:746
  15.1 0.4 %collective-permute-done.2.b2_ref.r2_ref = f32[160,128]{1,0:T(8,128)S(1)} collective-permute-done((f32[160,128]{1,0:T(8,128)S(1)}, f32[160,128]{1,0:T(8,128)S(1)}, u32[]{:S(2)}, u32[]{:S(2)}) %collective-permute-start.2) | collective-permute-done | bytes 81952 | tf_op jit(solution)/shard_map/ppermute | solution.py:746
  15.6 0.2 %faces.1.m_ref = f32[24,128]{1,0:T(8,128)S(1)} custom-call(f32[128,128]{1,0:T(8,128)S(1)} %get-tuple-element.36.own_ref, f32[80,128]{1,0:T(8,128)S(1)} %get-tuple-element.58.kept_ref, f32[160,128]{1,0:T(8,128)S(1)} %collective-permute-done.2.b2_ref.r2_ref, f32[88,128]{1,0:T(8,128)S(1)} %collective-permute-done.3.b1_ref.r1_ref, ...), custom_call_target="tpu_custom_call" | custom-call | tf_op jit(solution)/shard_map/faces/pallas_call | solution.py:398
  15.8 0.1 collective-permute-start.7
  15.9 0.0 collective-permute-done.6.last_ref
  15.9 0.0 collective-permute-done.4.one_ref
  15.9 0.0 collective-permute-done.5.two_ref
  15.9 1.8 %fine.1 = (f32[1024,128]{1,0:T(8,128)S(1)}, f32[1024,128]{1,0:T(8,128)S(1)}, f32[1024,128]{1,0:T(8,128)S(1)}, f32[1024,128]{1,0:T(8,128)S(1)}, f32[768,128]{1,0:T(8,128)S(1)}, /*index=5*/f32[128,128]{1,0:T(8,128)S(1)}) custom-call(f32[288,128]{1,0:T(8,128)S(1)} %get-tuple-element.38.strip_ref, f32[160,128]{1,0:T(8,128)S(1)} %collective-permute-done.2.b2_ref.r2_ref, ...), custom_call_target="tpu_custom_call" | custom-call | flops 9830400 | bytes 3932160 | tf_op jit(solution)/shard_map/fine/pallas_call | solution.py:651
  17.8 0.0 collective-permute-done.7.r_ref
  17.8 1.3 %finish.1 = f32[768,128]{1,0:T(8,128)} custom-call(f32[1024,128]{1,0:T(8,128)S(1)} %get-tuple-element.52.cx_ref, f32[1024,128]{1,0:T(8,128)S(1)} %get-tuple-element.53.inv_ref, f32[1024,128]{1,0:T(8,128)S(1)} %get-tuple-element.54.q_ref, f32[1024,128]{1,0:T(8,128)S(1)} %get-tuple-element.55.v_ref, f32[768,128]{1,0:T(8,128)S(1)} %get-tuple-element.56.sum_ref, ...), custom_call_target="tpu_custom_call" | custom-call | tf_op jit(solution)/shard_map/finish/pallas_call | solution.py:726
Async XLA Ops:
  0.0 13.9 %copy-start.1 = (f32[32,24,128]{2,1,0:T(8,128)S(1)}, f32[32,24,128]{2,1,0:T(8,128)}, u32[]{:S(2)}) copy-start(f32[32,24,128]{2,1,0:T(8,128)} %param.5) | copy-start | bytes 1179652
  2.5 11.4 %copy-start = (f32[32,24,128]{2,1,0:T(8,128)S(1)}, f32[32,24,128]{2,1,0:T(8,128)}, u32[]{:S(2)}) copy-start(f32[32,24,128]{2,1,0:T(8,128)} %param.3) | copy-start | bytes 1179652
  2.5 6.1 %collective-permute-start = (f32[216,128]{1,0:T(8,128)S(1)}, f32[216,128]{1,0:T(8,128)S(1)}, u32[]{:S(2)}, u32[]{:S(2)}) collective-permute-start(f32[216,128]{1,0:T(8,128)S(1)} %get-tuple-element.34.q_ref), channel_id=1, source_target_pairs={{0,1},{1,0},{2,3},{3,2},{4,5},{5,4},{6,7},{7,6},{8,9},{9,8},{10,11... | collective-permute-start | bytes 331784 | tf_op jit(solution)/shard_map/ppermute | solution.py:746
  5.5 10.4 %collective-permute-start.6 = (f32[256,128]{1,0:T(8,128)S(1)}, f32[256,128]{1,0:T(8,128)S(1)}, u32[]{:S(2)}, u32[]{:S(2)}) collective-permute-start(f32[256,128]{1,0:T(8,128)S(1)} %get-tuple-element.43), channel_id=1, source_target_pairs={{0,2},{1,3},{2,4},{3,5},{4,6},{5,7},{6,8},{7,9},{8,10},{9,11},{10,... | collective-permute-start | bytes 393224 | tf_op jit(solution)/shard_map/ppermute | solution.py:746
  5.5 2.5 %collective-permute-start.1 = (f32[72,128]{1,0:T(8,128)S(1)}, f32[72,128]{1,0:T(8,128)S(1)}, u32[]{:S(2)}, u32[]{:S(2)}) collective-permute-start(f32[72,128]{1,0:T(8,128)S(1)} %get-tuple-element.35), channel_id=1, source_target_pairs={{0,2},{1,3},{2,0},{3,1},{4,6},{5,7},{6,4},{7,5},{8,10},{9,11},{10,... | collective-permute-start | bytes 110600 | tf_op jit(solution)/shard_map/ppermute | solution.py:746
  8.9 6.6 %collective-permute-start.2 = (f32[160,128]{1,0:T(8,128)S(1)}, f32[160,128]{1,0:T(8,128)S(1)}, u32[]{:S(2)}, u32[]{:S(2)}) collective-permute-start(f32[160,128]{1,0:T(8,128)S(1)} %get-tuple-element.39), channel_id=1, source_target_pairs={{0,30},{1,31},{2,4},{3,5},{4,2},{5,3},{6,8},{7,9},{8,6},{9,7},{10,... | collective-permute-start | bytes 245768 | tf_op jit(solution)/shard_map/ppermute | solution.py:746
  12.3 3.6 %collective-permute-start.4 = (f32[128,128]{1,0:T(8,128)S(1)}, f32[128,128]{1,0:T(8,128)S(1)}, u32[]{:S(2)}, u32[]{:S(2)}) collective-permute-start(f32[128,128]{1,0:T(8,128)S(1)} %get-tuple-element.41), channel_id=1, source_target_pairs={{0,30},{1,31},{2,0},{3,1},{4,2},{5,3},{6,4},{7,5},{8,6},{9,7},{10,... | collective-permute-start | bytes 196616 | tf_op jit(solution)/shard_map/ppermute | solution.py:746
  13.4 2.5 %collective-permute-start.5 = (f32[128,128]{1,0:T(8,128)S(1)}, f32[128,128]{1,0:T(8,128)S(1)}, u32[]{:S(2)}, u32[]{:S(2)}) collective-permute-start(f32[128,128]{1,0:T(8,128)S(1)} %get-tuple-element.42), channel_id=1, source_target_pairs={{0,30},{1,31},{2,0},{3,1},{4,2},{5,3},{6,4},{7,5},{8,6},{9,7},{10,... | collective-permute-start | bytes 196616 | tf_op jit(solution)/shard_map/ppermute | solution.py:746
  13.9 1.2 %collective-permute-start.3 = (f32[88,128]{1,0:T(8,128)S(1)}, f32[88,128]{1,0:T(8,128)S(1)}, u32[]{:S(2)}, u32[]{:S(2)}) collective-permute-start(f32[88,128]{1,0:T(8,128)S(1)} %get-tuple-element.40), channel_id=1, source_target_pairs={{0,2},{1,3},{2,0},{3,1},{4,6},{5,7},{6,4},{7,5},{8,10},{9,11},{10,... | collective-permute-start | bytes 135176 | tf_op jit(solution)/shard_map/ppermute | solution.py:746
  15.8 2.0 %collective-permute-start.7 = (f32[24,128]{1,0:T(8,128)S(1)}, f32[24,128]{1,0:T(8,128)S(1)}, u32[]{:S(2)}, u32[]{:S(2)}) collective-permute-start(f32[24,128]{1,0:T(8,128)S(1)} %faces.1.m_ref), channel_id=1, source_target_pairs={{0,2},{1,3},{2,0},{3,1},{4,6},{5,7},{6,4},{7,5},{8,10},{9,11},{10,... | collective-permute-start | bytes 36872 | tf_op jit(solution)/shard_map/ppermute | solution.py:746

commit v8 on v7

--- a/solution.py
+++ b/solution.py
@@ -124,7 +124,7 @@
     sub, lane = iota((SUB, LANES), 0), iota((SUB, LANES), 1)
     low = sub < RIM
     row, wide = iota((nx, LANES), 0), iota((nx, LANES), 1)
-    slot = part(wide, 2 * RIM)[0]
+    slot, spot = part(wide, 2 * RIM)
 
     def plane(ref, z):
         return ref[z % nz * nx : (z % nz + 1) * nx]
@@ -164,15 +164,14 @@
     zs = nz // ZS
     half = zs // 2
     def strips():
-        for a, ref in enumerate((u_ref, c_ref, r_ref)):
-            for pair in range(half):
-                strip = jnp.zeros((nx, LANES), f32)
-                for g in range(ZS):
-                    for second in range(2):
-                        at = 2 * g + second
-                        moved = rolled(plane(ref, g * zs + pair + second * half), at * 2 * RIM + RIM, 1)
-                        strip = jnp.where(slot == at, moved, strip)
-                q_ref[(a * half + pair) * nx : (a * half + pair + 1) * nx] = strip
+        for zi in range(zs):
+            strip = jnp.zeros((nx, LANES), f32)
+            for g in range(ZS):
+                z, at = g * zs + zi, g * GROUP + RIM
+                outer = jnp.where(spot < 2, rolled(plane(u_ref, z), at + RIM + 1, 1), rolled(plane(r_ref, z), at + 2 * RIM + 1, 1))
+                strip = jnp.where(slot == 2 * g + 1, outer, strip)
+                strip = jnp.where(slot == 2 * g, rolled(plane(c_ref, z), at, 1), strip)
+            q_ref[zi * nx : (zi + 1) * nx] = strip
 
     def finish():
         coarse = jnp.zeros((SUB, LANES), f32)
@@ -183,31 +182,40 @@
         coarse = coarse * (1.0 / CELLS)
         strips()
 
-        base = 3 * half * nx
+        base = zs * nx + SUB
         for a, ref in enumerate((u_ref, c_ref)):
             for Z in range(nz // SUB):
                 at = Z * SUB * nx
                 first, last = picked(ref, at, nx), picked(ref, at + nx - 1, nx)
-                spot = a * nz + Z * SUB
-                own_ref[spot : spot + SUB] = first
-                own_ref[2 * nz + spot : 2 * nz + spot + SUB] = last
-                f1_ref[spot : spot + SUB] = jnp.where(even, last, first)
-                q_ref[base + spot : base + spot + SUB] = jnp.where(
+                to = a * nz + Z * SUB
+                own_ref[to : to + SUB] = first
+                own_ref[2 * nz + to : 2 * nz + to + SUB] = last
+                f1_ref[to : to + SUB] = jnp.where(even, last, first)
+                q_ref[base + to : base + to + SUB] = jnp.where(
                     lane < HALF, rolled(first, REACH, 1), rolled(last, REACH + HALF, 1)
                 )
         q_ref[base + 2 * nz : base + 2 * nz + SUB] = coarse
         f1_ref[2 * nz :] = coarse
+        corners = jnp.zeros((SUB, LANES), f32)
+        group = part(lane, GROUP)[0]
+        for Z in range(nz // SUB):
+            at = Z * SUB * nx
+            first, last = picked(u_ref, at, nx), picked(u_ref, at + nx - 1, nx)
+            both = jnp.where(low, first, rolled(last, RIM, 0)), jnp.where(low, rolled(first, RIM, 0), last)
+            for second in range(2):
+                g = 2 * Z + second
+                corners = jnp.where(group == g, rolled(both[second], g * GROUP + RIM, 1), corners)
+        q_ref[zs * nx : base] = corners
 
     section(finish)
 
 
 def pack(u, s, c, nz, nx):
-    half = nz // ZS // 2
     pieces = 4
     return pl.pallas_call(
         functools.partial(pack_kernel, nz=nz, nx=nx),
         out_shape=(
-            tiles(3 * half * nx // SUB + 2 * nz // SUB + 1),
+            tiles(nz // ZS * nx // SUB + 2 * nz // SUB + 2),
             tiles(2 * nz // SUB + 1),
             tiles(nz),
             tiles(nz // 2),
@@ -236,27 +244,51 @@
     sub, lane = iota((SUB, LANES), 0), iota((SUB, LANES), 1)
     low = sub < RIM
     spot = part(iota((nx, LANES), 1), GROUP)[1]
-    joined = []
-    for a in range(3):
-        group = [None] * zs
+    thin, row = part(lane, GROUP)[1], iota((nx, LANES), 0)
+
+    def before(spot, left, own, right):
+        moved = rolled(jnp.where(spot < RIM, own, right), 2 * RIM, 1)
+        return jnp.where(spot < 2 * RIM, jnp.where(spot < RIM, left, own), moved)
+
+    def behind(spot, left, own, right):
+        lower, at = spot < 2 * RIM, 2 * RIM
+        split = spot < at + 2 + SWEEPS
+        residual = jnp.where(
+            lower,
+            rolled(jnp.where(split, left, own), -(at + 1), 1),
+            rolled(jnp.where(split, own, right), -1, 1),
+        )
+        split = spot == at
+        u = jnp.where(
+            lower,
+            rolled(jnp.where(split, left, own), RIM - 1 - at, 1),
+            rolled(jnp.where(split, own, right), RIM - 1, 1),
+        )
+        return residual, u
+
+    at = slice(zs * nx, zs * nx + SUB)
+    corners = before(thin, ql_ref[at], q_ref[at], qr_ref[at])
+    joined = [], [], []
+    for zi in range(zs):
+        at = slice(zi * nx, (zi + 1) * nx)
+        parts = ql_ref[at], q_ref[at], qr_ref[at]
+        residual, u = behind(spot, *parts)
+        u = jnp.where(row == 0, corners[zi : zi + 1], u)
+        u = jnp.where(row == nx - 1, corners[RIM + zi : RIM + zi + 1], u)
+        for group, strip in zip(joined, (u, before(spot, *parts), residual)):
+            group.append(strip)
+    for a, group in enumerate(joined):
+        for zi in range(zs):
+            strip_ref[(a * zs + zi) * nx : (a * zs + zi + 1) * nx] = group[zi]
         for pair in range(half):
-            at = slice((a * half + pair) * nx, (a * half + pair + 1) * nx)
-            left, own, right = ql_ref[at], q_ref[at], qr_ref[at]
-            moved = rolled(jnp.where(spot < RIM, own, right), 2 * RIM, 1)
-            one = jnp.where(spot < 2 * RIM, jnp.where(spot < RIM, left, own), moved)
-            moved = rolled(jnp.where(spot < 3 * RIM, left, own), -2 * RIM, 1)
-            two = jnp.where(spot < 2 * RIM, moved, jnp.where(spot < 3 * RIM, own, right))
-            group[pair], group[pair + half] = one, two
+            one, two = group[pair], group[pair + half]
             first = jnp.where(low, one[:SUB], rolled(two[:SUB], RIM, 0))
             last = jnp.where(low, rolled(two[nx - SUB :], RIM, 0), one[nx - SUB :])
             to = slice((a * half + pair) * SUB, (a * half + pair + 1) * SUB)
             b1_ref[to] = jnp.where(even, last, first)
             b2_ref[to] = jnp.where(even, first, last)
-        for zi in range(zs):
-            strip_ref[(a * zs + zi) * nx : (a * zs + zi + 1) * nx] = group[zi]
-        joined.append(group)
-
-    source, target = 3 * half * nx, 3 * half * SUB
+
+    source, target = zs * nx + SUB, 3 * half * SUB
     lower, outer = lane < HALF, part(lane, HALF)[1] < REACH
     for Z in range(nz // SUB):
         u, c = (

time: 19.3 us -> 18.9 us (0.979)
  waiting for transfers between devices: 2.52 us -> 1.99 us
    ppermute x8, waiting for transfers between devices: 2.52 us -> 1.99 us  [send(): return lax.ppermute(x, ('gx', 'gy'), pairs)]
where the time goes in v8:
time: 18.9 us; the launch traced here: 18.8 us
  starting transfers between devices  9.87 us (52%)
  Pallas kernels  6.83 us (36%)
  waiting for transfers between devices  1.99 us (11%)
    ppermute x8, starting transfers between devices, send(): return lax.ppermute(x, ('gx', 'gy'), pairs)  9.87 us
    pallas_call x1, Pallas kernels, pack(): pl.pallas_call(functools.partial(pack_kernel, nz=nz, nx=nx), out_shape=(t...  2.53 us
    ppermute x8, waiting for transfers between devices, send(): return lax.ppermute(x, ('gx', 'gy'), pairs)  1.99 us
    pallas_call x1, Pallas kernels, fine(): pl.pallas_call(functools.partial(fine_kernel, nz=nz, nx=nx), out_shape=(f...  1.85 us
    pallas_call x1, Pallas kernels, finish(): pl.pallas_call(functools.partial(finish_kernel, nz=nz, nx=nx), out_shape=...  1.27 us
    pallas_call x1, Pallas kernels, begin(): pl.pallas_call(functools.partial(begin_kernel, nz=nz, nx=nx), out_shape=(...  0.59 us
  transfers between devices with their start and end apart: 8, of which 4 were waited for; matrix products, arithmetic and copies ran while one was open for 0% of the time, Pallas kernels for 16%

profile of v8, /device:TPU:0, one launch (start us, length us, event | category | flops | bytes accessed | tf_op | source)
XLA Modules:
  0.0 18.8 jit_solution(704742160335678160)
XLA Ops:
  0.0 0.0 copy-start
  0.0 0.0 copy-start.1
  0.0 2.5 %pack.1 = (f32[176,128]{1,0:T(8,128)S(1)}, f32[72,128]{1,0:T(8,128)S(1)}, f32[256,128]{1,0:T(8,128)S(1)}, f32[128,128]{1,0:T(8,128)S(1)}, f32[128,128]{1,0:T(8,1...) custom-call(f32[768,128]{1,0:T(8,128)} %bitcast.4, f32[768,128]{1,0:T(8,128)} %bitcast.10, f32[768,128]{1,0:T(8,128)} %bitcast.7), custom_call_target="tpu_custom_call" | custom-call | tf_op jit(solution)/shard_map/pack/pallas_call | solution.py:215
  2.5 3.0 %collective-permute-start = (f32[176,128]{1,0:T(8,128)S(1)}, f32[176,128]{1,0:T(8,128)S(1)}, u32[]{:S(2)}, u32[]{:S(2)}) collective-permute-start(f32[176,128]{1,0:T(8,128)S(1)} %get-tuple-element.34.q_ref), channel_id=1, source_target_pairs={{0,1},{1,0},{2,3},{3,2},{4,5},{5,4},{6,7},{7,6},{8,9},{9,8},{10,11... | collective-permute-start | bytes 270344 | tf_op jit(solution)/shard_map/ppermute | solution.py:778
  5.6 0.0 collective-permute-start.6
  5.6 1.6 %collective-permute-start.1 = (f32[72,128]{1,0:T(8,128)S(1)}, f32[72,128]{1,0:T(8,128)S(1)}, u32[]{:S(2)}, u32[]{:S(2)}) collective-permute-start(f32[72,128]{1,0:T(8,128)S(1)} %get-tuple-element.35), channel_id=1, source_target_pairs={{0,2},{1,3},{2,0},{3,1},{4,6},{5,7},{6,4},{7,5},{8,10},{9,11},{10,... | collective-permute-start | bytes 110600 | tf_op jit(solution)/shard_map/ppermute | solution.py:778
  7.2 0.9 %collective-permute-done.1.f1_ref = f32[72,128]{1,0:T(8,128)S(1)} collective-permute-done((f32[72,128]{1,0:T(8,128)S(1)}, f32[72,128]{1,0:T(8,128)S(1)}, u32[]{:S(2)}, u32[]{:S(2)}) %collective-permute-start.1) | collective-permute-done | bytes 36896 | tf_op jit(solution)/shard_map/ppermute | solution.py:778
  8.1 0.1 collective-permute-done.ql_ref.qr_ref
  8.2 0.3 %join.1 = (f32[88,128]{1,0:T(8,128)S(1)}, f32[160,128]{1,0:T(8,128)S(1)}, f32[288,128]{1,0:T(8,128)S(1)}, f32[80,128]{1,0:T(8,128)S(1)}) custom-call(f32[176,128]{1,0:T(8,128)S(1)} %get-tuple-element.34.q_ref, f32[176,128]{1,0:T(8,128)S(1)} %collective-permute-done.ql_ref.qr_ref, f32[176,128]{1,0:T(8,128)S(1)} %collective-permute-done.ql_ref.qr_ref, ...), custom_call_target="tpu_custom_call" | custom-call | tf_op jit(solution)/shard_map/join/pallas_call | solution.py:348
  8.5 3.3 %collective-permute-start.2 = (f32[160,128]{1,0:T(8,128)S(1)}, f32[160,128]{1,0:T(8,128)S(1)}, u32[]{:S(2)}, u32[]{:S(2)}) collective-permute-start(f32[160,128]{1,0:T(8,128)S(1)} %get-tuple-element.39), channel_id=1, source_target_pairs={{0,30},{1,31},{2,4},{3,5},{4,2},{5,3},{6,8},{7,9},{8,6},{9,7},{10,... | collective-permute-start | bytes 245768 | tf_op jit(solution)/shard_map/ppermute | solution.py:778
  11.8 1.2 %collective-permute-start.4 = (f32[128,128]{1,0:T(8,128)S(1)}, f32[128,128]{1,0:T(8,128)S(1)}, u32[]{:S(2)}, u32[]{:S(2)}) collective-permute-start(f32[128,128]{1,0:T(8,128)S(1)} %get-tuple-element.41), channel_id=1, source_target_pairs={{0,30},{1,31},{2,0},{3,1},{4,2},{5,3},{6,4},{7,5},{8,6},{9,7},{10,... | collective-permute-start | bytes 196616 | tf_op jit(solution)/shard_map/ppermute | solution.py:778
  13.0 0.7 %collective-permute-start.5 = (f32[128,128]{1,0:T(8,128)S(1)}, f32[128,128]{1,0:T(8,128)S(1)}, u32[]{:S(2)}, u32[]{:S(2)}) collective-permute-start(f32[128,128]{1,0:T(8,128)S(1)} %get-tuple-element.42), channel_id=1, source_target_pairs={{0,30},{1,31},{2,0},{3,1},{4,2},{5,3},{6,4},{7,5},{8,6},{9,7},{10,... | collective-permute-start | bytes 196616 | tf_op jit(solution)/shard_map/ppermute | solution.py:778
  13.7 0.0 collective-permute-start.3
  13.7 0.0 copy-done
  13.7 0.0 copy-done.1
  13.7 0.6 %begin.1 = (f32[768,128]{1,0:T(8,128)S(1)}, f32[768,128]{1,0:T(8,128)S(1)}, f32[768,128]{1,0:T(8,128)S(1)}, f32[768,128]{1,0:T(8,128)S(1)}, f32[256,128]{1,0:T(8...) custom-call(f32[288,128]{1,0:T(8,128)S(1)} %get-tuple-element.38.strip_ref, f32[768,128]{1,0:T(8,128)S(1)} %bitcast.5, ...), custom_call_target="tpu_custom_call" | custom-call | flops 3932160 | bytes 3932160 | tf_op jit(solution)/shard_map/begin/pallas_call | solution.py:519
  14.3 0.6 %collective-permute-done.3.b1_ref.r1_ref = f32[88,128]{1,0:T(8,128)S(1)} collective-permute-done((f32[88,128]{1,0:T(8,128)S(1)}, f32[88,128]{1,0:T(8,128)S(1)}, u32[]{:S(2)}, u32[]{:S(2)}) %collective-permute-start.3) | collective-permute-done | bytes 45088 | tf_op jit(solution)/shard_map/ppermute | solution.py:778
  14.9 0.3 %collective-permute-done.2.b2_ref.r2_ref = f32[160,128]{1,0:T(8,128)S(1)} collective-permute-done((f32[160,128]{1,0:T(8,128)S(1)}, f32[160,128]{1,0:T(8,128)S(1)}, u32[]{:S(2)}, u32[]{:S(2)}) %collective-permute-start.2) | collective-permute-done | bytes 81952 | tf_op jit(solution)/shard_map/ppermute | solution.py:778
  15.3 0.2 %faces.1.m_ref = f32[24,128]{1,0:T(8,128)S(1)} custom-call(f32[128,128]{1,0:T(8,128)S(1)} %get-tuple-element.36.own_ref, f32[80,128]{1,0:T(8,128)S(1)} %get-tuple-element.58.kept_ref, f32[160,128]{1,0:T(8,128)S(1)} %collective-permute-done.2.b2_ref.r2_ref, f32[88,128]{1,0:T(8,128)S(1)} %collective-permute-done.3.b1_ref.r1_ref, ...), custom_call_target="tpu_custom_call" | custom-call | tf_op jit(solution)/shard_map/faces/pallas_call | solution.py:430
  15.5 0.1 collective-permute-start.7
  15.6 0.0 collective-permute-done.6.last_ref
  15.6 0.0 collective-permute-done.4.one_ref
  15.6 0.0 collective-permute-done.5.two_ref
  15.6 1.8 %fine.1 = (f32[1024,128]{1,0:T(8,128)S(1)}, f32[1024,128]{1,0:T(8,128)S(1)}, f32[1024,128]{1,0:T(8,128)S(1)}, f32[1024,128]{1,0:T(8,128)S(1)}, f32[768,128]{1,0:T(8,128)S(1)}, /*index=5*/f32[128,128]{1,0:T(8,128)S(1)}) custom-call(f32[288,128]{1,0:T(8,128)S(1)} %get-tuple-element.38.strip_ref, f32[160,128]{1,0:T(8,128)S(1)} %collective-permute-done.2.b2_ref.r2_ref, ...), custom_call_target="tpu_custom_call" | custom-call | flops 9830400 | bytes 3932160 | tf_op jit(solution)/shard_map/fine/pallas_call | solution.py:683
  17.5 0.0 collective-permute-done.7.r_ref
  17.5 1.3 %finish.1 = f32[768,128]{1,0:T(8,128)} custom-call(f32[1024,128]{1,0:T(8,128)S(1)} %get-tuple-element.52.cx_ref, f32[1024,128]{1,0:T(8,128)S(1)} %get-tuple-element.53.inv_ref, f32[1024,128]{1,0:T(8,128)S(1)} %get-tuple-element.54.q_ref, f32[1024,128]{1,0:T(8,128)S(1)} %get-tuple-element.55.v_ref, f32[768,128]{1,0:T(8,128)S(1)} %get-tuple-element.56.sum_ref, ...), custom_call_target="tpu_custom_call" | custom-call | tf_op jit(solution)/shard_map/finish/pallas_call | solution.py:758
Async XLA Ops:
  0.0 13.7 %copy-start = (f32[32,24,128]{2,1,0:T(8,128)S(1)}, f32[32,24,128]{2,1,0:T(8,128)}, u32[]{:S(2)}) copy-start(f32[32,24,128]{2,1,0:T(8,128)} %param.3) | copy-start | bytes 1179652
  0.0 13.7 %copy-start.1 = (f32[32,24,128]{2,1,0:T(8,128)S(1)}, f32[32,24,128]{2,1,0:T(8,128)}, u32[]{:S(2)}) copy-start(f32[32,24,128]{2,1,0:T(8,128)} %param.5) | copy-start | bytes 1179652
  2.5 5.7 %collective-permute-start = (f32[176,128]{1,0:T(8,128)S(1)}, f32[176,128]{1,0:T(8,128)S(1)}, u32[]{:S(2)}, u32[]{:S(2)}) collective-permute-start(f32[176,128]{1,0:T(8,128)S(1)} %get-tuple-element.34.q_ref), channel_id=1, source_target_pairs={{0,1},{1,0},{2,3},{3,2},{4,5},{5,4},{6,7},{7,6},{8,9},{9,8},{10,11... | collective-permute-start | bytes 270344 | tf_op jit(solution)/shard_map/ppermute | solution.py:778
  5.6 10.0 %collective-permute-start.6 = (f32[256,128]{1,0:T(8,128)S(1)}, f32[256,128]{1,0:T(8,128)S(1)}, u32[]{:S(2)}, u32[]{:S(2)}) collective-permute-start(f32[256,128]{1,0:T(8,128)S(1)} %get-tuple-element.43), channel_id=1, source_target_pairs={{0,2},{1,3},{2,4},{3,5},{4,6},{5,7},{6,8},{7,9},{8,10},{9,11},{10,... | collective-permute-start | bytes 393224 | tf_op jit(solution)/shard_map/ppermute | solution.py:778
  5.6 2.5 %collective-permute-start.1 = (f32[72,128]{1,0:T(8,128)S(1)}, f32[72,128]{1,0:T(8,128)S(1)}, u32[]{:S(2)}, u32[]{:S(2)}) collective-permute-start(f32[72,128]{1,0:T(8,128)S(1)} %get-tuple-element.35), channel_id=1, source_target_pairs={{0,2},{1,3},{2,0},{3,1},{4,6},{5,7},{6,4},{7,5},{8,10},{9,11},{10,... | collective-permute-start | bytes 110600 | tf_op jit(solution)/shard_map/ppermute | solution.py:778
  8.5 6.7 %collective-permute-start.2 = (f32[160,128]{1,0:T(8,128)S(1)}, f32[160,128]{1,0:T(8,128)S(1)}, u32[]{:S(2)}, u32[]{:S(2)}) collective-permute-start(f32[160,128]{1,0:T(8,128)S(1)} %get-tuple-element.39), channel_id=1, source_target_pairs={{0,30},{1,31},{2,4},{3,5},{4,2},{5,3},{6,8},{7,9},{8,6},{9,7},{10,... | collective-permute-start | bytes 245768 | tf_op jit(solution)/shard_map/ppermute | solution.py:778
  11.8 3.8 %collective-permute-start.4 = (f32[128,128]{1,0:T(8,128)S(1)}, f32[128,128]{1,0:T(8,128)S(1)}, u32[]{:S(2)}, u32[]{:S(2)}) collective-permute-start(f32[128,128]{1,0:T(8,128)S(1)} %get-tuple-element.41), channel_id=1, source_target_pairs={{0,30},{1,31},{2,0},{3,1},{4,2},{5,3},{6,4},{7,5},{8,6},{9,7},{10,... | collective-permute-start | bytes 196616 | tf_op jit(solution)/shard_map/ppermute | solution.py:778
  13.0 2.6 %collective-permute-start.5 = (f32[128,128]{1,0:T(8,128)S(1)}, f32[128,128]{1,0:T(8,128)S(1)}, u32[]{:S(2)}, u32[]{:S(2)}) collective-permute-start(f32[128,128]{1,0:T(8,128)S(1)} %get-tuple-element.42), channel_id=1, source_target_pairs={{0,30},{1,31},{2,0},{3,1},{4,2},{5,3},{6,4},{7,5},{8,6},{9,7},{10,... | collective-permute-start | bytes 196616 | tf_op jit(solution)/shard_map/ppermute | solution.py:778
  13.7 1.2 %collective-permute-start.3 = (f32[88,128]{1,0:T(8,128)S(1)}, f32[88,128]{1,0:T(8,128)S(1)}, u32[]{:S(2)}, u32[]{:S(2)}) collective-permute-start(f32[88,128]{1,0:T(8,128)S(1)} %get-tuple-element.40), channel_id=1, source_target_pairs={{0,2},{1,3},{2,0},{3,1},{4,6},{5,7},{6,4},{7,5},{8,10},{9,11},{10,... | collective-permute-start | bytes 135176 | tf_op jit(solution)/shard_map/ppermute | solution.py:778
  15.5 2.0 %collective-permute-start.7 = (f32[24,128]{1,0:T(8,128)S(1)}, f32[24,128]{1,0:T(8,128)S(1)}, u32[]{:S(2)}, u32[]{:S(2)}) collective-permute-start(f32[24,128]{1,0:T(8,128)S(1)} %faces.1.m_ref), channel_id=1, source_target_pairs={{0,2},{1,3},{2,0},{3,1},{4,6},{5,7},{6,4},{7,5},{8,10},{9,11},{10,... | collective-permute-start | bytes 36872 | tf_op jit(solution)/shard_map/ppermute | solution.py:778

commit v9 on v8

--- a/solution.py
+++ b/solution.py
@@ -207,11 +207,11 @@
                 corners = jnp.where(group == g, rolled(both[second], g * GROUP + RIM, 1), corners)
         q_ref[zs * nx : base] = corners
 
-    section(finish)
+    finish()
 
 
 def pack(u, s, c, nz, nx):
-    pieces = 4
+    pieces = 1
     return pl.pallas_call(
         functools.partial(pack_kernel, nz=nz, nx=nx),
         out_shape=(

time: 18.9 us -> 18.7 us (0.989)
  Pallas kernels: 6.83 us -> 6.61 us
    pallas_call x1, Pallas kernels: 2.53 us -> 2.31 us  [pack(): pl.pallas_call(functools.partial(pack_kernel, nz=nz, nx=nx), out_shape=(t...]
where the time goes in v9:
time: 18.7 us; the launch traced here: 18.6 us
  starting transfers between devices  9.87 us (53%)
  Pallas kernels  6.61 us (35%)
  waiting for transfers between devices  1.99 us (11%)
    ppermute x8, starting transfers between devices, send(): return lax.ppermute(x, ('gx', 'gy'), pairs)  9.87 us
    pallas_call x1, Pallas kernels, pack(): pl.pallas_call(functools.partial(pack_kernel, nz=nz, nx=nx), out_shape=(t...  2.31 us
    ppermute x8, waiting for transfers between devices, send(): return lax.ppermute(x, ('gx', 'gy'), pairs)  1.99 us
    pallas_call x1, Pallas kernels, fine(): pl.pallas_call(functools.partial(fine_kernel, nz=nz, nx=nx), out_shape=(f...  1.85 us
    pallas_call x1, Pallas kernels, finish(): pl.pallas_call(functools.partial(finish_kernel, nz=nz, nx=nx), out_shape=...  1.27 us
    pallas_call x1, Pallas kernels, begin(): pl.pallas_call(functools.partial(begin_kernel, nz=nz, nx=nx), out_shape=(...  0.59 us
  transfers between devices with their start and end apart: 8, of which 4 were waited for; matrix products, arithmetic and copies ran while one was open for 0% of the time, Pallas kernels for 16%

profile of v9, /device:TPU:0, one launch (start us, length us, event | category | flops | bytes accessed | tf_op | source)
XLA Modules:
  0.0 18.6 jit_solution(6306489970991017699)
XLA Ops:
  0.0 0.0 copy-start
  0.0 0.0 copy-start.1
  0.0 2.3 %pack.1 = (f32[176,128]{1,0:T(8,128)S(1)}, f32[72,128]{1,0:T(8,128)S(1)}, f32[256,128]{1,0:T(8,128)S(1)}, f32[128,128]{1,0:T(8,128)S(1)}, f32[128,128]{1,0:T(8,1...) custom-call(f32[768,128]{1,0:T(8,128)} %bitcast.4, f32[768,128]{1,0:T(8,128)} %bitcast.10, f32[768,128]{1,0:T(8,128)} %bitcast.7), custom_call_target="tpu_custom_call" | custom-call | tf_op jit(solution)/shard_map/pack/pallas_call | solution.py:215
  2.3 3.0 %collective-permute-start = (f32[176,128]{1,0:T(8,128)S(1)}, f32[176,128]{1,0:T(8,128)S(1)}, u32[]{:S(2)}, u32[]{:S(2)}) collective-permute-start(f32[176,128]{1,0:T(8,128)S(1)} %get-tuple-element.34.q_ref), channel_id=1, source_target_pairs={{0,1},{1,0},{2,3},{3,2},{4,5},{5,4},{6,7},{7,6},{8,9},{9,8},{10,11... | collective-permute-start | bytes 270344 | tf_op jit(solution)/shard_map/ppermute | solution.py:778
  5.4 0.0 collective-permute-start.6
  5.4 1.6 %collective-permute-start.1 = (f32[72,128]{1,0:T(8,128)S(1)}, f32[72,128]{1,0:T(8,128)S(1)}, u32[]{:S(2)}, u32[]{:S(2)}) collective-permute-start(f32[72,128]{1,0:T(8,128)S(1)} %get-tuple-element.35), channel_id=1, source_target_pairs={{0,2},{1,3},{2,0},{3,1},{4,6},{5,7},{6,4},{7,5},{8,10},{9,11},{10,... | collective-permute-start | bytes 110600 | tf_op jit(solution)/shard_map/ppermute | solution.py:778
  7.0 0.9 %collective-permute-done.1.f1_ref = f32[72,128]{1,0:T(8,128)S(1)} collective-permute-done((f32[72,128]{1,0:T(8,128)S(1)}, f32[72,128]{1,0:T(8,128)S(1)}, u32[]{:S(2)}, u32[]{:S(2)}) %collective-permute-start.1) | collective-permute-done | bytes 36896 | tf_op jit(solution)/shard_map/ppermute | solution.py:778
  7.8 0.1 collective-permute-done.ql_ref.qr_ref
  8.0 0.3 %join.1 = (f32[88,128]{1,0:T(8,128)S(1)}, f32[160,128]{1,0:T(8,128)S(1)}, f32[288,128]{1,0:T(8,128)S(1)}, f32[80,128]{1,0:T(8,128)S(1)}) custom-call(f32[176,128]{1,0:T(8,128)S(1)} %get-tuple-element.34.q_ref, f32[176,128]{1,0:T(8,128)S(1)} %collective-permute-done.ql_ref.qr_ref, f32[176,128]{1,0:T(8,128)S(1)} %collective-permute-done.ql_ref.qr_ref, ...), custom_call_target="tpu_custom_call" | custom-call | tf_op jit(solution)/shard_map/join/pallas_call | solution.py:348
  8.3 3.3 %collective-permute-start.2 = (f32[160,128]{1,0:T(8,128)S(1)}, f32[160,128]{1,0:T(8,128)S(1)}, u32[]{:S(2)}, u32[]{:S(2)}) collective-permute-start(f32[160,128]{1,0:T(8,128)S(1)} %get-tuple-element.39), channel_id=1, source_target_pairs={{0,30},{1,31},{2,4},{3,5},{4,2},{5,3},{6,8},{7,9},{8,6},{9,7},{10,... | collective-permute-start | bytes 245768 | tf_op jit(solution)/shard_map/ppermute | solution.py:778
  11.6 1.2 %collective-permute-start.4 = (f32[128,128]{1,0:T(8,128)S(1)}, f32[128,128]{1,0:T(8,128)S(1)}, u32[]{:S(2)}, u32[]{:S(2)}) collective-permute-start(f32[128,128]{1,0:T(8,128)S(1)} %get-tuple-element.41), channel_id=1, source_target_pairs={{0,30},{1,31},{2,0},{3,1},{4,2},{5,3},{6,4},{7,5},{8,6},{9,7},{10,... | collective-permute-start | bytes 196616 | tf_op jit(solution)/shard_map/ppermute | solution.py:778
  12.8 0.7 %collective-permute-start.5 = (f32[128,128]{1,0:T(8,128)S(1)}, f32[128,128]{1,0:T(8,128)S(1)}, u32[]{:S(2)}, u32[]{:S(2)}) collective-permute-start(f32[128,128]{1,0:T(8,128)S(1)} %get-tuple-element.42), channel_id=1, source_target_pairs={{0,30},{1,31},{2,0},{3,1},{4,2},{5,3},{6,4},{7,5},{8,6},{9,7},{10,... | collective-permute-start | bytes 196616 | tf_op jit(solution)/shard_map/ppermute | solution.py:778
  13.5 0.0 collective-permute-start.3
  13.5 0.0 copy-done
  13.5 0.0 copy-done.1
  13.5 0.6 %begin.1 = (f32[768,128]{1,0:T(8,128)S(1)}, f32[768,128]{1,0:T(8,128)S(1)}, f32[768,128]{1,0:T(8,128)S(1)}, f32[768,128]{1,0:T(8,128)S(1)}, f32[256,128]{1,0:T(8...) custom-call(f32[288,128]{1,0:T(8,128)S(1)} %get-tuple-element.38.strip_ref, f32[768,128]{1,0:T(8,128)S(1)} %bitcast.5, ...), custom_call_target="tpu_custom_call" | custom-call | flops 3932160 | bytes 3932160 | tf_op jit(solution)/shard_map/begin/pallas_call | solution.py:519
  14.1 0.6 %collective-permute-done.3.b1_ref.r1_ref = f32[88,128]{1,0:T(8,128)S(1)} collective-permute-done((f32[88,128]{1,0:T(8,128)S(1)}, f32[88,128]{1,0:T(8,128)S(1)}, u32[]{:S(2)}, u32[]{:S(2)}) %collective-permute-start.3) | collective-permute-done | bytes 45088 | tf_op jit(solution)/shard_map/ppermute | solution.py:778
  14.7 0.3 %collective-permute-done.2.b2_ref.r2_ref = f32[160,128]{1,0:T(8,128)S(1)} collective-permute-done((f32[160,128]{1,0:T(8,128)S(1)}, f32[160,128]{1,0:T(8,128)S(1)}, u32[]{:S(2)}, u32[]{:S(2)}) %collective-permute-start.2) | collective-permute-done | bytes 81952 | tf_op jit(solution)/shard_map/ppermute | solution.py:778
  15.1 0.2 %faces.1.m_ref = f32[24,128]{1,0:T(8,128)S(1)} custom-call(f32[128,128]{1,0:T(8,128)S(1)} %get-tuple-element.36.own_ref, f32[80,128]{1,0:T(8,128)S(1)} %get-tuple-element.58.kept_ref, f32[160,128]{1,0:T(8,128)S(1)} %collective-permute-done.2.b2_ref.r2_ref, f32[88,128]{1,0:T(8,128)S(1)} %collective-permute-done.3.b1_ref.r1_ref, ...), custom_call_target="tpu_custom_call" | custom-call | tf_op jit(solution)/shard_map/faces/pallas_call | solution.py:430
  15.3 0.1 collective-permute-start.7
  15.4 0.0 collective-permute-done.6.last_ref
  15.4 0.0 collective-permute-done.4.one_ref
  15.4 0.0 collective-permute-done.5.two_ref
  15.4 1.8 %fine.1 = (f32[1024,128]{1,0:T(8,128)S(1)}, f32[1024,128]{1,0:T(8,128)S(1)}, f32[1024,128]{1,0:T(8,128)S(1)}, f32[1024,128]{1,0:T(8,128)S(1)}, f32[768,128]{1,0:T(8,128)S(1)}, /*index=5*/f32[128,128]{1,0:T(8,128)S(1)}) custom-call(f32[288,128]{1,0:T(8,128)S(1)} %get-tuple-element.38.strip_ref, f32[160,128]{1,0:T(8,128)S(1)} %collective-permute-done.2.b2_ref.r2_ref, ...), custom_call_target="tpu_custom_call" | custom-call | flops 9830400 | bytes 3932160 | tf_op jit(solution)/shard_map/fine/pallas_call | solution.py:683
  17.3 0.0 collective-permute-done.7.r_ref
  17.3 1.3 %finish.1 = f32[768,128]{1,0:T(8,128)} custom-call(f32[1024,128]{1,0:T(8,128)S(1)} %get-tuple-element.52.cx_ref, f32[1024,128]{1,0:T(8,128)S(1)} %get-tuple-element.53.inv_ref, f32[1024,128]{1,0:T(8,128)S(1)} %get-tuple-element.54.q_ref, f32[1024,128]{1,0:T(8,128)S(1)} %get-tuple-element.55.v_ref, f32[768,128]{1,0:T(8,128)S(1)} %get-tuple-element.56.sum_ref, ...), custom_call_target="tpu_custom_call" | custom-call | tf_op jit(solution)/shard_map/finish/pallas_call | solution.py:758
Async XLA Ops:
  0.0 13.5 %copy-start = (f32[32,24,128]{2,1,0:T(8,128)S(1)}, f32[32,24,128]{2,1,0:T(8,128)}, u32[]{:S(2)}) copy-start(f32[32,24,128]{2,1,0:T(8,128)} %param.3) | copy-start | bytes 1179652
  0.0 13.5 %copy-start.1 = (f32[32,24,128]{2,1,0:T(8,128)S(1)}, f32[32,24,128]{2,1,0:T(8,128)}, u32[]{:S(2)}) copy-start(f32[32,24,128]{2,1,0:T(8,128)} %param.5) | copy-start | bytes 1179652
  2.3 5.7 %collective-permute-start = (f32[176,128]{1,0:T(8,128)S(1)}, f32[176,128]{1,0:T(8,128)S(1)}, u32[]{:S(2)}, u32[]{:S(2)}) collective-permute-start(f32[176,128]{1,0:T(8,128)S(1)} %get-tuple-element.34.q_ref), channel_id=1, source_target_pairs={{0,1},{1,0},{2,3},{3,2},{4,5},{5,4},{6,7},{7,6},{8,9},{9,8},{10,11... | collective-permute-start | bytes 270344 | tf_op jit(solution)/shard_map/ppermute | solution.py:778
  5.4 10.0 %collective-permute-start.6 = (f32[256,128]{1,0:T(8,128)S(1)}, f32[256,128]{1,0:T(8,128)S(1)}, u32[]{:S(2)}, u32[]{:S(2)}) collective-permute-start(f32[256,128]{1,0:T(8,128)S(1)} %get-tuple-element.43), channel_id=1, source_target_pairs={{0,2},{1,3},{2,4},{3,5},{4,6},{5,7},{6,8},{7,9},{8,10},{9,11},{10,... | collective-permute-start | bytes 393224 | tf_op jit(solution)/shard_map/ppermute | solution.py:778
  5.4 2.5 %collective-permute-start.1 = (f32[72,128]{1,0:T(8,128)S(1)}, f32[72,128]{1,0:T(8,128)S(1)}, u32[]{:S(2)}, u32[]{:S(2)}) collective-permute-start(f32[72,128]{1,0:T(8,128)S(1)} %get-tuple-element.35), channel_id=1, source_target_pairs={{0,2},{1,3},{2,0},{3,1},{4,6},{5,7},{6,4},{7,5},{8,10},{9,11},{10,... | collective-permute-start | bytes 110600 | tf_op jit(solution)/shard_map/ppermute | solution.py:778
  8.3 6.7 %collective-permute-start.2 = (f32[160,128]{1,0:T(8,128)S(1)}, f32[160,128]{1,0:T(8,128)S(1)}, u32[]{:S(2)}, u32[]{:S(2)}) collective-permute-start(f32[160,128]{1,0:T(8,128)S(1)} %get-tuple-element.39), channel_id=1, source_target_pairs={{0,30},{1,31},{2,4},{3,5},{4,2},{5,3},{6,8},{7,9},{8,6},{9,7},{10,... | collective-permute-start | bytes 245768 | tf_op jit(solution)/shard_map/ppermute | solution.py:778
  11.6 3.8 %collective-permute-start.4 = (f32[128,128]{1,0:T(8,128)S(1)}, f32[128,128]{1,0:T(8,128)S(1)}, u32[]{:S(2)}, u32[]{:S(2)}) collective-permute-start(f32[128,128]{1,0:T(8,128)S(1)} %get-tuple-element.41), channel_id=1, source_target_pairs={{0,30},{1,31},{2,0},{3,1},{4,2},{5,3},{6,4},{7,5},{8,6},{9,7},{10,... | collective-permute-start | bytes 196616 | tf_op jit(solution)/shard_map/ppermute | solution.py:778
  12.8 2.6 %collective-permute-start.5 = (f32[128,128]{1,0:T(8,128)S(1)}, f32[128,128]{1,0:T(8,128)S(1)}, u32[]{:S(2)}, u32[]{:S(2)}) collective-permute-start(f32[128,128]{1,0:T(8,128)S(1)} %get-tuple-element.42), channel_id=1, source_target_pairs={{0,30},{1,31},{2,0},{3,1},{4,2},{5,3},{6,4},{7,5},{8,6},{9,7},{10,... | collective-permute-start | bytes 196616 | tf_op jit(solution)/shard_map/ppermute | solution.py:778
  13.5 1.2 %collective-permute-start.3 = (f32[88,128]{1,0:T(8,128)S(1)}, f32[88,128]{1,0:T(8,128)S(1)}, u32[]{:S(2)}, u32[]{:S(2)}) collective-permute-start(f32[88,128]{1,0:T(8,128)S(1)} %get-tuple-element.40), channel_id=1, source_target_pairs={{0,2},{1,3},{2,0},{3,1},{4,6},{5,7},{6,4},{7,5},{8,10},{9,11},{10,... | collective-permute-start | bytes 135176 | tf_op jit(solution)/shard_map/ppermute | solution.py:778
  15.3 2.0 %collective-permute-start.7 = (f32[24,128]{1,0:T(8,128)S(1)}, f32[24,128]{1,0:T(8,128)S(1)}, u32[]{:S(2)}, u32[]{:S(2)}) collective-permute-start(f32[24,128]{1,0:T(8,128)S(1)} %faces.1.m_ref), channel_id=1, source_target_pairs={{0,2},{1,3},{2,0},{3,1},{4,6},{5,7},{6,4},{7,5},{8,10},{9,11},{10,... | collective-permute-start | bytes 36872 | tf_op jit(solution)/shard_map/ppermute | solution.py:778

commit v10 on v9

--- a/solution.py
+++ b/solution.py
@@ -86,10 +86,6 @@
     source = jnp.clip(column * COARSEN, 0, LANES - COARSEN)
     here = (plane == place) & (column >= 0) & (column < WIDTH)
     return jnp.where(here, gathered(rows, source), 0.0)
-
-
-def section(run):
-    pl.when(lax.axis_index("gx") >= 0)(run)
 
 
 def block_rows(values):

time: 18.7 us -> 18.7 us (level)
  no operation moved by 1% of the time
where the time goes in v10:
time: 18.7 us; the launch traced here: 18.6 us
  starting transfers between devices  9.87 us (53%)
  Pallas kernels  6.61 us (35%)
  waiting for transfers between devices  1.99 us (11%)
    ppermute x8, starting transfers between devices, send(): return lax.ppermute(x, ('gx', 'gy'), pairs)  9.87 us
    pallas_call x1, Pallas kernels, pack(): pl.pallas_call(functools.partial(pack_kernel, nz=nz, nx=nx), out_shape=(t...  2.31 us
    ppermute x8, waiting for transfers between devices, send(): return lax.ppermute(x, ('gx', 'gy'), pairs)  1.99 us
    pallas_call x1, Pallas kernels, fine(): pl.pallas_call(functools.partial(fine_kernel, nz=nz, nx=nx), out_shape=(f...  1.85 us
    pallas_call x1, Pallas kernels, finish(): pl.pallas_call(functools.partial(finish_kernel, nz=nz, nx=nx), out_shape=...  1.27 us
    pallas_call x1, Pallas kernels, begin(): pl.pallas_call(functools.partial(begin_kernel, nz=nz, nx=nx), out_shape=(...  0.59 us
  transfers between devices with their start and end apart: 8, of which 4 were waited for; matrix products, arithmetic and copies ran while one was open for 0% of the time, Pallas kernels for 16%

profile of v10, /device:TPU:0, one launch (start us, length us, event | category | flops | bytes accessed | tf_op | source)
XLA Modules:
  0.0 18.6 jit_solution(6306489970991017699)
XLA Ops:
  0.0 0.0 copy-start
  0.0 0.0 copy-start.1
  0.0 2.3 %pack.1 = (f32[176,128]{1,0:T(8,128)S(1)}, f32[72,128]{1,0:T(8,128)S(1)}, f32[256,128]{1,0:T(8,128)S(1)}, f32[128,128]{1,0:T(8,128)S(1)}, f32[128,128]{1,0:T(8,1...) custom-call(f32[768,128]{1,0:T(8,128)} %bitcast.4, f32[768,128]{1,0:T(8,128)} %bitcast.10, f32[768,128]{1,0:T(8,128)} %bitcast.7), custom_call_target="tpu_custom_call" | custom-call | tf_op jit(solution)/shard_map/pack/pallas_call | solution.py:211
  2.3 3.0 %collective-permute-start = (f32[176,128]{1,0:T(8,128)S(1)}, f32[176,128]{1,0:T(8,128)S(1)}, u32[]{:S(2)}, u32[]{:S(2)}) collective-permute-start(f32[176,128]{1,0:T(8,128)S(1)} %get-tuple-element.34.q_ref), channel_id=1, source_target_pairs={{0,1},{1,0},{2,3},{3,2},{4,5},{5,4},{6,7},{7,6},{8,9},{9,8},{10,11... | collective-permute-start | bytes 270344 | tf_op jit(solution)/shard_map/ppermute | solution.py:774
  5.4 0.0 collective-permute-start.6
  5.4 1.6 %collective-permute-start.1 = (f32[72,128]{1,0:T(8,128)S(1)}, f32[72,128]{1,0:T(8,128)S(1)}, u32[]{:S(2)}, u32[]{:S(2)}) collective-permute-start(f32[72,128]{1,0:T(8,128)S(1)} %get-tuple-element.35), channel_id=1, source_target_pairs={{0,2},{1,3},{2,0},{3,1},{4,6},{5,7},{6,4},{7,5},{8,10},{9,11},{10,... | collective-permute-start | bytes 110600 | tf_op jit(solution)/shard_map/ppermute | solution.py:774
  7.0 0.9 %collective-permute-done.1.f1_ref = f32[72,128]{1,0:T(8,128)S(1)} collective-permute-done((f32[72,128]{1,0:T(8,128)S(1)}, f32[72,128]{1,0:T(8,128)S(1)}, u32[]{:S(2)}, u32[]{:S(2)}) %collective-permute-start.1) | collective-permute-done | bytes 36896 | tf_op jit(solution)/shard_map/ppermute | solution.py:774
  7.8 0.1 collective-permute-done.ql_ref.qr_ref
  8.0 0.3 %join.1 = (f32[88,128]{1,0:T(8,128)S(1)}, f32[160,128]{1,0:T(8,128)S(1)}, f32[288,128]{1,0:T(8,128)S(1)}, f32[80,128]{1,0:T(8,128)S(1)}) custom-call(f32[176,128]{1,0:T(8,128)S(1)} %get-tuple-element.34.q_ref, f32[176,128]{1,0:T(8,128)S(1)} %collective-permute-done.ql_ref.qr_ref, f32[176,128]{1,0:T(8,128)S(1)} %collective-permute-done.ql_ref.qr_ref, ...), custom_call_target="tpu_custom_call" | custom-call | tf_op jit(solution)/shard_map/join/pallas_call | solution.py:344
  8.3 3.3 %collective-permute-start.2 = (f32[160,128]{1,0:T(8,128)S(1)}, f32[160,128]{1,0:T(8,128)S(1)}, u32[]{:S(2)}, u32[]{:S(2)}) collective-permute-start(f32[160,128]{1,0:T(8,128)S(1)} %get-tuple-element.39), channel_id=1, source_target_pairs={{0,30},{1,31},{2,4},{3,5},{4,2},{5,3},{6,8},{7,9},{8,6},{9,7},{10,... | collective-permute-start | bytes 245768 | tf_op jit(solution)/shard_map/ppermute | solution.py:774
  11.6 1.2 %collective-permute-start.4 = (f32[128,128]{1,0:T(8,128)S(1)}, f32[128,128]{1,0:T(8,128)S(1)}, u32[]{:S(2)}, u32[]{:S(2)}) collective-permute-start(f32[128,128]{1,0:T(8,128)S(1)} %get-tuple-element.41), channel_id=1, source_target_pairs={{0,30},{1,31},{2,0},{3,1},{4,2},{5,3},{6,4},{7,5},{8,6},{9,7},{10,... | collective-permute-start | bytes 196616 | tf_op jit(solution)/shard_map/ppermute | solution.py:774
  12.8 0.7 %collective-permute-start.5 = (f32[128,128]{1,0:T(8,128)S(1)}, f32[128,128]{1,0:T(8,128)S(1)}, u32[]{:S(2)}, u32[]{:S(2)}) collective-permute-start(f32[128,128]{1,0:T(8,128)S(1)} %get-tuple-element.42), channel_id=1, source_target_pairs={{0,30},{1,31},{2,0},{3,1},{4,2},{5,3},{6,4},{7,5},{8,6},{9,7},{10,... | collective-permute-start | bytes 196616 | tf_op jit(solution)/shard_map/ppermute | solution.py:774
  13.5 0.0 collective-permute-start.3
  13.5 0.0 copy-done
  13.5 0.0 copy-done.1
  13.5 0.6 %begin.1 = (f32[768,128]{1,0:T(8,128)S(1)}, f32[768,128]{1,0:T(8,128)S(1)}, f32[768,128]{1,0:T(8,128)S(1)}, f32[768,128]{1,0:T(8,128)S(1)}, f32[256,128]{1,0:T(8...) custom-call(f32[288,128]{1,0:T(8,128)S(1)} %get-tuple-element.38.strip_ref, f32[768,128]{1,0:T(8,128)S(1)} %bitcast.5, ...), custom_call_target="tpu_custom_call" | custom-call | flops 3932160 | bytes 3932160 | tf_op jit(solution)/shard_map/begin/pallas_call | solution.py:515
  14.1 0.6 %collective-permute-done.3.b1_ref.r1_ref = f32[88,128]{1,0:T(8,128)S(1)} collective-permute-done((f32[88,128]{1,0:T(8,128)S(1)}, f32[88,128]{1,0:T(8,128)S(1)}, u32[]{:S(2)}, u32[]{:S(2)}) %collective-permute-start.3) | collective-permute-done | bytes 45088 | tf_op jit(solution)/shard_map/ppermute | solution.py:774
  14.7 0.3 %collective-permute-done.2.b2_ref.r2_ref = f32[160,128]{1,0:T(8,128)S(1)} collective-permute-done((f32[160,128]{1,0:T(8,128)S(1)}, f32[160,128]{1,0:T(8,128)S(1)}, u32[]{:S(2)}, u32[]{:S(2)}) %collective-permute-start.2) | collective-permute-done | bytes 81952 | tf_op jit(solution)/shard_map/ppermute | solution.py:774
  15.1 0.2 %faces.1.m_ref = f32[24,128]{1,0:T(8,128)S(1)} custom-call(f32[128,128]{1,0:T(8,128)S(1)} %get-tuple-element.36.own_ref, f32[80,128]{1,0:T(8,128)S(1)} %get-tuple-element.58.kept_ref, f32[160,128]{1,0:T(8,128)S(1)} %collective-permute-done.2.b2_ref.r2_ref, f32[88,128]{1,0:T(8,128)S(1)} %collective-permute-done.3.b1_ref.r1_ref, ...), custom_call_target="tpu_custom_call" | custom-call | tf_op jit(solution)/shard_map/faces/pallas_call | solution.py:426
  15.3 0.1 collective-permute-start.7
  15.4 0.0 collective-permute-done.6.last_ref
  15.4 0.0 collective-permute-done.4.one_ref
  15.4 0.0 collective-permute-done.5.two_ref
  15.4 1.8 %fine.1 = (f32[1024,128]{1,0:T(8,128)S(1)}, f32[1024,128]{1,0:T(8,128)S(1)}, f32[1024,128]{1,0:T(8,128)S(1)}, f32[1024,128]{1,0:T(8,128)S(1)}, f32[768,128]{1,0:T(8,128)S(1)}, /*index=5*/f32[128,128]{1,0:T(8,128)S(1)}) custom-call(f32[288,128]{1,0:T(8,128)S(1)} %get-tuple-element.38.strip_ref, f32[160,128]{1,0:T(8,128)S(1)} %collective-permute-done.2.b2_ref.r2_ref, ...), custom_call_target="tpu_custom_call" | custom-call | flops 9830400 | bytes 3932160 | tf_op jit(solution)/shard_map/fine/pallas_call | solution.py:679
  17.3 0.0 collective-permute-done.7.r_ref
  17.3 1.3 %finish.1 = f32[768,128]{1,0:T(8,128)} custom-call(f32[1024,128]{1,0:T(8,128)S(1)} %get-tuple-element.52.cx_ref, f32[1024,128]{1,0:T(8,128)S(1)} %get-tuple-element.53.inv_ref, f32[1024,128]{1,0:T(8,128)S(1)} %get-tuple-element.54.q_ref, f32[1024,128]{1,0:T(8,128)S(1)} %get-tuple-element.55.v_ref, f32[768,128]{1,0:T(8,128)S(1)} %get-tuple-element.56.sum_ref, ...), custom_call_target="tpu_custom_call" | custom-call | tf_op jit(solution)/shard_map/finish/pallas_call | solution.py:754
Async XLA Ops:
  0.0 13.5 %copy-start = (f32[32,24,128]{2,1,0:T(8,128)S(1)}, f32[32,24,128]{2,1,0:T(8,128)}, u32[]{:S(2)}) copy-start(f32[32,24,128]{2,1,0:T(8,128)} %param.3) | copy-start | bytes 1179652
  0.0 13.5 %copy-start.1 = (f32[32,24,128]{2,1,0:T(8,128)S(1)}, f32[32,24,128]{2,1,0:T(8,128)}, u32[]{:S(2)}) copy-start(f32[32,24,128]{2,1,0:T(8,128)} %param.5) | copy-start | bytes 1179652
  2.3 5.7 %collective-permute-start = (f32[176,128]{1,0:T(8,128)S(1)}, f32[176,128]{1,0:T(8,128)S(1)}, u32[]{:S(2)}, u32[]{:S(2)}) collective-permute-start(f32[176,128]{1,0:T(8,128)S(1)} %get-tuple-element.34.q_ref), channel_id=1, source_target_pairs={{0,1},{1,0},{2,3},{3,2},{4,5},{5,4},{6,7},{7,6},{8,9},{9,8},{10,11... | collective-permute-start | bytes 270344 | tf_op jit(solution)/shard_map/ppermute | solution.py:774
  5.4 10.0 %collective-permute-start.6 = (f32[256,128]{1,0:T(8,128)S(1)}, f32[256,128]{1,0:T(8,128)S(1)}, u32[]{:S(2)}, u32[]{:S(2)}) collective-permute-start(f32[256,128]{1,0:T(8,128)S(1)} %get-tuple-element.43), channel_id=1, source_target_pairs={{0,2},{1,3},{2,4},{3,5},{4,6},{5,7},{6,8},{7,9},{8,10},{9,11},{10,... | collective-permute-start | bytes 393224 | tf_op jit(solution)/shard_map/ppermute | solution.py:774
  5.4 2.5 %collective-permute-start.1 = (f32[72,128]{1,0:T(8,128)S(1)}, f32[72,128]{1,0:T(8,128)S(1)}, u32[]{:S(2)}, u32[]{:S(2)}) collective-permute-start(f32[72,128]{1,0:T(8,128)S(1)} %get-tuple-element.35), channel_id=1, source_target_pairs={{0,2},{1,3},{2,0},{3,1},{4,6},{5,7},{6,4},{7,5},{8,10},{9,11},{10,... | collective-permute-start | bytes 110600 | tf_op jit(solution)/shard_map/ppermute | solution.py:774
  8.3 6.7 %collective-permute-start.2 = (f32[160,128]{1,0:T(8,128)S(1)}, f32[160,128]{1,0:T(8,128)S(1)}, u32[]{:S(2)}, u32[]{:S(2)}) collective-permute-start(f32[160,128]{1,0:T(8,128)S(1)} %get-tuple-element.39), channel_id=1, source_target_pairs={{0,30},{1,31},{2,4},{3,5},{4,2},{5,3},{6,8},{7,9},{8,6},{9,7},{10,... | collective-permute-start | bytes 245768 | tf_op jit(solution)/shard_map/ppermute | solution.py:774
  11.6 3.8 %collective-permute-start.4 = (f32[128,128]{1,0:T(8,128)S(1)}, f32[128,128]{1,0:T(8,128)S(1)}, u32[]{:S(2)}, u32[]{:S(2)}) collective-permute-start(f32[128,128]{1,0:T(8,128)S(1)} %get-tuple-element.41), channel_id=1, source_target_pairs={{0,30},{1,31},{2,0},{3,1},{4,2},{5,3},{6,4},{7,5},{8,6},{9,7},{10,... | collective-permute-start | bytes 196616 | tf_op jit(solution)/shard_map/ppermute | solution.py:774
  12.8 2.6 %collective-permute-start.5 = (f32[128,128]{1,0:T(8,128)S(1)}, f32[128,128]{1,0:T(8,128)S(1)}, u32[]{:S(2)}, u32[]{:S(2)}) collective-permute-start(f32[128,128]{1,0:T(8,128)S(1)} %get-tuple-element.42), channel_id=1, source_target_pairs={{0,30},{1,31},{2,0},{3,1},{4,2},{5,3},{6,4},{7,5},{8,6},{9,7},{10,... | collective-permute-start | bytes 196616 | tf_op jit(solution)/shard_map/ppermute | solution.py:774
  13.5 1.2 %collective-permute-start.3 = (f32[88,128]{1,0:T(8,128)S(1)}, f32[88,128]{1,0:T(8,128)S(1)}, u32[]{:S(2)}, u32[]{:S(2)}) collective-permute-start(f32[88,128]{1,0:T(8,128)S(1)} %get-tuple-element.40), channel_id=1, source_target_pairs={{0,2},{1,3},{2,0},{3,1},{4,6},{5,7},{6,4},{7,5},{8,10},{9,11},{10,... | collective-permute-start | bytes 135176 | tf_op jit(solution)/shard_map/ppermute | solution.py:774
  15.3 2.0 %collective-permute-start.7 = (f32[24,128]{1,0:T(8,128)S(1)}, f32[24,128]{1,0:T(8,128)S(1)}, u32[]{:S(2)}, u32[]{:S(2)}) collective-permute-start(f32[24,128]{1,0:T(8,128)S(1)} %faces.1.m_ref), channel_id=1, source_target_pairs={{0,2},{1,3},{2,0},{3,1},{4,6},{5,7},{6,4},{7,5},{8,10},{9,11},{10,... | collective-permute-start | bytes 36872 | tf_op jit(solution)/shard_map/ppermute | solution.py:774

commit v11 on v10

--- a/solution.py
+++ b/solution.py
@@ -309,12 +309,12 @@
     for u, c in zip(joined[0], joined[1]):
         flux = flux + (c + rolled(c, -1, 1)) * (u - rolled(u, -1, 1))
     flux = block_rows((0.5 / CELLS) * flux)
-    flux = flux + rolled(flux, -GROUP, 1)
-    near, far = RIM - 1, 3 * RIM - 1
-    change = jnp.where(place == RIM - 1, -rolled(flux, RIM - 1 - near, 1), 0.0)
-    change = jnp.where(place == RIM, rolled(flux, RIM - near, 1), change)
-    change = jnp.where(place == RIM + WIDTH - 1, -rolled(flux, RIM + WIDTH - 1 - far, 1), change)
-    change = jnp.where(place == RIM + WIDTH, rolled(flux, RIM + WIDTH - far, 1), change)
+    plane = part(lane, SPREAD)[0] * SPREAD
+    at_left, after = (place == RIM - 1) | (place == RIM), (place == RIM) | (place == RIM + WIDTH)
+    at_face = at_left | (place == RIM + WIDTH - 1) | (place == RIM + WIDTH)
+    face = plane + jnp.where(at_left, RIM - 1, 3 * RIM - 1)
+    flux = jnp.take_along_axis(flux, face, axis=1) + jnp.take_along_axis(flux, face + GROUP, axis=1)
+    change = jnp.where(at_face, jnp.where(after, flux, -flux), 0.0)
     rows = nx // COARSEN
     nearest = jnp.where(even, rows - 1, 0)
     for Z in range(nz // COARSEN):
@@ -324,14 +324,12 @@
     mate = f1_ref[2 * nz : 2 * nz + SUB]
     mate = jnp.where(even, rolled(mate, rows - RIM, 0), rolled(mate, 1 - RIM, 0))
     cond = jnp.where(sub == rows, mate, rolled(window, -RIM, 0))
-    rhs = window + change
-    kept_ref[2 * nz : 2 * nz + SUB] = cond
-    kept_ref[2 * nz + SUB :] = rhs
+    coarse = jnp.where(sub < RIM, window + change, rolled(cond, RIM, 0))
+    kept_ref[2 * nz :] = coarse
     to = target + nz
-    b1_ref[to:] = cond
-    b2_ref[to : to + SUB] = cond
-    b2_ref[to + SUB : to + 2 * SUB] = rhs
-    to = to + 2 * SUB
+    b1_ref[to:] = coarse
+    b2_ref[to : to + SUB] = coarse
+    to = to + SUB
     for a in range(2):
         for Z in range(nz // SUB):
             at = to + a * nz + Z * SUB
@@ -345,9 +343,9 @@
         functools.partial(join_kernel, nz=nz, nx=nx),
         out_shape=(
             tiles(size),
-            tiles(size + 1 + 2 * nz // SUB),
+            tiles(size + 2 * nz // SUB),
             jax.ShapeDtypeStruct((3 * zs * nx, LANES), f32),
-            tiles(2 * nz // SUB + 2),
+            tiles(2 * nz // SUB + 1),
         ),
         in_specs=[VMEM] * 5,
         out_specs=(VMEM,) * 4,
@@ -382,7 +380,7 @@
         return all_rows(0.5 * (mine(nz) + rolled(other, HALF, 1)) * (mine(0) - other))
 
     odd = jnp.logical_not(even)
-    far_rows = base + nz + 2 * SUB
+    far_rows = base + nz + SUB
     flux = jnp.zeros((SUB, LANES), f32)
     for Z in range(nz // COARSEN):
         u, c = (
@@ -402,15 +400,14 @@
         before, after = jnp.where(even, other, own), jnp.where(even, own, other)
         return jnp.where(sub <= rows, rolled(before, 1, 0), rolled(after, rows + 1, 0))
 
-    at = base + nz + SUB
-    rhs = stacked(kept_ref[2 * nz + SUB :], r2_ref[at : at + SUB])
+    at = base + nz
+    coarse, near_c, far_c = kept_ref[2 * nz :], r1_ref[at : at + SUB], r2_ref[at : at + SUB]
+    rhs = stacked(coarse, far_c)
     sign = jnp.where(even, 1.0, -1.0)
     rhs = rhs + jnp.where(sub == rows, sign * far, jnp.where(sub == rows + 1, -sign * far, 0.0))
     rhs = rhs - jnp.where(sub == jnp.where(even, 2 * rows, 1), mate, 0.0)
-
-    at = at - SUB
-    near_c, far_c = r1_ref[at : at + SUB], r2_ref[at : at + SUB]
-    cond = stacked(kept_ref[2 * nz : 2 * nz + SUB], far_c)
+    coarse, near_c, far_c = (rolled(x, -RIM, 0) for x in (coarse, near_c, far_c))
+    cond = stacked(coarse, far_c)
     before = jnp.where(even, rolled(far_c, -rows, 0), rolled(near_c, 1 - rows, 0))
     after = jnp.where(even, rolled(near_c, 2 * rows + 1, 0), rolled(far_c, rows + 1, 0))
     cond = jnp.where(sub == 0, before, jnp.where(sub == 2 * rows + 1, after, cond))

time: 18.7 us -> 18.7 us (level)
  no operation moved by 1% of the time
where the time goes in v11:
time: 18.7 us; the launch traced here: 18.5 us
  starting transfers between devices  9.88 us (53%)
  Pallas kernels  6.57 us (35%)
  waiting for transfers between devices  1.97 us (11%)
    ppermute x8, starting transfers between devices, send(): return lax.ppermute(x, ('gx', 'gy'), pairs)  9.88 us
    pallas_call x1, Pallas kernels, pack(): pl.pallas_call(functools.partial(pack_kernel, nz=nz, nx=nx), out_shape=(t...  2.29 us
    ppermute x8, waiting for transfers between devices, send(): return lax.ppermute(x, ('gx', 'gy'), pairs)  1.97 us
    pallas_call x1, Pallas kernels, fine(): pl.pallas_call(functools.partial(fine_kernel, nz=nz, nx=nx), out_shape=(f...  1.85 us
    pallas_call x1, Pallas kernels, finish(): pl.pallas_call(functools.partial(finish_kernel, nz=nz, nx=nx), out_shape=...  1.29 us
    pallas_call x1, Pallas kernels, begin(): pl.pallas_call(functools.partial(begin_kernel, nz=nz, nx=nx), out_shape=(...  0.59 us
  transfers between devices with their start and end apart: 8, of which 4 were waited for; matrix products, arithmetic and copies ran while one was open for 0% of the time, Pallas kernels for 16%

profile of v11, /device:TPU:0, one launch (start us, length us, event | category | flops | bytes accessed | tf_op | source)
XLA Modules:
  0.0 18.5 jit_solution(13445154507084573845)
XLA Ops:
  0.0 0.0 copy-start
  0.0 0.0 copy-start.1
  0.0 2.3 %pack.1 = (f32[176,128]{1,0:T(8,128)S(1)}, f32[72,128]{1,0:T(8,128)S(1)}, f32[256,128]{1,0:T(8,128)S(1)}, f32[128,128]{1,0:T(8,128)S(1)}, f32[128,128]{1,0:T(8,1...) custom-call(f32[768,128]{1,0:T(8,128)} %bitcast.4, f32[768,128]{1,0:T(8,128)} %bitcast.10, f32[768,128]{1,0:T(8,128)} %bitcast.7), custom_call_target="tpu_custom_call" | custom-call | tf_op jit(solution)/shard_map/pack/pallas_call | solution.py:211
  2.3 3.0 %collective-permute-start = (f32[176,128]{1,0:T(8,128)S(1)}, f32[176,128]{1,0:T(8,128)S(1)}, u32[]{:S(2)}, u32[]{:S(2)}) collective-permute-start(f32[176,128]{1,0:T(8,128)S(1)} %get-tuple-element.34.q_ref), channel_id=1, source_target_pairs={{0,1},{1,0},{2,3},{3,2},{4,5},{5,4},{6,7},{7,6},{8,9},{9,8},{10,11... | collective-permute-start | bytes 270344 | tf_op jit(solution)/shard_map/ppermute | solution.py:771
  5.3 0.0 collective-permute-start.6
  5.3 1.6 %collective-permute-start.1 = (f32[72,128]{1,0:T(8,128)S(1)}, f32[72,128]{1,0:T(8,128)S(1)}, u32[]{:S(2)}, u32[]{:S(2)}) collective-permute-start(f32[72,128]{1,0:T(8,128)S(1)} %get-tuple-element.35), channel_id=1, source_target_pairs={{0,2},{1,3},{2,0},{3,1},{4,6},{5,7},{6,4},{7,5},{8,10},{9,11},{10,... | collective-permute-start | bytes 110600 | tf_op jit(solution)/shard_map/ppermute | solution.py:771
  6.9 0.9 %collective-permute-done.1.f1_ref = f32[72,128]{1,0:T(8,128)S(1)} collective-permute-done((f32[72,128]{1,0:T(8,128)S(1)}, f32[72,128]{1,0:T(8,128)S(1)}, u32[]{:S(2)}, u32[]{:S(2)}) %collective-permute-start.1) | collective-permute-done | bytes 36896 | tf_op jit(solution)/shard_map/ppermute | solution.py:771
  7.8 0.1 collective-permute-done.ql_ref.qr_ref
  8.0 0.3 %join.1 = (f32[88,128]{1,0:T(8,128)S(1)}, f32[152,128]{1,0:T(8,128)S(1)}, f32[288,128]{1,0:T(8,128)S(1)}, f32[72,128]{1,0:T(8,128)S(1)}) custom-call(f32[176,128]{1,0:T(8,128)S(1)} %get-tuple-element.34.q_ref, f32[176,128]{1,0:T(8,128)S(1)} %collective-permute-done.ql_ref.qr_ref, f32[176,128]{1,0:T(8,128)S(1)} %collective-permute-done.ql_ref.qr_ref, ...), custom_call_target="tpu_custom_call" | custom-call | tf_op jit(solution)/shard_map/join/pallas_call | solution.py:342
  8.3 3.3 %collective-permute-start.2 = (f32[152,128]{1,0:T(8,128)S(1)}, f32[152,128]{1,0:T(8,128)S(1)}, u32[]{:S(2)}, u32[]{:S(2)}) collective-permute-start(f32[152,128]{1,0:T(8,128)S(1)} %get-tuple-element.39), channel_id=1, source_target_pairs={{0,30},{1,31},{2,4},{3,5},{4,2},{5,3},{6,8},{7,9},{8,6},{9,7},{10,... | collective-permute-start | bytes 233480 | tf_op jit(solution)/shard_map/ppermute | solution.py:771
  11.5 1.2 %collective-permute-start.4 = (f32[128,128]{1,0:T(8,128)S(1)}, f32[128,128]{1,0:T(8,128)S(1)}, u32[]{:S(2)}, u32[]{:S(2)}) collective-permute-start(f32[128,128]{1,0:T(8,128)S(1)} %get-tuple-element.41), channel_id=1, source_target_pairs={{0,30},{1,31},{2,0},{3,1},{4,2},{5,3},{6,4},{7,5},{8,6},{9,7},{10,... | collective-permute-start | bytes 196616 | tf_op jit(solution)/shard_map/ppermute | solution.py:771
  12.8 0.7 %collective-permute-start.5 = (f32[128,128]{1,0:T(8,128)S(1)}, f32[128,128]{1,0:T(8,128)S(1)}, u32[]{:S(2)}, u32[]{:S(2)}) collective-permute-start(f32[128,128]{1,0:T(8,128)S(1)} %get-tuple-element.42), channel_id=1, source_target_pairs={{0,30},{1,31},{2,0},{3,1},{4,2},{5,3},{6,4},{7,5},{8,6},{9,7},{10,... | collective-permute-start | bytes 196616 | tf_op jit(solution)/shard_map/ppermute | solution.py:771
  13.4 0.0 collective-permute-start.3
  13.4 0.0 copy-done
  13.4 0.0 copy-done.1
  13.4 0.6 %begin.1 = (f32[768,128]{1,0:T(8,128)S(1)}, f32[768,128]{1,0:T(8,128)S(1)}, f32[768,128]{1,0:T(8,128)S(1)}, f32[768,128]{1,0:T(8,128)S(1)}, f32[256,128]{1,0:T(8...) custom-call(f32[288,128]{1,0:T(8,128)S(1)} %get-tuple-element.38.strip_ref, f32[768,128]{1,0:T(8,128)S(1)} %bitcast.5, ...), custom_call_target="tpu_custom_call" | custom-call | flops 3932160 | bytes 3932160 | tf_op jit(solution)/shard_map/begin/pallas_call | solution.py:512
  14.0 0.6 %collective-permute-done.3.b1_ref.r1_ref = f32[88,128]{1,0:T(8,128)S(1)} collective-permute-done((f32[88,128]{1,0:T(8,128)S(1)}, f32[88,128]{1,0:T(8,128)S(1)}, u32[]{:S(2)}, u32[]{:S(2)}) %collective-permute-start.3) | collective-permute-done | bytes 45088 | tf_op jit(solution)/shard_map/ppermute | solution.py:771
  14.7 0.3 %collective-permute-done.2.b2_ref.r2_ref = f32[152,128]{1,0:T(8,128)S(1)} collective-permute-done((f32[152,128]{1,0:T(8,128)S(1)}, f32[152,128]{1,0:T(8,128)S(1)}, u32[]{:S(2)}, u32[]{:S(2)}) %collective-permute-start.2) | collective-permute-done | bytes 77856 | tf_op jit(solution)/shard_map/ppermute | solution.py:771
  14.9 0.2 %faces.1.m_ref = f32[24,128]{1,0:T(8,128)S(1)} custom-call(f32[128,128]{1,0:T(8,128)S(1)} %get-tuple-element.36.own_ref, f32[72,128]{1,0:T(8,128)S(1)} %get-tuple-element.58.kept_ref, f32[152,128]{1,0:T(8,128)S(1)} %collective-permute-done.2.b2_ref.r2_ref, f32[88,128]{1,0:T(8,128)S(1)} %collective-permute-done.3.b1_ref.r1_ref, ...), custom_call_target="tpu_custom_call" | custom-call | tf_op jit(solution)/shard_map/faces/pallas_call | solution.py:423
  15.2 0.1 collective-permute-start.7
  15.3 0.0 collective-permute-done.6.last_ref
  15.3 0.0 collective-permute-done.4.one_ref
  15.3 0.0 collective-permute-done.5.two_ref
  15.3 1.9 %fine.1 = (f32[1024,128]{1,0:T(8,128)S(1)}, f32[1024,128]{1,0:T(8,128)S(1)}, f32[1024,128]{1,0:T(8,128)S(1)}, f32[1024,128]{1,0:T(8,128)S(1)}, f32[768,128]{1,0:T(8,128)S(1)}, /*index=5*/f32[128,128]{1,0:T(8,128)S(1)}) custom-call(f32[288,128]{1,0:T(8,128)S(1)} %get-tuple-element.38.strip_ref, f32[152,128]{1,0:T(8,128)S(1)} %collective-permute-done.2.b2_ref.r2_ref, ...), custom_call_target="tpu_custom_call" | custom-call | flops 9830400 | bytes 3932160 | tf_op jit(solution)/shard_map/fine/pallas_call | solution.py:676
  17.2 0.0 collective-permute-done.7.r_ref
  17.2 1.3 %finish.1 = f32[768,128]{1,0:T(8,128)} custom-call(f32[1024,128]{1,0:T(8,128)S(1)} %get-tuple-element.52.cx_ref, f32[1024,128]{1,0:T(8,128)S(1)} %get-tuple-element.53.inv_ref, f32[1024,128]{1,0:T(8,128)S(1)} %get-tuple-element.54.q_ref, f32[1024,128]{1,0:T(8,128)S(1)} %get-tuple-element.55.v_ref, f32[768,128]{1,0:T(8,128)S(1)} %get-tuple-element.56.sum_ref, ...), custom_call_target="tpu_custom_call" | custom-call | tf_op jit(solution)/shard_map/finish/pallas_call | solution.py:751
Async XLA Ops:
  0.0 13.4 %copy-start = (f32[32,24,128]{2,1,0:T(8,128)S(1)}, f32[32,24,128]{2,1,0:T(8,128)}, u32[]{:S(2)}) copy-start(f32[32,24,128]{2,1,0:T(8,128)} %param.3) | copy-start | bytes 1179652
  0.0 13.4 %copy-start.1 = (f32[32,24,128]{2,1,0:T(8,128)S(1)}, f32[32,24,128]{2,1,0:T(8,128)}, u32[]{:S(2)}) copy-start(f32[32,24,128]{2,1,0:T(8,128)} %param.5) | copy-start | bytes 1179652
  2.3 5.7 %collective-permute-start = (f32[176,128]{1,0:T(8,128)S(1)}, f32[176,128]{1,0:T(8,128)S(1)}, u32[]{:S(2)}, u32[]{:S(2)}) collective-permute-start(f32[176,128]{1,0:T(8,128)S(1)} %get-tuple-element.34.q_ref), channel_id=1, source_target_pairs={{0,1},{1,0},{2,3},{3,2},{4,5},{5,4},{6,7},{7,6},{8,9},{9,8},{10,11... | collective-permute-start | bytes 270344 | tf_op jit(solution)/shard_map/ppermute | solution.py:771
  5.3 10.0 %collective-permute-start.6 = (f32[256,128]{1,0:T(8,128)S(1)}, f32[256,128]{1,0:T(8,128)S(1)}, u32[]{:S(2)}, u32[]{:S(2)}) collective-permute-start(f32[256,128]{1,0:T(8,128)S(1)} %get-tuple-element.43), channel_id=1, source_target_pairs={{0,2},{1,3},{2,4},{3,5},{4,6},{5,7},{6,8},{7,9},{8,10},{9,11},{10,... | collective-permute-start | bytes 393224 | tf_op jit(solution)/shard_map/ppermute | solution.py:771
  5.3 2.5 %collective-permute-start.1 = (f32[72,128]{1,0:T(8,128)S(1)}, f32[72,128]{1,0:T(8,128)S(1)}, u32[]{:S(2)}, u32[]{:S(2)}) collective-permute-start(f32[72,128]{1,0:T(8,128)S(1)} %get-tuple-element.35), channel_id=1, source_target_pairs={{0,2},{1,3},{2,0},{3,1},{4,6},{5,7},{6,4},{7,5},{8,10},{9,11},{10,... | collective-permute-start | bytes 110600 | tf_op jit(solution)/shard_map/ppermute | solution.py:771
  8.3 6.7 %collective-permute-start.2 = (f32[152,128]{1,0:T(8,128)S(1)}, f32[152,128]{1,0:T(8,128)S(1)}, u32[]{:S(2)}, u32[]{:S(2)}) collective-permute-start(f32[152,128]{1,0:T(8,128)S(1)} %get-tuple-element.39), channel_id=1, source_target_pairs={{0,30},{1,31},{2,4},{3,5},{4,2},{5,3},{6,8},{7,9},{8,6},{9,7},{10,... | collective-permute-start | bytes 233480 | tf_op jit(solution)/shard_map/ppermute | solution.py:771
  11.5 3.8 %collective-permute-start.4 = (f32[128,128]{1,0:T(8,128)S(1)}, f32[128,128]{1,0:T(8,128)S(1)}, u32[]{:S(2)}, u32[]{:S(2)}) collective-permute-start(f32[128,128]{1,0:T(8,128)S(1)} %get-tuple-element.41), channel_id=1, source_target_pairs={{0,30},{1,31},{2,0},{3,1},{4,2},{5,3},{6,4},{7,5},{8,6},{9,7},{10,... | collective-permute-start | bytes 196616 | tf_op jit(solution)/shard_map/ppermute | solution.py:771
  12.8 2.6 %collective-permute-start.5 = (f32[128,128]{1,0:T(8,128)S(1)}, f32[128,128]{1,0:T(8,128)S(1)}, u32[]{:S(2)}, u32[]{:S(2)}) collective-permute-start(f32[128,128]{1,0:T(8,128)S(1)} %get-tuple-element.42), channel_id=1, source_target_pairs={{0,30},{1,31},{2,0},{3,1},{4,2},{5,3},{6,4},{7,5},{8,6},{9,7},{10,... | collective-permute-start | bytes 196616 | tf_op jit(solution)/shard_map/ppermute | solution.py:771
  13.4 1.2 %collective-permute-start.3 = (f32[88,128]{1,0:T(8,128)S(1)}, f32[88,128]{1,0:T(8,128)S(1)}, u32[]{:S(2)}, u32[]{:S(2)}) collective-permute-start(f32[88,128]{1,0:T(8,128)S(1)} %get-tuple-element.40), channel_id=1, source_target_pairs={{0,2},{1,3},{2,0},{3,1},{4,6},{5,7},{6,4},{7,5},{8,10},{9,11},{10,... | collective-permute-start | bytes 135176 | tf_op jit(solution)/shard_map/ppermute | solution.py:771
  15.2 2.0 %collective-permute-start.7 = (f32[24,128]{1,0:T(8,128)S(1)}, f32[24,128]{1,0:T(8,128)S(1)}, u32[]{:S(2)}, u32[]{:S(2)}) collective-permute-start(f32[24,128]{1,0:T(8,128)S(1)} %faces.1.m_ref), channel_id=1, source_target_pairs={{0,2},{1,3},{2,0},{3,1},{4,6},{5,7},{6,4},{7,5},{8,10},{9,11},{10,... | collective-permute-start | bytes 36872 | tf_op jit(solution)/shard_map/ppermute | solution.py:771

commit v12 on v11

--- a/solution.py
+++ b/solution.py
@@ -29,6 +29,7 @@
 WIDTH = LANES // COARSEN
 SPREAD = 2 * WIDTH
 REACH = (COARSE_SWEEPS - 1) * COARSEN
+SPARE = 2 * REACH // WIDTH
 CELLS = COARSEN**3
 
 f32 = jnp.float32
@@ -179,7 +180,9 @@
         strips()
 
         base = zs * nx + SUB
+        within = part(lane, HALF)[1]
         for a, ref in enumerate((u_ref, c_ref)):
+            outer = []
             for Z in range(nz // SUB):
                 at = Z * SUB * nx
                 first, last = picked(ref, at, nx), picked(ref, at + nx - 1, nx)
@@ -187,10 +190,12 @@
                 own_ref[to : to + SUB] = first
                 own_ref[2 * nz + to : 2 * nz + to + SUB] = last
                 f1_ref[to : to + SUB] = jnp.where(even, last, first)
-                q_ref[base + to : base + to + SUB] = jnp.where(
-                    lane < HALF, rolled(first, REACH, 1), rolled(last, REACH + HALF, 1)
-                )
-        q_ref[base + 2 * nz : base + 2 * nz + SUB] = coarse
+                outer.append(jnp.where(lane < HALF, rolled(first, REACH, 1), rolled(last, REACH + HALF, 1)))
+            kept = outer.pop()
+            for k, tile_k in enumerate(outer):
+                to = base + (a * SPARE + k) * SUB
+                q_ref[to : to + SUB] = jnp.where(within < 2 * REACH, tile_k, rolled(kept, (SPARE - k) * WIDTH, 1))
+        q_ref[base + 2 * SPARE * SUB :] = coarse
         f1_ref[2 * nz :] = coarse
         corners = jnp.zeros((SUB, LANES), f32)
         group = part(lane, GROUP)[0]
@@ -211,7 +216,7 @@
     return pl.pallas_call(
         functools.partial(pack_kernel, nz=nz, nx=nx),
         out_shape=(
-            tiles(nz // ZS * nx // SUB + 2 * nz // SUB + 2),
+            tiles(nz // ZS * nx // SUB + 2 * SPARE + 2),
             tiles(2 * nz // SUB + 1),
             tiles(nz),
             tiles(nz // 2),
@@ -286,11 +291,24 @@
 
     source, target = zs * nx + SUB, 3 * half * SUB
     lower, outer = lane < HALF, part(lane, HALF)[1] < REACH
+    within = part(lane, HALF)[1]
+
+    def outer_columns(a, Z):
+        def sent(ref, k):
+            at = source + (a * SPARE + k) * SUB
+            return ref[at : at + SUB]
+
+        if Z < SPARE:
+            return jnp.where(outer, sent(ql_ref, Z), sent(qr_ref, Z))
+        out = rolled(sent(qr_ref, SPARE - 1), -WIDTH, 1)
+        for k in reversed(range(SPARE - 1)):
+            for ref, end in ((qr_ref, (k + 1) * WIDTH), (ql_ref, min(REACH, (k + 1) * WIDTH))):
+                if (ref is ql_ref or end > REACH) and k * WIDTH < REACH:
+                    out = jnp.where(within < end, rolled(sent(ref, k), (k - SPARE) * WIDTH, 1), out)
+        return out
+
     for Z in range(nz // SUB):
-        u, c = (
-            jnp.where(outer, ql_ref[at : at + SUB], qr_ref[at : at + SUB])
-            for at in (source + Z * SUB, source + nz + Z * SUB)
-        )
+        u, c = outer_columns(0, Z), outer_columns(1, Z)
         kept_ref[Z * SUB : (Z + 1) * SUB] = u
         kept_ref[nz + Z * SUB : nz + (Z + 1) * SUB] = c
         first, last = jnp.where(lower, u, rolled(c, HALF, 1)), jnp.where(lower, rolled(u, HALF, 1), c)
@@ -298,7 +316,7 @@
         b1_ref[to] = jnp.where(even, last, first)
         b2_ref[to] = jnp.where(even, first, last)
 
-    at = slice(source + 2 * nz, source + 2 * nz + SUB)
+    at = slice(source + 2 * SPARE * SUB, source + (2 * SPARE + 1) * SUB)
     place = part(lane, SPREAD)[1]
     window = jnp.where(
         place < RIM,

time: 18.7 us -> 18.6 us (level)
  no operation moved by 1% of the time
where the time goes in v12:
time: 18.6 us; the launch traced here: 18.5 us
  starting transfers between devices  9.93 us (53%)
  Pallas kernels  6.63 us (36%)
  waiting for transfers between devices  1.82 us (10%)
    ppermute x8, starting transfers between devices, send(): return lax.ppermute(x, ('gx', 'gy'), pairs)  9.93 us
    pallas_call x1, Pallas kernels, pack(): pl.pallas_call(functools.partial(pack_kernel, nz=nz, nx=nx), out_shape=(t...  2.3 us
    pallas_call x1, Pallas kernels, fine(): pl.pallas_call(functools.partial(fine_kernel, nz=nz, nx=nx), out_shape=(f...  1.85 us
    ppermute x8, waiting for transfers between devices, send(): return lax.ppermute(x, ('gx', 'gy'), pairs)  1.82 us
    pallas_call x1, Pallas kernels, finish(): pl.pallas_call(functools.partial(finish_kernel, nz=nz, nx=nx), out_shape=...  1.29 us
    pallas_call x1, Pallas kernels, begin(): pl.pallas_call(functools.partial(begin_kernel, nz=nz, nx=nx), out_shape=(...  0.59 us
  transfers between devices with their start and end apart: 8, of which 4 were waited for; matrix products, arithmetic and copies ran while one was open for 0% of the time, Pallas kernels for 16%

profile of v12, /device:TPU:0, one launch (start us, length us, event | category | flops | bytes accessed | tf_op | source)
XLA Modules:
  0.0 18.5 jit_solution(3222899737258247643)
XLA Ops:
  0.0 0.0 copy-start
  0.0 0.0 copy-start.1
  0.0 2.3 %pack.1 = (f32[160,128]{1,0:T(8,128)S(1)}, f32[72,128]{1,0:T(8,128)S(1)}, f32[256,128]{1,0:T(8,128)S(1)}, f32[128,128]{1,0:T(8,128)S(1)}, f32[128,128]{1,0:T(8,1...) custom-call(f32[768,128]{1,0:T(8,128)} %bitcast.4, f32[768,128]{1,0:T(8,128)} %bitcast.10, f32[768,128]{1,0:T(8,128)} %bitcast.7), custom_call_target="tpu_custom_call" | custom-call | tf_op jit(solution)/shard_map/pack/pallas_call | solution.py:216
  2.3 3.0 %collective-permute-start = (f32[160,128]{1,0:T(8,128)S(1)}, f32[160,128]{1,0:T(8,128)S(1)}, u32[]{:S(2)}, u32[]{:S(2)}) collective-permute-start(f32[160,128]{1,0:T(8,128)S(1)} %get-tuple-element.34.q_ref), channel_id=1, source_target_pairs={{0,1},{1,0},{2,3},{3,2},{4,5},{5,4},{6,7},{7,6},{8,9},{9,8},{10,11... | collective-permute-start | bytes 245768 | tf_op jit(solution)/shard_map/ppermute | solution.py:789
  5.3 0.0 collective-permute-start.6
  5.4 1.6 %collective-permute-start.1 = (f32[72,128]{1,0:T(8,128)S(1)}, f32[72,128]{1,0:T(8,128)S(1)}, u32[]{:S(2)}, u32[]{:S(2)}) collective-permute-start(f32[72,128]{1,0:T(8,128)S(1)} %get-tuple-element.35), channel_id=1, source_target_pairs={{0,2},{1,3},{2,0},{3,1},{4,6},{5,7},{6,4},{7,5},{8,10},{9,11},{10,... | collective-permute-start | bytes 110600 | tf_op jit(solution)/shard_map/ppermute | solution.py:789
  7.0 0.9 %collective-permute-done.1.f1_ref = f32[72,128]{1,0:T(8,128)S(1)} collective-permute-done((f32[72,128]{1,0:T(8,128)S(1)}, f32[72,128]{1,0:T(8,128)S(1)}, u32[]{:S(2)}, u32[]{:S(2)}) %collective-permute-start.1) | collective-permute-done | bytes 36896 | tf_op jit(solution)/shard_map/ppermute | solution.py:789
  7.8 0.0 collective-permute-done.ql_ref.qr_ref
  7.8 0.3 %join.1 = (f32[88,128]{1,0:T(8,128)S(1)}, f32[152,128]{1,0:T(8,128)S(1)}, f32[288,128]{1,0:T(8,128)S(1)}, f32[72,128]{1,0:T(8,128)S(1)}) custom-call(f32[160,128]{1,0:T(8,128)S(1)} %get-tuple-element.34.q_ref, f32[160,128]{1,0:T(8,128)S(1)} %collective-permute-done.ql_ref.qr_ref, f32[160,128]{1,0:T(8,128)S(1)} %collective-permute-done.ql_ref.qr_ref, ...), custom_call_target="tpu_custom_call" | custom-call | tf_op jit(solution)/shard_map/join/pallas_call | solution.py:360
  8.2 3.3 %collective-permute-start.2 = (f32[152,128]{1,0:T(8,128)S(1)}, f32[152,128]{1,0:T(8,128)S(1)}, u32[]{:S(2)}, u32[]{:S(2)}) collective-permute-start(f32[152,128]{1,0:T(8,128)S(1)} %get-tuple-element.39), channel_id=1, source_target_pairs={{0,30},{1,31},{2,4},{3,5},{4,2},{5,3},{6,8},{7,9},{8,6},{9,7},{10,... | collective-permute-start | bytes 233480 | tf_op jit(solution)/shard_map/ppermute | solution.py:789
  11.5 1.2 %collective-permute-start.4 = (f32[128,128]{1,0:T(8,128)S(1)}, f32[128,128]{1,0:T(8,128)S(1)}, u32[]{:S(2)}, u32[]{:S(2)}) collective-permute-start(f32[128,128]{1,0:T(8,128)S(1)} %get-tuple-element.41), channel_id=1, source_target_pairs={{0,30},{1,31},{2,0},{3,1},{4,2},{5,3},{6,4},{7,5},{8,6},{9,7},{10,... | collective-permute-start | bytes 196616 | tf_op jit(solution)/shard_map/ppermute | solution.py:789
  12.7 0.7 %collective-permute-start.5 = (f32[128,128]{1,0:T(8,128)S(1)}, f32[128,128]{1,0:T(8,128)S(1)}, u32[]{:S(2)}, u32[]{:S(2)}) collective-permute-start(f32[128,128]{1,0:T(8,128)S(1)} %get-tuple-element.42), channel_id=1, source_target_pairs={{0,30},{1,31},{2,0},{3,1},{4,2},{5,3},{6,4},{7,5},{8,6},{9,7},{10,... | collective-permute-start | bytes 196616 | tf_op jit(solution)/shard_map/ppermute | solution.py:789
  13.4 0.0 collective-permute-start.3
  13.4 0.0 copy-done
  13.4 0.0 copy-done.1
  13.4 0.6 %begin.1 = (f32[768,128]{1,0:T(8,128)S(1)}, f32[768,128]{1,0:T(8,128)S(1)}, f32[768,128]{1,0:T(8,128)S(1)}, f32[768,128]{1,0:T(8,128)S(1)}, f32[256,128]{1,0:T(8...) custom-call(f32[288,128]{1,0:T(8,128)S(1)} %get-tuple-element.38.strip_ref, f32[768,128]{1,0:T(8,128)S(1)} %bitcast.5, ...), custom_call_target="tpu_custom_call" | custom-call | flops 3932160 | bytes 3932160 | tf_op jit(solution)/shard_map/begin/pallas_call | solution.py:530
  14.0 0.6 %collective-permute-done.3.b1_ref.r1_ref = f32[88,128]{1,0:T(8,128)S(1)} collective-permute-done((f32[88,128]{1,0:T(8,128)S(1)}, f32[88,128]{1,0:T(8,128)S(1)}, u32[]{:S(2)}, u32[]{:S(2)}) %collective-permute-start.3) | collective-permute-done | bytes 45088 | tf_op jit(solution)/shard_map/ppermute | solution.py:789
  14.6 0.2 %collective-permute-done.2.b2_ref.r2_ref = f32[152,128]{1,0:T(8,128)S(1)} collective-permute-done((f32[152,128]{1,0:T(8,128)S(1)}, f32[152,128]{1,0:T(8,128)S(1)}, u32[]{:S(2)}, u32[]{:S(2)}) %collective-permute-start.2) | collective-permute-done | bytes 77856 | tf_op jit(solution)/shard_map/ppermute | solution.py:789
  14.9 0.2 %faces.1.m_ref = f32[24,128]{1,0:T(8,128)S(1)} custom-call(f32[128,128]{1,0:T(8,128)S(1)} %get-tuple-element.36.own_ref, f32[72,128]{1,0:T(8,128)S(1)} %get-tuple-element.58.kept_ref, f32[152,128]{1,0:T(8,128)S(1)} %collective-permute-done.2.b2_ref.r2_ref, f32[88,128]{1,0:T(8,128)S(1)} %collective-permute-done.3.b1_ref.r1_ref, ...), custom_call_target="tpu_custom_call" | custom-call | tf_op jit(solution)/shard_map/faces/pallas_call | solution.py:441
  15.1 0.1 collective-permute-start.7
  15.2 0.0 collective-permute-done.6.last_ref
  15.2 0.0 collective-permute-done.4.one_ref
  15.2 0.1 collective-permute-done.5.two_ref
  15.3 1.9 %fine.1 = (f32[1024,128]{1,0:T(8,128)S(1)}, f32[1024,128]{1,0:T(8,128)S(1)}, f32[1024,128]{1,0:T(8,128)S(1)}, f32[1024,128]{1,0:T(8,128)S(1)}, f32[768,128]{1,0:T(8,128)S(1)}, /*index=5*/f32[128,128]{1,0:T(8,128)S(1)}) custom-call(f32[288,128]{1,0:T(8,128)S(1)} %get-tuple-element.38.strip_ref, f32[152,128]{1,0:T(8,128)S(1)} %collective-permute-done.2.b2_ref.r2_ref, ...), custom_call_target="tpu_custom_call" | custom-call | flops 9830400 | bytes 3932160 | tf_op jit(solution)/shard_map/fine/pallas_call | solution.py:694
  17.2 0.0 collective-permute-done.7.r_ref
  17.2 1.3 %finish.1 = f32[768,128]{1,0:T(8,128)} custom-call(f32[1024,128]{1,0:T(8,128)S(1)} %get-tuple-element.52.cx_ref, f32[1024,128]{1,0:T(8,128)S(1)} %get-tuple-element.53.inv_ref, f32[1024,128]{1,0:T(8,128)S(1)} %get-tuple-element.54.q_ref, f32[1024,128]{1,0:T(8,128)S(1)} %get-tuple-element.55.v_ref, f32[768,128]{1,0:T(8,128)S(1)} %get-tuple-element.56.sum_ref, ...), custom_call_target="tpu_custom_call" | custom-call | tf_op jit(solution)/shard_map/finish/pallas_call | solution.py:769
Async XLA Ops:
  0.0 13.4 %copy-start = (f32[32,24,128]{2,1,0:T(8,128)S(1)}, f32[32,24,128]{2,1,0:T(8,128)}, u32[]{:S(2)}) copy-start(f32[32,24,128]{2,1,0:T(8,128)} %param.3) | copy-start | bytes 1179652
  0.0 13.4 %copy-start.1 = (f32[32,24,128]{2,1,0:T(8,128)S(1)}, f32[32,24,128]{2,1,0:T(8,128)}, u32[]{:S(2)}) copy-start(f32[32,24,128]{2,1,0:T(8,128)} %param.5) | copy-start | bytes 1179652
  2.3 5.5 %collective-permute-start = (f32[160,128]{1,0:T(8,128)S(1)}, f32[160,128]{1,0:T(8,128)S(1)}, u32[]{:S(2)}, u32[]{:S(2)}) collective-permute-start(f32[160,128]{1,0:T(8,128)S(1)} %get-tuple-element.34.q_ref), channel_id=1, source_target_pairs={{0,1},{1,0},{2,3},{3,2},{4,5},{5,4},{6,7},{7,6},{8,9},{9,8},{10,11... | collective-permute-start | bytes 245768 | tf_op jit(solution)/shard_map/ppermute | solution.py:789
  5.3 9.9 %collective-permute-start.6 = (f32[256,128]{1,0:T(8,128)S(1)}, f32[256,128]{1,0:T(8,128)S(1)}, u32[]{:S(2)}, u32[]{:S(2)}) collective-permute-start(f32[256,128]{1,0:T(8,128)S(1)} %get-tuple-element.43), channel_id=1, source_target_pairs={{0,2},{1,3},{2,4},{3,5},{4,6},{5,7},{6,8},{7,9},{8,10},{9,11},{10,... | collective-permute-start | bytes 393224 | tf_op jit(solution)/shard_map/ppermute | solution.py:789
  5.4 2.5 %collective-permute-start.1 = (f32[72,128]{1,0:T(8,128)S(1)}, f32[72,128]{1,0:T(8,128)S(1)}, u32[]{:S(2)}, u32[]{:S(2)}) collective-permute-start(f32[72,128]{1,0:T(8,128)S(1)} %get-tuple-element.35), channel_id=1, source_target_pairs={{0,2},{1,3},{2,0},{3,1},{4,6},{5,7},{6,4},{7,5},{8,10},{9,11},{10,... | collective-permute-start | bytes 110600 | tf_op jit(solution)/shard_map/ppermute | solution.py:789
  8.2 6.7 %collective-permute-start.2 = (f32[152,128]{1,0:T(8,128)S(1)}, f32[152,128]{1,0:T(8,128)S(1)}, u32[]{:S(2)}, u32[]{:S(2)}) collective-permute-start(f32[152,128]{1,0:T(8,128)S(1)} %get-tuple-element.39), channel_id=1, source_target_pairs={{0,30},{1,31},{2,4},{3,5},{4,2},{5,3},{6,8},{7,9},{8,6},{9,7},{10,... | collective-permute-start | bytes 233480 | tf_op jit(solution)/shard_map/ppermute | solution.py:789
  11.5 3.7 %collective-permute-start.4 = (f32[128,128]{1,0:T(8,128)S(1)}, f32[128,128]{1,0:T(8,128)S(1)}, u32[]{:S(2)}, u32[]{:S(2)}) collective-permute-start(f32[128,128]{1,0:T(8,128)S(1)} %get-tuple-element.41), channel_id=1, source_target_pairs={{0,30},{1,31},{2,0},{3,1},{4,2},{5,3},{6,4},{7,5},{8,6},{9,7},{10,... | collective-permute-start | bytes 196616 | tf_op jit(solution)/shard_map/ppermute | solution.py:789
  12.7 2.6 %collective-permute-start.5 = (f32[128,128]{1,0:T(8,128)S(1)}, f32[128,128]{1,0:T(8,128)S(1)}, u32[]{:S(2)}, u32[]{:S(2)}) collective-permute-start(f32[128,128]{1,0:T(8,128)S(1)} %get-tuple-element.42), channel_id=1, source_target_pairs={{0,30},{1,31},{2,0},{3,1},{4,2},{5,3},{6,4},{7,5},{8,6},{9,7},{10,... | collective-permute-start | bytes 196616 | tf_op jit(solution)/shard_map/ppermute | solution.py:789
  13.4 1.2 %collective-permute-start.3 = (f32[88,128]{1,0:T(8,128)S(1)}, f32[88,128]{1,0:T(8,128)S(1)}, u32[]{:S(2)}, u32[]{:S(2)}) collective-permute-start(f32[88,128]{1,0:T(8,128)S(1)} %get-tuple-element.40), channel_id=1, source_target_pairs={{0,2},{1,3},{2,0},{3,1},{4,6},{5,7},{6,4},{7,5},{8,10},{9,11},{10,... | collective-permute-start | bytes 135176 | tf_op jit(solution)/shard_map/ppermute | solution.py:789
  15.1 2.0 %collective-permute-start.7 = (f32[24,128]{1,0:T(8,128)S(1)}, f32[24,128]{1,0:T(8,128)S(1)}, u32[]{:S(2)}, u32[]{:S(2)}) collective-permute-start(f32[24,128]{1,0:T(8,128)S(1)} %faces.1.m_ref), channel_id=1, source_target_pairs={{0,2},{1,3},{2,0},{3,1},{4,6},{5,7},{6,4},{7,5},{8,10},{9,11},{10,... | collective-permute-start | bytes 36872 | tf_op jit(solution)/shard_map/ppermute | solution.py:789
